TPU v7x, 32 devices: a whole 2x2x4 slice. The times are simulated.
32 devices in a mesh: dp: 8 (over z, x), head: 4 (over y, core).
Axes of the slice: x: 2, y: 2, z: 4, core: 2. Of those that a mesh axis runs over, the one named last changes fastest.
Arguments:
- post_in: float32 [16384, 512], P(('dp', 'head')), may hold values from -6 to 6
- dual_in: float32 [16384, 512], P(('dp', 'head')), may hold values from -6 to 6
- segment_ids: int32 [8, 2048], P('dp'), may hold values from 0 to 7, never falling along the last dimension, each value on 1 to 1024 neighbouring positions
- post_cot: float32 [16384, 512], P(('dp', 'head')), may hold values from -6 to 6
- dual_cot: float32 [16384, 512], P(('dp', 'head')), may hold values from -6 to 6
- attend_weight: float32 [512, 1536], P('dp', 'head'), may hold values from -0.25 to 0.25
- output_weight: float32 [512, 512], P('head', 'dp'), may hold values from -1 to 1
- expand_weight: float32 [512, 2048], P('dp', 'head'), may hold values from -0.25 to 0.25
- contract_weight: float32 [2048, 512], P('head', 'dp'), may hold values from -0.125 to 0.125
- head_bias: float32 [8, 384], P('head', 'dp'), may hold values from -4 to 4
- norm_params: float32 [6, 512], replicated, may hold values from -1.2 to 1.6, as said below
- attend_momentum: float32 [512, 1536], P('dp', 'head'), may hold values from -0.0048828125 to 0.0048828125
- output_momentum: float32 [512, 512], P('head', 'dp'), may hold values from -0.0048828125 to 0.0048828125
- expand_momentum: float32 [512, 2048], P('dp', 'head'), may hold values from -0.0048828125 to 0.0048828125
- contract_momentum: float32 [2048, 512], P('head', 'dp'), may hold values from -0.0048828125 to 0.0048828125
- bias_momentum: float32 [8, 384], P('head', 'dp'), may hold values from -0.01953125 to 0.01953125
- norm_momentum: float32 [6, 512], replicated, may hold values from -0.0048828125 to 0.0048828125
- attend_variance: float32 [512, 1536], P('dp', 'head'), may hold values from 7.138615e-07 to 2.855446e-06
- output_variance: float32 [512, 512], P('head', 'dp'), may hold values from 7.138615e-07 to 2.855446e-06
- expand_variance: float32 [512, 2048], P('dp', 'head'), may hold values from 7.138615e-07 to 2.855446e-06
- contract_variance: float32 [2048, 512], P('head', 'dp'), may hold values from 7.138615e-07 to 2.855446e-06
- bias_variance: float32 [8, 384], P('head', 'dp'), may hold values from 1.1421784e-05 to 4.5687135e-05
- norm_variance: float32 [6, 512], replicated, may hold values from 3.1727177e-07 to 1.2690871e-06
- clip_limit: float32 [1], replicated, may hold values from 1 to 2
Outputs:
- post_out: float32 [16384, 512], P(('dp', 'head'))
- dual_out: float32 [16384, 512], P(('dp', 'head'))
- post_grad: float32 [16384, 512], P(('dp', 'head'))
- grad_norm: float32 [1], replicated
- attend_momentum_new: float32 [512, 1536], P('dp', 'head')
- attend_variance_new: float32 [512, 1536], P('dp', 'head')
- attend_master_new: float32 [512, 1536], P('dp', 'head')
- attend_copy_new: bfloat16 [512, 1536], P('dp', 'head')
- output_momentum_new: float32 [512, 512], P('head', 'dp')
- output_variance_new: float32 [512, 512], P('head', 'dp')
- output_master_new: float32 [512, 512], P('head', 'dp')
- output_copy_new: bfloat16 [512, 512], P('head', 'dp')
- expand_momentum_new: float32 [512, 2048], P('dp', 'head')
- expand_variance_new: float32 [512, 2048], P('dp', 'head')
- expand_master_new: float32 [512, 2048], P('dp', 'head')
- expand_copy_new: bfloat16 [512, 2048], P('dp', 'head')
- contract_momentum_new: float32 [2048, 512], P('head', 'dp')
- contract_variance_new: float32 [2048, 512], P('head', 'dp')
- contract_master_new: float32 [2048, 512], P('head', 'dp')
- contract_copy_new: bfloat16 [2048, 512], P('head', 'dp')
- bias_momentum_new: float32 [8, 384], P('head', 'dp')
- bias_variance_new: float32 [8, 384], P('head', 'dp')
- bias_master_new: float32 [8, 384], P('head', 'dp')
- bias_copy_new: bfloat16 [8, 384], P('head', 'dp')
- norm_momentum_new: float32 [6, 512], replicated
- norm_variance_new: float32 [6, 512], replicated
- norm_master_new: float32 [6, 512], replicated
- norm_clipped: float32 [6, 512], replicated
Inputs may be any that keep to these rules, and one draw needn't show every extreme that they name: `segment_ids`: within each group the document numbers never fall; each document has 1 to 1024 tokens, and one has exactly 1024. `norm_params`: rows 0 and 3 are gains near 1; the other rows are biases near 0.
All inputs are finite; a program needn't handle non-finite values.
Results may differ from a plain program's by a relative error of at most 0.035.
The roundings to bfloat16 on the way count: a program that leaves them out, or rounds other values in their place, can miss the bound.
Values may be sent and summed in bfloat16 or wider, within the bound.
No kernel may reach another device: no remote copies, remote signals or barrier semaphores. Data moves between devices by JAX's collectives and lax.ppermute only.
A program may use at most 128 MiB of HBM per device.

v0:
```python
import jax
import jax.numpy as jnp
from jax import lax
from jax.sharding import PartitionSpec as P

D = 512
HEADS = 8
QBLK = 512


EPS_NORM = 1e-05
NEG_LARGE = -1e30
RATE_ATTEND = 0.04
RATE_OUTPUT = 0.12
RATE_EXPAND = 0.04
RATE_CONTRACT = 0.04
RATE_BIAS = 0.16
RATE_NORM = 0.3
DECAY = 0.01
ADAM_EPS = 1e-08
BETA = 0.5
BIAS_CORRECTION = 0.875


def layer_norm(stream_rows, gain_row, shift_row):
    row_mean = jnp.mean(stream_rows, axis=-1, keepdims=True)
    centered = stream_rows - row_mean
    row_var = jnp.mean(centered * centered, axis=-1, keepdims=True)
    return centered * lax.rsqrt(row_var + EPS_NORM) * gain_row + shift_row


def adam_update(master, momentum, variance, gradient, factor, correction, rate):
    clipped = factor * gradient
    momentum_new = BETA * momentum + (1.0 - BETA) * clipped
    variance_new = BETA * variance + (1.0 - BETA) * clipped * clipped
    master_new = master - rate * (
        momentum_new / correction / (jnp.sqrt(variance_new / correction) + ADAM_EPS)
        + DECAY * master
    )
    return (momentum_new, variance_new, master_new)


def per_device(
    post_in,
    dual_in,
    segment_ids,
    post_cot,
    dual_cot,
    attend_weight,
    output_weight,
    expand_weight,
    contract_weight,
    head_bias,
    norm_params,
    attend_momentum,
    output_momentum,
    expand_momentum,
    contract_momentum,
    bias_momentum,
    norm_momentum,
    attend_variance,
    output_variance,
    expand_variance,
    contract_variance,
    bias_variance,
    norm_variance,
    clip_limit,
):
    head_dim = D // HEADS
    score_scale = head_dim ** (-0.5)
    copy_attend, copy_output, copy_expand, copy_contract, copy_bias = (
        lax.all_gather(attend_weight.astype(jnp.bfloat16), "dp", axis=0, tiled=True),
        lax.all_gather(output_weight.astype(jnp.bfloat16), "dp", axis=1, tiled=True),
        lax.all_gather(expand_weight.astype(jnp.bfloat16), "dp", axis=0, tiled=True),
        lax.all_gather(contract_weight.astype(jnp.bfloat16), "dp", axis=1, tiled=True),
        lax.all_gather(head_bias.astype(jnp.bfloat16), "dp", axis=1, tiled=True),
    )
    local_heads = copy_bias.shape[0]
    bias_rows = copy_bias.astype(jnp.float32)
    query_bias = bias_rows[:, :head_dim]
    value_bias = bias_rows[:, head_dim : 2 * head_dim]
    inner_bias = bias_rows[:, 2 * head_dim :].reshape(-1)
    segment = segment_ids[0]
    first_rows = lax.all_gather(post_in.astype(jnp.bfloat16), "head", axis=0, tiled=True)
    row_count = first_rows.shape[0]
    positions = jnp.arange(row_count, dtype=jnp.int32)
    starts = jnp.arange(row_count // QBLK, dtype=jnp.int32) * QBLK

    def project_qkv(inputs):
        qkv_rows = jnp.dot(inputs, copy_attend, preferred_element_type=jnp.float32).reshape(
            row_count, local_heads, 3, head_dim
        )
        queries = (qkv_rows[:, :, 0] + query_bias).astype(jnp.bfloat16)
        key_rows = qkv_rows[:, :, 1].astype(jnp.bfloat16)
        values = (qkv_rows[:, :, 2] + value_bias).astype(jnp.bfloat16)
        return (queries, key_rows, values)

    def block_scores(queries, key_rows, offset):
        query_block = lax.dynamic_slice_in_dim(queries, offset, QBLK, 0)
        query_seg = lax.dynamic_slice_in_dim(segment, offset, QBLK, 0)
        query_pos = offset + jnp.arange(QBLK, dtype=jnp.int32)
        scores = (
            jnp.einsum("qhe,khe->hqk", query_block, key_rows, preferred_element_type=jnp.float32)
            * score_scale
        )
        allowed = (query_seg[:, None] == segment[None, :]) & (
            positions[None, :] <= query_pos[:, None]
        )
        return (jnp.where(allowed[None], scores, NEG_LARGE), query_block)

    def inner_layer(inputs):
        pre_rows = jnp.dot(inputs, copy_expand, preferred_element_type=jnp.float32) + inner_bias
        return (pre_rows, jnp.where(pre_rows > 0, pre_rows, 0.0).astype(jnp.bfloat16))

    queries, key_rows, values = project_qkv(first_rows)

    def attend_one(offset):
        scores, query_block = block_scores(queries, key_rows, offset)
        row_top = jnp.max(scores, axis=-1, keepdims=True)
        exponent = jnp.exp(scores - row_top)
        row_total = jnp.sum(exponent, axis=-1, keepdims=True)
        attn_probs = (exponent / row_total).astype(jnp.bfloat16)
        block_out = jnp.einsum(
            "hqk,khe->qhe", attn_probs, values, preferred_element_type=jnp.float32
        ).astype(jnp.bfloat16)
        return (block_out, row_top[..., 0] + jnp.log(row_total[..., 0]))

    block_outs, log_sums = lax.map(attend_one, starts)
    attn_mixed = block_outs.reshape(row_count, local_heads * head_dim)
    attn_out = (
        lax.psum_scatter(
            jnp.dot(attn_mixed, copy_output, preferred_element_type=jnp.float32),
            "head",
            scatter_dimension=0,
            tiled=True,
        )
        + norm_params[2]
    )
    post_norm, norm_pull_one = jax.vjp(
        layer_norm, post_in + attn_out, norm_params[0], norm_params[1]
    )
    second_rows = lax.all_gather(post_norm.astype(jnp.bfloat16), "head", axis=0, tiled=True)
    hidden_pre, hidden = inner_layer(second_rows)
    ffn_out = (
        lax.psum_scatter(
            jnp.dot(hidden, copy_contract, preferred_element_type=jnp.float32),
            "head",
            scatter_dimension=0,
            tiled=True,
        )
        + norm_params[5]
    )
    post_out, norm_pull_two = jax.vjp(
        layer_norm, post_norm + ffn_out, norm_params[3], norm_params[4]
    )
    dual_out = dual_in + attn_out + ffn_out
    grad_mid2, grad_gain2, grad_shift2 = norm_pull_two(post_cot)
    grad_ffn = grad_mid2 + dual_cot
    second_used, grad_ffn_rows = (
        lax.all_gather(post_norm.astype(jnp.bfloat16), "head", axis=0, tiled=True),
        lax.all_gather(grad_ffn.astype(jnp.bfloat16), "head", axis=0, tiled=True),
    )
    hidden_pre, hidden = inner_layer(second_used)
    grad_hidden = jnp.dot(grad_ffn_rows, copy_contract.T, preferred_element_type=jnp.float32)
    grad_contract = jnp.dot(hidden.T, grad_ffn_rows, preferred_element_type=jnp.float32)
    grad_pre = jnp.where(hidden_pre > 0, grad_hidden, 0.0).astype(jnp.bfloat16)
    grad_inner_bias = jnp.sum(grad_pre.astype(jnp.float32), axis=0)
    grad_expand = jnp.dot(second_used.T, grad_pre, preferred_element_type=jnp.float32)
    grad_norm_rows = lax.psum_scatter(
        jnp.dot(grad_pre, copy_expand.T, preferred_element_type=jnp.float32),
        "head",
        scatter_dimension=0,
        tiled=True,
    )
    grad_mid1, grad_gain1, grad_shift1 = norm_pull_one(grad_mid2 + grad_norm_rows)
    grad_attn = grad_mid1 + dual_cot
    first_used, grad_attn_rows = (
        lax.all_gather(post_in.astype(jnp.bfloat16), "head", axis=0, tiled=True),
        lax.all_gather(grad_attn.astype(jnp.bfloat16), "head", axis=0, tiled=True),
    )
    queries, key_rows, values = project_qkv(first_used)
    grad_output = jnp.dot(attn_mixed.T, grad_attn_rows, preferred_element_type=jnp.float32)
    grad_mixed = (
        jnp.dot(grad_attn_rows, copy_output.T, preferred_element_type=jnp.float32)
        .astype(jnp.bfloat16)
        .reshape(row_count, local_heads, head_dim)
    )

    def back_block(running, scan_item):
        grad_keys, grad_values = running
        offset, log_sum = scan_item
        scores, query_block = block_scores(queries, key_rows, offset)
        attn_probs = jnp.exp(scores - log_sum[..., None])
        grad_block = lax.dynamic_slice_in_dim(grad_mixed, offset, QBLK, 0)
        grad_probs = jnp.einsum(
            "qhe,khe->hqk", grad_block, values, preferred_element_type=jnp.float32
        )
        row_delta = jnp.sum(attn_probs * grad_probs, axis=-1, keepdims=True)
        grad_scores = (attn_probs * (grad_probs - row_delta)).astype(jnp.bfloat16)
        grad_query_block = (
            jnp.einsum("hqk,khe->qhe", grad_scores, key_rows, preferred_element_type=jnp.float32)
            * score_scale
        )
        grad_keys = (
            grad_keys
            + jnp.einsum(
                "hqk,qhe->khe", grad_scores, query_block, preferred_element_type=jnp.float32
            )
            * score_scale
        )
        grad_values = grad_values + jnp.einsum(
            "hqk,qhe->khe",
            attn_probs.astype(jnp.bfloat16),
            grad_block,
            preferred_element_type=jnp.float32,
        )
        return ((grad_keys, grad_values), grad_query_block)

    zero_grad = jnp.zeros((row_count, local_heads, head_dim), jnp.float32)
    (grad_keys, grad_values), grad_queries = lax.scan(
        back_block, (zero_grad, zero_grad), (starts, log_sums)
    )
    grad_queries = grad_queries.reshape(row_count, local_heads, head_dim).astype(jnp.bfloat16)
    grad_keys = grad_keys.astype(jnp.bfloat16)
    grad_values = grad_values.astype(jnp.bfloat16)
    grad_qkv = jnp.stack([grad_queries, grad_keys, grad_values], axis=2).reshape(
        row_count, local_heads * 3 * head_dim
    )
    grad_attend = jnp.dot(first_used.T, grad_qkv, preferred_element_type=jnp.float32)
    grad_rows = lax.psum_scatter(
        jnp.dot(grad_qkv, copy_attend.T, preferred_element_type=jnp.float32).astype(jnp.bfloat16),
        "head",
        scatter_dimension=0,
        tiled=True,
    ).astype(jnp.float32)
    post_grad = grad_mid1 + grad_rows
    grad_bias = jnp.concatenate(
        [
            jnp.sum(grad_queries.astype(jnp.float32), axis=0),
            jnp.sum(grad_values.astype(jnp.float32), axis=0),
            grad_inner_bias.reshape(local_heads, -1),
        ],
        axis=1,
    )
    summed = (
        lax.psum(grad_attend.astype(jnp.bfloat16), "dp").astype(jnp.float32),
        lax.psum(grad_output.astype(jnp.bfloat16), "dp").astype(jnp.float32),
        lax.psum(grad_expand.astype(jnp.bfloat16), "dp").astype(jnp.float32),
        lax.psum(grad_contract.astype(jnp.bfloat16), "dp").astype(jnp.float32),
        lax.psum(grad_bias.astype(jnp.bfloat16), "dp").astype(jnp.float32),
    )
    dp_count = lax.axis_size("dp")
    dp_index = lax.axis_index("dp")
    share_attend = lax.dynamic_slice_in_dim(
        summed[0], dp_index * (summed[0].shape[0] // dp_count), summed[0].shape[0] // dp_count, 0
    )
    share_output = lax.dynamic_slice_in_dim(
        summed[1], dp_index * (summed[1].shape[1] // dp_count), summed[1].shape[1] // dp_count, 1
    )
    share_expand = lax.dynamic_slice_in_dim(
        summed[2], dp_index * (summed[2].shape[0] // dp_count), summed[2].shape[0] // dp_count, 0
    )
    share_contract = lax.dynamic_slice_in_dim(
        summed[3], dp_index * (summed[3].shape[1] // dp_count), summed[3].shape[1] // dp_count, 1
    )
    share_bias = lax.dynamic_slice_in_dim(
        summed[4], dp_index * (summed[4].shape[1] // dp_count), summed[4].shape[1] // dp_count, 1
    )
    own_squares = (
        jnp.sum(share_attend * share_attend)
        + jnp.sum(share_output * share_output)
        + jnp.sum(share_expand * share_expand)
        + jnp.sum(share_contract * share_contract)
        + jnp.sum(share_bias * share_bias)
    )
    norm_part = jnp.stack(
        [
            grad_gain1,
            grad_shift1,
            jnp.sum(grad_attn, axis=0),
            grad_gain2,
            grad_shift2,
            jnp.sum(grad_ffn, axis=0),
        ]
    )
    norm_grads, total_squares = lax.psum((norm_part, own_squares), ("dp", "head"))
    total_norm = jnp.sqrt(total_squares + jnp.sum(norm_grads * norm_grads))
    factor = clip_limit[0] / jnp.maximum(total_norm, clip_limit[0])
    correction = BIAS_CORRECTION
    attend_m, attend_v, attend_w = adam_update(
        attend_weight,
        attend_momentum,
        attend_variance,
        share_attend,
        factor,
        correction,
        RATE_ATTEND,
    )
    output_m, output_v, output_w = adam_update(
        output_weight,
        output_momentum,
        output_variance,
        share_output,
        factor,
        correction,
        RATE_OUTPUT,
    )
    expand_m, expand_v, expand_w = adam_update(
        expand_weight,
        expand_momentum,
        expand_variance,
        share_expand,
        factor,
        correction,
        RATE_EXPAND,
    )
    contract_m, contract_v, contract_w = adam_update(
        contract_weight,
        contract_momentum,
        contract_variance,
        share_contract,
        factor,
        correction,
        RATE_CONTRACT,
    )
    bias_m, bias_v, bias_w = adam_update(
        head_bias, bias_momentum, bias_variance, share_bias, factor, correction, RATE_BIAS
    )
    norm_m, norm_v, norm_w = adam_update(
        norm_params, norm_momentum, norm_variance, norm_grads, factor, correction, RATE_NORM
    )
    norm_clipped = factor * norm_grads
    return (
        post_out,
        dual_out,
        post_grad,
        total_norm.reshape(1),
        attend_m,
        attend_v,
        attend_w,
        attend_w.astype(jnp.bfloat16),
        output_m,
        output_v,
        output_w,
        output_w.astype(jnp.bfloat16),
        expand_m,
        expand_v,
        expand_w,
        expand_w.astype(jnp.bfloat16),
        contract_m,
        contract_v,
        contract_w,
        contract_w.astype(jnp.bfloat16),
        bias_m,
        bias_v,
        bias_w,
        bias_w.astype(jnp.bfloat16),
        norm_m,
        norm_v,
        norm_w,
        norm_clipped,
    )


def solution(mesh):
    in_specs = (
        P(("dp", "head"), None),
        P(("dp", "head"), None),
        P("dp", None),
        P(("dp", "head"), None),
        P(("dp", "head"), None),
        P("dp", "head"),
        P("head", "dp"),
        P("dp", "head"),
        P("head", "dp"),
        P("head", "dp"),
        P(),
        P("dp", "head"),
        P("head", "dp"),
        P("dp", "head"),
        P("head", "dp"),
        P("head", "dp"),
        P(),
        P("dp", "head"),
        P("head", "dp"),
        P("dp", "head"),
        P("head", "dp"),
        P("head", "dp"),
        P(),
        P(),
    )
    out_specs = (
        P(("dp", "head"), None),
        P(("dp", "head"), None),
        P(("dp", "head"), None),
        P(),
        P("dp", "head"),
        P("dp", "head"),
        P("dp", "head"),
        P("dp", "head"),
        P("head", "dp"),
        P("head", "dp"),
        P("head", "dp"),
        P("head", "dp"),
        P("dp", "head"),
        P("dp", "head"),
        P("dp", "head"),
        P("dp", "head"),
        P("head", "dp"),
        P("head", "dp"),
        P("head", "dp"),
        P("head", "dp"),
        P("head", "dp"),
        P("head", "dp"),
        P("head", "dp"),
        P("head", "dp"),
        P(),
        P(),
        P(),
        P(),
    )
    return jax.shard_map(
        per_device, mesh=mesh, in_specs=in_specs, out_specs=out_specs, check_vma=False
    )
```

profile of v0, /device:TPU:0, one launch (start us, length us, event | category | flops | bytes accessed | tf_op | source)
XLA Modules:
  0.0 674.9 jit_solution(18120549515253987965)
XLA Ops:
  10.1 22.1 %all-gather = bf16[8,48,2]{1,2,0:T(2,128)(2,1)S(1)} all-gather(bf16[1,48,2]{1,2,0:T(2,128)(2,1)S(1)} %convert_bitcast_fusion.2), channel_id=1, replica_groups=mesh['dp'=8,'head'=4] {'dp'}, dimensions={0}, use_global_device_ids=true | all-gather | bytes 1728 | tf_op jit(solution)/shard_map/all_gather | solution.py:76
  34.0 30.5 %all_gather.32 = bf16[128,512]{0,1:T(8,128)(2,1)S(1)} all-gather(bf16[128,64]{0,1:T(8,128)(2,1)S(1)} %convert_element_type.159), channel_id=1, replica_groups=mesh['dp'=8,'head'=4] {'dp'}, dimensions={1}, use_global_device_ids=true | all-gather | bytes 147456 | tf_op jit(solution)/shard_map/all_gather | solution.py:73
  64.5 30.9 %all_gather.30 = bf16[512,384]{1,0:T(8,128)(2,1)S(1)} all-gather(bf16[64,384]{1,0:T(8,128)(2,1)S(1)} %convert_element_type.153), channel_id=1, replica_groups=mesh['dp'=8,'head'=4] {'dp'}, dimensions={0}, use_global_device_ids=true | all-gather | bytes 442368 | tf_op jit(solution)/shard_map/all_gather | solution.py:72
  95.5 2.7 fusion.93
  98.9 49.5 %while.28 = (s32[]{:T(128)}, bf16[4,512,2,64]{1,3,2,0:T(8,128)(2,1)S(1)}, f32[4,2,512]{2,1,0:T(2,128)}, s32[4]{0:T(128)S(1)}, s32[2048]{0:T(1024)S(1)}, /*index=...) while((s32[]{:T(128)}, ...), condition=%wide.region_3.4_spmd.clone, body=%wide.region_0.3_spmd.clone.sunk | while | flops 565247488 | bytes 30722240 | solution.py:128
  105.5 2.5 fusion.151
  108.0 2.7 fusion.152
  117.9 2.5 fusion.151
  120.4 2.7 fusion.152
  130.3 2.5 fusion.151
  132.8 2.7 fusion.152
  142.6 2.5 fusion.151
  145.2 2.7 fusion.152
  149.8 2.7 fusion.94
  153.2 41.2 %reduce-scatter.5.cloned.1.call-done = f32[512,512]{1,0:T(8,128)} async-done(((f32[2048,512]{1,0:T(8,128)}), f32[512,512]{1,0:T(8,128)}) %reduce-scatter.5.cloned.1.call-update) | async-done | bytes 1048592 | tf_op jit(solution)/shard_map/reduce_scatter | solution.py:131
  198.6 31.4 %all_gather.35 = bf16[512,512]{0,1:T(8,128)(2,1)S(1)} all-gather(bf16[512,64]{0,1:T(8,128)(2,1)S(1)} %convert_element_type.163), channel_id=1, replica_groups=mesh['dp'=8,'head'=4] {'dp'}, dimensions={1}, use_global_device_ids=true | all-gather | bytes 589824 | tf_op jit(solution)/shard_map/all_gather | solution.py:75
  230.0 31.4 %all_gather.34 = bf16[512,512]{1,0:T(8,128)(2,1)S(1)} all-gather(bf16[64,512]{1,0:T(8,128)(2,1)S(1)} %convert_element_type.161), channel_id=1, replica_groups=mesh['dp'=8,'head'=4] {'dp'}, dimensions={0}, use_global_device_ids=true | all-gather | bytes 589824 | tf_op jit(solution)/shard_map/all_gather | solution.py:74
  261.4 3.0 fusion.95
  266.4 3.3 fusion.53
  269.7 44.8 %reduce-scatter.7.cloned.1.call-done = f32[512,512]{1,0:T(8,128)} async-done(((f32[2048,512]{1,0:T(8,128)}), f32[512,512]{1,0:T(8,128)}) %reduce-scatter.7.cloned.1.call-update) | async-done | bytes 1048592 | tf_op jit(solution)/shard_map/reduce_scatter | solution.py:145
  314.5 3.4 fusion.87
  323.1 22.7 %all-gather.10.cloned.1.call-done = bf16[2048,512]{1,0:T(8,128)(2,1)} async-done(((bf16[512,512]{1,0:T(8,128)(2,1)}), bf16[2048,512]{1,0:T(8,128)(2,1)}) %all-gather.10.cloned.1.call-update) | async-done | bytes 2097168 | tf_op jit(solution)/shard_map/all_gather | solution.py:161
  345.8 5.0 fusion.92
  352.1 3.3 fusion.96
  355.5 44.6 %reduce-scatter.9.cloned.1.call-done = f32[512,512]{1,0:T(8,128)} async-done(((f32[2048,512]{1,0:T(8,128)}), f32[512,512]{1,0:T(8,128)}) %reduce-scatter.9.cloned.1.call-update) | async-done | bytes 1048592 | tf_op jit(solution)/shard_map/reduce_scatter | solution.py:169
  400.1 2.5 multiply_reduce_fusion.2
  404.4 2.5 fusion.55
  407.0 4.4 convolution_convert_fusion.3
  411.4 3.9 convolution_convert_fusion.2
  415.3 14.3 %all-gather.12.cloned.1.call-done = bf16[2048,512]{1,0:T(8,128)(2,1)} async-done(((bf16[512,512]{1,0:T(8,128)(2,1)}), bf16[2048,512]{1,0:T(8,128)(2,1)}) %all-gather.12.cloned.1.call-update) | async-done | bytes 2097168 | tf_op jit(solution)/shard_map/all_gather | solution.py:179
  429.7 2.4 convolution_convert_fusion.1
  432.1 73.0 %while.29 = (s32[]{:T(128)}, f32[2048,2,64]{0,2,1:T(8,128)S(1)}, f32[2048,2,64]{0,2,1:T(8,128)}, bf16[4,512,2,64]{1,3,2,0:T(8,128)(2,1)}, s32[4]{0:T(128)}, /*in...) while((s32[]{:T(128)}, f32[2048,2,64]{0,2,1:T(8,128)S(1)}, ...), condition=%wide.region_17.18_spmd.clone, body=%wide.region_15.17_spmd.clone.sunk | while | flops 1378156032 | bytes 86292840 | solution.py:220
  439.6 2.6 fusion.165
  442.2 3.2 multiply_reduce_fusion.9
  445.4 2.6 multiply_convert_fusion.2
  457.7 2.6 fusion.165
  460.3 3.2 multiply_reduce_fusion.9
  463.6 2.6 multiply_convert_fusion.2
  475.9 2.6 fusion.165
  478.5 3.2 multiply_reduce_fusion.9
  481.7 2.6 multiply_convert_fusion.2
  494.0 2.6 fusion.165
  496.6 3.2 multiply_reduce_fusion.9
  499.9 2.6 multiply_convert_fusion.2
  512.6 4.1 convolution_convert_fusion
  520.6 21.8 %psum.53 = bf16[2,384]{1,0:T(2,128)(2,1)S(1)} all-reduce(bf16[2,384]{1,0:T(2,128)(2,1)S(1)} %pad_maximum_fusion.1), channel_id=1, replica_groups=mesh['dp'=8,'head'=4] {'dp'}, use_global_device_ids=true, to_apply=%region_30.31 | all-reduce | flops 768 | bytes 3072 | tf_op jit(solution)/shard_map/psum | solution.py:250
  543.0 60.0 %all-reduce.4.cloned.1.call-done = (bf16[512,384]{1,0:T(8,128)(2,1)}, bf16[128,512]{0,1:T(8,128)(2,1)}, bf16[512,512]{1,0:T(8,128)(2,1)}, bf16[512,512]{0,1:T(8,128)(2,1)}) async-done(((bf16[512,384]{1,0:T(8,128)(2,1)}, bf16[128,512]{0,1:T(8,128)(2,1)}, bf16[512,512]{1,0:T(8,128)(2,1)}, bf16[512,512]{0,1:T(8,128)(2,1)}), (bf16[512,384]{1,0:T(8,128)(2,1)}, bf16[128,512]{0,1:T(8,128)(2,1)}, ...) | async-done | bytes 1572880 | tf_op jit(solution)/shard_map/psum | solution.py:246
  612.7 40.6 %all-reduce = (f32[]{:T(128)}, f32[6,512]{1,0:T(8,128)S(1)}) all-reduce(f32[]{:T(128)S(6)} %add.346, f32[6,512]{1,0:T(8,128)} %stack.28), channel_id=1, replica_groups=mesh['dp'=8,'head'=4] {'dp','head'}, use_global_device_ids=true, to_apply=%region_32.33 | all-reduce | flops 3073 | bytes 24584 | tf_op jit(solution)/shard_map/psum | solution.py:286
  (270 shorter events, 103.0 us)
Async XLA Ops:
  7.2 88.3 %all-gather.6.cloned.1.call-start = ((), (), s32[]{:S(2)}) async-start(), calls=%async_computation.4 | async-start | bytes 2621440 | tf_op jit(solution)/shard_map/all_gather | solution.py:84
  9.4 185.0 %reduce-scatter.5.cloned.1.call-start = ((), (), s32[]{:S(2)}) async-start(), calls=%async_computation.5 | async-start | bytes 5242880 | tf_op jit(solution)/shard_map/reduce_scatter | solution.py:131
  32.3 65.9 %copy-start.46 = (f32[384,2]{0,1:T(2,128)}, f32[384,2]{0,1:T(2,128)S(1)}, u32[]{:S(2)}) copy-start(f32[384,2]{0,1:T(2,128)S(1)} %reshape.315) | copy-start | bytes 9220
  95.4 2.8 copy-start.25
  148.4 4.0 copy-start.7
  149.8 2.8 copy-start.38
  149.8 44.6 %copy-start.17 = (f32[512,512]{1,0:T(8,128)S(1)}, f32[512,512]{1,0:T(8,128)}, u32[]{:S(2)}) copy-start(f32[512,512]{1,0:T(8,128)} %param.28) | copy-start | bytes 3145732
  152.5 46.0 %copy-start.29 = (f32[64,512]{1,0:T(8,128)S(1)}, f32[64,512]{1,0:T(8,128)}, u32[]{:S(2)}) copy-start(f32[64,512]{1,0:T(8,128)} %param.35) | copy-start | bytes 393220
  152.5 46.0 %copy-start.30 = (f32[512,64]{0,1:T(8,128)S(1)}, f32[512,64]{0,1:T(8,128)}, u32[]{:S(2)}) copy-start(f32[512,64]{0,1:T(8,128)} %param.36) | copy-start | bytes 393220
  152.5 108.8 %all-gather.8.cloned.1.call-start = ((), (), s32[]{:S(2)}) async-start(), calls=%async_computation.6 | async-start | bytes 2621440 | tf_op jit(solution)/shard_map/all_gather | solution.py:142
  153.2 42.7 %copy-start.41 = (f32[1,512]{1,0:T(1,128)}, f32[1,512]{1,0:T(1,128)S(1)}, u32[]{:S(2)}) copy-start(f32[1,512]{1,0:T(1,128)S(1)} %get-tuple-element.402) | copy-start | bytes 6148
  197.2 117.3 %reduce-scatter.7.cloned.1.call-start = ((), (), s32[]{:S(2)}) async-start(), calls=%async_computation.7 | async-start | bytes 5242880 | tf_op jit(solution)/shard_map/reduce_scatter | solution.py:145
  230.0 34.4 %copy-start.21 = (bf16[512,512]{0,1:T(8,128)(2,1)}, bf16[512,512]{0,1:T(8,128)(2,1)S(1)}, u32[]{:S(2)}) copy-start(bf16[512,512]{0,1:T(8,128)(2,1)S(1)} %all_gather.35) | copy-start | bytes 1572868
  261.4 3.1 copy-start.9
  261.4 5.0 copy-start.43
  269.6 48.6 %copy-start.13 = (f32[512,512]{1,0:T(8,128)S(1)}, f32[512,512]{1,0:T(8,128)}, u32[]{:S(2)}) copy-start(f32[512,512]{1,0:T(8,128)} %param.31) | copy-start | bytes 3145732
  269.7 76.1 %all-gather.10.cloned.1.call-start = ((), (), s32[]{:S(2)}) async-start(), calls=%async_computation.8 | async-start | bytes 2621440 | tf_op jit(solution)/shard_map/all_gather | solution.py:161
  314.5 5.5 copy-start.14
  314.5 5.5 copy-start.42
  314.5 5.5 copy-start.49
  318.0 4.1 copy-start.15
  323.0 77.1 %reduce-scatter.9.cloned.1.call-start = ((), (), s32[]{:S(2)}) async-start(), calls=%async_computation.9 | async-start | bytes 5242880 | tf_op jit(solution)/shard_map/reduce_scatter | solution.py:169
  345.8 6.3 copy-start.10
  355.4 74.2 %all-gather.12.cloned.1.call-start = ((), (), s32[]{:S(2)}) async-start(), calls=%async_computation.10 | async-start | bytes 2621440 | tf_op jit(solution)/shard_map/all_gather | solution.py:179
  400.1 4.3 copy-start.16
  404.4 7.0 %copy-start.44 = (f32[1,2,2,128]{3,1,2,0:T(2,128)S(1)}, f32[1,2,2,128]{3,1,2,0:T(2,128)}, u32[]{:S(2)}) copy-start(f32[1,2,2,128]{3,1,2,0:T(2,128)} %copy.106) | copy-start | bytes 6148
  406.9 196.1 %all-reduce.4.cloned.1.call-start = ((), (), s32[]{:S(2)}) async-start(), calls=%async_computation.12 | async-start | bytes 3145728 | tf_op jit(solution)/shard_map/psum | solution.py:246
  407.0 4.4 copy-start.1
  411.4 20.7 %copy-start.8 = (bf16[2048,2,64]{0,2,1:T(8,128)(2,1)S(1)}, bf16[2048,2,64]{0,2,1:T(8,128)(2,1)}, u32[]{:S(2)}) copy-start(bf16[2048,2,64]{0,2,1:T(8,128)(2,1)} %copy-done.7) | copy-start | bytes 1572868
  442.2 3.3 copy-start.19
  445.4 2.6 copy-start.22
  460.3 3.3 copy-start.19
  463.6 2.6 copy-start.22
  478.5 3.3 copy-start.19
  496.6 3.3 copy-start.19
  507.2 3.2 copy-start.6
  512.5 5.7 copy-start.47
  512.5 5.7 copy-start.48
  512.5 5.7 copy-start.50
  512.5 7.0 %copy-start.24 = (bf16[4,512,2,64]{1,3,2,0:T(8,128)(2,1)S(1)}, bf16[4,512,2,64]{1,3,2,0:T(8,128)(2,1)}, u32[]{:S(2)}) copy-start(bf16[4,512,2,64]{1,3,2,0:T(8,128)(2,1)} %get-tuple-element.152) | copy-start | bytes 1572868
  512.5 145.5 %copy-start.32 = (f32[128,64]{0,1:T(8,128)S(1)}, f32[128,64]{0,1:T(8,128)}, u32[]{:S(2)}) copy-start(f32[128,64]{0,1:T(8,128)} %param.34) | copy-start | bytes 98308
  512.6 146.9 %copy-start.31 = (f32[64,384]{1,0:T(8,128)S(1)}, f32[64,384]{1,0:T(8,128)}, u32[]{:S(2)}) copy-start(f32[64,384]{1,0:T(8,128)} %param.33) | copy-start | bytes 294916
  512.6 152.0 %reduce-scatter.11.cloned.1.call-start = ((), (), s32[]{:S(2)}) async-start(), calls=%async_computation.11 | async-start | bytes 2621440 | tf_op jit(solution)/shard_map/reduce_scatter | solution.py:230
  516.8 144.5 %copy-start.33 = (f32[64,512]{1,0:T(8,128)S(1)}, f32[64,512]{1,0:T(8,128)}, u32[]{:S(2)}) copy-start(f32[64,512]{1,0:T(8,128)} %param.47) | copy-start | bytes 393220
  516.8 144.5 %copy-start.34 = (f32[64,512]{1,0:T(8,128)S(1)}, f32[64,512]{1,0:T(8,128)}, u32[]{:S(2)}) copy-start(f32[64,512]{1,0:T(8,128)} %param.41) | copy-start | bytes 393220
  516.8 146.2 %copy-start.35 = (f32[512,64]{0,1:T(8,128)S(1)}, f32[512,64]{0,1:T(8,128)}, u32[]{:S(2)}) copy-start(f32[512,64]{0,1:T(8,128)} %param.48) | copy-start | bytes 393220
  516.8 146.2 %copy-start.36 = (f32[512,64]{0,1:T(8,128)S(1)}, f32[512,64]{0,1:T(8,128)}, u32[]{:S(2)}) copy-start(f32[512,64]{0,1:T(8,128)} %param.42) | copy-start | bytes 393220
  516.8 147.8 %copy-start.4 = (f32[512,512]{1,0:T(8,128)S(1)}, f32[512,512]{1,0:T(8,128)}, u32[]{:S(2)}) copy-start(f32[512,512]{1,0:T(8,128)} %copy-done.3) | copy-start | bytes 3145732
  (25 other events, 39.0 us)
Sparse Core Ops, SparseCore 0:
  10.2 25.2 all-gather.5
  152.6 41.7 reduce-scatter.4
  197.3 22.5 all-gather.7
  269.8 44.7 reduce-scatter.6
  323.1 22.5 all-gather.9
  355.6 44.4 reduce-scatter.8
  407.0 22.5 all-gather.11
  512.6 90.3 all-reduce.3
  605.7 31.0 reduce-scatter.10
where the time goes:
time: 684 us; the launch traced here: 675 us
  waiting for transfers between devices  228 us (33%)
  blocking collectives  209 us (31%)
  matrix products  96.2 us (14%)
  other arithmetic  79.2 us (12%)
  local copies, waits for them, and re-layouts  24.6 us (4%)
  between operations  21.3 us (3%)
  loops' own time  16.6 us (2%)
    psum x1, waiting for transfers between devices, per_device(): lax.psum(grad_attend.astype(jnp.bfloat16), 'dp').astype(jnp.float32)  60 us
    reduce_scatter x1, waiting for transfers between devices, per_device(): lax.psum_scatter(jnp.dot(hidden, copy_contract, preferred_element_type=jn...  44.8 us
    reduce_scatter x1, waiting for transfers between devices, per_device(): lax.psum_scatter(jnp.dot(grad_pre, copy_expand.T, preferred_element_type=...  44.6 us
    reduce_scatter x1, waiting for transfers between devices, per_device(): lax.psum_scatter(jnp.dot(attn_mixed, copy_output, preferred_element_type=...  41.2 us
    psum x1, blocking collectives, per_device(): lax.psum((norm_part, own_squares), ('dp', 'head'))  40.6 us
    all_gather x1, blocking collectives, per_device(): lax.all_gather(contract_weight.astype(jnp.bfloat16), 'dp', axis=1, tiled=...  31.4 us
    all_gather x1, blocking collectives, per_device(): lax.all_gather(expand_weight.astype(jnp.bfloat16), 'dp', axis=0, tiled=True)  31.4 us
    all_gather x1, blocking collectives, per_device(): lax.all_gather(attend_weight.astype(jnp.bfloat16), 'dp', axis=0, tiled=True)  30.9 us
  transfers between devices with their start and end apart: 9, of which 6 were waited for; matrix products, arithmetic and copies ran while one was open for 5% of the time, Pallas kernels for 0%

commit v1 on v0

v1 whole, which is shorter than its diff:
```python
import functools

import jax
import jax.numpy as jnp
from jax import lax
from jax.experimental import pallas as pl
from jax.experimental.pallas import tpu as pltpu
from jax.sharding import PartitionSpec as P

D = 512
HEADS = 8
HD = 64
TQ = 256
TK = 256
SEQ_MOST = 1024
KEY_BLOCKS = SEQ_MOST // TK + 1
CH = 64

EPS_NORM = 1e-05
NEG_LARGE = -1e30
LOG2E = 1.4426950408889634
SCORE_SCALE = HD ** (-0.5)
RATE_ATTEND = 0.04
RATE_OUTPUT = 0.12
RATE_EXPAND = 0.04
RATE_CONTRACT = 0.04
RATE_BIAS = 0.16
RATE_NORM = 0.3
DECAY = 0.01
ADAM_EPS = 1e-08
BETA = 0.5
BIAS_CORRECTION = 0.875
BF = jnp.bfloat16
F32 = jnp.float32
VMEM = pl.BlockSpec(memory_space=pltpu.VMEM)
SMEM = pl.BlockSpec(memory_space=pltpu.SMEM)


def dot(a, b, ca, cb):
    return lax.dot_general(a, b, (((ca,), (cb,)), ((), ())), preferred_element_type=F32)


def bits_of(count):
    bits = []
    while count > 1:
        count //= 2
        bits.append(count)
    return bits


def swap(v, step):
    axis, bit = step
    count = lax.axis_size(axis)
    return lax.ppermute(v, axis, [(i, i ^ bit) for i in range(count)])


def offsets(steps, axis):
    offs = [0]
    for name, bit in steps:
        offs = offs + [o ^ (bit if name == axis else 0) for o in offs]
    return offs


def gather_steps(v, steps):
    acc = v[None]
    for step in steps:
        acc = jnp.concatenate([acc, swap(acc, step)], axis=0)
    return acc


def place(steps, axis, off):
    pos = 0
    for k, (name, bit) in enumerate(steps):
        if name == axis:
            pos = pos + ((off // bit) % 2) * (1 << k)
    return pos


def scatter_steps(keep, send, steps):
    for step in reversed(steps):
        got = swap(send, step)
        half = keep.shape[0] // 2
        if half == 0:
            return keep, got
        total = keep.astype(F32) + got.astype(F32)
        send = total[half:].astype(BF)
        keep = total[:half].astype(BF)
    return keep, send


def lane_mask_stack(v, lh):
    if lh == 1:
        return v
    lane = lax.broadcasted_iota(jnp.int32, v.shape, 1)
    zero = jnp.zeros_like(v)
    return jnp.concatenate(
        [jnp.where((lane >= l * HD) & (lane < (l + 1) * HD), v, zero) for l in range(lh)], axis=0
    )


def head_rows_merge(vt, lh):
    return jnp.concatenate(
        [vt[l * HD : (l + 1) * HD, l * TQ : (l + 1) * TQ] for l in range(lh)], axis=0
    )


def attend_kernel(lh, n_dp, n_h, dp_offs, idx_ref, lo_ref, start_ref, w_ref, *refs):
    rows = refs[:n_h]
    pieces = refs[n_h : 2 * n_h]
    q_ref, k_ref, v_ref, o_ref, lse_ref, wg_ref, w_s, b_s, vt_s, s_s, acc_s = refs[2 * n_h :]
    g, h = idx_ref[0], idx_ref[1]
    width = lh * HD
    ds_rows = D // n_dp
    rw = rows[0].shape[0]
    shares = b_s.shape[1] // lh
    for p in range(n_dp):
        block = g ^ dp_offs[p]
        w_s[pl.ds(pl.multiple_of(block * ds_rows, ds_rows), ds_rows), :] = w_ref[p, :ds_rows, :]
        b_s[pl.ds(block, 1), :] = w_ref[p, ds_rows : ds_rows + 16, : lh * shares][:1].astype(F32)
    wide = w_s[...].astype(F32)
    wg = jnp.concatenate(
        [
            wide[:, l * 3 * HD + kind * HD : l * 3 * HD + (kind + 1) * HD]
            for kind in range(3)
            for l in range(lh)
        ],
        axis=1,
    ).astype(BF)
    wg_ref[...] = wg
    per_head = [
        jnp.concatenate([b_s[b : b + 1, l * shares : (l + 1) * shares] for b in range(n_dp)], axis=1)
        for l in range(lh)
    ]
    q_bias = jnp.concatenate([r[:, :HD] for r in per_head], axis=1)
    v_bias = jnp.concatenate([r[:, HD : 2 * HD] for r in per_head], axis=1)
    inner = jnp.concatenate([r[:, 2 * HD :] for r in per_head], axis=1)
    inner_rows = jnp.concatenate(
        [inner[:, i * width : (i + 1) * width] for i in range(inner.shape[1] // width)]
        + [jnp.zeros((16 - inner.shape[1] // width, width), F32)],
        axis=0,
    ).astype(BF)
    for off in range(n_h):
        base = pl.multiple_of((h ^ off) * rw, rw)
        qkv = dot(rows[off][...], wg_ref[...], 1, 0)
        q_ref[pl.ds(base, rw), :] = (qkv[:, :width] + q_bias).astype(BF)
        k_ref[pl.ds(base, rw), :] = qkv[:, width : 2 * width].astype(BF)
        v_ref[pl.ds(base, rw), :] = (qkv[:, 2 * width :] + v_bias).astype(BF)
        pieces[off][pl.ds(rw, 16), :] = inner_rows
    n_rows = q_ref.shape[0]
    vt_s[:width, :] = v_ref[...].T
    vt_s[width:, :] = jnp.ones((16, n_rows), BF)
    factor = SCORE_SCALE * LOG2E
    cols = lh * TQ

    def query_block(qb, carry):
        r0 = pl.multiple_of(qb * TQ, TQ)
        q2 = lane_mask_stack(q_ref[pl.ds(r0, TQ), :], lh)
        start = jnp.concatenate([start_ref[:, pl.ds(r0, TQ)]] * lh, axis=1)
        lo = lo_ref[qb]
        column = lax.broadcasted_iota(jnp.int32, (1, cols), 1) % TQ

        def scores(kb, top):
            c0 = pl.multiple_of(kb * TK, TK)
            s = dot(k_ref[pl.ds(c0, TK), :], q2, 1, 1)
            key = lax.broadcasted_iota(jnp.int32, (TK, cols), 0)
            ok = (key >= start - c0) & (key <= column + (r0 - c0))
            s = jnp.where(ok, s, NEG_LARGE)
            s_s[kb - lo] = s
            return jnp.maximum(top, jnp.max(s.reshape(TK // 8, 8, cols), axis=0))

        top = lax.fori_loop(lo, qb + 1, scores, jnp.full((8, cols), NEG_LARGE, F32))
        top = jnp.max(top, axis=0, keepdims=True)
        acc_s[...] = jnp.zeros_like(acc_s)

        def mix(kb, carry):
            c0 = pl.multiple_of(kb * TK, TK)
            p = jnp.exp2((s_s[kb - lo] - top) * factor).astype(BF)
            acc_s[...] += dot(vt_s[:, pl.ds(c0, TK)], p, 1, 0)
            return carry

        lax.fori_loop(lo, qb + 1, mix, 0)
        total = acc_s[width : width + 1, :]
        out_t = head_rows_merge(acc_s[:width, :] / total, lh)
        o_ref[pl.ds(r0, TQ), :] = out_t.T.astype(BF)
        lse_ref[qb] = jnp.broadcast_to(top * factor + jnp.log2(total), (8, cols))
        return carry

    lax.fori_loop(0, n_rows // TQ, query_block, 0)
    for off in range(n_h):
        base = pl.multiple_of((h ^ off) * rw, rw)
        pieces[off][:rw, :] = o_ref[pl.ds(base, rw), :]


def norm_back(grad, xhat, rstd, gain):
    g = grad * gain
    return rstd * (
        g - jnp.mean(g, axis=-1, keepdims=True) - xhat * jnp.mean(g * xhat, axis=-1, keepdims=True)
    )


def fold(v):
    return jnp.sum(v.reshape(v.shape[0] // 8, 8, v.shape[1]), axis=0)


def middle_kernel(lh, n_dp, n_h, e_steps, c_steps, idx_ref, norm_ref, *refs):
    width = lh * HD
    mixed = refs[:n_h]
    e_ref, c_ref, post_in, dual_in, post_cot, dual_cot = refs[n_h : n_h + 6]
    outs = refs[n_h + 6 :]
    post_out, dual_out, gmid1_ref = outs[:3]
    gm = outs[3 : 3 + n_h]
    ge_keep, ge_send, gc_keep, gc_send, small_ref = outs[3 + n_h : 8 + n_h]
    (e_s, c_s, o_s, mix_s, bias_s, hid_s, acc_s, xh_s, rs_s, pn_s, xb_s, xt_s, gb_s, gmid2_s, ffb_s) = outs[
        8 + n_h :
    ]
    g, h = idx_ref[0], idx_ref[1]
    rw = post_in.shape[0]
    ds_rows = D // n_dp
    units = hid_s.shape[2]
    row = lambda i: norm_ref[i : i + 1, :]

    e_dp, e_h = offsets(e_steps, "dp"), offsets(e_steps, "head")
    c_dp, c_h = offsets(c_steps, "dp"), offsets(c_steps, "head")
    for p in range(n_dp * n_h):
        at = pl.ds(pl.multiple_of((g ^ e_dp[p]) * ds_rows, ds_rows), ds_rows)
        e_s[e_h[p], at, :] = e_ref[p]
        at = pl.ds(pl.multiple_of((g ^ c_dp[p]) * ds_rows, ds_rows), ds_rows)
        c_s[c_h[p], at, :] = c_ref[p, :, :units]
        o_s[at, c_h[p] * width : (c_h[p] + 1) * width] = c_ref[p, :, units:]
    for off in range(n_h):
        mix_s[:, off * width : (off + 1) * width] = mixed[off][:rw, :]
        tail = mixed[off][rw : rw + 16, :].astype(F32)
        bias_s[off] = jnp.concatenate([tail[i : i + 1, :] for i in range(units // width)], axis=1)

    acc_s[...] = dot(mix_s[...], o_s[...], 1, 1)

    def chunk_one(i, carry):
        at = pl.ds(pl.multiple_of(i * CH, CH), CH)
        attn_out = acc_s[at, :] + row(2)
        v = post_in[at, :] + attn_out
        centered = v - jnp.mean(v, axis=-1, keepdims=True)
        rstd = lax.rsqrt(jnp.mean(centered * centered, axis=-1, keepdims=True) + EPS_NORM)
        xhat = centered * rstd
        pn = xhat * row(0) + row(1)
        xh_s[at, :] = xhat
        rs_s[at, :] = jnp.broadcast_to(rstd, (CH, 128))
        pn_s[at, :] = pn
        xb_s[at, :] = pn.astype(BF)
        dual_out[at, :] = dual_in[at, :] + attn_out
        return carry

    lax.fori_loop(0, rw // CH, chunk_one, 0)
    xt_s[...] = xb_s[...].T
    acc_s[...] = jnp.zeros_like(acc_s)

    def inner(oh, carry):
        pre = dot(xb_s[...], e_s[oh], 1, 0) + bias_s[oh]
        hid = jnp.maximum(pre, 0.0).astype(BF)
        hid_s[oh] = hid
        acc_s[...] += dot(hid, c_s[oh], 1, 1)
        return carry

    lax.fori_loop(0, n_h, inner, 0)

    def chunk_two(i, carry):
        gain_sum, shift_sum, ffn_sum = carry
        at = pl.ds(pl.multiple_of(i * CH, CH), CH)
        ffn_out = acc_s[at, :] + row(5)
        v = pn_s[at, :] + ffn_out
        centered = v - jnp.mean(v, axis=-1, keepdims=True)
        rstd = lax.rsqrt(jnp.mean(centered * centered, axis=-1, keepdims=True) + EPS_NORM)
        xhat = centered * rstd
        post_out[at, :] = xhat * row(3) + row(4)
        dual_out[at, :] = dual_out[at, :] + ffn_out
        cot = post_cot[at, :]
        gmid2 = norm_back(cot, xhat, rstd, row(3))
        gffn = gmid2 + dual_cot[at, :]
        gmid2_s[at, :] = gmid2
        gb_s[at, :] = gffn.astype(BF)
        return gain_sum + fold(cot * xhat), shift_sum + fold(cot), ffn_sum + fold(gffn)

    zero = jnp.zeros((8, D), F32)
    gain2, shift2, ffn_sum = lax.fori_loop(0, rw // CH, chunk_two, (zero, zero, zero))
    acc_s[...] = jnp.zeros_like(acc_s)
    gt = gb_s[...].T
    hid_t = gt

    def inner_back(pair, carry):
        for low in range(2):
            oh = pair * 2 + low
            ge, gc = (ge_keep, gc_keep) if low == 0 else (ge_send, gc_send)
            hid = hid_s[oh]
            gh = dot(gb_s[...], c_s[oh], 1, 0)
            gp = jnp.where(hid > 0, gh, 0.0).astype(BF)
            ffb_s[oh] = jnp.sum(gp.astype(F32), axis=0, keepdims=True)
            acc_s[...] += dot(gp, e_s[oh], 1, 1)
            grad_c = dot(hid_t, hid, 1, 0).astype(BF)
            grad_e = dot(xt_s[...], gp, 1, 0).astype(BF)
            for b in range(n_dp):
                ge[place(e_steps, "dp", b ^ g) + place(e_steps, "head", oh - low)] = grad_e[
                    b * ds_rows : (b + 1) * ds_rows
                ]
                gc[place(c_steps, "dp", b ^ g) + place(c_steps, "head", oh - low), :, :units] = grad_c[
                    b * ds_rows : (b + 1) * ds_rows
                ]
        return carry

    lax.fori_loop(0, n_h // 2, inner_back, 0)

    def chunk_three(i, carry):
        gain_sum, shift_sum, attn_sum = carry
        at = pl.ds(pl.multiple_of(i * CH, CH), CH)
        grad = gmid2_s[at, :] + acc_s[at, :]
        xhat = xh_s[at, :]
        gmid1 = norm_back(grad, xhat, rs_s[at, :1], row(0))
        gmid1_ref[at, :] = gmid1
        gattn = gmid1 + dual_cot[at, :]
        gb_s[at, :] = gattn.astype(BF)
        return gain_sum + fold(grad * xhat), shift_sum + fold(grad), attn_sum + fold(gattn)

    gain1, shift1, attn_sum = lax.fori_loop(0, rw // CH, chunk_three, (zero, zero, zero))
    grad_mixed = dot(gb_s[...], o_s[...], 1, 0).astype(BF)
    for off in range(n_h):
        gm[off][...] = grad_mixed[:, off * width : (off + 1) * width]
    grad_o = dot(gb_s[...].T, mix_s[...], 1, 0).astype(BF)
    for oh in range(n_h):
        gc = gc_keep if oh % 2 == 0 else gc_send
        for b in range(n_dp):
            gc[place(c_steps, "dp", b ^ g) + place(c_steps, "head", oh - oh % 2), :, units:] = grad_o[
                b * ds_rows : (b + 1) * ds_rows, oh * width : (oh + 1) * width
            ]
    for i, part in enumerate((gain1, shift1, attn_sum, gain2, shift2, ffn_sum)):
        line = jnp.sum(part, axis=0, keepdims=True)
        for j in range(D // 128):
            small_ref[4 * i + j : 4 * i + j + 1, :] = line[:, j * 128 : (j + 1) * 128]
    for oh in range(n_h):
        first = 24 + (h ^ oh) * (units // 128)
        for j in range(units // 128):
            small_ref[pl.ds(first + j, 1), :] = ffb_s[oh, :, j * 128 : (j + 1) * 128]


def attend_back_kernel(lh, n_h, idx_ref, lo_ref, start_ref, q_ref, k_ref, v_ref, o_ref, lse_ref, small_in, *refs):
    gm = refs[:n_h]
    gqkv_ref, small_ref, do_s, kt_s, dk_s, dv_s, dq_s = refs[n_h:]
    h = idx_ref[1]
    width = lh * HD
    rw = gm[0].shape[0]
    n_rows = q_ref.shape[0]
    cols = lh * TQ
    factor = SCORE_SCALE * LOG2E
    for off in range(n_h):
        do_s[pl.ds(pl.multiple_of((h ^ off) * rw, rw), rw), :] = gm[off][...]
    kt_s[...] = k_ref[...].T
    dk_s[...] = jnp.zeros_like(dk_s)
    dv_s[...] = jnp.zeros_like(dv_s)

    def query_block(qb, q_sum):
        r0 = pl.multiple_of(qb * TQ, TQ)
        at = pl.ds(r0, TQ)
        q2 = lane_mask_stack(q_ref[at, :], lh)
        do = do_s[at, :]
        do2 = lane_mask_stack(do, lh)
        prod = (do.astype(F32) * o_ref[at, :].astype(F32)).T
        delta = jnp.concatenate(
            [jnp.sum(prod[l * HD : (l + 1) * HD, :], axis=0, keepdims=True) for l in range(lh)], axis=1
        )
        lse = lse_ref[qb][:1]
        start = jnp.concatenate([start_ref[:, at]] * lh, axis=1)
        lo = lo_ref[qb]
        column = lax.broadcasted_iota(jnp.int32, (1, cols), 1) % TQ
        dq_s[...] = jnp.zeros_like(dq_s)

        def pair(kb, carry):
            c0 = pl.multiple_of(kb * TK, TK)
            keys = pl.ds(c0, TK)
            s = dot(k_ref[keys, :], q2, 1, 1)
            key = lax.broadcasted_iota(jnp.int32, (TK, cols), 0)
            ok = (key >= start - c0) & (key <= column + (r0 - c0))
            p = jnp.exp2(jnp.where(ok, s, NEG_LARGE) * factor - lse)
            dp = dot(v_ref[keys, :], do2, 1, 1)
            grad = (p * (dp - delta)).astype(BF)
            dv_s[keys, :] += dot(p.astype(BF), do2, 1, 0)
            dk_s[keys, :] += dot(grad, q2, 1, 0)
            dq_s[...] += dot(kt_s[:, keys], grad, 1, 0)
            return carry

        lax.fori_loop(lo, qb + 1, pair, 0)
        dq = (head_rows_merge(dq_s[...], lh) * SCORE_SCALE).T.astype(BF)
        gqkv_ref[at, :width] = dq
        return q_sum + jnp.sum(dq.astype(F32), axis=0, keepdims=True)

    q_sum = lax.fori_loop(0, n_rows // TQ, query_block, jnp.zeros((1, width), F32))
    gqkv_ref[:, width : 2 * width] = (dk_s[...] * SCORE_SCALE).astype(BF)
    dv = dv_s[...].astype(BF)
    gqkv_ref[:, 2 * width :] = dv
    v_sum = jnp.sum(dv.astype(F32), axis=0, keepdims=True)
    small_ref[:40, :] = small_in[...]
    small_ref[40:, :] = jnp.zeros((8, 128), F32)
    for l in range(lh):
        small_ref[pl.ds(40 + h * lh + l, 1), :] = jnp.concatenate(
            [q_sum[:, l * HD : (l + 1) * HD], v_sum[:, l * HD : (l + 1) * HD]], axis=1
        )


def rows_back_kernel(n_h, idx_ref, gqkv_ref, wg_ref, *outs):
    h = idx_ref[1]
    rw = outs[0].shape[0]
    for off in range(n_h):
        at = pl.ds(pl.multiple_of((h ^ off) * rw, rw), rw)
        outs[off][...] = dot(gqkv_ref[at, :], wg_ref[...], 1, 1).astype(BF)


def attend_grad_kernel(lh, n_dp, n_h, steps, idx_ref, gqkv_ref, *refs):
    rows = refs[:n_h]
    out_ref, acc_s = refs[n_h:]
    g, h = idx_ref[0], idx_ref[1]
    rw = rows[0].shape[0]
    ds_rows = D // n_dp
    width = lh * HD
    for off in range(n_h):
        at = pl.ds(pl.multiple_of((h ^ off) * rw, rw), rw)
        part = dot(rows[off][...], gqkv_ref[at, :], 0, 0)
        acc_s[...] = part if off == 0 else acc_s[...] + part
    full = acc_s[...]
    full = jnp.concatenate(
        [full[:, kind * width + l * HD : kind * width + (l + 1) * HD] for l in range(lh) for kind in range(3)],
        axis=1,
    ).astype(BF)
    for b in range(n_dp):
        out_ref[place(steps, "dp", b ^ g)] = full[b * ds_rows : (b + 1) * ds_rows]


def call(body, outs, scratch, n_smem, args, limit, flops, nbytes):
    return pl.pallas_call(
        body,
        out_shape=outs,
        in_specs=[SMEM] * n_smem + [VMEM] * (len(args) - n_smem),
        out_specs=jax.tree.map(lambda _: VMEM, outs),
        scratch_shapes=scratch,
        compiler_params=pltpu.CompilerParams(vmem_limit_bytes=limit << 20),
        cost_estimate=pl.CostEstimate(flops=int(flops), bytes_accessed=int(nbytes), transcendentals=0),
    )(*args)


def sds(shape, dtype):
    return jax.ShapeDtypeStruct(shape, dtype)


def adam_update(master, momentum, variance, gradient, factor, rate):
    clipped = factor * gradient
    momentum_new = BETA * momentum + (1.0 - BETA) * clipped
    variance_new = BETA * variance + (1.0 - BETA) * clipped * clipped
    master_new = master - rate * (
        momentum_new / BIAS_CORRECTION / (jnp.sqrt(variance_new / BIAS_CORRECTION) + ADAM_EPS)
        + DECAY * master
    )
    return (momentum_new, variance_new, master_new)


def per_device(
    post_in,
    dual_in,
    segment_ids,
    post_cot,
    dual_cot,
    attend_weight,
    output_weight,
    expand_weight,
    contract_weight,
    head_bias,
    norm_params,
    attend_momentum,
    output_momentum,
    expand_momentum,
    contract_momentum,
    bias_momentum,
    norm_momentum,
    attend_variance,
    output_variance,
    expand_variance,
    contract_variance,
    bias_variance,
    norm_variance,
    clip_limit,
):
    n_dp, n_h = lax.axis_size("dp"), lax.axis_size("head")
    g, h = lax.axis_index("dp"), lax.axis_index("head")
    idx = jnp.stack([g, h]).astype(jnp.int32)
    rw = post_in.shape[0]
    n_rows = rw * n_h
    lh = HEADS // n_h
    width = lh * HD
    ds_rows = attend_weight.shape[0]
    a_cols = attend_weight.shape[1]
    units = expand_weight.shape[1]
    shares = head_bias.shape[1]
    dp_bits, h_bits = bits_of(n_dp), bits_of(n_h)
    a_steps = [("dp", b) for b in dp_bits]
    e_steps = [("dp", b) for b in dp_bits] + [("head", b) for b in h_bits]
    c_steps = (
        [("dp", b) for b in dp_bits[:-1]]
        + [("head", b) for b in h_bits[:-1]]
        + [("dp", dp_bits[-1])]
        + [("head", h_bits[-1])]
    )

    rows_own = post_in.astype(BF)
    bias_block = jnp.pad(
        head_bias.astype(BF).reshape(1, lh * shares), ((0, 15), (0, a_cols - lh * shares))
    )
    a_msg = jnp.concatenate([attend_weight.astype(BF), bias_block], axis=0)
    e_msg = expand_weight.astype(BF)
    c_msg = jnp.concatenate([contract_weight.T.astype(BF), output_weight.T.astype(BF)], axis=1)

    rows = {0: rows_own}
    for bit in h_bits:
        for off in list(rows):
            rows[off ^ bit] = swap(rows[off], ("head", bit))
    rows = [rows[off] for off in range(n_h)]
    a_all = gather_steps(a_msg, a_steps)
    e_all = gather_steps(e_msg, e_steps)
    c_all = gather_steps(c_msg, c_steps)

    segment = segment_ids[0]
    start = jnp.zeros_like(segment)
    for s in range(HEADS):
        start = start + jnp.where(segment > s, jnp.sum((segment == s).astype(jnp.int32)), 0)
    lo = start[::TQ] // TK
    start = start[None]

    n_q = n_rows // TQ
    cols = lh * TQ
    attend_out = call(
        functools.partial(attend_kernel, lh, n_dp, n_h, offsets(a_steps, "dp")),
        [sds((rw + 16, width), BF)] * n_h
        + [sds((n_rows, width), BF)] * 4
        + [sds((n_q, 8, cols), F32), sds((D, 3 * width), BF)],
        [
            pltpu.VMEM((D, a_cols), BF),
            pltpu.VMEM((n_dp, lh * shares), F32),
            pltpu.VMEM((width + 16, n_rows), BF),
            pltpu.VMEM((KEY_BLOCKS, TK, cols), F32),
            pltpu.VMEM((width + 16, cols), F32),
        ],
        2,
        [idx, lo, start, a_all] + rows,
        32,
        3e9,
        6e6,
    )
    pieces = attend_out[:n_h]
    q, k, v, o, lse, wg = attend_out[n_h:]
    mixed = [pieces[0]] + [
        lax.ppermute(pieces[off], "head", [(i, i ^ off) for i in range(n_h)]) for off in range(1, n_h)
    ]

    half = n_dp * n_h // 2
    middle_out = call(
        functools.partial(middle_kernel, lh, n_dp, n_h, e_steps, c_steps),
        [sds((rw, D), F32)] * 3
        + [sds((rw, width), BF)] * n_h
        + [sds((half, ds_rows, units), BF)] * 2
        + [sds((half, ds_rows, units + width), BF)] * 2
        + [sds((40, 128), F32)],
        [
            pltpu.VMEM((n_h, D, units), BF),
            pltpu.VMEM((n_h, D, units), BF),
            pltpu.VMEM((D, n_h * width), BF),
            pltpu.VMEM((rw, n_h * width), BF),
            pltpu.VMEM((n_h, 1, units), F32),
            pltpu.VMEM((n_h, rw, units), BF),
            pltpu.VMEM((rw, D), F32),
            pltpu.VMEM((rw, D), F32),
            pltpu.VMEM((rw, 128), F32),
            pltpu.VMEM((rw, D), F32),
            pltpu.VMEM((rw, D), BF),
            pltpu.VMEM((D, rw), BF),
            pltpu.VMEM((rw, D), BF),
            pltpu.VMEM((rw, D), F32),
            pltpu.VMEM((n_h, 1, units), F32),
        ],
        1,
        [idx, norm_params] + mixed + [e_all, c_all, post_in, dual_in, post_cot, dual_cot],
        52,
        8e9,
        16e6,
    )
    post_out, dual_out, grad_mid1 = middle_out[:3]
    gm = middle_out[3 : 3 + n_h]
    ge_keep, ge_send, gc_keep, gc_send, small_mid = middle_out[3 + n_h :]
    gm = [gm[0]] + [
        lax.ppermute(gm[off], "head", [(i, i ^ off) for i in range(n_h)]) for off in range(1, n_h)
    ]
    ge = scatter_steps(ge_keep, ge_send, e_steps)
    gc = scatter_steps(gc_keep, gc_send, c_steps)

    gqkv, small = call(
        functools.partial(attend_back_kernel, lh, n_h),
        [sds((n_rows, 3 * width), BF), sds((48, 128), F32)],
        [
            pltpu.VMEM((n_rows, width), BF),
            pltpu.VMEM((width, n_rows), BF),
            pltpu.VMEM((n_rows, width), F32),
            pltpu.VMEM((n_rows, width), F32),
            pltpu.VMEM((width, cols), F32),
        ],
        2,
        [idx, lo, start, q, k, v, o, lse, small_mid] + gm,
        32,
        4e9,
        6e6,
    )
    back = call(
        functools.partial(rows_back_kernel, n_h),
        [sds((rw, D), BF)] * n_h,
        [],
        1,
        [idx, gqkv, wg],
        24,
        8e8,
        4e6,
    )
    ga = call(
        functools.partial(attend_grad_kernel, lh, n_dp, n_h, a_steps),
        sds((n_dp, ds_rows, a_cols), BF),
        [pltpu.VMEM((D, 3 * width), F32)],
        1,
        [idx, gqkv] + rows,
        24,
        8e8,
        4e6,
    )
    ga = scatter_steps(ga[: n_dp // 2], ga[n_dp // 2 :], a_steps)
    back = {off: [back[off]] for off in range(n_h)}
    for bit in reversed(h_bits):
        sent = [off for off in back if off & bit]
        for off in sent:
            parts = back.pop(off)
            total = functools.reduce(lambda a, b: a + b, [p.astype(F32) for p in parts]).astype(BF)
            back[off ^ bit].append(swap(total, ("head", bit)))
    post_grad = functools.reduce(lambda a, b: a + b, [p.astype(F32) for p in back[0]], grad_mid1)

    for step in [("head", b) for b in reversed(h_bits)] + [("dp", b) for b in reversed(dp_bits)]:
        small = small + swap(small, step)

    join = lambda pair: (pair[0][0].astype(F32) + pair[1][0].astype(F32))
    share_attend = join(ga)
    share_expand = join(ge)
    share_co = join(gc)
    share_contract = share_co[:, :units].T
    share_output = share_co[:, units:].T
    norm_grads = small[:24].reshape(6, D)
    bias_full = jnp.concatenate(
        [
            lax.dynamic_slice_in_dim(small, 40 + h * lh, lh, 0),
            lax.dynamic_slice_in_dim(small, 24 + h * 2 * lh, 2 * lh, 0).reshape(lh, 256),
        ],
        axis=1,
    )
    share_bias = lax.dynamic_slice_in_dim(bias_full, g * shares, shares, 1)
    squares = jnp.sum(share_attend * share_attend) + jnp.sum(share_expand * share_expand) + jnp.sum(share_co * share_co)
    squares = jnp.full((8, 128), squares)
    for step in [("head", b) for b in reversed(h_bits)] + [("dp", b) for b in reversed(dp_bits)]:
        squares = squares + swap(squares, step)
    total_norm = jnp.sqrt(squares[0, 0] + jnp.sum(small * small))
    factor = clip_limit[0] / jnp.maximum(total_norm, clip_limit[0])
    results = []
    for w, m, va, gr, rate, low in (
        (attend_weight, attend_momentum, attend_variance, share_attend, RATE_ATTEND, True),
        (output_weight, output_momentum, output_variance, share_output, RATE_OUTPUT, True),
        (expand_weight, expand_momentum, expand_variance, share_expand, RATE_EXPAND, True),
        (contract_weight, contract_momentum, contract_variance, share_contract, RATE_CONTRACT, True),
        (head_bias, bias_momentum, bias_variance, share_bias, RATE_BIAS, True),
        (norm_params, norm_momentum, norm_variance, norm_grads, RATE_NORM, False),
    ):
        m_new, v_new, w_new = adam_update(w, m, va, gr, factor, rate)
        results += [m_new, v_new, w_new]
        if low:
            results.append(w_new.astype(BF))
    return (post_out, dual_out, post_grad, total_norm.reshape(1), *results, factor * norm_grads)


def solution(mesh):
    rows = P(("dp", "head"), None)
    tall, flat, rep = P("dp", "head"), P("head", "dp"), P()
    weights = (tall, flat, tall, flat, flat, rep)
    in_specs = (rows, rows, P("dp", None), rows, rows) + weights * 3 + (rep,)
    out_specs = (rows, rows, rows, rep)
    for spec in (tall, flat, tall, flat, flat):
        out_specs += (spec,) * 4
    out_specs += (rep,) * 4
    return jax.shard_map(per_device, mesh=mesh, in_specs=in_specs, out_specs=out_specs, check_vma=False)
```

time: 684 us -> 238 us (0.35); the launches traced: 675 us -> 237 us
  blocking collectives: 209 us -> 0 us
  waiting for transfers between devices: 228 us -> 82.2 us
  matrix products: 96.2 us -> 0 us
  Pallas kernels: 0 us -> 54.9 us
  other arithmetic: 79.2 us -> 28.4 us
  starting transfers between devices: 0.37 us -> 50.1 us
  loops' own time: 16.6 us -> 0 us
  between operations: 21.3 us -> 6.6 us
  local copies, waits for them, and re-layouts: 24.6 us -> 15.2 us
    all_gather x5 -> x0, blocking collectives: 146 us -> none  [the longest x1 31.4 us: per_device(): lax.all_gather(contract_weight.astype(jnp.bfloat16), 'dp', axis=1, tiled=...]
    reduce_scatter x4 -> x0, waiting for transfers between devices: 131 us -> none  [the longest x1 44.8 us: per_device(): lax.psum_scatter(jnp.dot(hidden, copy_contract, preferred_element_type=jn...]
    dot_general x40 -> x0, matrix products: 96.2 us -> none  [the longest x8 14.1 us: block_scores(): jnp.einsum('qhe,khe->hqk', query_block, key_rows, preferred_element_type=...]
    ppermute x0 -> x48, waiting for transfers between devices: none -> 82.2 us  [the longest x42 73.6 us: swap(): return lax.ppermute(v, axis, [(i, i ^ bit) for i in range(count)])]
    psum x2 -> x0, blocking collectives: 62.4 us -> none  [the longest x1 40.6 us: per_device(): lax.psum((norm_part, own_squares), ('dp', 'head'))]
    psum x1 -> x0, waiting for transfers between devices: 60 us -> none  [per_device(): lax.psum(grad_attend.astype(jnp.bfloat16), 'dp').astype(jnp.float32)]
    pallas_call x0 -> x5, Pallas kernels: none -> 54.9 us  [call(): pl.pallas_call(body, out_shape=outs, in_specs=[SMEM] * n_smem + [VMEM] *...]
    ppermute x0 -> x48, starting transfers between devices: none -> 50.1 us  [the longest x42 46.3 us: swap(): return lax.ppermute(v, axis, [(i, i ^ bit) for i in range(count)])]
  transfers between devices with their start and end apart: 9 -> 48, of which waited for: 6 -> 27; matrix products, arithmetic and copies ran while one was open for 5% -> 15% of each run, Pallas kernels for 0% -> 14%
where the time goes in v1:
time: 238 us; the launch traced here: 237 us
  waiting for transfers between devices  82.2 us (35%)
  Pallas kernels  54.9 us (23%)
  starting transfers between devices  50.1 us (21%)
  other arithmetic  28.4 us (12%)
  local copies, waits for them, and re-layouts  15.2 us (6%)
  between operations  6.6 us (3%)
    ppermute x42, waiting for transfers between devices, swap(): return lax.ppermute(v, axis, [(i, i ^ bit) for i in range(count)])  73.6 us
    pallas_call x5, Pallas kernels, call(): pl.pallas_call(body, out_shape=outs, in_specs=[SMEM] * n_smem + [VMEM] *...  54.9 us
    ppermute x42, starting transfers between devices, swap(): return lax.ppermute(v, axis, [(i, i ^ bit) for i in range(count)])  46.3 us
    unnamed x89, local copies, waits for them, and re-layouts  6.67 us
    ppermute x3, waiting for transfers between devices, per_device(): lax.ppermute(gm[off], 'head', [(i, i ^ off) for i in range(n_h)])  5.69 us
    concatenate x4, local copies, waits for them, and re-layouts, gather_steps(): acc = jnp.concatenate([acc, swap(acc, step)], axis=0)  5.56 us
    add x1, other arithmetic, per_device(): start + jnp.where(segment > s, jnp.sum((segment == s).astype(jnp.int32)), 0)  5.27 us
    another operation x10, other arithmetic  5.19 us
  transfers between devices with their start and end apart: 48, of which 27 were waited for; matrix products, arithmetic and copies ran while one was open for 15% of the time, Pallas kernels for 14%

profile of v1, /device:TPU:0, one launch (start us, length us, event | category | flops | bytes accessed | tf_op | source)
XLA Modules:
  0.0 237.5 jit_solution(7673603495538764048)
XLA Ops:
  0.7 1.3 convert_element_type.209.refs_0_
  2.0 3.0 %collective-permute-start.4 = (bf16[512,512]{1,0:T(8,128)(2,1)S(1)}, bf16[512,512]{1,0:T(8,128)(2,1)S(1)}, u32[]{:S(2)}, u32[]{:S(2)}) collective-permute-start(bf16[512,512]{1,0:T(8,128)(2,1)S(1)} %convert_element_type.209.refs_0_), channel_id=1, source_target_pairs={{0,2},{1,3},{2,0},{3,1},{4,6},{5,7},{6,4},{7,5},{8,10},{9,11},{10,... | collective-permute-start | bytes 1572872 | tf_op jit(solution)/shard_map/ppermute | solution.py:54
  6.8 2.7 %collective-permute-start.14 = (bf16[1,64,640]{2,1,0:T(8,128)(2,1)S(1)}, bf16[1,64,640]{2,1,0:T(8,128)(2,1)S(1)}, u32[]{:S(2)}, u32[]{:S(2)}) collective-permute-start(bf16[1,64,640]{2,1,0:T(8,128)(2,1)S(1)} %maximum_bitcast_fusion), channel_id=1, source_target_pairs={{0,16},{4,20},{8,24},{12,28},{16,0},{20,4},{24,8},{28,12},{1,17},{... | collective-permute-start | bytes 245768 | tf_op jit(solution)/shard_map/ppermute | solution.py:54
  9.4 1.5 constant_dynamic-update-slice_fusion.4
  11.4 2.7 %collective-permute-start = (bf16[1,80,384]{2,1,0:T(8,128)(2,1)S(1)}, bf16[1,80,384]{2,1,0:T(8,128)(2,1)S(1)}, u32[]{:S(2)}, u32[]{:S(2)}) collective-permute-start(bf16[1,80,384]{2,1,0:T(8,128)(2,1)S(1)} %fusion.8), channel_id=1, source_target_pairs={{0,16},{4,20},{8,24},{12,28},{16,0},{20,4},{24,8},{28,12},{1,17},{... | collective-permute-start | bytes 184328 | tf_op jit(solution)/shard_map/ppermute | solution.py:54
  15.5 4.0 %collective-permute-done.9 = bf16[1,64,512]{2,1,0:T(8,128)(2,1)S(1)} collective-permute-done((bf16[1,64,512]{2,1,0:T(8,128)(2,1)S(1)}, bf16[1,64,512]{2,1,0:T(8,128)(2,1)S(1)}, u32[]{:S(2)}, u32[]{:S(2)}) %collective-permute-start.9) | collective-permute-done | bytes 65568 | tf_op jit(solution)/shard_map/ppermute | solution.py:54
  19.6 2.1 collective-permute-start.15
  21.7 3.2 %collective-permute-done.10 = bf16[2,64,512]{2,1,0:T(8,128)(2,1)S(1)} collective-permute-done((bf16[2,64,512]{2,1,0:T(8,128)(2,1)S(1)}, bf16[2,64,512]{2,1,0:T(8,128)(2,1)S(1)}, u32[]{:S(2)}, u32[]{:S(2)}) %collective-permute-start.10) | collective-permute-done | bytes 131104 | tf_op jit(solution)/shard_map/ppermute | solution.py:54
  24.9 1.6 collective-permute-start.11
  27.3 1.7 collective-permute-start.1
  29.6 1.8 collective-permute-done.11
  32.0 5.4 %collective-permute-done.16 = bf16[4,64,640]{2,1,0:T(8,128)(2,1)S(1)} collective-permute-done((bf16[4,64,640]{2,1,0:T(8,128)(2,1)S(1)}, bf16[4,64,640]{2,1,0:T(8,128)(2,1)S(1)}, u32[]{:S(2)}, u32[]{:S(2)}) %collective-permute-start.16) | collective-permute-done | bytes 327712 | tf_op jit(solution)/shard_map/ppermute | solution.py:54
  37.5 1.6 collective-permute-start.17
  42.6 3.0 %collective-permute-done.12 = bf16[8,64,512]{2,1,0:T(8,128)(2,1)S(1)} collective-permute-done((bf16[8,64,512]{2,1,0:T(8,128)(2,1)S(1)}, bf16[8,64,512]{2,1,0:T(8,128)(2,1)S(1)}, u32[]{:S(2)}, u32[]{:S(2)}) %collective-permute-start.12) | collective-permute-done | bytes 524320 | tf_op jit(solution)/shard_map/ppermute | solution.py:54
  46.4 1.7 collective-permute-done.17
  49.2 5.3 %fusion.23.start_ref = s32[1,2048]{1,0:T(1,128)S(1)} fusion(s32[1,2048]{1,0:T(1,128)S(1)} %copy-done.28, s32[]{:T(128)} %get-tuple-element.90, s32[]{:T(128)} %get-tuple-element.89, s32[]{:T(128)} %get-tuple-element.85, s32[]{:T(128)} %get-tuple-element.87, s32[]{:T(128)} %get-tuple-element.91, s32[]{:T(128)} %get-tuple-element.86, s32[]{:T(128)} %get-tuple-element.88, ...), kind=kLoop, calls=%fused_computation.112 | loop fusion | flops 47104 | bytes 16416 | tf_op jit(solution)/shard_map/add | solution.py:527
  55.1 1.6 collective-permute-start.2
  56.8 6.2 %collective-permute-done.2 = bf16[4,80,384]{2,1,0:T(8,128)(2,1)S(1)} collective-permute-done((bf16[4,80,384]{2,1,0:T(8,128)(2,1)S(1)}, bf16[4,80,384]{2,1,0:T(8,128)(2,1)S(1)}, u32[]{:S(2)}, u32[]{:S(2)}) %collective-permute-start.2) | collective-permute-done | bytes 245792 | tf_op jit(solution)/shard_map/ppermute | solution.py:54
  63.2 13.7 %shard_map.447 = (bf16[528,128]{1,0:T(8,128)(2,1)S(1)}, bf16[528,128]{1,0:T(8,128)(2,1)S(1)}, bf16[528,128]{1,0:T(8,128)(2,1)S(1)}, bf16[528,128]{1,0:T(8,128)(2...) custom-call(s32[2]{0:T(128)S(1)} %pad_add_fusion.idx_ref, ...), custom_call_target="tpu_custom_call" | custom-call | flops 3000000000 | bytes 6000000 | tf_op jit(solution)/shard_map/pallas_call | solution.py:434
  80.2 2.3 constant_dynamic-update-slice_fusion.16.refs_5_
  83.4 2.0 collective-permute-done.8.refs_3_
  85.4 21.4 %shard_map.448 = (f32[512,512]{1,0:T(8,128)}, f32[512,512]{1,0:T(8,128)}, f32[512,512]{1,0:T(8,128)}, bf16[512,128]{1,0:T(8,128)(2,1)S(1)}, bf16[512,128]{1,0:T(...) custom-call(s32[2]{0:T(128)S(1)} %pad_add_fusion.idx_ref, ...), custom_call_target="tpu_custom_call" | custom-call | flops 8000000000 | bytes 16000000 | tf_op jit(solution)/shard_map/pallas_call | solution.py:434
  109.7 4.0 %collective-permute-done.20.refs_2_ = bf16[512,128]{1,0:T(8,128)(2,1)S(1)} collective-permute-done((bf16[512,128]{1,0:T(8,128)(2,1)S(1)}, bf16[512,128]{1,0:T(8,128)(2,1)S(1)}, u32[]{:S(2)}, u32[]{:S(2)}) %collective-permute-start.20) | collective-permute-done | bytes 131104 | tf_op jit(solution)/shard_map/ppermute | solution.py:592
  113.6 1.5 collective-permute-done.21.refs_3_
  115.2 15.3 %shard_map.449 = (bf16[2048,384]{1,0:T(8,128)(2,1)S(1)}, f32[48,128]{1,0:T(8,128)S(1)}) custom-call(s32[2]{0:T(128)S(1)} %pad_add_fusion.idx_ref, s32[8]{0:T(128)S(1)} %and_select_fusion.lo_ref, s32[1,2048]{1,0:T(1,128)S(1)} %fusion.23.start_ref, bf16[2048,128]{1,0:T(8,128)(2,1)S(1)} %get-tuple-element.63.q_ref, ...), custom_call_target="tpu_custom_call" | custom-call | flops 4000000000 | bytes 6000000 | tf_op jit(solution)/shard_map/pallas_call | solution.py:434
  131.2 1.9 shard_map.451
  135.6 3.3 %collective-permute-done.44 = f32[48,128]{1,0:T(8,128)S(1)} collective-permute-done((f32[48,128]{1,0:T(8,128)S(1)}, f32[48,128]{1,0:T(8,128)S(1)}, u32[]{:S(2)}, u32[]{:S(2)}) %collective-permute-start.44) | collective-permute-done | bytes 24608 | tf_op jit(solution)/shard_map/ppermute | solution.py:54
  139.0 1.9 collective-permute-start.45
  142.8 3.4 %collective-permute-start.46 = (f32[48,128]{1,0:T(8,128)S(1)}, f32[48,128]{1,0:T(8,128)S(1)}, u32[]{:S(2)}, u32[]{:S(2)}) collective-permute-start(f32[48,128]{1,0:T(8,128)S(1)} %add.283), channel_id=1, source_target_pairs={{0,8},{4,12},{8,0},{12,4},{16,24},{20,28},{24,16},{28,20},{1,9},{5... | collective-permute-start | bytes 73736 | tf_op jit(solution)/shard_map/ppermute | solution.py:54
  147.8 2.6 %shard_map.450 = (bf16[512,512]{1,0:T(8,128)(2,1)S(1)}, bf16[512,512]{1,0:T(8,128)(2,1)S(1)}, bf16[512,512]{1,0:T(8,128)(2,1)S(1)}, bf16[512,512]{1,0:T(8,128)(2,1)}) custom-call(s32[2]{0:T(128)S(1)} %copy-done.5, bf16[2048,384]{1,0:T(8,128)(2,1)S(1)} %get-tuple-element.73.gqkv_ref, bf16[512,384]{1,0:T(8,128)(2,1)S(1)} %copy-done.7), custom_call_target="tpu_custom_call" | custom-call | flops 800000000 | bytes 4000000 | tf_op jit(solution)/shard_map/pallas_call | solution.py:434
  151.0 6.5 %collective-permute-start.47 = (f32[48,128]{1,0:T(8,128)S(1)}, f32[48,128]{1,0:T(8,128)S(1)}, u32[]{:S(2)}, u32[]{:S(2)}) collective-permute-start(f32[48,128]{1,0:T(8,128)S(1)} %add.284), channel_id=1, source_target_pairs={{0,16},{4,20},{8,24},{12,28},{16,0},{20,4},{24,8},{28,12},{1,17},{... | collective-permute-start | bytes 73736 | tf_op jit(solution)/shard_map/ppermute | solution.py:54
  158.6 2.0 add_convert_fusion.1
  161.2 1.7 add_convert_fusion
  164.5 9.7 %collective-permute-done.29 = bf16[8,64,512]{2,1,0:T(8,128)(2,1)S(1)} collective-permute-done((bf16[8,64,512]{2,1,0:T(8,128)(2,1)S(1)}, bf16[8,64,512]{2,1,0:T(8,128)(2,1)S(1)}, u32[]{:S(2)}, u32[]{:S(2)}) %collective-permute-start.29) | collective-permute-done | bytes 524320 | tf_op jit(solution)/shard_map/ppermute | solution.py:54
  174.6 6.1 %collective-permute-done.34 = bf16[8,64,640]{2,1,0:T(8,128)(2,1)S(1)} collective-permute-done((bf16[8,64,640]{2,1,0:T(8,128)(2,1)S(1)}, bf16[8,64,640]{2,1,0:T(8,128)(2,1)S(1)}, u32[]{:S(2)}, u32[]{:S(2)}) %collective-permute-start.34) | collective-permute-done | bytes 655392 | tf_op jit(solution)/shard_map/ppermute | solution.py:54
  180.9 1.6 collective-permute-start.35
  183.1 1.6 collective-permute-done.30
  184.8 1.8 collective-permute-start.31
  186.6 1.4 collective-permute-done.35
  188.2 2.1 collective-permute-start.36
  191.3 2.4 %collective-permute-done.36 = bf16[2,64,640]{2,1,0:T(8,128)(2,1)S(1)} collective-permute-done((bf16[2,64,640]{2,1,0:T(8,128)(2,1)S(1)}, bf16[2,64,640]{2,1,0:T(8,128)(2,1)S(1)}, u32[]{:S(2)}, u32[]{:S(2)}) %collective-permute-start.36) | collective-permute-done | bytes 163872 | tf_op jit(solution)/shard_map/ppermute | solution.py:54
  194.5 1.6 collective-permute-done.32
  201.8 1.6 collective-permute-start.24
  204.6 11.7 %collective-permute-done.39 = f32[8,128]{1,0:T(8,128)S(1)} collective-permute-done((f32[8,128]{1,0:T(8,128)S(1)}, f32[8,128]{1,0:T(8,128)S(1)}, u32[]{:S(2)}, u32[]{:S(2)}) %collective-permute-start.39) | collective-permute-done | bytes 4128 | tf_op jit(solution)/shard_map/ppermute | solution.py:54
  217.4 2.6 %collective-permute-done.40 = f32[8,128]{1,0:T(8,128)S(1)} collective-permute-done((f32[8,128]{1,0:T(8,128)S(1)}, f32[8,128]{1,0:T(8,128)S(1)}, u32[]{:S(2)}, u32[]{:S(2)}) %collective-permute-start.40) | collective-permute-done | bytes 4128 | tf_op jit(solution)/shard_map/ppermute | solution.py:54
  219.9 2.5 %collective-permute-start.41 = (f32[8,128]{1,0:T(8,128)S(1)}, f32[8,128]{1,0:T(8,128)S(1)}, u32[]{:S(2)}, u32[]{:S(2)}) collective-permute-start(f32[8,128]{1,0:T(8,128)S(1)} %add.278), channel_id=1, source_target_pairs={{0,8},{4,12},{8,0},{12,4},{16,24},{20,28},{24,16},{28,20},{1,9},{5... | collective-permute-start | bytes 12296 | tf_op jit(solution)/shard_map/ppermute | solution.py:54
  222.5 2.7 %convert_add_fusion = f32[512,512]{1,0:T(8,128)} fusion(bf16[512,512]{1,0:T(8,128)(2,1)S(1)} %collective-permute-done.24, bf16[512,512]{1,0:T(8,128)(2,1)} %collective-permute-done.22, f32[512,512]{1,0:T(8,128)} %get-tuple-element.62, bf16[512,512]{1,0:T(8,128)(2,1)S(1)} %get-tuple-element.75), kind=kLoop, calls=%fused_computation.4 | loop fusion | flops 1572864 | bytes 3670016 | tf_op jit(solution)/shard_map/add | solution.py:641
  225.8 4.0 %collective-permute-done.42 = f32[8,128]{1,0:T(8,128)S(1)} collective-permute-done((f32[8,128]{1,0:T(8,128)S(1)}, f32[8,128]{1,0:T(8,128)S(1)}, u32[]{:S(2)}, u32[]{:S(2)}) %collective-permute-start.42) | collective-permute-done | bytes 4128 | tf_op jit(solution)/shard_map/ppermute | solution.py:54
  (220 shorter events, 44.0 us)
Async XLA Ops:
  2.0 52.5 %collective-permute-start.4 = (bf16[512,512]{1,0:T(8,128)(2,1)S(1)}, bf16[512,512]{1,0:T(8,128)(2,1)S(1)}, u32[]{:S(2)}, u32[]{:S(2)}) collective-permute-start(bf16[512,512]{1,0:T(8,128)(2,1)S(1)} %convert_element_type.209.refs_0_), channel_id=1, source_target_pairs={{0,2},{1,3},{2,0},{3,1},{4,6},{5,7},{6,4},{7,5},{8,10},{9,11},{10,... | collective-permute-start | bytes 1572872 | tf_op jit(solution)/shard_map/ppermute | solution.py:54
  5.1 58.1 %collective-permute-start.3 = (bf16[512,512]{1,0:T(8,128)(2,1)S(1)}, bf16[512,512]{1,0:T(8,128)(2,1)S(1)}, u32[]{:S(2)}, u32[]{:S(2)}) collective-permute-start(bf16[512,512]{1,0:T(8,128)(2,1)S(1)} %convert_element_type.209.refs_0_), channel_id=1, source_target_pairs={{0,1},{1,0},{2,3},{3,2},{4,5},{5,4},{6,7},{7,6},{8,9},{9,8},{10,11... | collective-permute-start | bytes 1572872 | tf_op jit(solution)/shard_map/ppermute | solution.py:54
  6.8 12.8 %collective-permute-start.14 = (bf16[1,64,640]{2,1,0:T(8,128)(2,1)S(1)}, bf16[1,64,640]{2,1,0:T(8,128)(2,1)S(1)}, u32[]{:S(2)}, u32[]{:S(2)}) collective-permute-start(bf16[1,64,640]{2,1,0:T(8,128)(2,1)S(1)} %maximum_bitcast_fusion), channel_id=1, source_target_pairs={{0,16},{4,20},{8,24},{12,28},{16,0},{20,4},{24,8},{28,12},{1,17},{... | collective-permute-start | bytes 245768 | tf_op jit(solution)/shard_map/ppermute | solution.py:54
  11.0 8.5 %collective-permute-start.9 = (bf16[1,64,512]{2,1,0:T(8,128)(2,1)S(1)}, bf16[1,64,512]{2,1,0:T(8,128)(2,1)S(1)}, u32[]{:S(2)}, u32[]{:S(2)}) collective-permute-start(bf16[1,64,512]{2,1,0:T(8,128)(2,1)S(1)} %get-tuple-element.118), channel_id=1, source_target_pairs={{0,16},{4,20},{8,24},{12,28},{16,0},{20,4},{24,8},{28,12},{1,17},{... | collective-permute-start | bytes 196616 | tf_op jit(solution)/shard_map/ppermute | solution.py:54
  11.4 15.8 %collective-permute-start = (bf16[1,80,384]{2,1,0:T(8,128)(2,1)S(1)}, bf16[1,80,384]{2,1,0:T(8,128)(2,1)S(1)}, u32[]{:S(2)}, u32[]{:S(2)}) collective-permute-start(bf16[1,80,384]{2,1,0:T(8,128)(2,1)S(1)} %fusion.8), channel_id=1, source_target_pairs={{0,16},{4,20},{8,24},{12,28},{16,0},{20,4},{24,8},{28,12},{1,17},{... | collective-permute-start | bytes 184328 | tf_op jit(solution)/shard_map/ppermute | solution.py:54
  19.5 5.4 %collective-permute-start.10 = (bf16[2,64,512]{2,1,0:T(8,128)(2,1)S(1)}, bf16[2,64,512]{2,1,0:T(8,128)(2,1)S(1)}, u32[]{:S(2)}, u32[]{:S(2)}) collective-permute-start(bf16[2,64,512]{2,1,0:T(8,128)(2,1)S(1)} %pad_maximum_fusion.7), channel_id=1, source_target_pairs={{0,8},{4,12},{8,0},{12,4},{16,24},{20,28},{24,16},{28,20},{1,9},{5... | collective-permute-start | bytes 393224 | tf_op jit(solution)/shard_map/ppermute | solution.py:54
  19.6 7.0 %collective-permute-start.15 = (bf16[2,64,640]{2,1,0:T(8,128)(2,1)S(1)}, bf16[2,64,640]{2,1,0:T(8,128)(2,1)S(1)}, u32[]{:S(2)}, u32[]{:S(2)}) collective-permute-start(bf16[2,64,640]{2,1,0:T(8,128)(2,1)S(1)} %pad_maximum_fusion.6), channel_id=1, source_target_pairs={{0,8},{4,12},{8,0},{12,4},{16,24},{20,28},{24,16},{28,20},{1,9},{5... | collective-permute-start | bytes 491528 | tf_op jit(solution)/shard_map/ppermute | solution.py:54
  24.9 6.4 %collective-permute-start.11 = (bf16[4,64,512]{2,1,0:T(8,128)(2,1)S(1)}, bf16[4,64,512]{2,1,0:T(8,128)(2,1)S(1)}, u32[]{:S(2)}, u32[]{:S(2)}) collective-permute-start(bf16[4,64,512]{2,1,0:T(8,128)(2,1)S(1)} %pad_maximum_fusion.4), channel_id=1, source_target_pairs={{0,4},{4,0},{8,12},{12,8},{16,20},{20,16},{24,28},{28,24},{1,5},{5... | collective-permute-start | bytes 786440 | tf_op jit(solution)/shard_map/ppermute | solution.py:54
  26.7 10.7 %collective-permute-start.16 = (bf16[4,64,640]{2,1,0:T(8,128)(2,1)S(1)}, bf16[4,64,640]{2,1,0:T(8,128)(2,1)S(1)}, u32[]{:S(2)}, u32[]{:S(2)}) collective-permute-start(bf16[4,64,640]{2,1,0:T(8,128)(2,1)S(1)} %pad_maximum_fusion.3), channel_id=1, source_target_pairs={{0,2},{1,3},{2,0},{3,1},{4,6},{5,7},{6,4},{7,5},{8,10},{9,11},{10,... | collective-permute-start | bytes 983048 | tf_op jit(solution)/shard_map/ppermute | solution.py:54
  27.3 27.8 %collective-permute-start.1 = (bf16[2,80,384]{2,1,0:T(8,128)(2,1)S(1)}, bf16[2,80,384]{2,1,0:T(8,128)(2,1)S(1)}, u32[]{:S(2)}, u32[]{:S(2)}) collective-permute-start(bf16[2,80,384]{2,1,0:T(8,128)(2,1)S(1)} %pad_maximum_fusion.8), channel_id=1, source_target_pairs={{0,8},{4,12},{8,0},{12,4},{16,24},{20,28},{24,16},{28,20},{1,9},{5... | collective-permute-start | bytes 368648 | tf_op jit(solution)/shard_map/ppermute | solution.py:54
  31.4 14.1 %collective-permute-start.12 = (bf16[8,64,512]{2,1,0:T(8,128)(2,1)S(1)}, bf16[8,64,512]{2,1,0:T(8,128)(2,1)S(1)}, u32[]{:S(2)}, u32[]{:S(2)}) collective-permute-start(bf16[8,64,512]{2,1,0:T(8,128)(2,1)S(1)} %pad_maximum_fusion.1), channel_id=1, source_target_pairs={{0,2},{1,3},{2,0},{3,1},{4,6},{5,7},{6,4},{7,5},{8,10},{9,11},{10,... | collective-permute-start | bytes 1572872 | tf_op jit(solution)/shard_map/ppermute | solution.py:54
  37.5 10.7 %collective-permute-start.17 = (bf16[8,64,640]{2,1,0:T(8,128)(2,1)S(1)}, bf16[8,64,640]{2,1,0:T(8,128)(2,1)S(1)}, u32[]{:S(2)}, u32[]{:S(2)}) collective-permute-start(bf16[8,64,640]{2,1,0:T(8,128)(2,1)S(1)} %pad_maximum_fusion), channel_id=1, source_target_pairs={{0,4},{4,0},{8,12},{12,8},{16,20},{20,16},{24,28},{28,24},{1,5},{5... | collective-permute-start | bytes 1966088 | tf_op jit(solution)/shard_map/ppermute | solution.py:54
  46.4 32.4 %collective-permute-start.13 = (bf16[16,64,512]{2,1,0:T(8,128)(2,1)}, bf16[16,64,512]{2,1,0:T(8,128)(2,1)}, u32[]{:S(2)}, u32[]{:S(2)}) collective-permute-start(bf16[16,64,512]{2,1,0:T(8,128)(2,1)} %get-tuple-element.121), channel_id=1, source_target_pairs={{0,1},{1,0},{2,3},{3,2},{4,5},{5,4},{6,7},{7,6},{8,9},{9,8},{10,11... | collective-permute-start | bytes 3145736 | tf_op jit(solution)/shard_map/ppermute | solution.py:54
  49.2 31.0 %collective-permute-start.18 = (bf16[16,64,640]{2,1,0:T(8,128)(2,1)}, bf16[16,64,640]{2,1,0:T(8,128)(2,1)}, u32[]{:S(2)}, u32[]{:S(2)}) collective-permute-start(bf16[16,64,640]{2,1,0:T(8,128)(2,1)} %get-tuple-element.119), channel_id=1, source_target_pairs={{0,1},{1,0},{2,3},{3,2},{4,5},{5,4},{6,7},{7,6},{8,9},{9,8},{10,11... | collective-permute-start | bytes 3932168 | tf_op jit(solution)/shard_map/ppermute | solution.py:54
  54.5 8.6 %collective-permute-start.5 = (bf16[512,512]{1,0:T(8,128)(2,1)S(1)}, bf16[512,512]{1,0:T(8,128)(2,1)S(1)}, u32[]{:S(2)}, u32[]{:S(2)}) collective-permute-start(bf16[512,512]{1,0:T(8,128)(2,1)S(1)} %collective-permute-done.4.refs_2_), channel_id=1, source_target_pairs={{0,1},{1,0},{2,3},{3,2},{4,5},{5,4},{6,7},{7,6},{8,9},{9,8},{10,11... | collective-permute-start | bytes 1572872 | tf_op jit(solution)/shard_map/ppermute | solution.py:54
  55.1 8.0 %collective-permute-start.2 = (bf16[4,80,384]{2,1,0:T(8,128)(2,1)S(1)}, bf16[4,80,384]{2,1,0:T(8,128)(2,1)S(1)}, u32[]{:S(2)}, u32[]{:S(2)}) collective-permute-start(bf16[4,80,384]{2,1,0:T(8,128)(2,1)S(1)} %pad_maximum_fusion.5), channel_id=1, source_target_pairs={{0,4},{4,0},{8,12},{12,8},{16,20},{20,16},{24,28},{28,24},{1,5},{5... | collective-permute-start | bytes 737288 | tf_op jit(solution)/shard_map/ppermute | solution.py:54
  76.9 5.6 %collective-permute-start.6 = (bf16[528,128]{1,0:T(8,128)(2,1)S(1)}, bf16[528,128]{1,0:T(8,128)(2,1)S(1)}, u32[]{:S(2)}, u32[]{:S(2)}) collective-permute-start(bf16[528,128]{1,0:T(8,128)(2,1)S(1)} %get-tuple-element.57), channel_id=1, source_target_pairs={{0,1},{1,0},{2,3},{3,2},{4,5},{5,4},{6,7},{7,6},{8,9},{9,8},{10,11... | collective-permute-start | bytes 405512 | tf_op jit(solution)/shard_map/ppermute | solution.py:554
  77.0 6.5 %collective-permute-start.7 = (bf16[528,128]{1,0:T(8,128)(2,1)S(1)}, bf16[528,128]{1,0:T(8,128)(2,1)S(1)}, u32[]{:S(2)}, u32[]{:S(2)}) collective-permute-start(bf16[528,128]{1,0:T(8,128)(2,1)S(1)} %get-tuple-element.58), channel_id=1, source_target_pairs={{0,2},{1,3},{2,0},{3,1},{4,6},{5,7},{6,4},{7,5},{8,10},{9,11},{10,... | collective-permute-start | bytes 405512 | tf_op jit(solution)/shard_map/ppermute | solution.py:554
  77.6 7.9 %collective-permute-start.8 = (bf16[528,128]{1,0:T(8,128)(2,1)S(1)}, bf16[528,128]{1,0:T(8,128)(2,1)S(1)}, u32[]{:S(2)}, u32[]{:S(2)}) collective-permute-start(bf16[528,128]{1,0:T(8,128)(2,1)S(1)} %get-tuple-element.59), channel_id=1, source_target_pairs={{0,3},{1,2},{2,1},{3,0},{4,7},{5,6},{6,5},{7,4},{8,11},{9,10},{10,... | collective-permute-start | bytes 405512 | tf_op jit(solution)/shard_map/ppermute | solution.py:554
  106.8 51.7 %collective-permute-start.28 = (bf16[16,64,512]{2,1,0:T(8,128)(2,1)}, bf16[16,64,512]{2,1,0:T(8,128)(2,1)}, u32[]{:S(2)}, u32[]{:S(2)}) collective-permute-start(bf16[16,64,512]{2,1,0:T(8,128)(2,1)} %get-tuple-element.80), channel_id=1, source_target_pairs={{0,1},{1,0},{2,3},{3,2},{4,5},{5,4},{6,7},{7,6},{8,9},{9,8},{10,11... | collective-permute-start | bytes 3145736 | tf_op jit(solution)/shard_map/ppermute | solution.py:54
  107.1 2.6 %collective-permute-start.19 = (bf16[512,128]{1,0:T(8,128)(2,1)S(1)}, bf16[512,128]{1,0:T(8,128)(2,1)S(1)}, u32[]{:S(2)}, u32[]{:S(2)}) collective-permute-start(bf16[512,128]{1,0:T(8,128)(2,1)S(1)} %get-tuple-element.70), channel_id=1, source_target_pairs={{0,1},{1,0},{2,3},{3,2},{4,5},{5,4},{6,7},{7,6},{8,9},{9,8},{10,11... | collective-permute-start | bytes 393224 | tf_op jit(solution)/shard_map/ppermute | solution.py:592
  107.3 6.3 %collective-permute-start.20 = (bf16[512,128]{1,0:T(8,128)(2,1)S(1)}, bf16[512,128]{1,0:T(8,128)(2,1)S(1)}, u32[]{:S(2)}, u32[]{:S(2)}) collective-permute-start(bf16[512,128]{1,0:T(8,128)(2,1)S(1)} %get-tuple-element.71), channel_id=1, source_target_pairs={{0,2},{1,3},{2,0},{3,1},{4,6},{5,7},{6,4},{7,5},{8,10},{9,11},{10,... | collective-permute-start | bytes 393224 | tf_op jit(solution)/shard_map/ppermute | solution.py:592
  107.8 7.3 %collective-permute-start.21 = (bf16[512,128]{1,0:T(8,128)(2,1)S(1)}, bf16[512,128]{1,0:T(8,128)(2,1)S(1)}, u32[]{:S(2)}, u32[]{:S(2)}) collective-permute-start(bf16[512,128]{1,0:T(8,128)(2,1)S(1)} %get-tuple-element.72), channel_id=1, source_target_pairs={{0,3},{1,2},{2,1},{3,0},{4,7},{5,6},{6,5},{7,4},{8,11},{9,10},{10,... | collective-permute-start | bytes 393224 | tf_op jit(solution)/shard_map/ppermute | solution.py:592
  108.9 51.7 %collective-permute-start.33 = (bf16[16,64,640]{2,1,0:T(8,128)(2,1)}, bf16[16,64,640]{2,1,0:T(8,128)(2,1)}, u32[]{:S(2)}, u32[]{:S(2)}) collective-permute-start(bf16[16,64,640]{2,1,0:T(8,128)(2,1)} %get-tuple-element.82), channel_id=1, source_target_pairs={{0,1},{1,0},{2,3},{3,2},{4,5},{5,4},{6,7},{7,6},{8,9},{9,8},{10,11... | collective-permute-start | bytes 3932168 | tf_op jit(solution)/shard_map/ppermute | solution.py:54
  133.8 17.2 %collective-permute-start.25 = (bf16[4,64,384]{2,1,0:T(8,128)(2,1)}, bf16[4,64,384]{2,1,0:T(8,128)(2,1)}, u32[]{:S(2)}, u32[]{:S(2)}) collective-permute-start(bf16[4,64,384]{2,1,0:T(8,128)(2,1)} %slice.129), channel_id=1, source_target_pairs={{0,4},{4,0},{8,12},{12,8},{16,20},{20,16},{24,28},{28,24},{1,5},{5... | collective-permute-start | bytes 589832 | tf_op jit(solution)/shard_map/ppermute | solution.py:54
  133.8 1.3 collective-permute-start.43
  135.1 3.8 %collective-permute-start.44 = (f32[48,128]{1,0:T(8,128)S(1)}, f32[48,128]{1,0:T(8,128)S(1)}, u32[]{:S(2)}, u32[]{:S(2)}) collective-permute-start(f32[48,128]{1,0:T(8,128)S(1)} %add.281), channel_id=1, source_target_pairs={{0,2},{1,3},{2,0},{3,1},{4,6},{5,7},{6,4},{7,5},{8,10},{9,11},{10,... | collective-permute-start | bytes 73736 | tf_op jit(solution)/shard_map/ppermute | solution.py:54
  139.0 3.8 %collective-permute-start.45 = (f32[48,128]{1,0:T(8,128)S(1)}, f32[48,128]{1,0:T(8,128)S(1)}, u32[]{:S(2)}, u32[]{:S(2)}) collective-permute-start(f32[48,128]{1,0:T(8,128)S(1)} %add.282), channel_id=1, source_target_pairs={{0,4},{4,0},{8,12},{12,8},{16,20},{20,16},{24,28},{28,24},{1,5},{5... | collective-permute-start | bytes 73736 | tf_op jit(solution)/shard_map/ppermute | solution.py:54
  142.8 7.7 %collective-permute-start.46 = (f32[48,128]{1,0:T(8,128)S(1)}, f32[48,128]{1,0:T(8,128)S(1)}, u32[]{:S(2)}, u32[]{:S(2)}) collective-permute-start(f32[48,128]{1,0:T(8,128)S(1)} %add.283), channel_id=1, source_target_pairs={{0,8},{4,12},{8,0},{12,4},{16,24},{20,28},{24,16},{28,20},{1,9},{5... | collective-permute-start | bytes 73736 | tf_op jit(solution)/shard_map/ppermute | solution.py:54
  150.4 50.2 %collective-permute-start.23 = (bf16[512,512]{1,0:T(8,128)(2,1)}, bf16[512,512]{1,0:T(8,128)(2,1)}, u32[]{:S(2)}, u32[]{:S(2)}) collective-permute-start(bf16[512,512]{1,0:T(8,128)(2,1)} %get-tuple-element.78), channel_id=1, source_target_pairs={{0,1},{1,0},{2,3},{3,2},{4,5},{5,4},{6,7},{7,6},{8,9},{9,8},{10,11... | collective-permute-start | bytes 1572872 | tf_op jit(solution)/shard_map/ppermute | solution.py:54
  150.4 72.0 %collective-permute-start.22 = (bf16[512,512]{1,0:T(8,128)(2,1)S(1)}, bf16[512,512]{1,0:T(8,128)(2,1)}, u32[]{:S(2)}, u32[]{:S(2)}) collective-permute-start(bf16[512,512]{1,0:T(8,128)(2,1)S(1)} %get-tuple-element.76), channel_id=1, source_target_pairs={{0,1},{1,0},{2,3},{3,2},{4,5},{5,4},{6,7},{7,6},{8,9},{9,8},{10,11... | collective-permute-start | bytes 1572872 | tf_op jit(solution)/shard_map/ppermute | solution.py:54
  151.0 12.0 %collective-permute-start.47 = (f32[48,128]{1,0:T(8,128)S(1)}, f32[48,128]{1,0:T(8,128)S(1)}, u32[]{:S(2)}, u32[]{:S(2)}) collective-permute-start(f32[48,128]{1,0:T(8,128)S(1)} %add.284), channel_id=1, source_target_pairs={{0,16},{4,20},{8,24},{12,28},{16,0},{20,4},{24,8},{28,12},{1,17},{... | collective-permute-start | bytes 73736 | tf_op jit(solution)/shard_map/ppermute | solution.py:54
  158.5 5.9 %collective-permute-start.26 = (bf16[2,64,384]{2,1,0:T(8,128)(2,1)S(1)}, bf16[2,64,384]{2,1,0:T(8,128)(2,1)S(1)}, u32[]{:S(2)}, u32[]{:S(2)}) collective-permute-start(bf16[2,64,384]{2,1,0:T(8,128)(2,1)S(1)} %slice.131), channel_id=1, source_target_pairs={{0,8},{4,12},{8,0},{12,4},{16,24},{20,28},{24,16},{28,20},{1,9},{5... | collective-permute-start | bytes 294920 | tf_op jit(solution)/shard_map/ppermute | solution.py:54
  160.6 13.6 %collective-permute-start.29 = (bf16[8,64,512]{2,1,0:T(8,128)(2,1)S(1)}, bf16[8,64,512]{2,1,0:T(8,128)(2,1)S(1)}, u32[]{:S(2)}, u32[]{:S(2)}) collective-permute-start(bf16[8,64,512]{2,1,0:T(8,128)(2,1)S(1)} %slice.135), channel_id=1, source_target_pairs={{0,2},{1,3},{2,0},{3,1},{4,6},{5,7},{6,4},{7,5},{8,10},{9,11},{10,... | collective-permute-start | bytes 1572872 | tf_op jit(solution)/shard_map/ppermute | solution.py:54
  163.0 17.7 %collective-permute-start.34 = (bf16[8,64,640]{2,1,0:T(8,128)(2,1)S(1)}, bf16[8,64,640]{2,1,0:T(8,128)(2,1)S(1)}, u32[]{:S(2)}, u32[]{:S(2)}) collective-permute-start(bf16[8,64,640]{2,1,0:T(8,128)(2,1)S(1)} %slice.143), channel_id=1, source_target_pairs={{0,4},{4,0},{8,12},{12,8},{16,20},{20,16},{24,28},{28,24},{1,5},{5... | collective-permute-start | bytes 1966088 | tf_op jit(solution)/shard_map/ppermute | solution.py:54
  164.5 18.1 %collective-permute-start.27 = (bf16[1,64,384]{2,1,0:T(8,128)(2,1)S(1)}, bf16[1,64,384]{2,1,0:T(8,128)(2,1)S(1)}, u32[]{:S(2)}, u32[]{:S(2)}) collective-permute-start(bf16[1,64,384]{2,1,0:T(8,128)(2,1)S(1)} %slice.133), channel_id=1, source_target_pairs={{0,16},{4,20},{8,24},{12,28},{16,0},{20,4},{24,8},{28,12},{1,17},{... | collective-permute-start | bytes 147464 | tf_op jit(solution)/shard_map/ppermute | solution.py:54
  174.4 10.3 %collective-permute-start.30 = (bf16[4,64,512]{2,1,0:T(8,128)(2,1)S(1)}, bf16[4,64,512]{2,1,0:T(8,128)(2,1)S(1)}, u32[]{:S(2)}, u32[]{:S(2)}) collective-permute-start(bf16[4,64,512]{2,1,0:T(8,128)(2,1)S(1)} %slice.137), channel_id=1, source_target_pairs={{0,4},{4,0},{8,12},{12,8},{16,20},{20,16},{24,28},{28,24},{1,5},{5... | collective-permute-start | bytes 786440 | tf_op jit(solution)/shard_map/ppermute | solution.py:54
  180.9 7.1 %collective-permute-start.35 = (bf16[4,64,640]{2,1,0:T(8,128)(2,1)S(1)}, bf16[4,64,640]{2,1,0:T(8,128)(2,1)S(1)}, u32[]{:S(2)}, u32[]{:S(2)}) collective-permute-start(bf16[4,64,640]{2,1,0:T(8,128)(2,1)S(1)} %slice.145), channel_id=1, source_target_pairs={{0,2},{1,3},{2,0},{3,1},{4,6},{5,7},{6,4},{7,5},{8,10},{9,11},{10,... | collective-permute-start | bytes 983048 | tf_op jit(solution)/shard_map/ppermute | solution.py:54
  184.8 5.7 %collective-permute-start.31 = (bf16[2,64,512]{2,1,0:T(8,128)(2,1)S(1)}, bf16[2,64,512]{2,1,0:T(8,128)(2,1)S(1)}, u32[]{:S(2)}, u32[]{:S(2)}) collective-permute-start(bf16[2,64,512]{2,1,0:T(8,128)(2,1)S(1)} %slice.139), channel_id=1, source_target_pairs={{0,8},{4,12},{8,0},{12,4},{16,24},{20,28},{24,16},{28,20},{1,9},{5... | collective-permute-start | bytes 393224 | tf_op jit(solution)/shard_map/ppermute | solution.py:54
  188.2 5.6 %collective-permute-start.36 = (bf16[2,64,640]{2,1,0:T(8,128)(2,1)S(1)}, bf16[2,64,640]{2,1,0:T(8,128)(2,1)S(1)}, u32[]{:S(2)}, u32[]{:S(2)}) collective-permute-start(bf16[2,64,640]{2,1,0:T(8,128)(2,1)S(1)} %slice.147), channel_id=1, source_target_pairs={{0,8},{4,12},{8,0},{12,4},{16,24},{20,28},{24,16},{28,20},{1,9},{5... | collective-permute-start | bytes 491528 | tf_op jit(solution)/shard_map/ppermute | solution.py:54
  190.6 5.4 %collective-permute-start.32 = (bf16[1,64,512]{2,1,0:T(8,128)(2,1)S(1)}, bf16[1,64,512]{2,1,0:T(8,128)(2,1)S(1)}, u32[]{:S(2)}, u32[]{:S(2)}) collective-permute-start(bf16[1,64,512]{2,1,0:T(8,128)(2,1)S(1)} %slice.141), channel_id=1, source_target_pairs={{0,16},{4,20},{8,24},{12,28},{16,0},{20,4},{24,8},{28,12},{1,17},{... | collective-permute-start | bytes 196616 | tf_op jit(solution)/shard_map/ppermute | solution.py:54
  193.8 5.4 %collective-permute-start.37 = (bf16[1,64,640]{2,1,0:T(8,128)(2,1)S(1)}, bf16[1,64,640]{2,1,0:T(8,128)(2,1)S(1)}, u32[]{:S(2)}, u32[]{:S(2)}) collective-permute-start(bf16[1,64,640]{2,1,0:T(8,128)(2,1)S(1)} %slice.149), channel_id=1, source_target_pairs={{0,16},{4,20},{8,24},{12,28},{16,0},{20,4},{24,8},{28,12},{1,17},{... | collective-permute-start | bytes 245768 | tf_op jit(solution)/shard_map/ppermute | solution.py:54
  200.5 2.9 %collective-permute-start.38 = (f32[8,128]{1,0:T(8,128)S(1)}, f32[8,128]{1,0:T(8,128)S(1)}, u32[]{:S(2)}, u32[]{:S(2)}) collective-permute-start(f32[8,128]{1,0:T(8,128)S(1)} %broadcast_in_dim.58), channel_id=1, source_target_pairs={{0,1},{1,0},{2,3},{3,2},{4,5},{5,4},{6,7},{7,6},{8,9},{9,8},{10,11... | collective-permute-start | bytes 12296 | tf_op jit(solution)/shard_map/ppermute | solution.py:54
  201.8 20.6 %collective-permute-start.24 = (bf16[512,512]{1,0:T(8,128)(2,1)S(1)}, bf16[512,512]{1,0:T(8,128)(2,1)S(1)}, u32[]{:S(2)}, u32[]{:S(2)}) collective-permute-start(bf16[512,512]{1,0:T(8,128)(2,1)S(1)} %add_convert_fusion.4), channel_id=1, source_target_pairs={{0,2},{1,3},{2,0},{3,1},{4,6},{5,7},{6,4},{7,5},{8,10},{9,11},{10,... | collective-permute-start | bytes 1572872 | tf_op jit(solution)/shard_map/ppermute | solution.py:54
  203.4 12.9 %collective-permute-start.39 = (f32[8,128]{1,0:T(8,128)S(1)}, f32[8,128]{1,0:T(8,128)S(1)}, u32[]{:S(2)}, u32[]{:S(2)}) collective-permute-start(f32[8,128]{1,0:T(8,128)S(1)} %broadcast_add_fusion), channel_id=1, source_target_pairs={{0,2},{1,3},{2,0},{3,1},{4,6},{5,7},{6,4},{7,5},{8,10},{9,11},{10,... | collective-permute-start | bytes 12296 | tf_op jit(solution)/shard_map/ppermute | solution.py:54
  216.3 3.6 %collective-permute-start.40 = (f32[8,128]{1,0:T(8,128)S(1)}, f32[8,128]{1,0:T(8,128)S(1)}, u32[]{:S(2)}, u32[]{:S(2)}) collective-permute-start(f32[8,128]{1,0:T(8,128)S(1)} %fusion.41), channel_id=1, source_target_pairs={{0,4},{4,0},{8,12},{12,8},{16,20},{20,16},{24,28},{28,24},{1,5},{5... | collective-permute-start | bytes 12296 | tf_op jit(solution)/shard_map/ppermute | solution.py:54
  219.9 5.4 %collective-permute-start.41 = (f32[8,128]{1,0:T(8,128)S(1)}, f32[8,128]{1,0:T(8,128)S(1)}, u32[]{:S(2)}, u32[]{:S(2)}) collective-permute-start(f32[8,128]{1,0:T(8,128)S(1)} %add.278), channel_id=1, source_target_pairs={{0,8},{4,12},{8,0},{12,4},{16,24},{20,28},{24,16},{28,20},{1,9},{5... | collective-permute-start | bytes 12296 | tf_op jit(solution)/shard_map/ppermute | solution.py:54
  225.3 4.6 %collective-permute-start.42 = (f32[8,128]{1,0:T(8,128)S(1)}, f32[8,128]{1,0:T(8,128)S(1)}, u32[]{:S(2)}, u32[]{:S(2)}) collective-permute-start(f32[8,128]{1,0:T(8,128)S(1)} %add.279), channel_id=1, source_target_pairs={{0,16},{4,20},{8,24},{12,28},{16,0},{20,4},{24,8},{28,12},{1,17},{... | collective-permute-start | bytes 12296 | tf_op jit(solution)/shard_map/ppermute | solution.py:54
  (41 other events, 525.1 us)

commit v2 on v1

--- a/solution.py
+++ b/solution.py
@@ -20,17 +20,13 @@
 NEG_LARGE = -1e30
 LOG2E = 1.4426950408889634
 SCORE_SCALE = HD ** (-0.5)
-RATE_ATTEND = 0.04
-RATE_OUTPUT = 0.12
-RATE_EXPAND = 0.04
-RATE_CONTRACT = 0.04
-RATE_BIAS = 0.16
-RATE_NORM = 0.3
+RATES = (0.04, 0.12, 0.04, 0.04, 0.16, 0.3)
 DECAY = 0.01
 ADAM_EPS = 1e-08
 BETA = 0.5
 BIAS_CORRECTION = 0.875
 BF = jnp.bfloat16
+FLOPS_PER_US = 10**9
 F32 = jnp.float32
 VMEM = pl.BlockSpec(memory_space=pltpu.VMEM)
 SMEM = pl.BlockSpec(memory_space=pltpu.SMEM)
@@ -61,11 +57,8 @@
     return offs
 
 
-def gather_steps(v, steps):
-    acc = v[None]
-    for step in steps:
-        acc = jnp.concatenate([acc, swap(acc, step)], axis=0)
-    return acc
+def after(v, *ready):
+    return lax.optimization_barrier((v, *ready))[0]
 
 
 def place(steps, axis, off):
@@ -76,16 +69,68 @@
     return pos
 
 
-def scatter_steps(keep, send, steps):
-    for step in reversed(steps):
-        got = swap(send, step)
-        half = keep.shape[0] // 2
-        if half == 0:
-            return keep, got
-        total = keep.astype(F32) + got.astype(F32)
-        send = total[half:].astype(BF)
-        keep = total[:half].astype(BF)
-    return keep, send
+class Scatter:
+    def __init__(self, keep, send, steps):
+        self.keep, self.steps = keep, list(steps)
+        self.got = swap(send, self.steps[-1])
+        self.send = send
+
+    def advance(self, *ready):
+        if len(self.steps) == 1:
+            return ()
+        self.steps.pop()
+        half = self.keep.shape[0] // 2
+        total = self.keep.astype(F32) + after(self.got, *ready).astype(F32)
+        self.keep, self.send = total[:half].astype(BF), total[half:].astype(BF)
+        self.got = swap(self.send, self.steps[-1])
+        return (self.send,)
+
+
+class Total:
+    def __init__(self, value, steps):
+        self.value, self.steps = value, list(steps)
+        self.got = swap(value, self.steps[-1])
+
+    def advance(self, *ready):
+        if not self.steps:
+            return ()
+        self.steps.pop()
+        self.value = self.value + after(self.got, *ready)
+        if self.steps:
+            self.got = swap(self.value, self.steps[-1])
+        return (self.value,)
+
+    def result(self):
+        while self.steps:
+            self.advance(self.value)
+        return self.value
+
+
+class RowSums:
+    def __init__(self, pieces, bits):
+        self.parts, self.bits = {off: [piece] for off, piece in enumerate(pieces)}, list(bits)
+        self.flights = []
+        self.start()
+
+    def start(self, *ready):
+        bit = self.bits.pop()
+        sends = []
+        for off in [off for off in self.parts if off & bit]:
+            parts = self.parts.pop(off)
+            total = parts[0]
+            if len(parts) > 1:
+                total = functools.reduce(
+                    lambda a, b: a + b, [parts[0].astype(F32)] + [after(p, *ready).astype(F32) for p in parts[1:]]
+                ).astype(BF)
+            self.parts[off ^ bit].append(swap(total, ("head", bit)))
+            sends.append(total)
+        return tuple(sends)
+
+    def advance(self, *ready):
+        return self.start(*ready) if self.bits else ()
+
+    def finish(self, value, *ready):
+        return functools.reduce(lambda a, b: a + b, [after(p, *ready).astype(F32) for p in self.parts[0]], value)
 
 
 def lane_mask_stack(v, lh):
@@ -104,10 +149,9 @@
     )
 
 
-def attend_kernel(lh, n_dp, n_h, dp_offs, idx_ref, lo_ref, start_ref, w_ref, *refs):
+def qkv_kernel(lh, n_dp, n_h, dp_offs, idx_ref, w_own, w_got, *refs):
     rows = refs[:n_h]
-    pieces = refs[n_h : 2 * n_h]
-    q_ref, k_ref, v_ref, o_ref, lse_ref, wg_ref, w_s, b_s, vt_s, s_s, acc_s = refs[2 * n_h :]
+    q_ref, k_ref, v_ref, vt_ref, wg_ref, inner_ref, w_s, b_s = refs[n_h:]
     g, h = idx_ref[0], idx_ref[1]
     width = lh * HD
     ds_rows = D // n_dp
@@ -115,6 +159,7 @@
     shares = b_s.shape[1] // lh
     for p in range(n_dp):
         block = g ^ dp_offs[p]
+        w_ref, p = (w_own, p) if p < n_dp // 2 else (w_got, p - n_dp // 2)
         w_s[pl.ds(pl.multiple_of(block * ds_rows, ds_rows), ds_rows), :] = w_ref[p, :ds_rows, :]
         b_s[pl.ds(block, 1), :] = w_ref[p, ds_rows : ds_rows + 16, : lh * shares][:1].astype(F32)
     wide = w_s[...].astype(F32)
@@ -134,7 +179,7 @@
     q_bias = jnp.concatenate([r[:, :HD] for r in per_head], axis=1)
     v_bias = jnp.concatenate([r[:, HD : 2 * HD] for r in per_head], axis=1)
     inner = jnp.concatenate([r[:, 2 * HD :] for r in per_head], axis=1)
-    inner_rows = jnp.concatenate(
+    inner_ref[...] = jnp.concatenate(
         [inner[:, i * width : (i + 1) * width] for i in range(inner.shape[1] // width)]
         + [jnp.zeros((16 - inner.shape[1] // width, width), F32)],
         axis=0,
@@ -145,18 +190,28 @@
         q_ref[pl.ds(base, rw), :] = (qkv[:, :width] + q_bias).astype(BF)
         k_ref[pl.ds(base, rw), :] = qkv[:, width : 2 * width].astype(BF)
         v_ref[pl.ds(base, rw), :] = (qkv[:, 2 * width :] + v_bias).astype(BF)
-        pieces[off][pl.ds(rw, 16), :] = inner_rows
-    n_rows = q_ref.shape[0]
-    vt_s[:width, :] = v_ref[...].T
-    vt_s[width:, :] = jnp.ones((16, n_rows), BF)
+    vt_ref[:width, :] = v_ref[...].T
+    vt_ref[width:, :] = jnp.ones((16, v_ref.shape[0]), BF)
+
+
+def attend_kernel(lh, offs, idx_ref, seg_ref, q_ref, k_ref, vt_ref, inner_ref, *refs):
+    pieces = refs[: len(offs)]
+    lse_ref, s_s, acc_s, start_s = refs[len(offs) :]
+    h = idx_ref[1]
+    width = lh * HD
+    rw = pieces[0].shape[0] - 16
+    start_s[...] = document_starts(seg_ref[...])
     factor = SCORE_SCALE * LOG2E
     cols = lh * TQ
 
-    def query_block(qb, carry):
-        r0 = pl.multiple_of(qb * TQ, TQ)
+    def query_block(piece_ref, place_at, base, i, carry):
+        inside = pl.multiple_of(i * TQ, TQ)
+        r0 = pl.multiple_of(base + inside, TQ)
+        qb = r0 // TQ
         q2 = lane_mask_stack(q_ref[pl.ds(r0, TQ), :], lh)
-        start = jnp.concatenate([start_ref[:, pl.ds(r0, TQ)]] * lh, axis=1)
-        lo = lo_ref[qb]
+        start = start_s[:, pl.ds(r0, TQ)]
+        lo = (jnp.min(start) * (1.0 / TK)).astype(jnp.int32)
+        start = jnp.concatenate([start.astype(jnp.int32)] * lh, axis=1)
         column = lax.broadcasted_iota(jnp.int32, (1, cols), 1) % TQ
 
         def scores(kb, top):
@@ -175,20 +230,29 @@
         def mix(kb, carry):
             c0 = pl.multiple_of(kb * TK, TK)
             p = jnp.exp2((s_s[kb - lo] - top) * factor).astype(BF)
-            acc_s[...] += dot(vt_s[:, pl.ds(c0, TK)], p, 1, 0)
+            acc_s[...] += dot(vt_ref[:, pl.ds(c0, TK)], p, 1, 0)
             return carry
 
         lax.fori_loop(lo, qb + 1, mix, 0)
         total = acc_s[width : width + 1, :]
         out_t = head_rows_merge(acc_s[:width, :] / total, lh)
-        o_ref[pl.ds(r0, TQ), :] = out_t.T.astype(BF)
-        lse_ref[qb] = jnp.broadcast_to(top * factor + jnp.log2(total), (8, cols))
+        piece_ref[pl.ds(inside, TQ), :] = out_t.T.astype(BF)
+        lse_ref[place_at + i] = jnp.broadcast_to(top * factor + jnp.log2(total), (8, cols))
         return carry
 
-    lax.fori_loop(0, n_rows // TQ, query_block, 0)
-    for off in range(n_h):
-        base = pl.multiple_of((h ^ off) * rw, rw)
-        pieces[off][:rw, :] = o_ref[pl.ds(base, rw), :]
+    for n, off in enumerate(offs):
+        body = functools.partial(query_block, pieces[n], n * (rw // TQ), (h ^ off) * rw)
+        lax.fori_loop(0, rw // TQ, body, 0)
+        pieces[n][rw:, :] = inner_ref[...]
+
+
+def document_starts(segment):
+    seg = segment.astype(F32)
+    start = jnp.zeros(seg.shape, F32)
+    for s in range(HEADS):
+        count = jnp.sum(jnp.where(seg == float(s), 1.0, 0.0), axis=1, keepdims=True)
+        start = start + jnp.where(seg > float(s), count, 0.0)
+    return start
 
 
 def norm_back(grad, xhat, rstd, gain):
@@ -205,8 +269,9 @@
 def middle_kernel(lh, n_dp, n_h, e_steps, c_steps, idx_ref, norm_ref, *refs):
     width = lh * HD
     mixed = refs[:n_h]
-    e_ref, c_ref, post_in, dual_in, post_cot, dual_cot = refs[n_h : n_h + 6]
-    outs = refs[n_h + 6 :]
+    e_parts, c_parts = refs[n_h : n_h + 4], refs[n_h + 4 : n_h + 8]
+    post_in, dual_in, post_cot, dual_cot = refs[n_h + 8 : n_h + 12]
+    outs = refs[n_h + 12 :]
     post_out, dual_out, gmid1_ref = outs[:3]
     gm = outs[3 : 3 + n_h]
     ge_keep, ge_send, gc_keep, gc_send, small_ref = outs[3 + n_h : 8 + n_h]
@@ -221,12 +286,14 @@
 
     e_dp, e_h = offsets(e_steps, "dp"), offsets(e_steps, "head")
     c_dp, c_h = offsets(c_steps, "dp"), offsets(c_steps, "head")
+    quarter = n_dp * n_h // 4
     for p in range(n_dp * n_h):
         at = pl.ds(pl.multiple_of((g ^ e_dp[p]) * ds_rows, ds_rows), ds_rows)
-        e_s[e_h[p], at, :] = e_ref[p]
+        e_ref, c_ref, i = e_parts[p // quarter], c_parts[p // quarter], p % quarter
+        e_s[e_h[p], at, :] = e_ref[i]
         at = pl.ds(pl.multiple_of((g ^ c_dp[p]) * ds_rows, ds_rows), ds_rows)
-        c_s[c_h[p], at, :] = c_ref[p, :, :units]
-        o_s[at, c_h[p] * width : (c_h[p] + 1) * width] = c_ref[p, :, units:]
+        c_s[c_h[p], at, :] = c_ref[i, :, :units]
+        o_s[at, c_h[p] * width : (c_h[p] + 1) * width] = c_ref[i, :, units:]
     for off in range(n_h):
         mix_s[:, off * width : (off + 1) * width] = mixed[off][:rw, :]
         tail = mixed[off][rw : rw + 16, :].astype(F32)
@@ -339,9 +406,9 @@
             small_ref[pl.ds(first + j, 1), :] = ffb_s[oh, :, j * 128 : (j + 1) * 128]
 
 
-def attend_back_kernel(lh, n_h, idx_ref, lo_ref, start_ref, q_ref, k_ref, v_ref, o_ref, lse_ref, small_in, *refs):
-    gm = refs[:n_h]
-    gqkv_ref, small_ref, do_s, kt_s, dk_s, dv_s, dq_s = refs[n_h:]
+def attend_back_kernel(lh, n_h, idx_ref, seg_ref, q_ref, k_ref, v_ref, lse_near, lse_far, small_in, *refs):
+    gm, pieces = refs[:n_h], refs[n_h : 2 * n_h]
+    gqkv_ref, small_ref, do_s, o_ref, lse_ref, kt_s, dk_s, dv_s, dq_s, start_s = refs[2 * n_h :]
     h = idx_ref[1]
     width = lh * HD
     rw = gm[0].shape[0]
@@ -349,7 +416,13 @@
     cols = lh * TQ
     factor = SCORE_SCALE * LOG2E
     for off in range(n_h):
-        do_s[pl.ds(pl.multiple_of((h ^ off) * rw, rw), rw), :] = gm[off][...]
+        at = pl.ds(pl.multiple_of((h ^ off) * rw, rw), rw)
+        do_s[at, :] = gm[off][...]
+        o_ref[at, :] = pieces[off][:rw, :]
+        lse_part, n = (lse_near, off) if off < n_h // 2 else (lse_far, off - n_h // 2)
+        for i in range(rw // TQ):
+            lse_ref[(h ^ off) * (rw // TQ) + i] = lse_part[n * (rw // TQ) + i]
+    start_s[...] = document_starts(seg_ref[...])
     kt_s[...] = k_ref[...].T
     dk_s[...] = jnp.zeros_like(dk_s)
     dv_s[...] = jnp.zeros_like(dv_s)
@@ -365,8 +438,9 @@
             [jnp.sum(prod[l * HD : (l + 1) * HD, :], axis=0, keepdims=True) for l in range(lh)], axis=1
         )
         lse = lse_ref[qb][:1]
-        start = jnp.concatenate([start_ref[:, at]] * lh, axis=1)
-        lo = lo_ref[qb]
+        start = start_s[:, at]
+        lo = (jnp.min(start) * (1.0 / TK)).astype(jnp.int32)
+        start = jnp.concatenate([start.astype(jnp.int32)] * lh, axis=1)
         column = lax.broadcasted_iota(jnp.int32, (1, cols), 1) % TQ
         dq_s[...] = jnp.zeros_like(dq_s)
 
@@ -430,7 +504,59 @@
         out_ref[place(steps, "dp", b ^ g)] = full[b * ds_rows : (b + 1) * ds_rows]
 
 
-def call(body, outs, scratch, n_smem, args, limit, flops, nbytes):
+def total_of_pair(keep_ref, got_ref):
+    return keep_ref[0].astype(F32) + got_ref[0].astype(F32)
+
+
+def squares_kernel(*refs):
+    out_ref = refs[-1]
+    acc = jnp.zeros((8, 128), F32)
+    for i in range(0, len(refs) - 1, 2):
+        v = total_of_pair(refs[i], refs[i + 1])
+        v = fold(v * v)
+        if v.shape[1] % 128:
+            v = jnp.concatenate([v, jnp.zeros((8, 128 - v.shape[1] % 128), F32)], axis=1)
+        for j in range(v.shape[1] // 128):
+            acc = acc + v[:, j * 128 : (j + 1) * 128]
+    out_ref[...] = acc
+
+
+def adam_kernel(units, clip_ref, sq_ref, sq_got, small_ref, *refs):
+    ga, ge, gc = refs[0:2], refs[2:4], refs[4:6]
+    share_bias, norm_grads = refs[6:8]
+    params, momenta, variances = refs[8:14], refs[14:20], refs[20:26]
+    norm_ref, clipped_ref = refs[26:28]
+    outs = list(refs[28:])
+    small = small_ref[...]
+    squares = jnp.sum(sq_ref[...] + sq_got[...]) + jnp.sum(small * small)
+    norm = jnp.sqrt(jnp.full((8, 128), squares))
+    norm_ref[...] = norm
+    limit = clip_ref[0]
+    factor = (limit / jnp.maximum(norm, limit))[:1, :1]
+    share_co = total_of_pair(*gc)
+    grads = (
+        total_of_pair(*ga),
+        share_co[:, units:],
+        total_of_pair(*ge),
+        share_co[:, :units],
+        share_bias[...],
+        norm_grads[...],
+    )
+    for w, m, va, grad, rate in zip(params, momenta, variances, grads, RATES):
+        clipped = factor * grad
+        momentum_new = BETA * m[...] + (1.0 - BETA) * clipped
+        variance_new = BETA * va[...] + (1.0 - BETA) * clipped * clipped
+        step = momentum_new / BIAS_CORRECTION / (jnp.sqrt(variance_new / BIAS_CORRECTION) + ADAM_EPS)
+        master_new = w[...] - rate * (step + DECAY * w[...])
+        outs.pop(0)[...] = momentum_new
+        outs.pop(0)[...] = variance_new
+        outs.pop(0)[...] = master_new
+        if len(outs) > 2:
+            outs.pop(0)[...] = master_new.astype(BF)
+    clipped_ref[...] = factor * norm_grads[...]
+
+
+def call(body, outs, scratch, n_smem, args, limit, us):
     return pl.pallas_call(
         body,
         out_shape=outs,
@@ -438,23 +564,12 @@
         out_specs=jax.tree.map(lambda _: VMEM, outs),
         scratch_shapes=scratch,
         compiler_params=pltpu.CompilerParams(vmem_limit_bytes=limit << 20),
-        cost_estimate=pl.CostEstimate(flops=int(flops), bytes_accessed=int(nbytes), transcendentals=0),
+        cost_estimate=pl.CostEstimate(flops=us * FLOPS_PER_US, bytes_accessed=1 << 20, transcendentals=0),
     )(*args)
 
 
 def sds(shape, dtype):
     return jax.ShapeDtypeStruct(shape, dtype)
-
-
-def adam_update(master, momentum, variance, gradient, factor, rate):
-    clipped = factor * gradient
-    momentum_new = BETA * momentum + (1.0 - BETA) * clipped
-    variance_new = BETA * variance + (1.0 - BETA) * clipped * clipped
-    master_new = master - rate * (
-        momentum_new / BIAS_CORRECTION / (jnp.sqrt(variance_new / BIAS_CORRECTION) + ADAM_EPS)
-        + DECAY * master
-    )
-    return (momentum_new, variance_new, master_new)
 
 
 def per_device(
@@ -517,43 +632,73 @@
         for off in list(rows):
             rows[off ^ bit] = swap(rows[off], ("head", bit))
     rows = [rows[off] for off in range(n_h)]
-    a_all = gather_steps(a_msg, a_steps)
-    e_all = gather_steps(e_msg, e_steps)
-    c_all = gather_steps(c_msg, c_steps)
-
-    segment = segment_ids[0]
-    start = jnp.zeros_like(segment)
-    for s in range(HEADS):
-        start = start + jnp.where(segment > s, jnp.sum((segment == s).astype(jnp.int32)), 0)
-    lo = start[::TQ] // TK
-    start = start[None]
-
+
+    n_d, n_s = len(dp_bits), len(e_steps)
+    a_in, a_got = [a_msg[None]], []
+    for i, step in enumerate(a_steps):
+        a_got.append(swap(a_in[i], step))
+        if i < n_d - 1:
+            a_in.append(jnp.concatenate([a_in[i], a_got[i]], axis=0))
+    e_in, e_got, c_in, c_got = [e_msg[None]], [], [c_msg[None]], []
+
+    def exchange(*ready):
+        i = len(e_got)
+        if i == 0:
+            e_in[0], c_in[0] = after(e_in[0], *ready), after(c_in[0], *ready)
+        else:
+            e_in.append(jnp.concatenate([e_in[-1], after(e_got[-1], *ready)], axis=0))
+            c_in.append(jnp.concatenate([c_in[-1], after(c_got[-1], *ready)], axis=0))
+        e_got.append(swap(e_in[i], e_steps[i]))
+        c_got.append(swap(c_in[i], c_steps[i]))
+
+    for i in range(n_d - 1):
+        exchange(a_got[i])
     n_q = n_rows // TQ
     cols = lh * TQ
-    attend_out = call(
-        functools.partial(attend_kernel, lh, n_dp, n_h, offsets(a_steps, "dp")),
-        [sds((rw + 16, width), BF)] * n_h
-        + [sds((n_rows, width), BF)] * 4
-        + [sds((n_q, 8, cols), F32), sds((D, 3 * width), BF)],
-        [
-            pltpu.VMEM((D, a_cols), BF),
-            pltpu.VMEM((n_dp, lh * shares), F32),
-            pltpu.VMEM((width + 16, n_rows), BF),
-            pltpu.VMEM((KEY_BLOCKS, TK, cols), F32),
-            pltpu.VMEM((width + 16, cols), F32),
-        ],
-        2,
-        [idx, lo, start, a_all] + rows,
-        32,
-        3e9,
-        6e6,
-    )
-    pieces = attend_out[:n_h]
-    q, k, v, o, lse, wg = attend_out[n_h:]
+    q, k, v, vt, wg, inner = call(
+        functools.partial(qkv_kernel, lh, n_dp, n_h, offsets(a_steps, "dp")),
+        [sds((n_rows, width), BF)] * 3
+        + [sds((width + 16, n_rows), BF), sds((D, 3 * width), BF), sds((16, width), BF)],
+        [pltpu.VMEM((D, a_cols), BF), pltpu.VMEM((n_dp, lh * shares), F32)],
+        1,
+        [idx, after(a_in[-1], e_in[n_d - 2], c_in[n_d - 2]), a_got[-1]] + rows,
+        24,
+        4,
+    )
+
+    def attend(offs, q):
+        out = call(
+            functools.partial(attend_kernel, lh, offs),
+            [sds((rw + 16, width), BF)] * len(offs) + [sds((n_q // 2, 8, cols), F32)],
+            [
+                pltpu.VMEM((KEY_BLOCKS, TK, cols), F32),
+                pltpu.VMEM((width + 16, cols), F32),
+                pltpu.VMEM((1, n_rows), F32),
+            ],
+            1,
+            [idx, segment_ids, q, k, vt, inner],
+            24,
+            5,
+        )
+        return out[:-1], out[-1]
+
+    exchange(q)
+    far, lse_far = attend(range(n_h // 2, n_h), after(q, e_in[n_d - 1], c_in[n_d - 1]))
+    exchange(far[0])
+    near, lse_near = attend(range(n_h // 2), after(q, e_in[n_d], c_in[n_d]))
+    for i in range(n_d + 1, n_s - 1):
+        exchange()
+    pieces = list(near) + list(far)
     mixed = [pieces[0]] + [
         lax.ppermute(pieces[off], "head", [(i, i ^ off) for i in range(n_h)]) for off in range(1, n_h)
     ]
-
+    arrived = [near[0]] + mixed[n_h // 2 :]
+    e_in[-1], c_in[-1] = after(e_in[-1], *arrived), after(c_in[-1], *arrived)
+    e_got[-1], c_got[-1] = after(e_got[-1], *arrived), after(c_got[-1], *arrived)
+    e_parts = [e_in[-1], e_got[-1]]
+    e_parts += [swap(part, e_steps[-1]) for part in e_parts]
+    c_parts = [c_in[-1], c_got[-1]]
+    c_parts += [swap(part, c_steps[-1]) for part in c_parts]
     half = n_dp * n_h // 2
     middle_out = call(
         functools.partial(middle_kernel, lh, n_dp, n_h, e_steps, c_steps),
@@ -580,10 +725,9 @@
             pltpu.VMEM((n_h, 1, units), F32),
         ],
         1,
-        [idx, norm_params] + mixed + [e_all, c_all, post_in, dual_in, post_cot, dual_cot],
+        [idx, norm_params] + mixed + e_parts + c_parts + [post_in, dual_in, post_cot, dual_cot],
         52,
-        8e9,
-        16e6,
+        20,
     )
     post_out, dual_out, grad_mid1 = middle_out[:3]
     gm = middle_out[3 : 3 + n_h]
@@ -591,64 +735,58 @@
     gm = [gm[0]] + [
         lax.ppermute(gm[off], "head", [(i, i ^ off) for i in range(n_h)]) for off in range(1, n_h)
     ]
-    ge = scatter_steps(ge_keep, ge_send, e_steps)
-    gc = scatter_steps(gc_keep, gc_send, c_steps)
-
+    ge, gc = Scatter(ge_keep, ge_send, e_steps), Scatter(gc_keep, gc_send, c_steps)
+    gm[0] = after(gm[0], *ge.advance(), *gc.advance())
     gqkv, small = call(
         functools.partial(attend_back_kernel, lh, n_h),
         [sds((n_rows, 3 * width), BF), sds((48, 128), F32)],
         [
             pltpu.VMEM((n_rows, width), BF),
+            pltpu.VMEM((n_rows, width), BF),
+            pltpu.VMEM((n_q, 8, cols), F32),
             pltpu.VMEM((width, n_rows), BF),
             pltpu.VMEM((n_rows, width), F32),
             pltpu.VMEM((n_rows, width), F32),
             pltpu.VMEM((width, cols), F32),
+            pltpu.VMEM((1, n_rows), F32),
         ],
+        1,
+        [idx, segment_ids, q, k, v, lse_near, lse_far, small_mid] + gm + pieces,
+        32,
+        15,
+    )
+    total = Total(small, e_steps)
+    sent = ge.advance(gqkv) + gc.advance(gqkv)
+    ga = call(
+        functools.partial(attend_grad_kernel, lh, n_dp, n_h, a_steps),
+        sds((n_dp, ds_rows, a_cols), BF),
+        [pltpu.VMEM((D, 3 * width), F32)],
+        1,
+        [idx, after(gqkv, *sent)] + rows,
+        24,
         2,
-        [idx, lo, start, q, k, v, o, lse, small_mid] + gm,
-        32,
-        4e9,
-        6e6,
-    )
+    )
+    ga = Scatter(ga[: n_dp // 2], ga[n_dp // 2 :], a_steps)
     back = call(
         functools.partial(rows_back_kernel, n_h),
         [sds((rw, D), BF)] * n_h,
         [],
         1,
-        [idx, gqkv, wg],
+        [idx, after(gqkv, ga.send), wg],
         24,
-        8e8,
-        4e6,
-    )
-    ga = call(
-        functools.partial(attend_grad_kernel, lh, n_dp, n_h, a_steps),
-        sds((n_dp, ds_rows, a_cols), BF),
-        [pltpu.VMEM((D, 3 * width), F32)],
-        1,
-        [idx, gqkv] + rows,
-        24,
-        8e8,
-        4e6,
-    )
-    ga = scatter_steps(ga[: n_dp // 2], ga[n_dp // 2 :], a_steps)
-    back = {off: [back[off]] for off in range(n_h)}
-    for bit in reversed(h_bits):
-        sent = [off for off in back if off & bit]
-        for off in sent:
-            parts = back.pop(off)
-            total = functools.reduce(lambda a, b: a + b, [p.astype(F32) for p in parts]).astype(BF)
-            back[off ^ bit].append(swap(total, ("head", bit)))
-    post_grad = functools.reduce(lambda a, b: a + b, [p.astype(F32) for p in back[0]], grad_mid1)
-
-    for step in [("head", b) for b in reversed(h_bits)] + [("dp", b) for b in reversed(dp_bits)]:
-        small = small + swap(small, step)
-
-    join = lambda pair: (pair[0][0].astype(F32) + pair[1][0].astype(F32))
-    share_attend = join(ga)
-    share_expand = join(ge)
-    share_co = join(gc)
-    share_contract = share_co[:, :units].T
-    share_output = share_co[:, units:].T
+        2,
+    )
+    back = RowSums(back, sorted(h_bits, reverse=True))
+    sent = ()
+    for _ in range(len(h_bits) - 1):
+        sent = back.advance(*sent)
+    for i in range(n_s):
+        for chain in (ge, gc, total, ga):
+            sent = chain.advance(*sent) or sent
+            if i == 1 and chain is gc:
+                post_grad = back.finish(grad_mid1, *sent)
+                sent = (post_grad,)
+    small = total.result()
     norm_grads = small[:24].reshape(6, D)
     bias_full = jnp.concatenate(
         [
@@ -658,26 +796,34 @@
         axis=1,
     )
     share_bias = lax.dynamic_slice_in_dim(bias_full, g * shares, shares, 1)
-    squares = jnp.sum(share_attend * share_attend) + jnp.sum(share_expand * share_expand) + jnp.sum(share_co * share_co)
-    squares = jnp.full((8, 128), squares)
-    for step in [("head", b) for b in reversed(h_bits)] + [("dp", b) for b in reversed(dp_bits)]:
-        squares = squares + swap(squares, step)
-    total_norm = jnp.sqrt(squares[0, 0] + jnp.sum(small * small))
-    factor = clip_limit[0] / jnp.maximum(total_norm, clip_limit[0])
-    results = []
-    for w, m, va, gr, rate, low in (
-        (attend_weight, attend_momentum, attend_variance, share_attend, RATE_ATTEND, True),
-        (output_weight, output_momentum, output_variance, share_output, RATE_OUTPUT, True),
-        (expand_weight, expand_momentum, expand_variance, share_expand, RATE_EXPAND, True),
-        (contract_weight, contract_momentum, contract_variance, share_contract, RATE_CONTRACT, True),
-        (head_bias, bias_momentum, bias_variance, share_bias, RATE_BIAS, True),
-        (norm_params, norm_momentum, norm_variance, norm_grads, RATE_NORM, False),
-    ):
-        m_new, v_new, w_new = adam_update(w, m, va, gr, factor, rate)
-        results += [m_new, v_new, w_new]
-        if low:
-            results.append(w_new.astype(BF))
-    return (post_out, dual_out, post_grad, total_norm.reshape(1), *results, factor * norm_grads)
+    pairs = [ga.keep, ga.got, ge.keep, ge.got, gc.keep, gc.got]
+    pairs[0] = after(pairs[0], *sent)
+    squares = call(squares_kernel, sds((8, 128), F32), [], 0, pairs, 16, 1)
+    squares = Total(squares, e_steps)
+    for _ in e_steps[:-1]:
+        squares.advance()
+    flip = lambda arrays: [a.T if i in (1, 3) else a for i, a in enumerate(arrays)]
+    params = flip([attend_weight, output_weight, expand_weight, contract_weight, head_bias, norm_params])
+    momenta = flip(
+        [attend_momentum, output_momentum, expand_momentum, contract_momentum, bias_momentum, norm_momentum]
+    )
+    variances = flip(
+        [attend_variance, output_variance, expand_variance, contract_variance, bias_variance, norm_variance]
+    )
+    shapes = [sds((8, 128), F32), sds((6, D), F32)]
+    for i, w in enumerate(params):
+        shapes += [sds(w.shape, F32)] * 3 + ([sds(w.shape, BF)] if i < 5 else [])
+    norm, norm_clipped, *results = call(
+        functools.partial(adam_kernel, units),
+        shapes,
+        [],
+        1,
+        [clip_limit, squares.value, squares.got, small] + pairs + [share_bias, norm_grads] + params + momenta + variances,
+        24,
+        2,
+    )
+    results = [a.T if i // 4 in (1, 3) else a for i, a in enumerate(results)]
+    return (post_out, dual_out, post_grad, norm[0, :1], *results, norm_clipped)
 
 
 def solution(mesh):

time: 238 us -> 176 us (0.74)
  waiting for transfers between devices: 82.2 us -> 54.8 us
  other arithmetic: 28.4 us -> 5.75 us
  local copies, waits for them, and re-layouts: 15.2 us -> 3.23 us
  between operations: 6.6 us -> 2.1 us
  Pallas kernels: 54.9 us -> 58.5 us
    ppermute x42 -> x44, waiting for transfers between devices: 73.6 us -> 51.2 us  [swap(): return lax.ppermute(v, axis, [(i, i ^ bit) for i in range(count)])]
    add x12 -> x10, other arithmetic: 8.04 us -> 1.32 us  [the longest x1 1.28 us: finish(): a + b]
    concatenate x4 -> x3, local copies, waits for them, and re-layouts: 5.56 us -> 0.08 us  [the longest x1 0.04 us: exchange(): c_in.append(jnp.concatenate([c_in[-1], after(c_got[-1], *ready)], axis=0))]
    convert_element_type x6 -> x1, other arithmetic: 4.97 us -> 0.14 us  [start(): total = functools.reduce(lambda a, b: a + b, [parts[0].astype(F32)] + [af...]
    unnamed x89 -> x61, local copies, waits for them, and re-layouts: 6.67 us -> 2.27 us
    reduce_sum x5 -> x0, other arithmetic: 3.88 us -> none  [the longest x1 1.21 us: per_device(): total_norm = jnp.sqrt(squares[0, 0] + jnp.sum(small * small))]
    ppermute x3, waiting for transfers between devices: 5.69 us -> 1.99 us  [per_device(): lax.ppermute(gm[off], 'head', [(i, i ^ off) for i in range(n_h)])]
    pallas_call x5 -> x9, Pallas kernels: 54.9 us -> 58.5 us  [call(): pl.pallas_call(body, out_shape=outs, in_specs=[SMEM] * n_smem + [VMEM] *...]
  transfers between devices with their start and end apart: 48 -> 50, of which waited for: 27 -> 24; matrix products, arithmetic and copies ran while one was open for 15% -> 3% of each run, Pallas kernels for 14% -> 18%
where the time goes in v2:
time: 176 us
  Pallas kernels  58.5 us (33%)
  waiting for transfers between devices  54.8 us (31%)
  starting transfers between devices  51.7 us (29%)
  other arithmetic  5.75 us (3%)
  local copies, waits for them, and re-layouts  3.23 us (2%)
  between operations  2.1 us (1%)
    pallas_call x9, Pallas kernels, call(): pl.pallas_call(body, out_shape=outs, in_specs=[SMEM] * n_smem + [VMEM] *...  58.5 us
    ppermute x44, waiting for transfers between devices, swap(): return lax.ppermute(v, axis, [(i, i ^ bit) for i in range(count)])  51.2 us
    ppermute x44, starting transfers between devices, swap(): return lax.ppermute(v, axis, [(i, i ^ bit) for i in range(count)])  49.3 us
  transfers between devices with their start and end apart: 50, of which 24 were waited for; matrix products, arithmetic and copies ran while one was open for 3% of the time, Pallas kernels for 18%

profile of v2, /device:TPU:0, one launch (start us, length us, event | category | flops | bytes accessed | tf_op | source)
XLA Modules:
  0.0 175.9 jit_solution(4877301485461037177)
XLA Ops:
  0.7 1.4 convert_element_type.123.refs_0_
  2.1 3.0 %collective-permute-start.6 = (bf16[512,512]{1,0:T(8,128)(2,1)S(1)}, bf16[512,512]{1,0:T(8,128)(2,1)S(1)}, u32[]{:S(2)}, u32[]{:S(2)}) collective-permute-start(bf16[512,512]{1,0:T(8,128)(2,1)S(1)} %convert_element_type.123.refs_0_), channel_id=1, source_target_pairs={{0,2},{1,3},{2,0},{3,1},{4,6},{5,7},{6,4},{7,5},{8,10},{9,11},{10,... | collective-permute-start | bytes 1572872 | tf_op jit(solution)/shard_map/ppermute | solution.py:50
  5.3 2.7 %collective-permute-start = (bf16[1,80,384]{2,1,0:T(8,128)(2,1)S(1)}, bf16[1,80,384]{2,1,0:T(8,128)(2,1)S(1)}, u32[]{:S(2)}, u32[]{:S(2)}) collective-permute-start(bf16[1,80,384]{2,1,0:T(8,128)(2,1)S(1)} %fusion.2), channel_id=1, source_target_pairs={{0,16},{4,20},{8,24},{12,28},{16,0},{20,4},{24,8},{28,12},{1,17},{... | collective-permute-start | bytes 184328 | tf_op jit(solution)/shard_map/ppermute | solution.py:50
  8.0 4.0 %collective-permute-done = bf16[1,80,384]{2,1,0:T(8,128)(2,1)S(1)} collective-permute-done((bf16[1,80,384]{2,1,0:T(8,128)(2,1)S(1)}, bf16[1,80,384]{2,1,0:T(8,128)(2,1)S(1)}, u32[]{:S(2)}, u32[]{:S(2)}) %collective-permute-start) | collective-permute-done | bytes 61472 | tf_op jit(solution)/shard_map/ppermute | solution.py:50
  12.8 3.4 %collective-permute-start.3 = (bf16[1,64,640]{2,1,0:T(8,128)(2,1)S(1)}, bf16[1,64,640]{2,1,0:T(8,128)(2,1)S(1)}, u32[]{:S(2)}, u32[]{:S(2)}) collective-permute-start(bf16[1,64,640]{2,1,0:T(8,128)(2,1)S(1)} %maximum_bitcast_fusion), channel_id=1, source_target_pairs={{0,16},{4,20},{8,24},{12,28},{16,0},{20,4},{24,8},{28,12},{1,17},{... | collective-permute-start | bytes 245768 | tf_op jit(solution)/shard_map/ppermute | solution.py:50
  17.1 2.9 %collective-permute-start.2 = (bf16[1,64,512]{2,1,0:T(8,128)(2,1)S(1)}, bf16[1,64,512]{2,1,0:T(8,128)(2,1)S(1)}, u32[]{:S(2)}, u32[]{:S(2)}) collective-permute-start(bf16[1,64,512]{2,1,0:T(8,128)(2,1)S(1)} %convert_bitcast_fusion), channel_id=1, source_target_pairs={{0,16},{4,20},{8,24},{12,28},{16,0},{20,4},{24,8},{28,12},{1,17},{... | collective-permute-start | bytes 196616 | tf_op jit(solution)/shard_map/ppermute | solution.py:50
  20.0 1.6 collective-permute-start.4
  21.6 2.5 %collective-permute-done.2 = bf16[1,64,512]{2,1,0:T(8,128)(2,1)S(1)} collective-permute-done((bf16[1,64,512]{2,1,0:T(8,128)(2,1)S(1)}, bf16[1,64,512]{2,1,0:T(8,128)(2,1)S(1)}, u32[]{:S(2)}, u32[]{:S(2)}) %collective-permute-start.2) | collective-permute-done | bytes 65568 | tf_op jit(solution)/shard_map/ppermute | solution.py:50
  25.0 1.3 collective-permute-start.8
  26.3 1.8 %collective-permute-done.4.w_got = bf16[4,80,384]{2,1,0:T(8,128)(2,1)S(1)} collective-permute-done((bf16[4,80,384]{2,1,0:T(8,128)(2,1)S(1)}, bf16[4,80,384]{2,1,0:T(8,128)(2,1)S(1)}, u32[]{:S(2)}, u32[]{:S(2)}) %collective-permute-start.4) | collective-permute-done | bytes 245792 | tf_op jit(solution)/shard_map/ppermute | solution.py:50
  28.2 2.0 %shard_map.447 = (bf16[2048,128]{1,0:T(8,128)(2,1)S(1)}, bf16[2048,128]{1,0:T(8,128)(2,1)S(1)}, bf16[2048,128]{1,0:T(8,128)(2,1)S(1)}, bf16[144,2048]{1,0:T(8,12...) custom-call(s32[2]{0:T(128)S(1)} %pad_add_fusion.idx_ref, ...), custom_call_target="tpu_custom_call" | custom-call | flops 4000000000 | bytes 1048576 | tf_op jit(solution)/shard_map/pallas_call | solution.py:560
  30.8 1.4 collective-permute-done.8
  32.2 1.6 collective-permute-start.11
  33.8 1.6 collective-permute-start.9
  35.4 8.4 %shard_map.448 = (bf16[528,128]{1,0:T(8,128)(2,1)S(1)}, bf16[528,128]{1,0:T(8,128)(2,1)S(1)}, f32[4,8,512]{2,1,0:T(8,128)S(1)}) custom-call(s32[2]{0:T(128)S(1)} %pad_add_fusion.idx_ref, s32[1,2048]{1,0:T(1,128)S(1)} %copy-done.15, bf16[2048,128]{1,0:T(8,128)(2,1)S(1)} %get-tuple-element.133.q_ref, bf16[2048,128]{1,0:T(8,128)(2,1)S(1)} %get-tuple-element.127.k_ref, ...), custom_call_target="tpu_custom_call" | custom-call | flops 5000000000 | bytes 1048576 | tf_op jit(solution)/shard_map/pallas_call | solution.py:560
  45.0 2.1 %collective-permute-start.15 = (bf16[8,64,512]{2,1,0:T(8,128)(2,1)S(1)}, bf16[8,64,512]{2,1,0:T(8,128)(2,1)S(1)}, u32[]{:S(2)}, u32[]{:S(2)}) collective-permute-start(bf16[8,64,512]{2,1,0:T(8,128)(2,1)S(1)} %constant_dynamic-update-slice_fusion.10.refs_4_), channel_id=1, source_target_pairs={{0,2},{1,3},{2,0},{3,1},{4,6},{5,7},{6,4},{7,5},{8,10},{9,11},{10,... | collective-permute-start | bytes 1572872 | tf_op jit(solution)/shard_map/ppermute | solution.py:50
  47.1 5.7 %shard_map.449 = (bf16[528,128]{1,0:T(8,128)(2,1)S(1)}, bf16[528,128]{1,0:T(8,128)(2,1)S(1)}, f32[4,8,512]{2,1,0:T(8,128)S(1)}) custom-call(s32[2]{0:T(128)S(1)} %pad_add_fusion.idx_ref, s32[1,2048]{1,0:T(1,128)S(1)} %copy-done.15, bf16[2048,128]{1,0:T(8,128)(2,1)S(1)} %get-tuple-element.133.q_ref, bf16[2048,128]{1,0:T(8,128)(2,1)S(1)} %get-tuple-element.127.k_ref, ...), custom_call_target="tpu_custom_call" | custom-call | flops 5000000000 | bytes 1048576 | tf_op jit(solution)/shard_map/pallas_call | solution.py:560
  52.8 1.5 collective-permute-start.19
  54.3 4.1 %collective-permute-done.18.refs_9_ = bf16[8,64,640]{2,1,0:T(8,128)(2,1)S(1)} collective-permute-done((bf16[8,64,640]{2,1,0:T(8,128)(2,1)S(1)}, bf16[8,64,640]{2,1,0:T(8,128)(2,1)S(1)}, u32[]{:S(2)}, u32[]{:S(2)}) %collective-permute-start.18) | collective-permute-done | bytes 655392 | tf_op jit(solution)/shard_map/ppermute | solution.py:50
  59.0 4.6 %collective-permute-done.15.refs_5_ = bf16[8,64,512]{2,1,0:T(8,128)(2,1)S(1)} collective-permute-done((bf16[8,64,512]{2,1,0:T(8,128)(2,1)S(1)}, bf16[8,64,512]{2,1,0:T(8,128)(2,1)S(1)}, u32[]{:S(2)}, u32[]{:S(2)}) %collective-permute-start.15) | collective-permute-done | bytes 524320 | tf_op jit(solution)/shard_map/ppermute | solution.py:50
  64.0 1.6 collective-permute-done.12.refs_1_
  67.7 21.5 %shard_map.450 = (f32[512,512]{1,0:T(8,128)}, f32[512,512]{1,0:T(8,128)}, f32[512,512]{1,0:T(8,128)}, bf16[512,128]{1,0:T(8,128)(2,1)S(1)}, bf16[512,128]{1,0:T(...) custom-call(s32[2]{0:T(128)S(1)} %pad_add_fusion.idx_ref, ...), custom_call_target="tpu_custom_call" | custom-call | flops 20000000000 | bytes 1048576 | tf_op jit(solution)/shard_map/pallas_call | solution.py:560
  90.4 1.2 collective-permute-start.25
  92.1 1.6 add_convert_fusion.1
  96.2 1.7 collective-permute-done.25.refs_3_
  97.9 15.6 %shard_map.451 = (bf16[2048,384]{1,0:T(8,128)(2,1)S(1)}, f32[48,128]{1,0:T(8,128)S(1)}) custom-call(s32[2]{0:T(128)S(1)} %pad_add_fusion.idx_ref, s32[1,2048]{1,0:T(1,128)S(1)} %copy-done.15, bf16[2048,128]{1,0:T(8,128)(2,1)S(1)} %get-tuple-element.133.q_ref, bf16[2048,128]{1,0:T(8,128)(2,1)S(1)} %get-tuple-element.127.k_ref, ...), custom_call_target="tpu_custom_call" | custom-call | flops 15000000512 | bytes 1048576 | tf_op jit(solution)/shard_map/pallas_call | solution.py:560
  113.9 1.9 %shard_map.452 = bf16[8,64,384]{2,1,0:T(8,128)(2,1)S(1)} custom-call(s32[2]{0:T(128)S(1)} %pad_add_fusion.idx_ref, bf16[2048,384]{1,0:T(8,128)(2,1)S(1)} %get-tuple-element.161.gqkv_ref, bf16[512,512]{1,0:T(8,128)(2,1)S(1)} %convert_element_type.123.refs_0_, bf16[512,512]{1,0:T(8,128)(2,1)S(1)} %collective-permute-done.5.refs_1_, ...), custom_call_target="tpu_custom_call" | custom-call | flops 2000000000 | bytes 1048576 | tf_op jit(solution)/shard_map/pallas_call | solution.py:560
  115.8 1.8 %shard_map.453 = (bf16[512,512]{1,0:T(8,128)(2,1)S(1)}, bf16[512,512]{1,0:T(8,128)(2,1)S(1)}, bf16[512,512]{1,0:T(8,128)(2,1)S(1)}, bf16[512,512]{1,0:T(8,128)(2,1)S(1)}) custom-call(s32[2]{0:T(128)S(1)} %pad_add_fusion.idx_ref, bf16[2048,384]{1,0:T(8,128)(2,1)S(1)} %get-tuple-element.161.gqkv_ref, bf16[512,384]{1,0:T(8,128)(2,1)S(1)} %get-tuple-element.162.wg_ref), custom_call_target="tpu_custom_call" | custom-call | flops 2000000000 | bytes 1048576 | tf_op jit(solution)/shard_map/pallas_call | solution.py:560
  117.6 1.3 collective-permute-start.30
  119.0 1.6 collective-permute-start.29
  121.4 6.7 %collective-permute-done.29 = bf16[4,64,512]{2,1,0:T(8,128)(2,1)S(1)} collective-permute-done((bf16[4,64,512]{2,1,0:T(8,128)(2,1)S(1)}, bf16[4,64,512]{2,1,0:T(8,128)(2,1)S(1)}, u32[]{:S(2)}, u32[]{:S(2)}) %collective-permute-start.29) | collective-permute-done | bytes 262176 | tf_op jit(solution)/shard_map/ppermute | solution.py:50
  128.4 2.4 %collective-permute-done.28 = bf16[4,64,640]{2,1,0:T(8,128)(2,1)S(1)} collective-permute-done((bf16[4,64,640]{2,1,0:T(8,128)(2,1)S(1)}, bf16[4,64,640]{2,1,0:T(8,128)(2,1)S(1)}, u32[]{:S(2)}, u32[]{:S(2)}) %collective-permute-start.28) | collective-permute-done | bytes 327712 | tf_op jit(solution)/shard_map/ppermute | solution.py:50
  130.9 2.1 %collective-permute-start.31 = (bf16[2,64,640]{2,1,0:T(8,128)(2,1)S(1)}, bf16[2,64,640]{2,1,0:T(8,128)(2,1)S(1)}, u32[]{:S(2)}, u32[]{:S(2)}) collective-permute-start(bf16[2,64,640]{2,1,0:T(8,128)(2,1)S(1)} %slice.127), channel_id=1, source_target_pairs={{0,8},{4,12},{8,0},{12,4},{16,24},{20,28},{24,16},{28,20},{1,9},{5... | collective-permute-start | bytes 491528 | tf_op jit(solution)/shard_map/ppermute | solution.py:50
  133.4 3.8 %collective-permute-done.32 = bf16[2,64,512]{2,1,0:T(8,128)(2,1)S(1)} collective-permute-done((bf16[2,64,512]{2,1,0:T(8,128)(2,1)S(1)}, bf16[2,64,512]{2,1,0:T(8,128)(2,1)S(1)}, u32[]{:S(2)}, u32[]{:S(2)}) %collective-permute-start.32) | collective-permute-done | bytes 131104 | tf_op jit(solution)/shard_map/ppermute | solution.py:50
  137.2 2.4 %collective-permute-done.31 = bf16[2,64,640]{2,1,0:T(8,128)(2,1)S(1)} collective-permute-done((bf16[2,64,640]{2,1,0:T(8,128)(2,1)S(1)}, bf16[2,64,640]{2,1,0:T(8,128)(2,1)S(1)}, u32[]{:S(2)}, u32[]{:S(2)}) %collective-permute-start.31) | collective-permute-done | bytes 163872 | tf_op jit(solution)/shard_map/ppermute | solution.py:50
  139.7 3.5 %collective-permute-start.43 = (bf16[1,64,512]{2,1,0:T(8,128)(2,1)S(1)}, bf16[1,64,512]{2,1,0:T(8,128)(2,1)S(1)}, u32[]{:S(2)}, u32[]{:S(2)}) collective-permute-start(bf16[1,64,512]{2,1,0:T(8,128)(2,1)S(1)} %get-tuple-element.213), channel_id=1, source_target_pairs={{0,16},{4,20},{8,24},{12,28},{16,0},{20,4},{24,8},{28,12},{1,17},{... | collective-permute-start | bytes 196616 | tf_op jit(solution)/shard_map/ppermute | solution.py:50
  143.3 1.3 convert_add_fusion
  145.7 2.8 %collective-permute-done.39 = f32[48,128]{1,0:T(8,128)S(1)} collective-permute-done((f32[48,128]{1,0:T(8,128)S(1)}, f32[48,128]{1,0:T(8,128)S(1)}, u32[]{:S(2)}, u32[]{:S(2)}) %collective-permute-start.39) | collective-permute-done | bytes 24608 | tf_op jit(solution)/shard_map/ppermute | solution.py:50
  148.7 2.9 %collective-permute-start.42 = (bf16[1,64,384]{2,1,0:T(8,128)(2,1)S(1)}, bf16[1,64,384]{2,1,0:T(8,128)(2,1)S(1)}, u32[]{:S(2)}, u32[]{:S(2)}) collective-permute-start(bf16[1,64,384]{2,1,0:T(8,128)(2,1)S(1)} %get-tuple-element.216), channel_id=1, source_target_pairs={{0,16},{4,20},{8,24},{12,28},{16,0},{20,4},{24,8},{28,12},{1,17},{... | collective-permute-start | bytes 147464 | tf_op jit(solution)/shard_map/ppermute | solution.py:50
  152.3 2.9 %collective-permute-start.41 = (f32[48,128]{1,0:T(8,128)S(1)}, f32[48,128]{1,0:T(8,128)S(1)}, u32[]{:S(2)}, u32[]{:S(2)}) collective-permute-start(f32[48,128]{1,0:T(8,128)S(1)} %add.101), channel_id=1, source_target_pairs={{0,16},{4,20},{8,24},{12,28},{16,0},{20,4},{24,8},{28,12},{1,17},{... | collective-permute-start | bytes 73736 | tf_op jit(solution)/shard_map/ppermute | solution.py:50
  155.2 1.8 %collective-permute-done.41 = f32[48,128]{1,0:T(8,128)S(1)} collective-permute-done((f32[48,128]{1,0:T(8,128)S(1)}, f32[48,128]{1,0:T(8,128)S(1)}, u32[]{:S(2)}, u32[]{:S(2)}) %collective-permute-start.41) | collective-permute-done | bytes 24608 | tf_op jit(solution)/shard_map/ppermute | solution.py:50
  159.6 2.5 %collective-permute-done.46 = f32[8,128]{1,0:T(8,128)S(1)} collective-permute-done((f32[8,128]{1,0:T(8,128)S(1)}, f32[8,128]{1,0:T(8,128)S(1)}, u32[]{:S(2)}, u32[]{:S(2)}) %collective-permute-start.46) | collective-permute-done | bytes 4128 | tf_op jit(solution)/shard_map/ppermute | solution.py:50
  163.2 2.6 %collective-permute-done.47 = f32[8,128]{1,0:T(8,128)S(1)} collective-permute-done((f32[8,128]{1,0:T(8,128)S(1)}, f32[8,128]{1,0:T(8,128)S(1)}, u32[]{:S(2)}, u32[]{:S(2)}) %collective-permute-start.47) | collective-permute-done | bytes 4128 | tf_op jit(solution)/shard_map/ppermute | solution.py:50
  165.8 1.2 collective-permute-start.48
  167.0 2.4 %collective-permute-done.48 = f32[8,128]{1,0:T(8,128)S(1)} collective-permute-done((f32[8,128]{1,0:T(8,128)S(1)}, f32[8,128]{1,0:T(8,128)S(1)}, u32[]{:S(2)}, u32[]{:S(2)}) %collective-permute-start.48) | collective-permute-done | bytes 4128 | tf_op jit(solution)/shard_map/ppermute | solution.py:50
  169.4 2.9 %collective-permute-start.49 = (f32[8,128]{1,0:T(8,128)S(1)}, f32[8,128]{1,0:T(8,128)S(1)}, u32[]{:S(2)}, u32[]{:S(2)}) collective-permute-start(f32[8,128]{1,0:T(8,128)S(1)} %add.106.sq_ref), channel_id=1, source_target_pairs={{0,16},{4,20},{8,24},{12,28},{16,0},{20,4},{24,8},{28,12},{1,17},{... | collective-permute-start | bytes 12296 | tf_op jit(solution)/shard_map/ppermute | solution.py:50
  172.4 1.5 collective-permute-done.49.sq_got
  174.0 1.5 shard_map.455
  (176 shorter events, 19.5 us)
Async XLA Ops:
  2.1 15.0 %collective-permute-start.6 = (bf16[512,512]{1,0:T(8,128)(2,1)S(1)}, bf16[512,512]{1,0:T(8,128)(2,1)S(1)}, u32[]{:S(2)}, u32[]{:S(2)}) collective-permute-start(bf16[512,512]{1,0:T(8,128)(2,1)S(1)} %convert_element_type.123.refs_0_), channel_id=1, source_target_pairs={{0,2},{1,3},{2,0},{3,1},{4,6},{5,7},{6,4},{7,5},{8,10},{9,11},{10,... | collective-permute-start | bytes 1572872 | tf_op jit(solution)/shard_map/ppermute | solution.py:50
  5.1 23.0 %collective-permute-start.5 = (bf16[512,512]{1,0:T(8,128)(2,1)S(1)}, bf16[512,512]{1,0:T(8,128)(2,1)S(1)}, u32[]{:S(2)}, u32[]{:S(2)}) collective-permute-start(bf16[512,512]{1,0:T(8,128)(2,1)S(1)} %convert_element_type.123.refs_0_), channel_id=1, source_target_pairs={{0,1},{1,0},{2,3},{3,2},{4,5},{5,4},{6,7},{7,6},{8,9},{9,8},{10,11... | collective-permute-start | bytes 1572872 | tf_op jit(solution)/shard_map/ppermute | solution.py:50
  5.3 6.7 %collective-permute-start = (bf16[1,80,384]{2,1,0:T(8,128)(2,1)S(1)}, bf16[1,80,384]{2,1,0:T(8,128)(2,1)S(1)}, u32[]{:S(2)}, u32[]{:S(2)}) collective-permute-start(bf16[1,80,384]{2,1,0:T(8,128)(2,1)S(1)} %fusion.2), channel_id=1, source_target_pairs={{0,16},{4,20},{8,24},{12,28},{16,0},{20,4},{24,8},{28,12},{1,17},{... | collective-permute-start | bytes 184328 | tf_op jit(solution)/shard_map/ppermute | solution.py:50
  12.0 8.0 %collective-permute-start.1 = (bf16[2,80,384]{2,1,0:T(8,128)(2,1)S(1)}, bf16[2,80,384]{2,1,0:T(8,128)(2,1)S(1)}, u32[]{:S(2)}, u32[]{:S(2)}) collective-permute-start(bf16[2,80,384]{2,1,0:T(8,128)(2,1)S(1)} %pad_maximum_fusion.1), channel_id=1, source_target_pairs={{0,8},{4,12},{8,0},{12,4},{16,24},{20,28},{24,16},{28,20},{1,9},{5... | collective-permute-start | bytes 368648 | tf_op jit(solution)/shard_map/ppermute | solution.py:50
  12.8 8.8 %collective-permute-start.3 = (bf16[1,64,640]{2,1,0:T(8,128)(2,1)S(1)}, bf16[1,64,640]{2,1,0:T(8,128)(2,1)S(1)}, u32[]{:S(2)}, u32[]{:S(2)}) collective-permute-start(bf16[1,64,640]{2,1,0:T(8,128)(2,1)S(1)} %maximum_bitcast_fusion), channel_id=1, source_target_pairs={{0,16},{4,20},{8,24},{12,28},{16,0},{20,4},{24,8},{28,12},{1,17},{... | collective-permute-start | bytes 245768 | tf_op jit(solution)/shard_map/ppermute | solution.py:50
  17.1 11.1 %collective-permute-start.7 = (bf16[512,512]{1,0:T(8,128)(2,1)S(1)}, bf16[512,512]{1,0:T(8,128)(2,1)S(1)}, u32[]{:S(2)}, u32[]{:S(2)}) collective-permute-start(bf16[512,512]{1,0:T(8,128)(2,1)S(1)} %collective-permute-done.6.refs_2_), channel_id=1, source_target_pairs={{0,1},{1,0},{2,3},{3,2},{4,5},{5,4},{6,7},{7,6},{8,9},{9,8},{10,11... | collective-permute-start | bytes 1572872 | tf_op jit(solution)/shard_map/ppermute | solution.py:50
  17.1 7.0 %collective-permute-start.2 = (bf16[1,64,512]{2,1,0:T(8,128)(2,1)S(1)}, bf16[1,64,512]{2,1,0:T(8,128)(2,1)S(1)}, u32[]{:S(2)}, u32[]{:S(2)}) collective-permute-start(bf16[1,64,512]{2,1,0:T(8,128)(2,1)S(1)} %convert_bitcast_fusion), channel_id=1, source_target_pairs={{0,16},{4,20},{8,24},{12,28},{16,0},{20,4},{24,8},{28,12},{1,17},{... | collective-permute-start | bytes 196616 | tf_op jit(solution)/shard_map/ppermute | solution.py:50
  20.0 8.2 %collective-permute-start.4 = (bf16[4,80,384]{2,1,0:T(8,128)(2,1)S(1)}, bf16[4,80,384]{2,1,0:T(8,128)(2,1)S(1)}, u32[]{:S(2)}, u32[]{:S(2)}) collective-permute-start(bf16[4,80,384]{2,1,0:T(8,128)(2,1)S(1)} %pad_maximum_fusion.w_own), channel_id=1, source_target_pairs={{0,4},{4,0},{8,12},{12,8},{16,20},{20,16},{24,28},{28,24},{1,5},{5... | collective-permute-start | bytes 737288 | tf_op jit(solution)/shard_map/ppermute | solution.py:50
  24.2 6.6 %collective-permute-start.10 = (bf16[2,64,640]{2,1,0:T(8,128)(2,1)S(1)}, bf16[2,64,640]{2,1,0:T(8,128)(2,1)S(1)}, u32[]{:S(2)}, u32[]{:S(2)}) collective-permute-start(bf16[2,64,640]{2,1,0:T(8,128)(2,1)S(1)} %get-tuple-element.220), channel_id=1, source_target_pairs={{0,8},{4,12},{8,0},{12,4},{16,24},{20,28},{24,16},{28,20},{1,9},{5... | collective-permute-start | bytes 491528 | tf_op jit(solution)/shard_map/ppermute | solution.py:50
  25.0 7.2 %collective-permute-start.8 = (bf16[2,64,512]{2,1,0:T(8,128)(2,1)S(1)}, bf16[2,64,512]{2,1,0:T(8,128)(2,1)S(1)}, u32[]{:S(2)}, u32[]{:S(2)}) collective-permute-start(bf16[2,64,512]{2,1,0:T(8,128)(2,1)S(1)} %get-tuple-element.226), channel_id=1, source_target_pairs={{0,8},{4,12},{8,0},{12,4},{16,24},{20,28},{24,16},{28,20},{1,9},{5... | collective-permute-start | bytes 393224 | tf_op jit(solution)/shard_map/ppermute | solution.py:50
  32.2 11.5 %collective-permute-start.11 = (bf16[4,64,640]{2,1,0:T(8,128)(2,1)S(1)}, bf16[4,64,640]{2,1,0:T(8,128)(2,1)S(1)}, u32[]{:S(2)}, u32[]{:S(2)}) collective-permute-start(bf16[4,64,640]{2,1,0:T(8,128)(2,1)S(1)} %get-tuple-element.211), channel_id=1, source_target_pairs={{0,2},{1,3},{2,0},{3,1},{4,6},{5,7},{6,4},{7,5},{8,10},{9,11},{10,... | collective-permute-start | bytes 983048 | tf_op jit(solution)/shard_map/ppermute | solution.py:50
  33.8 11.1 %collective-permute-start.9 = (bf16[4,64,512]{2,1,0:T(8,128)(2,1)S(1)}, bf16[4,64,512]{2,1,0:T(8,128)(2,1)S(1)}, u32[]{:S(2)}, u32[]{:S(2)}) collective-permute-start(bf16[4,64,512]{2,1,0:T(8,128)(2,1)S(1)} %get-tuple-element.214), channel_id=1, source_target_pairs={{0,4},{4,0},{8,12},{12,8},{16,20},{20,16},{24,28},{28,24},{1,5},{5... | collective-permute-start | bytes 786440 | tf_op jit(solution)/shard_map/ppermute | solution.py:50
  43.8 14.6 %collective-permute-start.18 = (bf16[8,64,640]{2,1,0:T(8,128)(2,1)S(1)}, bf16[8,64,640]{2,1,0:T(8,128)(2,1)S(1)}, u32[]{:S(2)}, u32[]{:S(2)}) collective-permute-start(bf16[8,64,640]{2,1,0:T(8,128)(2,1)S(1)} %constant_dynamic-update-slice_fusion.14.refs_8_), channel_id=1, source_target_pairs={{0,4},{4,0},{8,12},{12,8},{16,20},{20,16},{24,28},{28,24},{1,5},{5... | collective-permute-start | bytes 1966088 | tf_op jit(solution)/shard_map/ppermute | solution.py:50
  44.9 7.9 %collective-permute-start.13 = (bf16[528,128]{1,0:T(8,128)(2,1)S(1)}, bf16[528,128]{1,0:T(8,128)(2,1)S(1)}, u32[]{:S(2)}, u32[]{:S(2)}) collective-permute-start(bf16[528,128]{1,0:T(8,128)(2,1)S(1)} %get-tuple-element.130.refs_6_), channel_id=1, source_target_pairs={{0,2},{1,3},{2,0},{3,1},{4,6},{5,7},{6,4},{7,5},{8,10},{9,11},{10,... | collective-permute-start | bytes 405512 | tf_op jit(solution)/shard_map/ppermute | solution.py:693
  44.9 7.9 %collective-permute-start.14 = (bf16[528,128]{1,0:T(8,128)(2,1)S(1)}, bf16[528,128]{1,0:T(8,128)(2,1)S(1)}, u32[]{:S(2)}, u32[]{:S(2)}) collective-permute-start(bf16[528,128]{1,0:T(8,128)(2,1)S(1)} %get-tuple-element.136.refs_7_), channel_id=1, source_target_pairs={{0,3},{1,2},{2,1},{3,0},{4,7},{5,6},{6,5},{7,4},{8,11},{9,10},{10,... | collective-permute-start | bytes 405512 | tf_op jit(solution)/shard_map/ppermute | solution.py:693
  45.0 18.6 %collective-permute-start.15 = (bf16[8,64,512]{2,1,0:T(8,128)(2,1)S(1)}, bf16[8,64,512]{2,1,0:T(8,128)(2,1)S(1)}, u32[]{:S(2)}, u32[]{:S(2)}) collective-permute-start(bf16[8,64,512]{2,1,0:T(8,128)(2,1)S(1)} %constant_dynamic-update-slice_fusion.10.refs_4_), channel_id=1, source_target_pairs={{0,2},{1,3},{2,0},{3,1},{4,6},{5,7},{6,4},{7,5},{8,10},{9,11},{10,... | collective-permute-start | bytes 1572872 | tf_op jit(solution)/shard_map/ppermute | solution.py:50
  52.8 12.8 %collective-permute-start.19 = (bf16[8,64,640]{2,1,0:T(8,128)(2,1)S(1)}, bf16[8,64,640]{2,1,0:T(8,128)(2,1)S(1)}, u32[]{:S(2)}, u32[]{:S(2)}) collective-permute-start(bf16[8,64,640]{2,1,0:T(8,128)(2,1)S(1)} %constant_dynamic-update-slice_fusion.14.refs_8_), channel_id=1, source_target_pairs={{0,1},{1,0},{2,3},{3,2},{4,5},{5,4},{6,7},{7,6},{8,9},{9,8},{10,11... | collective-permute-start | bytes 1966088 | tf_op jit(solution)/shard_map/ppermute | solution.py:50
  58.4 7.2 %collective-permute-start.20 = (bf16[8,64,640]{2,1,0:T(8,128)(2,1)S(1)}, bf16[8,64,640]{2,1,0:T(8,128)(2,1)S(1)}, u32[]{:S(2)}, u32[]{:S(2)}) collective-permute-start(bf16[8,64,640]{2,1,0:T(8,128)(2,1)S(1)} %collective-permute-done.18.refs_9_), channel_id=1, source_target_pairs={{0,1},{1,0},{2,3},{3,2},{4,5},{5,4},{6,7},{7,6},{8,9},{9,8},{10,11... | collective-permute-start | bytes 1966088 | tf_op jit(solution)/shard_map/ppermute | solution.py:50
  58.4 7.2 %collective-permute-start.16 = (bf16[8,64,512]{2,1,0:T(8,128)(2,1)S(1)}, bf16[8,64,512]{2,1,0:T(8,128)(2,1)S(1)}, u32[]{:S(2)}, u32[]{:S(2)}) collective-permute-start(bf16[8,64,512]{2,1,0:T(8,128)(2,1)S(1)} %constant_dynamic-update-slice_fusion.10.refs_4_), channel_id=1, source_target_pairs={{0,1},{1,0},{2,3},{3,2},{4,5},{5,4},{6,7},{7,6},{8,9},{9,8},{10,11... | collective-permute-start | bytes 1572872 | tf_op jit(solution)/shard_map/ppermute | solution.py:50
  63.5 2.1 %collective-permute-start.17 = (bf16[8,64,512]{2,1,0:T(8,128)(2,1)S(1)}, bf16[8,64,512]{2,1,0:T(8,128)(2,1)S(1)}, u32[]{:S(2)}, u32[]{:S(2)}) collective-permute-start(bf16[8,64,512]{2,1,0:T(8,128)(2,1)S(1)} %collective-permute-done.15.refs_5_), channel_id=1, source_target_pairs={{0,1},{1,0},{2,3},{3,2},{4,5},{5,4},{6,7},{7,6},{8,9},{9,8},{10,11... | collective-permute-start | bytes 1572872 | tf_op jit(solution)/shard_map/ppermute | solution.py:50
  89.2 2.9 %collective-permute-start.21 = (bf16[16,64,512]{2,1,0:T(8,128)(2,1)}, bf16[16,64,512]{2,1,0:T(8,128)(2,1)S(1)}, u32[]{:S(2)}, u32[]{:S(2)}) collective-permute-start(bf16[16,64,512]{2,1,0:T(8,128)(2,1)} %get-tuple-element.150), channel_id=1, source_target_pairs={{0,1},{1,0},{2,3},{3,2},{4,5},{5,4},{6,7},{7,6},{8,9},{9,8},{10,11... | collective-permute-start | bytes 3145736 | tf_op jit(solution)/shard_map/ppermute | solution.py:50
  89.4 5.0 %collective-permute-start.22 = (bf16[16,64,640]{2,1,0:T(8,128)(2,1)}, bf16[16,64,640]{2,1,0:T(8,128)(2,1)S(1)}, u32[]{:S(2)}, u32[]{:S(2)}) collective-permute-start(bf16[16,64,640]{2,1,0:T(8,128)(2,1)} %get-tuple-element.152), channel_id=1, source_target_pairs={{0,1},{1,0},{2,3},{3,2},{4,5},{5,4},{6,7},{7,6},{8,9},{9,8},{10,11... | collective-permute-start | bytes 3932168 | tf_op jit(solution)/shard_map/ppermute | solution.py:50
  89.7 6.2 %collective-permute-start.23 = (bf16[512,128]{1,0:T(8,128)(2,1)S(1)}, bf16[512,128]{1,0:T(8,128)(2,1)S(1)}, u32[]{:S(2)}, u32[]{:S(2)}) collective-permute-start(bf16[512,128]{1,0:T(8,128)(2,1)S(1)} %get-tuple-element.154), channel_id=1, source_target_pairs={{0,1},{1,0},{2,3},{3,2},{4,5},{5,4},{6,7},{7,6},{8,9},{9,8},{10,11... | collective-permute-start | bytes 393224 | tf_op jit(solution)/shard_map/ppermute | solution.py:736
  89.9 6.3 %collective-permute-start.24 = (bf16[512,128]{1,0:T(8,128)(2,1)S(1)}, bf16[512,128]{1,0:T(8,128)(2,1)S(1)}, u32[]{:S(2)}, u32[]{:S(2)}) collective-permute-start(bf16[512,128]{1,0:T(8,128)(2,1)S(1)} %get-tuple-element.155), channel_id=1, source_target_pairs={{0,2},{1,3},{2,0},{3,1},{4,6},{5,7},{6,4},{7,5},{8,10},{9,11},{10,... | collective-permute-start | bytes 393224 | tf_op jit(solution)/shard_map/ppermute | solution.py:736
  90.4 7.5 %collective-permute-start.25 = (bf16[512,128]{1,0:T(8,128)(2,1)S(1)}, bf16[512,128]{1,0:T(8,128)(2,1)S(1)}, u32[]{:S(2)}, u32[]{:S(2)}) collective-permute-start(bf16[512,128]{1,0:T(8,128)(2,1)S(1)} %get-tuple-element.156), channel_id=1, source_target_pairs={{0,3},{1,2},{2,1},{3,0},{4,7},{5,6},{6,5},{7,4},{8,11},{9,10},{10,... | collective-permute-start | bytes 393224 | tf_op jit(solution)/shard_map/ppermute | solution.py:736
  93.8 19.7 %collective-permute-start.26 = (bf16[8,64,512]{2,1,0:T(8,128)(2,1)S(1)}, bf16[8,64,512]{2,1,0:T(8,128)(2,1)S(1)}, u32[]{:S(2)}, u32[]{:S(2)}) collective-permute-start(bf16[8,64,512]{2,1,0:T(8,128)(2,1)S(1)} %slice.116), channel_id=1, source_target_pairs={{0,2},{1,3},{2,0},{3,1},{4,6},{5,7},{6,4},{7,5},{8,10},{9,11},{10,... | collective-permute-start | bytes 1572872 | tf_op jit(solution)/shard_map/ppermute | solution.py:50
  94.8 18.8 %collective-permute-start.27 = (bf16[8,64,640]{2,1,0:T(8,128)(2,1)S(1)}, bf16[8,64,640]{2,1,0:T(8,128)(2,1)S(1)}, u32[]{:S(2)}, u32[]{:S(2)}) collective-permute-start(bf16[8,64,640]{2,1,0:T(8,128)(2,1)S(1)} %slice.117), channel_id=1, source_target_pairs={{0,4},{4,0},{8,12},{12,8},{16,20},{20,16},{24,28},{28,24},{1,5},{5... | collective-permute-start | bytes 1966088 | tf_op jit(solution)/shard_map/ppermute | solution.py:50
  117.6 3.6 %collective-permute-start.30 = (bf16[512,512]{1,0:T(8,128)(2,1)S(1)}, bf16[512,512]{1,0:T(8,128)(2,1)S(1)}, u32[]{:S(2)}, u32[]{:S(2)}) collective-permute-start(bf16[512,512]{1,0:T(8,128)(2,1)S(1)} %get-tuple-element.165), channel_id=1, source_target_pairs={{0,1},{1,0},{2,3},{3,2},{4,5},{5,4},{6,7},{7,6},{8,9},{9,8},{10,11... | collective-permute-start | bytes 1572872 | tf_op jit(solution)/shard_map/ppermute | solution.py:50
  118.9 12.0 %collective-permute-start.34 = (f32[48,128]{1,0:T(8,128)S(1)}, f32[48,128]{1,0:T(8,128)S(1)}, u32[]{:S(2)}, u32[]{:S(2)}) collective-permute-start(f32[48,128]{1,0:T(8,128)S(1)} %get-tuple-element.168), channel_id=1, source_target_pairs={{0,1},{1,0},{2,3},{3,2},{4,5},{5,4},{6,7},{7,6},{8,9},{9,8},{10,11... | collective-permute-start | bytes 73736 | tf_op jit(solution)/shard_map/ppermute | solution.py:50
  119.0 9.1 %collective-permute-start.29 = (bf16[4,64,512]{2,1,0:T(8,128)(2,1)S(1)}, bf16[4,64,512]{2,1,0:T(8,128)(2,1)S(1)}, u32[]{:S(2)}, u32[]{:S(2)}) collective-permute-start(bf16[4,64,512]{2,1,0:T(8,128)(2,1)S(1)} %slice.119), channel_id=1, source_target_pairs={{0,4},{4,0},{8,12},{12,8},{16,20},{20,16},{24,28},{28,24},{1,5},{5... | collective-permute-start | bytes 786440 | tf_op jit(solution)/shard_map/ppermute | solution.py:50
  120.6 10.2 %collective-permute-start.28 = (bf16[4,64,640]{2,1,0:T(8,128)(2,1)S(1)}, bf16[4,64,640]{2,1,0:T(8,128)(2,1)S(1)}, u32[]{:S(2)}, u32[]{:S(2)}) collective-permute-start(bf16[4,64,640]{2,1,0:T(8,128)(2,1)S(1)} %slice.121), channel_id=1, source_target_pairs={{0,2},{1,3},{2,0},{3,1},{4,6},{5,7},{6,4},{7,5},{8,10},{9,11},{10,... | collective-permute-start | bytes 983048 | tf_op jit(solution)/shard_map/ppermute | solution.py:50
  120.8 12.2 %collective-permute-start.33 = (bf16[4,64,384]{2,1,0:T(8,128)(2,1)S(1)}, bf16[4,64,384]{2,1,0:T(8,128)(2,1)S(1)}, u32[]{:S(2)}, u32[]{:S(2)}) collective-permute-start(bf16[4,64,384]{2,1,0:T(8,128)(2,1)S(1)} %slice.122), channel_id=1, source_target_pairs={{0,4},{4,0},{8,12},{12,8},{16,20},{20,16},{24,28},{28,24},{1,5},{5... | collective-permute-start | bytes 589832 | tf_op jit(solution)/shard_map/ppermute | solution.py:50
  121.2 22.0 %collective-permute-start.35 = (bf16[512,512]{1,0:T(8,128)(2,1)S(1)}, bf16[512,512]{1,0:T(8,128)(2,1)S(1)}, u32[]{:S(2)}, u32[]{:S(2)}) collective-permute-start(bf16[512,512]{1,0:T(8,128)(2,1)S(1)} %get-tuple-element.174), channel_id=1, source_target_pairs={{0,1},{1,0},{2,3},{3,2},{4,5},{5,4},{6,7},{7,6},{8,9},{9,8},{10,11... | collective-permute-start | bytes 1572872 | tf_op jit(solution)/shard_map/ppermute | solution.py:50
  128.1 15.2 %collective-permute-start.36 = (bf16[512,512]{1,0:T(8,128)(2,1)S(1)}, bf16[512,512]{1,0:T(8,128)(2,1)S(1)}, u32[]{:S(2)}, u32[]{:S(2)}) collective-permute-start(bf16[512,512]{1,0:T(8,128)(2,1)S(1)} %add_convert_fusion.3), channel_id=1, source_target_pairs={{0,2},{1,3},{2,0},{3,1},{4,6},{5,7},{6,4},{7,5},{8,10},{9,11},{10,... | collective-permute-start | bytes 1572872 | tf_op jit(solution)/shard_map/ppermute | solution.py:50
  130.7 6.4 %collective-permute-start.32 = (bf16[2,64,512]{2,1,0:T(8,128)(2,1)S(1)}, bf16[2,64,512]{2,1,0:T(8,128)(2,1)S(1)}, u32[]{:S(2)}, u32[]{:S(2)}) collective-permute-start(bf16[2,64,512]{2,1,0:T(8,128)(2,1)S(1)} %slice.125), channel_id=1, source_target_pairs={{0,8},{4,12},{8,0},{12,4},{16,24},{20,28},{24,16},{28,20},{1,9},{5... | collective-permute-start | bytes 393224 | tf_op jit(solution)/shard_map/ppermute | solution.py:50
  130.9 8.8 %collective-permute-start.31 = (bf16[2,64,640]{2,1,0:T(8,128)(2,1)S(1)}, bf16[2,64,640]{2,1,0:T(8,128)(2,1)S(1)}, u32[]{:S(2)}, u32[]{:S(2)}) collective-permute-start(bf16[2,64,640]{2,1,0:T(8,128)(2,1)S(1)} %slice.127), channel_id=1, source_target_pairs={{0,8},{4,12},{8,0},{12,4},{16,24},{20,28},{24,16},{28,20},{1,9},{5... | collective-permute-start | bytes 491528 | tf_op jit(solution)/shard_map/ppermute | solution.py:50
  133.0 11.6 %collective-permute-start.38 = (f32[48,128]{1,0:T(8,128)S(1)}, f32[48,128]{1,0:T(8,128)S(1)}, u32[]{:S(2)}, u32[]{:S(2)}) collective-permute-start(f32[48,128]{1,0:T(8,128)S(1)} %add.91), channel_id=1, source_target_pairs={{0,2},{1,3},{2,0},{3,1},{4,6},{5,7},{6,4},{7,5},{8,10},{9,11},{10,... | collective-permute-start | bytes 73736 | tf_op jit(solution)/shard_map/ppermute | solution.py:50
  137.2 8.5 %collective-permute-start.37 = (bf16[2,64,384]{2,1,0:T(8,128)(2,1)S(1)}, bf16[2,64,384]{2,1,0:T(8,128)(2,1)S(1)}, u32[]{:S(2)}, u32[]{:S(2)}) collective-permute-start(bf16[2,64,384]{2,1,0:T(8,128)(2,1)S(1)} %slice.130), channel_id=1, source_target_pairs={{0,8},{4,12},{8,0},{12,4},{16,24},{20,28},{24,16},{28,20},{1,9},{5... | collective-permute-start | bytes 294920 | tf_op jit(solution)/shard_map/ppermute | solution.py:50
  139.7 17.4 %collective-permute-start.43 = (bf16[1,64,512]{2,1,0:T(8,128)(2,1)S(1)}, bf16[1,64,512]{2,1,0:T(8,128)(2,1)S(1)}, u32[]{:S(2)}, u32[]{:S(2)}) collective-permute-start(bf16[1,64,512]{2,1,0:T(8,128)(2,1)S(1)} %get-tuple-element.213), channel_id=1, source_target_pairs={{0,16},{4,20},{8,24},{12,28},{16,0},{20,4},{24,8},{28,12},{1,17},{... | collective-permute-start | bytes 196616 | tf_op jit(solution)/shard_map/ppermute | solution.py:50
  143.2 13.9 %collective-permute-start.44 = (bf16[1,64,640]{2,1,0:T(8,128)(2,1)S(1)}, bf16[1,64,640]{2,1,0:T(8,128)(2,1)S(1)}, u32[]{:S(2)}, u32[]{:S(2)}) collective-permute-start(bf16[1,64,640]{2,1,0:T(8,128)(2,1)S(1)} %get-tuple-element.209), channel_id=1, source_target_pairs={{0,16},{4,20},{8,24},{12,28},{16,0},{20,4},{24,8},{28,12},{1,17},{... | collective-permute-start | bytes 245768 | tf_op jit(solution)/shard_map/ppermute | solution.py:50
  144.6 3.9 %collective-permute-start.39 = (f32[48,128]{1,0:T(8,128)S(1)}, f32[48,128]{1,0:T(8,128)S(1)}, u32[]{:S(2)}, u32[]{:S(2)}) collective-permute-start(f32[48,128]{1,0:T(8,128)S(1)} %add.98), channel_id=1, source_target_pairs={{0,4},{4,0},{8,12},{12,8},{16,20},{20,16},{24,28},{28,24},{1,5},{5... | collective-permute-start | bytes 73736 | tf_op jit(solution)/shard_map/ppermute | solution.py:50
  148.5 3.8 %collective-permute-start.40 = (f32[48,128]{1,0:T(8,128)S(1)}, f32[48,128]{1,0:T(8,128)S(1)}, u32[]{:S(2)}, u32[]{:S(2)}) collective-permute-start(f32[48,128]{1,0:T(8,128)S(1)} %add.100), channel_id=1, source_target_pairs={{0,8},{4,12},{8,0},{12,4},{16,24},{20,28},{24,16},{28,20},{1,9},{5... | collective-permute-start | bytes 73736 | tf_op jit(solution)/shard_map/ppermute | solution.py:50
  148.7 8.4 %collective-permute-start.42 = (bf16[1,64,384]{2,1,0:T(8,128)(2,1)S(1)}, bf16[1,64,384]{2,1,0:T(8,128)(2,1)S(1)}, u32[]{:S(2)}, u32[]{:S(2)}) collective-permute-start(bf16[1,64,384]{2,1,0:T(8,128)(2,1)S(1)} %get-tuple-element.216), channel_id=1, source_target_pairs={{0,16},{4,20},{8,24},{12,28},{16,0},{20,4},{24,8},{28,12},{1,17},{... | collective-permute-start | bytes 147464 | tf_op jit(solution)/shard_map/ppermute | solution.py:50
  152.3 4.7 %collective-permute-start.41 = (f32[48,128]{1,0:T(8,128)S(1)}, f32[48,128]{1,0:T(8,128)S(1)}, u32[]{:S(2)}, u32[]{:S(2)}) collective-permute-start(f32[48,128]{1,0:T(8,128)S(1)} %add.101), channel_id=1, source_target_pairs={{0,16},{4,20},{8,24},{12,28},{16,0},{20,4},{24,8},{28,12},{1,17},{... | collective-permute-start | bytes 73736 | tf_op jit(solution)/shard_map/ppermute | solution.py:50
  158.5 3.6 %collective-permute-start.46 = (f32[8,128]{1,0:T(8,128)S(1)}, f32[8,128]{1,0:T(8,128)S(1)}, u32[]{:S(2)}, u32[]{:S(2)}) collective-permute-start(f32[8,128]{1,0:T(8,128)S(1)} %add.103), channel_id=1, source_target_pairs={{0,2},{1,3},{2,0},{3,1},{4,6},{5,7},{6,4},{7,5},{8,10},{9,11},{10,... | collective-permute-start | bytes 12296 | tf_op jit(solution)/shard_map/ppermute | solution.py:50
  162.2 3.6 %collective-permute-start.47 = (f32[8,128]{1,0:T(8,128)S(1)}, f32[8,128]{1,0:T(8,128)S(1)}, u32[]{:S(2)}, u32[]{:S(2)}) collective-permute-start(f32[8,128]{1,0:T(8,128)S(1)} %add.104), channel_id=1, source_target_pairs={{0,4},{4,0},{8,12},{12,8},{16,20},{20,16},{24,28},{28,24},{1,5},{5... | collective-permute-start | bytes 12296 | tf_op jit(solution)/shard_map/ppermute | solution.py:50
  165.8 3.6 %collective-permute-start.48 = (f32[8,128]{1,0:T(8,128)S(1)}, f32[8,128]{1,0:T(8,128)S(1)}, u32[]{:S(2)}, u32[]{:S(2)}) collective-permute-start(f32[8,128]{1,0:T(8,128)S(1)} %add.105), channel_id=1, source_target_pairs={{0,8},{4,12},{8,0},{12,4},{16,24},{20,28},{24,16},{28,20},{1,9},{5... | collective-permute-start | bytes 12296 | tf_op jit(solution)/shard_map/ppermute | solution.py:50
  169.4 4.5 %collective-permute-start.49 = (f32[8,128]{1,0:T(8,128)S(1)}, f32[8,128]{1,0:T(8,128)S(1)}, u32[]{:S(2)}, u32[]{:S(2)}) collective-permute-start(f32[8,128]{1,0:T(8,128)S(1)} %add.106.sq_ref), channel_id=1, source_target_pairs={{0,16},{4,20},{8,24},{12,28},{16,0},{20,4},{24,8},{28,12},{1,17},{... | collective-permute-start | bytes 12296 | tf_op jit(solution)/shard_map/ppermute | solution.py:50
  (30 other events, 305.5 us)

commit v3 on v2

--- a/solution.py
+++ b/solution.py
@@ -76,14 +76,15 @@
         self.send = send
 
     def advance(self, *ready):
-        if len(self.steps) == 1:
-            return ()
+        self.keep, self.send = self.take(*ready)
         self.steps.pop()
+        self.got = swap(self.send, self.steps[-1])
+        return (self.send,)
+
+    def take(self, *ready):
         half = self.keep.shape[0] // 2
         total = self.keep.astype(F32) + after(self.got, *ready).astype(F32)
-        self.keep, self.send = total[:half].astype(BF), total[half:].astype(BF)
-        self.got = swap(self.send, self.steps[-1])
-        return (self.send,)
+        return total[:half].astype(BF), total[half:].astype(BF)
 
 
 class Total:
@@ -266,7 +267,7 @@
     return jnp.sum(v.reshape(v.shape[0] // 8, 8, v.shape[1]), axis=0)
 
 
-def middle_kernel(lh, n_dp, n_h, e_steps, c_steps, idx_ref, norm_ref, *refs):
+def middle_kernel(lh, n_dp, n_h, e_steps, c_steps, es_steps, cs_steps, idx_ref, norm_ref, *refs):
     width = lh * HD
     mixed = refs[:n_h]
     e_parts, c_parts = refs[n_h : n_h + 4], refs[n_h + 4 : n_h + 8]
@@ -275,13 +276,13 @@
     post_out, dual_out, gmid1_ref = outs[:3]
     gm = outs[3 : 3 + n_h]
     ge_keep, ge_send, gc_keep, gc_send, small_ref = outs[3 + n_h : 8 + n_h]
-    (e_s, c_s, o_s, mix_s, bias_s, hid_s, acc_s, xh_s, rs_s, pn_s, xb_s, xt_s, gb_s, gmid2_s, ffb_s) = outs[
+    (e_s, c_s, o_s, mix_s, bias_s, hid_s, acc_s, xh_s, rs_s, pn_s, xb_s, xt_s, gb_s, gmid2_s, ffb_s, gp_s, gt_s) = outs[
         8 + n_h :
     ]
     g, h = idx_ref[0], idx_ref[1]
     rw = post_in.shape[0]
     ds_rows = D // n_dp
-    units = hid_s.shape[2]
+    units = hid_s.shape[1] // n_h
     row = lambda i: norm_ref[i : i + 1, :]
 
     e_dp, e_h = offsets(e_steps, "dp"), offsets(e_steps, "head")
@@ -290,9 +291,9 @@
     for p in range(n_dp * n_h):
         at = pl.ds(pl.multiple_of((g ^ e_dp[p]) * ds_rows, ds_rows), ds_rows)
         e_ref, c_ref, i = e_parts[p // quarter], c_parts[p // quarter], p % quarter
-        e_s[e_h[p], at, :] = e_ref[i]
+        e_s[at, e_h[p] * units : (e_h[p] + 1) * units] = e_ref[i]
         at = pl.ds(pl.multiple_of((g ^ c_dp[p]) * ds_rows, ds_rows), ds_rows)
-        c_s[c_h[p], at, :] = c_ref[i, :, :units]
+        c_s[at, c_h[p] * units : (c_h[p] + 1) * units] = c_ref[i, :, :units]
         o_s[at, c_h[p] * width : (c_h[p] + 1) * width] = c_ref[i, :, units:]
     for off in range(n_h):
         mix_s[:, off * width : (off + 1) * width] = mixed[off][:rw, :]
@@ -318,16 +319,11 @@
 
     lax.fori_loop(0, rw // CH, chunk_one, 0)
     xt_s[...] = xb_s[...].T
-    acc_s[...] = jnp.zeros_like(acc_s)
-
-    def inner(oh, carry):
-        pre = dot(xb_s[...], e_s[oh], 1, 0) + bias_s[oh]
-        hid = jnp.maximum(pre, 0.0).astype(BF)
-        hid_s[oh] = hid
-        acc_s[...] += dot(hid, c_s[oh], 1, 1)
-        return carry
-
-    lax.fori_loop(0, n_h, inner, 0)
+    for oh in range(n_h):
+        part = slice(oh * units, (oh + 1) * units)
+        pre = dot(xb_s[...], e_s[:, part], 1, 0) + bias_s[oh]
+        hid_s[:, part] = jnp.maximum(pre, 0.0).astype(BF)
+    acc_s[...] = dot(hid_s[...], c_s[...], 1, 1)
 
     def chunk_two(i, carry):
         gain_sum, shift_sum, ffn_sum = carry
@@ -348,31 +344,21 @@
 
     zero = jnp.zeros((8, D), F32)
     gain2, shift2, ffn_sum = lax.fori_loop(0, rw // CH, chunk_two, (zero, zero, zero))
-    acc_s[...] = jnp.zeros_like(acc_s)
-    gt = gb_s[...].T
-    hid_t = gt
-
-    def inner_back(pair, carry):
-        for low in range(2):
-            oh = pair * 2 + low
-            ge, gc = (ge_keep, gc_keep) if low == 0 else (ge_send, gc_send)
-            hid = hid_s[oh]
-            gh = dot(gb_s[...], c_s[oh], 1, 0)
-            gp = jnp.where(hid > 0, gh, 0.0).astype(BF)
-            ffb_s[oh] = jnp.sum(gp.astype(F32), axis=0, keepdims=True)
-            acc_s[...] += dot(gp, e_s[oh], 1, 1)
-            grad_c = dot(hid_t, hid, 1, 0).astype(BF)
-            grad_e = dot(xt_s[...], gp, 1, 0).astype(BF)
-            for b in range(n_dp):
-                ge[place(e_steps, "dp", b ^ g) + place(e_steps, "head", oh - low)] = grad_e[
-                    b * ds_rows : (b + 1) * ds_rows
-                ]
-                gc[place(c_steps, "dp", b ^ g) + place(c_steps, "head", oh - low), :, :units] = grad_c[
-                    b * ds_rows : (b + 1) * ds_rows
-                ]
-        return carry
-
-    lax.fori_loop(0, n_h // 2, inner_back, 0)
+    gt_s[...] = gb_s[...].T
+    for oh in range(n_h):
+        part = slice(oh * units, (oh + 1) * units)
+        ge, gc = (ge_keep, gc_keep) if oh % 2 == 0 else (ge_send, gc_send)
+        gh = dot(gb_s[...], c_s[:, part], 1, 0)
+        gp = jnp.where(hid_s[:, part] > 0, gh, 0.0).astype(BF)
+        gp_s[:, part] = gp
+        ffb_s[oh] = jnp.sum(gp.astype(F32), axis=0, keepdims=True)
+        grad_c = dot(gt_s[...], hid_s[:, part], 1, 0).astype(BF)
+        grad_e = dot(xt_s[...], gp, 1, 0).astype(BF)
+        e_at, c_at = place(es_steps, "head", oh - oh % 2), place(cs_steps, "head", oh - oh % 2)
+        for b in range(n_dp):
+            ge[place(es_steps, "dp", b ^ g) + e_at] = grad_e[b * ds_rows : (b + 1) * ds_rows]
+            gc[place(cs_steps, "dp", b ^ g) + c_at, :, :units] = grad_c[b * ds_rows : (b + 1) * ds_rows]
+    acc_s[...] = dot(gp_s[...], e_s[...], 1, 1)
 
     def chunk_three(i, carry):
         gain_sum, shift_sum, attn_sum = carry
@@ -393,7 +379,7 @@
     for oh in range(n_h):
         gc = gc_keep if oh % 2 == 0 else gc_send
         for b in range(n_dp):
-            gc[place(c_steps, "dp", b ^ g) + place(c_steps, "head", oh - oh % 2), :, units:] = grad_o[
+            gc[place(cs_steps, "dp", b ^ g) + place(cs_steps, "head", oh - oh % 2), :, units:] = grad_o[
                 b * ds_rows : (b + 1) * ds_rows, oh * width : (oh + 1) * width
             ]
     for i, part in enumerate((gain1, shift1, attn_sum, gain2, shift2, ffn_sum)):
@@ -406,64 +392,91 @@
             small_ref[pl.ds(first + j, 1), :] = ffb_s[oh, :, j * 128 : (j + 1) * 128]
 
 
+def first_key_blocks(start, lo_ref):
+    total = 0
+    for qb in range(start.shape[1] // TQ):
+        lo = (jnp.min(start[:, qb * TQ : (qb + 1) * TQ]) * (1.0 / TK)).astype(jnp.int32)
+        lo_ref[qb] = lo
+        total = total + (qb + 1 - lo)
+    return total
+
+
+def next_pair(qb, kb, lo_ref, last):
+    done = kb >= qb
+    following = jnp.minimum(qb + 1, last)
+    return jnp.where(done, following, qb), jnp.where(done, lo_ref[following], kb + 1)
+
+
 def attend_back_kernel(lh, n_h, idx_ref, seg_ref, q_ref, k_ref, v_ref, lse_near, lse_far, small_in, *refs):
     gm, pieces = refs[:n_h], refs[n_h : 2 * n_h]
-    gqkv_ref, small_ref, do_s, o_ref, lse_ref, kt_s, dk_s, dv_s, dq_s, start_s = refs[2 * n_h :]
+    gqkv_ref, small_ref, lo_s, q2_s, do2_s, delta_s, lse_s, start_s, kt_s, dk_s, dv_s, dq_s = refs[
+        2 * n_h : 2 * n_h + 12
+    ]
+    slots = (refs[2 * n_h + 12 : 2 * n_h + 14], refs[2 * n_h + 14 :])
     h = idx_ref[1]
     width = lh * HD
     rw = gm[0].shape[0]
     n_rows = q_ref.shape[0]
+    n_q = n_rows // TQ
     cols = lh * TQ
     factor = SCORE_SCALE * LOG2E
+    starts = document_starts(seg_ref[...])
+    n_pairs = first_key_blocks(starts, lo_s)
+    starts = starts.astype(jnp.int32)
+    for qb in range(n_q):
+        start_s[qb] = jnp.concatenate([starts[:, qb * TQ : (qb + 1) * TQ]] * lh, axis=1)
+        q2_s[qb] = lane_mask_stack(q_ref[qb * TQ : (qb + 1) * TQ, :], lh)
     for off in range(n_h):
-        at = pl.ds(pl.multiple_of((h ^ off) * rw, rw), rw)
-        do_s[at, :] = gm[off][...]
-        o_ref[at, :] = pieces[off][:rw, :]
         lse_part, n = (lse_near, off) if off < n_h // 2 else (lse_far, off - n_h // 2)
         for i in range(rw // TQ):
-            lse_ref[(h ^ off) * (rw // TQ) + i] = lse_part[n * (rw // TQ) + i]
-    start_s[...] = document_starts(seg_ref[...])
+            qb = (h ^ off) * (rw // TQ) + i
+            do = gm[off][i * TQ : (i + 1) * TQ, :]
+            do2_s[qb] = lane_mask_stack(do, lh)
+            prod = (do.astype(F32) * pieces[off][i * TQ : (i + 1) * TQ, :].astype(F32)).T
+            delta_s[qb] = jnp.concatenate(
+                [jnp.sum(prod[l * HD : (l + 1) * HD, :], axis=0, keepdims=True) for l in range(lh)], axis=1
+            )
+            lse_s[qb] = lse_part[n * (rw // TQ) + i][:1]
     kt_s[...] = k_ref[...].T
     dk_s[...] = jnp.zeros_like(dk_s)
     dv_s[...] = jnp.zeros_like(dv_s)
-
-    def query_block(qb, q_sum):
-        r0 = pl.multiple_of(qb * TQ, TQ)
-        at = pl.ds(r0, TQ)
-        q2 = lane_mask_stack(q_ref[at, :], lh)
-        do = do_s[at, :]
-        do2 = lane_mask_stack(do, lh)
-        prod = (do.astype(F32) * o_ref[at, :].astype(F32)).T
-        delta = jnp.concatenate(
-            [jnp.sum(prod[l * HD : (l + 1) * HD, :], axis=0, keepdims=True) for l in range(lh)], axis=1
-        )
-        lse = lse_ref[qb][:1]
-        start = start_s[:, at]
-        lo = (jnp.min(start) * (1.0 / TK)).astype(jnp.int32)
-        start = jnp.concatenate([start.astype(jnp.int32)] * lh, axis=1)
-        column = lax.broadcasted_iota(jnp.int32, (1, cols), 1) % TQ
-        dq_s[...] = jnp.zeros_like(dq_s)
-
-        def pair(kb, carry):
-            c0 = pl.multiple_of(kb * TK, TK)
-            keys = pl.ds(c0, TK)
-            s = dot(k_ref[keys, :], q2, 1, 1)
-            key = lax.broadcasted_iota(jnp.int32, (TK, cols), 0)
-            ok = (key >= start - c0) & (key <= column + (r0 - c0))
-            p = jnp.exp2(jnp.where(ok, s, NEG_LARGE) * factor - lse)
-            dp = dot(v_ref[keys, :], do2, 1, 1)
-            grad = (p * (dp - delta)).astype(BF)
-            dv_s[keys, :] += dot(p.astype(BF), do2, 1, 0)
-            dk_s[keys, :] += dot(grad, q2, 1, 0)
-            dq_s[...] += dot(kt_s[:, keys], grad, 1, 0)
-            return carry
-
-        lax.fori_loop(lo, qb + 1, pair, 0)
-        dq = (head_rows_merge(dq_s[...], lh) * SCORE_SCALE).T.astype(BF)
-        gqkv_ref[at, :width] = dq
-        return q_sum + jnp.sum(dq.astype(F32), axis=0, keepdims=True)
-
-    q_sum = lax.fori_loop(0, n_rows // TQ, query_block, jnp.zeros((1, width), F32))
+    dq_s[...] = jnp.zeros_like(dq_s)
+    column = lax.broadcasted_iota(jnp.int32, (1, cols), 1) % TQ
+
+    def products(qb, kb, slot):
+        keys = pl.ds(pl.multiple_of(kb * TK, TK), TK)
+        slot[0][...] = dot(k_ref[keys, :], q2_s[qb], 1, 1)
+        slot[1][...] = dot(v_ref[keys, :], do2_s[qb], 1, 1)
+
+    def gradients(qb, kb, slot, least):
+        c0 = pl.multiple_of(kb * TK, TK)
+        keys = pl.ds(c0, TK)
+        key = lax.broadcasted_iota(jnp.int32, (TK, cols), 0)
+        ok = (key >= start_s[qb] - c0 + least) & (key <= column + (qb * TQ - c0))
+        p = jnp.exp2(jnp.where(ok, slot[0][...], NEG_LARGE) * factor - lse_s[qb])
+        grad = (p * (slot[1][...] - delta_s[qb])).astype(BF)
+        dv_s[keys, :] += dot(p.astype(BF), do2_s[qb], 1, 0)
+        dk_s[keys, :] += dot(grad, q2_s[qb], 1, 0)
+        dq_s[qb] += dot(kt_s[:, keys], grad, 1, 0)
+
+    products(0, 0, slots[0])
+
+    def two_pairs(i, carry):
+        qb, kb = carry
+        one = next_pair(qb, kb, lo_s, n_q - 1)
+        products(*one, slots[1])
+        gradients(qb, kb, slots[0], 0)
+        two = next_pair(*one, lo_s, n_q - 1)
+        products(*two, slots[0])
+        gradients(*one, slots[1], jnp.where(2 * i + 1 < n_pairs, 0, 2 * n_rows))
+        return two
+
+    lax.fori_loop(0, (n_pairs + 1) // 2, two_pairs, (jnp.int32(0), jnp.int32(0)))
+    q_sum = jnp.zeros((1, width), F32)
+    for qb in range(n_q):
+        dq = (head_rows_merge(dq_s[qb], lh) * SCORE_SCALE).T.astype(BF)
+        gqkv_ref[qb * TQ : (qb + 1) * TQ, :width] = dq
+        q_sum = q_sum + jnp.sum(dq.astype(F32), axis=0, keepdims=True)
     gqkv_ref[:, width : 2 * width] = (dk_s[...] * SCORE_SCALE).astype(BF)
     dv = dv_s[...].astype(BF)
     gqkv_ref[:, 2 * width :] = dv
@@ -522,7 +535,6 @@
 
 
 def adam_kernel(units, clip_ref, sq_ref, sq_got, small_ref, *refs):
-    ga, ge, gc = refs[0:2], refs[2:4], refs[4:6]
     share_bias, norm_grads = refs[6:8]
     params, momenta, variances = refs[8:14], refs[14:20], refs[20:26]
     norm_ref, clipped_ref = refs[26:28]
@@ -533,12 +545,12 @@
     norm_ref[...] = norm
     limit = clip_ref[0]
     factor = (limit / jnp.maximum(norm, limit))[:1, :1]
-    share_co = total_of_pair(*gc)
+    shares = total_of_pair(refs[4], refs[5])
     grads = (
-        total_of_pair(*ga),
-        share_co[:, units:],
-        total_of_pair(*ge),
-        share_co[:, :units],
+        total_of_pair(refs[0], refs[1]),
+        shares[:, units:],
+        total_of_pair(refs[2], refs[3]),
+        shares[:, :units],
         share_bias[...],
         norm_grads[...],
     )
@@ -611,27 +623,21 @@
     shares = head_bias.shape[1]
     dp_bits, h_bits = bits_of(n_dp), bits_of(n_h)
     a_steps = [("dp", b) for b in dp_bits]
-    e_steps = [("dp", b) for b in dp_bits] + [("head", b) for b in h_bits]
-    c_steps = (
-        [("dp", b) for b in dp_bits[:-1]]
-        + [("head", b) for b in h_bits[:-1]]
-        + [("dp", dp_bits[-1])]
-        + [("head", h_bits[-1])]
-    )
-
-    rows_own = post_in.astype(BF)
+    dp_steps, h_steps = [("dp", b) for b in dp_bits], [("head", b) for b in h_bits]
+    e_steps = dp_steps + h_steps
+    c_steps = dp_steps[:-1] + h_steps[:-1] + dp_steps[-1:] + h_steps[-1:]
+    es_steps = dp_steps[:-1] + h_steps[:-1] + dp_steps[-1:] + h_steps[-1:]
+    cs_steps = dp_steps[:1] + h_steps[:-1] + dp_steps[-1:] + dp_steps[1:-1] + h_steps[-1:]
+    g_steps = dp_steps[:1] + dp_steps[-1:] + dp_steps[1:-1]
+
     bias_block = jnp.pad(
         head_bias.astype(BF).reshape(1, lh * shares), ((0, 15), (0, a_cols - lh * shares))
     )
     a_msg = jnp.concatenate([attend_weight.astype(BF), bias_block], axis=0)
-    e_msg = expand_weight.astype(BF)
-    c_msg = jnp.concatenate([contract_weight.T.astype(BF), output_weight.T.astype(BF)], axis=1)
-
-    rows = {0: rows_own}
-    for bit in h_bits:
-        for off in list(rows):
-            rows[off ^ bit] = swap(rows[off], ("head", bit))
-    rows = [rows[off] for off in range(n_h)]
+    m_msg = jnp.concatenate(
+        [expand_weight.astype(BF), contract_weight.T.astype(BF), output_weight.T.astype(BF)], axis=1
+    )
+    rows_own = after(post_in, a_msg).astype(BF)
 
     n_d, n_s = len(dp_bits), len(e_steps)
     a_in, a_got = [a_msg[None]], []
@@ -639,20 +645,26 @@
         a_got.append(swap(a_in[i], step))
         if i < n_d - 1:
             a_in.append(jnp.concatenate([a_in[i], a_got[i]], axis=0))
-    e_in, e_got, c_in, c_got = [e_msg[None]], [], [c_msg[None]], []
-
-    def exchange(*ready):
-        i = len(e_got)
-        if i == 0:
-            e_in[0], c_in[0] = after(e_in[0], *ready), after(c_in[0], *ready)
-        else:
-            e_in.append(jnp.concatenate([e_in[-1], after(e_got[-1], *ready)], axis=0))
-            c_in.append(jnp.concatenate([c_in[-1], after(c_got[-1], *ready)], axis=0))
-        e_got.append(swap(e_in[i], e_steps[i]))
-        c_got.append(swap(c_in[i], c_steps[i]))
-
+    m_in, m_got = m_msg[None], None
     for i in range(n_d - 1):
-        exchange(a_got[i])
+        if i > 0:
+            m_in = jnp.concatenate([m_in, after(m_got, a_got[i - 1])], axis=0)
+        m_got = swap(m_in, e_steps[i])
+    e_in, c_in = m_in[..., :units], m_in[..., units:]
+    e_got, c_got = m_got[..., :units], m_got[..., units:]
+
+    def exchange(i, *ready):
+        nonlocal e_in, c_in, e_got, c_got
+        e_in = jnp.concatenate([e_in, after(e_got, *ready)], axis=0)
+        c_in = jnp.concatenate([c_in, after(c_got, *ready)], axis=0)
+        e_got, c_got = swap(e_in, e_steps[i]), swap(c_in, c_steps[i])
+
+    rows = {0: rows_own}
+    for bit in h_bits:
+        for off in list(rows):
+            rows[off ^ bit] = swap(rows[off], ("head", bit))
+    rows = [rows[off] for off in range(n_h)]
+    exchange(n_d - 1)
     n_q = n_rows // TQ
     cols = lh * TQ
     q, k, v, vt, wg, inner = call(
@@ -661,7 +673,7 @@
         + [sds((width + 16, n_rows), BF), sds((D, 3 * width), BF), sds((16, width), BF)],
         [pltpu.VMEM((D, a_cols), BF), pltpu.VMEM((n_dp, lh * shares), F32)],
         1,
-        [idx, after(a_in[-1], e_in[n_d - 2], c_in[n_d - 2]), a_got[-1]] + rows,
+        [idx, after(a_in[-1], e_in, c_in), a_got[-1]] + rows,
         24,
         4,
     )
@@ -678,42 +690,43 @@
             1,
             [idx, segment_ids, q, k, vt, inner],
             24,
-            5,
+            1,
         )
         return out[:-1], out[-1]
 
-    exchange(q)
-    far, lse_far = attend(range(n_h // 2, n_h), after(q, e_in[n_d - 1], c_in[n_d - 1]))
-    exchange(far[0])
-    near, lse_near = attend(range(n_h // 2), after(q, e_in[n_d], c_in[n_d]))
+    exchange(n_d, q)
+    far, lse_far = attend(range(n_h // 2, n_h), after(q, e_in, c_in))
+    early = n_d + 1 == n_s - 1
+    crossed = [swap(e_in, e_steps[-1]), swap(c_in, c_steps[-1])] if early else []
+    near, lse_near = attend(range(n_h // 2), after(q, far[0], *crossed))
     for i in range(n_d + 1, n_s - 1):
-        exchange()
+        exchange(i, near[0])
     pieces = list(near) + list(far)
     mixed = [pieces[0]] + [
         lax.ppermute(pieces[off], "head", [(i, i ^ off) for i in range(n_h)]) for off in range(1, n_h)
     ]
     arrived = [near[0]] + mixed[n_h // 2 :]
-    e_in[-1], c_in[-1] = after(e_in[-1], *arrived), after(c_in[-1], *arrived)
-    e_got[-1], c_got[-1] = after(e_got[-1], *arrived), after(c_got[-1], *arrived)
-    e_parts = [e_in[-1], e_got[-1]]
-    e_parts += [swap(part, e_steps[-1]) for part in e_parts]
-    c_parts = [c_in[-1], c_got[-1]]
-    c_parts += [swap(part, c_steps[-1]) for part in c_parts]
+    if not early:
+        crossed = [swap(e_in, e_steps[-1]), swap(c_in, c_steps[-1])]
+    e_got, c_got = after(e_got, *arrived), after(c_got, *arrived)
+    e_parts = [e_in, e_got, crossed[0], swap(e_got, e_steps[-1])]
+    c_parts = [c_in, c_got, crossed[1], swap(c_got, c_steps[-1])]
+
     half = n_dp * n_h // 2
     middle_out = call(
-        functools.partial(middle_kernel, lh, n_dp, n_h, e_steps, c_steps),
+        functools.partial(middle_kernel, lh, n_dp, n_h, e_steps, c_steps, es_steps, cs_steps),
         [sds((rw, D), F32)] * 3
         + [sds((rw, width), BF)] * n_h
         + [sds((half, ds_rows, units), BF)] * 2
         + [sds((half, ds_rows, units + width), BF)] * 2
         + [sds((40, 128), F32)],
         [
-            pltpu.VMEM((n_h, D, units), BF),
-            pltpu.VMEM((n_h, D, units), BF),
+            pltpu.VMEM((D, n_h * units), BF),
+            pltpu.VMEM((D, n_h * units), BF),
             pltpu.VMEM((D, n_h * width), BF),
             pltpu.VMEM((rw, n_h * width), BF),
             pltpu.VMEM((n_h, 1, units), F32),
-            pltpu.VMEM((n_h, rw, units), BF),
+            pltpu.VMEM((rw, n_h * units), BF),
             pltpu.VMEM((rw, D), F32),
             pltpu.VMEM((rw, D), F32),
             pltpu.VMEM((rw, 128), F32),
@@ -723,10 +736,12 @@
             pltpu.VMEM((rw, D), BF),
             pltpu.VMEM((rw, D), F32),
             pltpu.VMEM((n_h, 1, units), F32),
+            pltpu.VMEM((rw, n_h * units), BF),
+            pltpu.VMEM((D, rw), BF),
         ],
         1,
         [idx, norm_params] + mixed + e_parts + c_parts + [post_in, dual_in, post_cot, dual_cot],
-        52,
+        34,
         20,
     )
     post_out, dual_out, grad_mid1 = middle_out[:3]
@@ -735,30 +750,34 @@
     gm = [gm[0]] + [
         lax.ppermute(gm[off], "head", [(i, i ^ off) for i in range(n_h)]) for off in range(1, n_h)
     ]
-    ge, gc = Scatter(ge_keep, ge_send, e_steps), Scatter(gc_keep, gc_send, c_steps)
+    ge, gc = Scatter(ge_keep, ge_send, es_steps), Scatter(gc_keep, gc_send, cs_steps)
     gm[0] = after(gm[0], *ge.advance(), *gc.advance())
     gqkv, small = call(
         functools.partial(attend_back_kernel, lh, n_h),
         [sds((n_rows, 3 * width), BF), sds((48, 128), F32)],
         [
-            pltpu.VMEM((n_rows, width), BF),
-            pltpu.VMEM((n_rows, width), BF),
-            pltpu.VMEM((n_q, 8, cols), F32),
+            pltpu.SMEM((n_q,), jnp.int32),
+            pltpu.VMEM((n_q, cols, width), BF),
+            pltpu.VMEM((n_q, cols, width), BF),
+            pltpu.VMEM((n_q, 1, cols), F32),
+            pltpu.VMEM((n_q, 1, cols), F32),
+            pltpu.VMEM((n_q, 1, cols), jnp.int32),
             pltpu.VMEM((width, n_rows), BF),
             pltpu.VMEM((n_rows, width), F32),
             pltpu.VMEM((n_rows, width), F32),
-            pltpu.VMEM((width, cols), F32),
-            pltpu.VMEM((1, n_rows), F32),
-        ],
+            pltpu.VMEM((n_q, width, cols), F32),
+        ]
+        + [pltpu.VMEM((TK, cols), F32)] * 4,
         1,
         [idx, segment_ids, q, k, v, lse_near, lse_far, small_mid] + gm + pieces,
         32,
         15,
     )
-    total = Total(small, e_steps)
     sent = ge.advance(gqkv) + gc.advance(gqkv)
+    total = Total(small, dp_steps + h_steps)
+    sent = total.advance(*sent)
     ga = call(
-        functools.partial(attend_grad_kernel, lh, n_dp, n_h, a_steps),
+        functools.partial(attend_grad_kernel, lh, n_dp, n_h, g_steps),
         sds((n_dp, ds_rows, a_cols), BF),
         [pltpu.VMEM((D, 3 * width), F32)],
         1,
@@ -766,7 +785,7 @@
         24,
         2,
     )
-    ga = Scatter(ga[: n_dp // 2], ga[n_dp // 2 :], a_steps)
+    ga = Scatter(ga[: n_dp // 2], ga[n_dp // 2 :], g_steps)
     back = call(
         functools.partial(rows_back_kernel, n_h),
         [sds((rw, D), BF)] * n_h,
@@ -776,16 +795,25 @@
         24,
         2,
     )
+    sent = (back[0],)
     back = RowSums(back, sorted(h_bits, reverse=True))
-    sent = ()
-    for _ in range(len(h_bits) - 1):
-        sent = back.advance(*sent)
-    for i in range(n_s):
-        for chain in (ge, gc, total, ga):
-            sent = chain.advance(*sent) or sent
-            if i == 1 and chain is gc:
-                post_grad = back.finish(grad_mid1, *sent)
-                sent = (post_grad,)
+    for i in range(n_s - 3):
+        sent = ge.advance(*sent)
+        sent = gc.advance(*sent)
+        if i == 0:
+            sent = total.advance(*sent)
+            for _ in range(len(h_bits) - 1):
+                sent = back.advance(*sent)
+        if i < n_d - 1:
+            sent = ga.advance(*sent)
+    sent = total.advance(*sent)
+    post_grad = back.finish(grad_mid1, *sent)
+    sent = (post_grad,)
+    pairs = [ga.keep, ga.got, ge.keep, ge.got, gc.keep, gc.got]
+    squares = call(squares_kernel, sds((8, 128), F32), [], 0, pairs, 16, 1)
+    squares = Total(squares, h_steps[:-1] + dp_steps[::-1] + h_steps[-1:])
+    for _ in e_steps[:-1]:
+        total.advance(*squares.advance(*sent))
     small = total.result()
     norm_grads = small[:24].reshape(6, D)
     bias_full = jnp.concatenate(
@@ -796,12 +824,6 @@
         axis=1,
     )
     share_bias = lax.dynamic_slice_in_dim(bias_full, g * shares, shares, 1)
-    pairs = [ga.keep, ga.got, ge.keep, ge.got, gc.keep, gc.got]
-    pairs[0] = after(pairs[0], *sent)
-    squares = call(squares_kernel, sds((8, 128), F32), [], 0, pairs, 16, 1)
-    squares = Total(squares, e_steps)
-    for _ in e_steps[:-1]:
-        squares.advance()
     flip = lambda arrays: [a.T if i in (1, 3) else a for i, a in enumerate(arrays)]
     params = flip([attend_weight, output_weight, expand_weight, contract_weight, head_bias, norm_params])
     momenta = flip(

time: 176 us -> 150 us (0.85)
  waiting for transfers between devices: 54.8 us -> 44.5 us
  Pallas kernels: 58.5 us -> 50.5 us
  starting transfers between devices: 51.7 us -> 47.5 us
  local copies, waits for them, and re-layouts: 3.23 us -> 1.05 us
    ppermute x44 -> x42, waiting for transfers between devices: 51.2 us -> 37.5 us  [swap(): return lax.ppermute(v, axis, [(i, i ^ bit) for i in range(count)])]
    pallas_call x9, Pallas kernels: 58.5 us -> 50.5 us  [call(): pl.pallas_call(body, out_shape=outs, in_specs=[SMEM] * n_smem + [VMEM] *...]
    ppermute x44 -> x42, starting transfers between devices: 49.3 us -> 44.2 us  [swap(): return lax.ppermute(v, axis, [(i, i ^ bit) for i in range(count)])]
    ppermute x3, waiting for transfers between devices: 1.6 us -> 4.75 us  [per_device(): lax.ppermute(pieces[off], 'head', [(i, i ^ off) for i in range(n_h)])]
    unnamed x61 -> x46, local copies, waits for them, and re-layouts: 2.27 us -> 0.13 us
  transfers between devices with their start and end apart: 50 -> 48, of which waited for: 24 -> 23; matrix products, arithmetic and copies ran while one was open for 3% -> 2% of each run, Pallas kernels for 18% -> 22%
where the time goes in v3:
time: 150 us
  Pallas kernels  50.5 us (34%)
  starting transfers between devices  47.5 us (32%)
  waiting for transfers between devices  44.5 us (30%)
  other arithmetic  4.72 us (3%)
  between operations  2.09 us (1%)
    pallas_call x9, Pallas kernels, call(): pl.pallas_call(body, out_shape=outs, in_specs=[SMEM] * n_smem + [VMEM] *...  50.5 us
    ppermute x42, starting transfers between devices, swap(): return lax.ppermute(v, axis, [(i, i ^ bit) for i in range(count)])  44.2 us
    ppermute x42, waiting for transfers between devices, swap(): return lax.ppermute(v, axis, [(i, i ^ bit) for i in range(count)])  37.5 us
    ppermute x3, waiting for transfers between devices, per_device(): lax.ppermute(pieces[off], 'head', [(i, i ^ off) for i in range(n_h)])  4.75 us
  transfers between devices with their start and end apart: 48, of which 23 were waited for; matrix products, arithmetic and copies ran while one was open for 2% of the time, Pallas kernels for 22%

profile of v3, /device:TPU:0, one launch (start us, length us, event | category | flops | bytes accessed | tf_op | source)
XLA Modules:
  0.0 150.3 jit_solution(8156446359181060018)
XLA Ops:
  0.7 1.4 convert_element_type.123.refs_0_
  2.1 3.0 %collective-permute-start.6 = (bf16[512,512]{1,0:T(8,128)(2,1)S(1)}, bf16[512,512]{1,0:T(8,128)(2,1)S(1)}, u32[]{:S(2)}, u32[]{:S(2)}) collective-permute-start(bf16[512,512]{1,0:T(8,128)(2,1)S(1)} %convert_element_type.123.refs_0_), channel_id=1, source_target_pairs={{0,2},{1,3},{2,0},{3,1},{4,6},{5,7},{6,4},{7,5},{8,10},{9,11},{10,... | collective-permute-start | bytes 1572872 | tf_op jit(solution)/shard_map/ppermute | solution.py:50
  5.3 2.7 %collective-permute-start = (bf16[1,80,384]{2,1,0:T(8,128)(2,1)S(1)}, bf16[1,80,384]{2,1,0:T(8,128)(2,1)S(1)}, u32[]{:S(2)}, u32[]{:S(2)}) collective-permute-start(bf16[1,80,384]{2,1,0:T(8,128)(2,1)S(1)} %fusion.5), channel_id=1, source_target_pairs={{0,16},{4,20},{8,24},{12,28},{16,0},{20,4},{24,8},{28,12},{1,17},{... | collective-permute-start | bytes 184328 | tf_op jit(solution)/shard_map/ppermute | solution.py:50
  8.5 3.6 %collective-permute-done = bf16[1,80,384]{2,1,0:T(8,128)(2,1)S(1)} collective-permute-done((bf16[1,80,384]{2,1,0:T(8,128)(2,1)S(1)}, bf16[1,80,384]{2,1,0:T(8,128)(2,1)S(1)}, u32[]{:S(2)}, u32[]{:S(2)}) %collective-permute-start) | collective-permute-done | bytes 61472 | tf_op jit(solution)/shard_map/ppermute | solution.py:50
  12.1 3.8 %collective-permute-start.1 = (bf16[2,80,384]{2,1,0:T(8,128)(2,1)S(1)}, bf16[2,80,384]{2,1,0:T(8,128)(2,1)S(1)}, u32[]{:S(2)}, u32[]{:S(2)}) collective-permute-start(bf16[2,80,384]{2,1,0:T(8,128)(2,1)S(1)} %pad_maximum_fusion.6), channel_id=1, source_target_pairs={{0,8},{4,12},{8,0},{12,4},{16,24},{20,28},{24,16},{28,20},{1,9},{5... | collective-permute-start | bytes 368648 | tf_op jit(solution)/shard_map/ppermute | solution.py:50
  15.9 2.5 %collective-permute-done.2 = bf16[1,64,1152]{2,1,0:T(8,128)(2,1)S(1)} collective-permute-done((bf16[1,64,1152]{2,1,0:T(8,128)(2,1)S(1)}, bf16[1,64,1152]{2,1,0:T(8,128)(2,1)S(1)}, u32[]{:S(2)}, u32[]{:S(2)}) %collective-permute-start.2) | collective-permute-done | bytes 147488 | tf_op jit(solution)/shard_map/ppermute | solution.py:50
  19.1 1.9 %collective-permute-done.1 = bf16[2,80,384]{2,1,0:T(8,128)(2,1)S(1)} collective-permute-done((bf16[2,80,384]{2,1,0:T(8,128)(2,1)S(1)}, bf16[2,80,384]{2,1,0:T(8,128)(2,1)S(1)}, u32[]{:S(2)}, u32[]{:S(2)}) %collective-permute-start.1) | collective-permute-done | bytes 122912 | tf_op jit(solution)/shard_map/ppermute | solution.py:50
  21.0 1.6 %collective-permute-start.4 = (bf16[4,80,384]{2,1,0:T(8,128)(2,1)S(1)}, bf16[4,80,384]{2,1,0:T(8,128)(2,1)S(1)}, u32[]{:S(2)}, u32[]{:S(2)}) collective-permute-start(bf16[4,80,384]{2,1,0:T(8,128)(2,1)S(1)} %pad_maximum_fusion.5.w_own), channel_id=1, source_target_pairs={{0,4},{4,0},{8,12},{12,8},{16,20},{20,16},{24,28},{28,24},{1,5},{5... | collective-permute-start | bytes 737288 | tf_op jit(solution)/shard_map/ppermute | solution.py:50
  22.6 4.7 %collective-permute-done.3 = bf16[2,64,1152]{2,1,0:T(8,128)(2,1)S(1)} collective-permute-done((bf16[2,64,1152]{2,1,0:T(8,128)(2,1)S(1)}, bf16[2,64,1152]{2,1,0:T(8,128)(2,1)S(1)}, u32[]{:S(2)}, u32[]{:S(2)}) %collective-permute-start.3) | collective-permute-done | bytes 294944 | tf_op jit(solution)/shard_map/ppermute | solution.py:50
  27.9 1.6 %collective-permute-start.8 = (bf16[4,64,512]{2,1,0:T(8,128)(2,1)S(1)}, bf16[4,64,512]{2,1,0:T(8,128)(2,1)S(1)}, u32[]{:S(2)}, u32[]{:S(2)}) collective-permute-start(bf16[4,64,512]{2,1,0:T(8,128)(2,1)S(1)} %pad_maximum_fusion.4), channel_id=1, source_target_pairs={{0,4},{4,0},{8,12},{12,8},{16,20},{20,16},{24,28},{28,24},{1,5},{5... | collective-permute-start | bytes 786440 | tf_op jit(solution)/shard_map/ppermute | solution.py:50
  29.5 2.0 %shard_map.447 = (bf16[2048,128]{1,0:T(8,128)(2,1)S(1)}, bf16[2048,128]{1,0:T(8,128)(2,1)S(1)}, bf16[2048,128]{1,0:T(8,128)(2,1)S(1)}, bf16[144,2048]{1,0:T(8,12...) custom-call(s32[2]{0:T(128)S(1)} %pad_add_fusion.idx_ref, ...), custom_call_target="tpu_custom_call" | custom-call | flops 4000000000 | bytes 1048576 | tf_op jit(solution)/shard_map/pallas_call | solution.py:572
  31.6 4.4 %collective-permute-done.9 = bf16[4,64,640]{2,1,0:T(8,128)(2,1)S(1)} collective-permute-done((bf16[4,64,640]{2,1,0:T(8,128)(2,1)S(1)}, bf16[4,64,640]{2,1,0:T(8,128)(2,1)S(1)}, u32[]{:S(2)}, u32[]{:S(2)}) %collective-permute-start.9) | collective-permute-done | bytes 327712 | tf_op jit(solution)/shard_map/ppermute | solution.py:50
  36.7 1.5 collective-permute-start.17
  38.7 8.8 %shard_map.448 = (bf16[528,128]{1,0:T(8,128)(2,1)S(1)}, bf16[528,128]{1,0:T(8,128)(2,1)S(1)}, f32[4,8,512]{2,1,0:T(8,128)S(1)}) custom-call(s32[2]{0:T(128)S(1)} %pad_add_fusion.idx_ref, s32[1,2048]{1,0:T(1,128)S(1)} %copy-done.19, bf16[2048,128]{1,0:T(8,128)(2,1)S(1)} %get-tuple-element.127.q_ref, bf16[2048,128]{1,0:T(8,128)(2,1)S(1)} %get-tuple-element.123.k_ref, ...), custom_call_target="tpu_custom_call" | custom-call | flops 1000000000 | bytes 1048576 | tf_op jit(solution)/shard_map/pallas_call | solution.py:572
  48.6 5.2 %shard_map.449 = (bf16[528,128]{1,0:T(8,128)(2,1)S(1)}, bf16[528,128]{1,0:T(8,128)(2,1)S(1)}, f32[4,8,512]{2,1,0:T(8,128)S(1)}) custom-call(s32[2]{0:T(128)S(1)} %pad_add_fusion.idx_ref, s32[1,2048]{1,0:T(1,128)S(1)} %copy-done.19, bf16[2048,128]{1,0:T(8,128)(2,1)S(1)} %get-tuple-element.127.q_ref, bf16[2048,128]{1,0:T(8,128)(2,1)S(1)} %get-tuple-element.123.k_ref, ...), custom_call_target="tpu_custom_call" | custom-call | flops 1000000000 | bytes 1048576 | tf_op jit(solution)/shard_map/pallas_call | solution.py:572
  53.8 2.1 %collective-permute-done.13.refs_2_ = bf16[528,128]{1,0:T(8,128)(2,1)S(1)} collective-permute-done((bf16[528,128]{1,0:T(8,128)(2,1)S(1)}, bf16[528,128]{1,0:T(8,128)(2,1)S(1)}, u32[]{:S(2)}, u32[]{:S(2)}) %collective-permute-start.13) | collective-permute-done | bytes 135200 | tf_op jit(solution)/shard_map/ppermute | solution.py:706
  56.4 1.0 collective-permute-start.18
  58.0 2.2 %collective-permute-done.12.refs_1_ = bf16[528,128]{1,0:T(8,128)(2,1)S(1)} collective-permute-done((bf16[528,128]{1,0:T(8,128)(2,1)S(1)}, bf16[528,128]{1,0:T(8,128)(2,1)S(1)}, u32[]{:S(2)}, u32[]{:S(2)}) %collective-permute-start.12) | collective-permute-done | bytes 135200 | tf_op jit(solution)/shard_map/ppermute | solution.py:706
  60.2 15.3 %shard_map.450 = (f32[512,512]{1,0:T(8,128)}, f32[512,512]{1,0:T(8,128)}, f32[512,512]{1,0:T(8,128)S(1)}, bf16[512,128]{1,0:T(8,128)(2,1)S(1)}, bf16[512,128]{1,...) custom-call(s32[2]{0:T(128)S(1)} %pad_add_fusion.idx_ref, ...), custom_call_target="tpu_custom_call" | custom-call | flops 20000000000 | bytes 1048576 | tf_op jit(solution)/shard_map/pallas_call | solution.py:572
  76.4 1.2 collective-permute-start.22
  80.5 1.2 collective-permute-start.26
  81.7 1.0 collective-permute-done.22.refs_2_
  82.7 1.2 collective-permute-done.23.refs_3_
  83.9 13.8 %shard_map.451 = (bf16[2048,384]{1,0:T(8,128)(2,1)S(1)}, f32[48,128]{1,0:T(8,128)S(1)}) custom-call(s32[2]{0:T(128)S(1)} %pad_add_fusion.idx_ref, s32[1,2048]{1,0:T(1,128)S(1)} %copy-done.19, bf16[2048,128]{1,0:T(8,128)(2,1)S(1)} %get-tuple-element.127.q_ref, bf16[2048,128]{1,0:T(8,128)(2,1)S(1)} %get-tuple-element.123.k_ref, ...), custom_call_target="tpu_custom_call" | custom-call | flops 15000000512 | bytes 1048576 | tf_op jit(solution)/shard_map/pallas_call | solution.py:572
  97.7 1.0 collective-permute-start.24
  98.9 1.5 %collective-permute-start.29 = (bf16[4,64,512]{2,1,0:T(8,128)(2,1)S(1)}, bf16[4,64,512]{2,1,0:T(8,128)(2,1)S(1)}, u32[]{:S(2)}, u32[]{:S(2)}) collective-permute-start(bf16[4,64,512]{2,1,0:T(8,128)(2,1)S(1)} %slice.141), channel_id=1, source_target_pairs={{0,2},{1,3},{2,0},{3,1},{4,6},{5,7},{6,4},{7,5},{8,10},{9,11},{10,... | collective-permute-start | bytes 786440 | tf_op jit(solution)/shard_map/ppermute | solution.py:50
  100.7 1.9 %shard_map.452 = bf16[8,64,384]{2,1,0:T(8,128)(2,1)S(1)} custom-call(s32[2]{0:T(128)S(1)} %pad_add_fusion.idx_ref, bf16[2048,384]{1,0:T(8,128)(2,1)S(1)} %get-tuple-element.155.gqkv_ref, bf16[512,512]{1,0:T(8,128)(2,1)S(1)} %convert_element_type.123.refs_0_, bf16[512,512]{1,0:T(8,128)(2,1)S(1)} %collective-permute-done.5.refs_1_, ...), custom_call_target="tpu_custom_call" | custom-call | flops 2000000000 | bytes 1048576 | tf_op jit(solution)/shard_map/pallas_call | solution.py:572
  102.6 1.8 %shard_map.453 = (bf16[512,512]{1,0:T(8,128)(2,1)S(1)}, bf16[512,512]{1,0:T(8,128)(2,1)S(1)}, bf16[512,512]{1,0:T(8,128)(2,1)S(1)}, bf16[512,512]{1,0:T(8,128)(2,1)S(1)}) custom-call(s32[2]{0:T(128)S(1)} %pad_add_fusion.idx_ref, bf16[2048,384]{1,0:T(8,128)(2,1)S(1)} %get-tuple-element.155.gqkv_ref, bf16[512,384]{1,0:T(8,128)(2,1)S(1)} %get-tuple-element.156.wg_ref), custom_call_target="tpu_custom_call" | custom-call | flops 2000000000 | bytes 1048576 | tf_op jit(solution)/shard_map/pallas_call | solution.py:572
  104.6 1.1 collective-permute-start.27
  105.7 1.1 collective-permute-start.31
  107.9 2.1 %collective-permute-done.28 = bf16[4,64,640]{2,1,0:T(8,128)(2,1)S(1)} collective-permute-done((bf16[4,64,640]{2,1,0:T(8,128)(2,1)S(1)}, bf16[4,64,640]{2,1,0:T(8,128)(2,1)S(1)}, u32[]{:S(2)}, u32[]{:S(2)}) %collective-permute-start.28) | collective-permute-done | bytes 327712 | tf_op jit(solution)/shard_map/ppermute | solution.py:50
  111.6 1.9 %collective-permute-done.31 = bf16[4,64,384]{2,1,0:T(8,128)(2,1)S(1)} collective-permute-done((bf16[4,64,384]{2,1,0:T(8,128)(2,1)S(1)}, bf16[4,64,384]{2,1,0:T(8,128)(2,1)S(1)}, u32[]{:S(2)}, u32[]{:S(2)}) %collective-permute-start.31) | collective-permute-done | bytes 196640 | tf_op jit(solution)/shard_map/ppermute | solution.py:50
  113.5 0.9 collective-permute-start.37
  114.5 1.0 collective-permute-done.35
  115.5 1.5 collective-permute-start.33
  117.2 3.0 %collective-permute-start.39 = (bf16[1,64,512]{2,1,0:T(8,128)(2,1)S(1)}, bf16[1,64,512]{2,1,0:T(8,128)(2,1)S(1)}, u32[]{:S(2)}, u32[]{:S(2)}) collective-permute-start(bf16[1,64,512]{2,1,0:T(8,128)(2,1)S(1)} %get-tuple-element.207), channel_id=1, source_target_pairs={{0,16},{4,20},{8,24},{12,28},{16,0},{20,4},{24,8},{28,12},{1,17},{... | collective-permute-start | bytes 196616 | tf_op jit(solution)/shard_map/ppermute | solution.py:50
  120.4 2.8 %collective-permute-start.40 = (bf16[1,64,640]{2,1,0:T(8,128)(2,1)S(1)}, bf16[1,64,640]{2,1,0:T(8,128)(2,1)S(1)}, u32[]{:S(2)}, u32[]{:S(2)}) collective-permute-start(bf16[1,64,640]{2,1,0:T(8,128)(2,1)S(1)} %get-tuple-element.205), channel_id=1, source_target_pairs={{0,16},{4,20},{8,24},{12,28},{16,0},{20,4},{24,8},{28,12},{1,17},{... | collective-permute-start | bytes 245768 | tf_op jit(solution)/shard_map/ppermute | solution.py:50
  123.5 1.5 collective-permute-start.46
  125.0 3.2 %collective-permute-done.40.refs_5_ = bf16[1,64,640]{2,1,0:T(8,128)(2,1)S(1)} collective-permute-done((bf16[1,64,640]{2,1,0:T(8,128)(2,1)S(1)}, bf16[1,64,640]{2,1,0:T(8,128)(2,1)S(1)}, u32[]{:S(2)}, u32[]{:S(2)}) %collective-permute-start.40) | collective-permute-done | bytes 81952 | tf_op jit(solution)/shard_map/ppermute | solution.py:50
  129.0 1.3 convert_add_fusion
  130.2 2.3 %collective-permute-start.47 = (f32[48,128]{1,0:T(8,128)S(1)}, f32[48,128]{1,0:T(8,128)S(1)}, u32[]{:S(2)}, u32[]{:S(2)}) collective-permute-start(f32[48,128]{1,0:T(8,128)S(1)} %add.105), channel_id=1, source_target_pairs={{0,16},{4,20},{8,24},{12,28},{16,0},{20,4},{24,8},{28,12},{1,17},{... | collective-permute-start | bytes 73736 | tf_op jit(solution)/shard_map/ppermute | solution.py:50
  133.2 3.9 %collective-permute-done.42 = f32[8,128]{1,0:T(8,128)S(1)} collective-permute-done((f32[8,128]{1,0:T(8,128)S(1)}, f32[8,128]{1,0:T(8,128)S(1)}, u32[]{:S(2)}, u32[]{:S(2)}) %collective-permute-start.42) | collective-permute-done | bytes 4128 | tf_op jit(solution)/shard_map/ppermute | solution.py:50
  137.1 2.4 %collective-permute-start.43 = (f32[8,128]{1,0:T(8,128)S(1)}, f32[8,128]{1,0:T(8,128)S(1)}, u32[]{:S(2)}, u32[]{:S(2)}) collective-permute-start(f32[8,128]{1,0:T(8,128)S(1)} %add.102), channel_id=1, source_target_pairs={{0,8},{4,12},{8,0},{12,4},{16,24},{20,28},{24,16},{28,20},{1,9},{5... | collective-permute-start | bytes 12296 | tf_op jit(solution)/shard_map/ppermute | solution.py:50
  139.4 1.6 %collective-permute-done.43 = f32[8,128]{1,0:T(8,128)S(1)} collective-permute-done((f32[8,128]{1,0:T(8,128)S(1)}, f32[8,128]{1,0:T(8,128)S(1)}, u32[]{:S(2)}, u32[]{:S(2)}) %collective-permute-start.43) | collective-permute-done | bytes 4128 | tf_op jit(solution)/shard_map/ppermute | solution.py:50
  142.1 2.5 %collective-permute-done.44 = f32[8,128]{1,0:T(8,128)S(1)} collective-permute-done((f32[8,128]{1,0:T(8,128)S(1)}, f32[8,128]{1,0:T(8,128)S(1)}, u32[]{:S(2)}, u32[]{:S(2)}) %collective-permute-start.44) | collective-permute-done | bytes 4128 | tf_op jit(solution)/shard_map/ppermute | solution.py:50
  144.6 1.3 collective-permute-start.45
  146.1 2.1 %collective-permute-done.45.sq_got = f32[8,128]{1,0:T(8,128)S(1)} collective-permute-done((f32[8,128]{1,0:T(8,128)S(1)}, f32[8,128]{1,0:T(8,128)S(1)}, u32[]{:S(2)}, u32[]{:S(2)}) %collective-permute-start.45) | collective-permute-done | bytes 4128 | tf_op jit(solution)/shard_map/ppermute | solution.py:50
  148.4 1.5 shard_map.455
  (163 shorter events, 15.4 us)
Async XLA Ops:
  2.1 17.0 %collective-permute-start.6 = (bf16[512,512]{1,0:T(8,128)(2,1)S(1)}, bf16[512,512]{1,0:T(8,128)(2,1)S(1)}, u32[]{:S(2)}, u32[]{:S(2)}) collective-permute-start(bf16[512,512]{1,0:T(8,128)(2,1)S(1)} %convert_element_type.123.refs_0_), channel_id=1, source_target_pairs={{0,2},{1,3},{2,0},{3,1},{4,6},{5,7},{6,4},{7,5},{8,10},{9,11},{10,... | collective-permute-start | bytes 1572872 | tf_op jit(solution)/shard_map/ppermute | solution.py:50
  5.1 24.4 %collective-permute-start.5 = (bf16[512,512]{1,0:T(8,128)(2,1)S(1)}, bf16[512,512]{1,0:T(8,128)(2,1)S(1)}, u32[]{:S(2)}, u32[]{:S(2)}) collective-permute-start(bf16[512,512]{1,0:T(8,128)(2,1)S(1)} %convert_element_type.123.refs_0_), channel_id=1, source_target_pairs={{0,1},{1,0},{2,3},{3,2},{4,5},{5,4},{6,7},{7,6},{8,9},{9,8},{10,11... | collective-permute-start | bytes 1572872 | tf_op jit(solution)/shard_map/ppermute | solution.py:50
  5.3 6.8 %collective-permute-start = (bf16[1,80,384]{2,1,0:T(8,128)(2,1)S(1)}, bf16[1,80,384]{2,1,0:T(8,128)(2,1)S(1)}, u32[]{:S(2)}, u32[]{:S(2)}) collective-permute-start(bf16[1,80,384]{2,1,0:T(8,128)(2,1)S(1)} %fusion.5), channel_id=1, source_target_pairs={{0,16},{4,20},{8,24},{12,28},{16,0},{20,4},{24,8},{28,12},{1,17},{... | collective-permute-start | bytes 184328 | tf_op jit(solution)/shard_map/ppermute | solution.py:50
  8.0 10.4 %collective-permute-start.2 = (bf16[1,64,1152]{2,1,0:T(8,128)(2,1)S(1)}, bf16[1,64,1152]{2,1,0:T(8,128)(2,1)S(1)}, u32[]{:S(2)}, u32[]{:S(2)}) collective-permute-start(bf16[1,64,1152]{2,1,0:T(8,128)(2,1)S(1)} %maximum_bitcast_fusion), channel_id=1, source_target_pairs={{0,16},{4,20},{8,24},{12,28},{16,0},{20,4},{24,8},{28,12},{1,17},{... | collective-permute-start | bytes 442376 | tf_op jit(solution)/shard_map/ppermute | solution.py:50
  12.1 8.9 %collective-permute-start.1 = (bf16[2,80,384]{2,1,0:T(8,128)(2,1)S(1)}, bf16[2,80,384]{2,1,0:T(8,128)(2,1)S(1)}, u32[]{:S(2)}, u32[]{:S(2)}) collective-permute-start(bf16[2,80,384]{2,1,0:T(8,128)(2,1)S(1)} %pad_maximum_fusion.6), channel_id=1, source_target_pairs={{0,8},{4,12},{8,0},{12,4},{16,24},{20,28},{24,16},{28,20},{1,9},{5... | collective-permute-start | bytes 368648 | tf_op jit(solution)/shard_map/ppermute | solution.py:50
  18.4 8.8 %collective-permute-start.3 = (bf16[2,64,1152]{2,1,0:T(8,128)(2,1)S(1)}, bf16[2,64,1152]{2,1,0:T(8,128)(2,1)S(1)}, u32[]{:S(2)}, u32[]{:S(2)}) collective-permute-start(bf16[2,64,1152]{2,1,0:T(8,128)(2,1)S(1)} %pad_maximum_fusion.2), channel_id=1, source_target_pairs={{0,8},{4,12},{8,0},{12,4},{16,24},{20,28},{24,16},{28,20},{1,9},{5... | collective-permute-start | bytes 884744 | tf_op jit(solution)/shard_map/ppermute | solution.py:50
  19.1 10.4 %collective-permute-start.7 = (bf16[512,512]{1,0:T(8,128)(2,1)S(1)}, bf16[512,512]{1,0:T(8,128)(2,1)S(1)}, u32[]{:S(2)}, u32[]{:S(2)}) collective-permute-start(bf16[512,512]{1,0:T(8,128)(2,1)S(1)} %collective-permute-done.6.refs_2_), channel_id=1, source_target_pairs={{0,1},{1,0},{2,3},{3,2},{4,5},{5,4},{6,7},{7,6},{8,9},{9,8},{10,11... | collective-permute-start | bytes 1572872 | tf_op jit(solution)/shard_map/ppermute | solution.py:50
  21.0 8.5 %collective-permute-start.4 = (bf16[4,80,384]{2,1,0:T(8,128)(2,1)S(1)}, bf16[4,80,384]{2,1,0:T(8,128)(2,1)S(1)}, u32[]{:S(2)}, u32[]{:S(2)}) collective-permute-start(bf16[4,80,384]{2,1,0:T(8,128)(2,1)S(1)} %pad_maximum_fusion.5.w_own), channel_id=1, source_target_pairs={{0,4},{4,0},{8,12},{12,8},{16,20},{20,16},{24,28},{28,24},{1,5},{5... | collective-permute-start | bytes 737288 | tf_op jit(solution)/shard_map/ppermute | solution.py:50
  27.3 8.6 %collective-permute-start.9 = (bf16[4,64,640]{2,1,0:T(8,128)(2,1)S(1)}, bf16[4,64,640]{2,1,0:T(8,128)(2,1)S(1)}, u32[]{:S(2)}, u32[]{:S(2)}) collective-permute-start(bf16[4,64,640]{2,1,0:T(8,128)(2,1)S(1)} %pad_maximum_fusion.3), channel_id=1, source_target_pairs={{0,2},{1,3},{2,0},{3,1},{4,6},{5,7},{6,4},{7,5},{8,10},{9,11},{10,... | collective-permute-start | bytes 983048 | tf_op jit(solution)/shard_map/ppermute | solution.py:50
  27.9 8.1 %collective-permute-start.8 = (bf16[4,64,512]{2,1,0:T(8,128)(2,1)S(1)}, bf16[4,64,512]{2,1,0:T(8,128)(2,1)S(1)}, u32[]{:S(2)}, u32[]{:S(2)}) collective-permute-start(bf16[4,64,512]{2,1,0:T(8,128)(2,1)S(1)} %pad_maximum_fusion.4), channel_id=1, source_target_pairs={{0,4},{4,0},{8,12},{12,8},{16,20},{20,16},{24,28},{28,24},{1,5},{5... | collective-permute-start | bytes 786440 | tf_op jit(solution)/shard_map/ppermute | solution.py:50
  36.0 12.6 %collective-permute-start.11 = (bf16[8,64,640]{2,1,0:T(8,128)(2,1)S(1)}, bf16[8,64,640]{2,1,0:T(8,128)(2,1)S(1)}, u32[]{:S(2)}, u32[]{:S(2)}) collective-permute-start(bf16[8,64,640]{2,1,0:T(8,128)(2,1)S(1)} %pad_maximum_fusion.refs_8_), channel_id=1, source_target_pairs={{0,1},{1,0},{2,3},{3,2},{4,5},{5,4},{6,7},{7,6},{8,9},{9,8},{10,11... | collective-permute-start | bytes 1966088 | tf_op jit(solution)/shard_map/ppermute | solution.py:50
  36.2 11.5 %collective-permute-start.10 = (bf16[8,64,512]{2,1,0:T(8,128)(2,1)S(1)}, bf16[8,64,512]{2,1,0:T(8,128)(2,1)S(1)}, u32[]{:S(2)}, u32[]{:S(2)}) collective-permute-start(bf16[8,64,512]{2,1,0:T(8,128)(2,1)S(1)} %pad_maximum_fusion.1.refs_4_), channel_id=1, source_target_pairs={{0,1},{1,0},{2,3},{3,2},{4,5},{5,4},{6,7},{7,6},{8,9},{9,8},{10,11... | collective-permute-start | bytes 1572872 | tf_op jit(solution)/shard_map/ppermute | solution.py:50
  36.7 19.7 %collective-permute-start.17 = (bf16[8,64,640]{2,1,0:T(8,128)(2,1)S(1)}, bf16[8,64,640]{2,1,0:T(8,128)(2,1)S(1)}, u32[]{:S(2)}, u32[]{:S(2)}) collective-permute-start(bf16[8,64,640]{2,1,0:T(8,128)(2,1)S(1)} %pad_maximum_fusion.refs_8_), channel_id=1, source_target_pairs={{0,4},{4,0},{8,12},{12,8},{16,20},{20,16},{24,28},{28,24},{1,5},{5... | collective-permute-start | bytes 1966088 | tf_op jit(solution)/shard_map/ppermute | solution.py:50
  38.2 19.2 %collective-permute-start.15 = (bf16[8,64,512]{2,1,0:T(8,128)(2,1)S(1)}, bf16[8,64,512]{2,1,0:T(8,128)(2,1)S(1)}, u32[]{:S(2)}, u32[]{:S(2)}) collective-permute-start(bf16[8,64,512]{2,1,0:T(8,128)(2,1)S(1)} %pad_maximum_fusion.1.refs_4_), channel_id=1, source_target_pairs={{0,2},{1,3},{2,0},{3,1},{4,6},{5,7},{6,4},{7,5},{8,10},{9,11},{10,... | collective-permute-start | bytes 1572872 | tf_op jit(solution)/shard_map/ppermute | solution.py:50
  47.5 8.4 %collective-permute-start.13 = (bf16[528,128]{1,0:T(8,128)(2,1)S(1)}, bf16[528,128]{1,0:T(8,128)(2,1)S(1)}, u32[]{:S(2)}, u32[]{:S(2)}) collective-permute-start(bf16[528,128]{1,0:T(8,128)(2,1)S(1)} %get-tuple-element.126.refs_6_), channel_id=1, source_target_pairs={{0,2},{1,3},{2,0},{3,1},{4,6},{5,7},{6,4},{7,5},{8,10},{9,11},{10,... | collective-permute-start | bytes 405512 | tf_op jit(solution)/shard_map/ppermute | solution.py:706
  47.7 8.7 %collective-permute-start.14 = (bf16[528,128]{1,0:T(8,128)(2,1)S(1)}, bf16[528,128]{1,0:T(8,128)(2,1)S(1)}, u32[]{:S(2)}, u32[]{:S(2)}) collective-permute-start(bf16[528,128]{1,0:T(8,128)(2,1)S(1)} %get-tuple-element.130.refs_7_), channel_id=1, source_target_pairs={{0,3},{1,2},{2,1},{3,0},{4,7},{5,6},{6,5},{7,4},{8,11},{9,10},{10,... | collective-permute-start | bytes 405512 | tf_op jit(solution)/shard_map/ppermute | solution.py:706
  56.4 3.7 %collective-permute-start.18 = (bf16[8,64,640]{2,1,0:T(8,128)(2,1)S(1)}, bf16[8,64,640]{2,1,0:T(8,128)(2,1)S(1)}, u32[]{:S(2)}, u32[]{:S(2)}) collective-permute-start(bf16[8,64,640]{2,1,0:T(8,128)(2,1)S(1)} %collective-permute-done.17.refs_9_), channel_id=1, source_target_pairs={{0,1},{1,0},{2,3},{3,2},{4,5},{5,4},{6,7},{7,6},{8,9},{9,8},{10,11... | collective-permute-start | bytes 1966088 | tf_op jit(solution)/shard_map/ppermute | solution.py:50
  57.4 2.7 %collective-permute-start.16 = (bf16[8,64,512]{2,1,0:T(8,128)(2,1)S(1)}, bf16[8,64,512]{2,1,0:T(8,128)(2,1)S(1)}, u32[]{:S(2)}, u32[]{:S(2)}) collective-permute-start(bf16[8,64,512]{2,1,0:T(8,128)(2,1)S(1)} %collective-permute-done.15.refs_5_), channel_id=1, source_target_pairs={{0,1},{1,0},{2,3},{3,2},{4,5},{5,4},{6,7},{7,6},{8,9},{9,8},{10,11... | collective-permute-start | bytes 1572872 | tf_op jit(solution)/shard_map/ppermute | solution.py:50
  57.5 2.6 %collective-permute-start.12 = (bf16[528,128]{1,0:T(8,128)(2,1)S(1)}, bf16[528,128]{1,0:T(8,128)(2,1)S(1)}, u32[]{:S(2)}, u32[]{:S(2)}) collective-permute-start(bf16[528,128]{1,0:T(8,128)(2,1)S(1)} %get-tuple-element.129.refs_5_), channel_id=1, source_target_pairs={{0,1},{1,0},{2,3},{3,2},{4,5},{5,4},{6,7},{7,6},{8,9},{9,8},{10,11... | collective-permute-start | bytes 405512 | tf_op jit(solution)/shard_map/ppermute | solution.py:706
  75.5 2.7 %collective-permute-start.19 = (bf16[16,64,512]{2,1,0:T(8,128)(2,1)S(1)}, bf16[16,64,512]{2,1,0:T(8,128)(2,1)S(1)}, u32[]{:S(2)}, u32[]{:S(2)}) collective-permute-start(bf16[16,64,512]{2,1,0:T(8,128)(2,1)S(1)} %get-tuple-element.142), channel_id=1, source_target_pairs={{0,1},{1,0},{2,3},{3,2},{4,5},{5,4},{6,7},{7,6},{8,9},{9,8},{10,11... | collective-permute-start | bytes 3145736 | tf_op jit(solution)/shard_map/ppermute | solution.py:50
  75.9 4.2 %collective-permute-start.20 = (bf16[16,64,640]{2,1,0:T(8,128)(2,1)S(1)}, bf16[16,64,640]{2,1,0:T(8,128)(2,1)S(1)}, u32[]{:S(2)}, u32[]{:S(2)}) collective-permute-start(bf16[16,64,640]{2,1,0:T(8,128)(2,1)S(1)} %get-tuple-element.144), channel_id=1, source_target_pairs={{0,1},{1,0},{2,3},{3,2},{4,5},{5,4},{6,7},{7,6},{8,9},{9,8},{10,11... | collective-permute-start | bytes 3932168 | tf_op jit(solution)/shard_map/ppermute | solution.py:50
  76.0 5.7 %collective-permute-start.21 = (bf16[512,128]{1,0:T(8,128)(2,1)S(1)}, bf16[512,128]{1,0:T(8,128)(2,1)S(1)}, u32[]{:S(2)}, u32[]{:S(2)}) collective-permute-start(bf16[512,128]{1,0:T(8,128)(2,1)S(1)} %get-tuple-element.146), channel_id=1, source_target_pairs={{0,1},{1,0},{2,3},{3,2},{4,5},{5,4},{6,7},{7,6},{8,9},{9,8},{10,11... | collective-permute-start | bytes 393224 | tf_op jit(solution)/shard_map/ppermute | solution.py:751
  76.4 6.3 %collective-permute-start.22 = (bf16[512,128]{1,0:T(8,128)(2,1)S(1)}, bf16[512,128]{1,0:T(8,128)(2,1)S(1)}, u32[]{:S(2)}, u32[]{:S(2)}) collective-permute-start(bf16[512,128]{1,0:T(8,128)(2,1)S(1)} %get-tuple-element.147), channel_id=1, source_target_pairs={{0,2},{1,3},{2,0},{3,1},{4,6},{5,7},{6,4},{7,5},{8,10},{9,11},{10,... | collective-permute-start | bytes 393224 | tf_op jit(solution)/shard_map/ppermute | solution.py:751
  77.6 6.3 %collective-permute-start.23 = (bf16[512,128]{1,0:T(8,128)(2,1)S(1)}, bf16[512,128]{1,0:T(8,128)(2,1)S(1)}, u32[]{:S(2)}, u32[]{:S(2)}) collective-permute-start(bf16[512,128]{1,0:T(8,128)(2,1)S(1)} %get-tuple-element.148), channel_id=1, source_target_pairs={{0,3},{1,2},{2,1},{3,0},{4,7},{5,6},{6,5},{7,4},{8,11},{9,10},{10,... | collective-permute-start | bytes 393224 | tf_op jit(solution)/shard_map/ppermute | solution.py:751
  78.6 20.1 %collective-permute-start.25 = (bf16[8,64,512]{2,1,0:T(8,128)(2,1)S(1)}, bf16[8,64,512]{2,1,0:T(8,128)(2,1)S(1)}, u32[]{:S(2)}, u32[]{:S(2)}) collective-permute-start(bf16[8,64,512]{2,1,0:T(8,128)(2,1)S(1)} %slice.138), channel_id=1, source_target_pairs={{0,4},{4,0},{8,12},{12,8},{16,20},{20,16},{24,28},{28,24},{1,5},{5... | collective-permute-start | bytes 1572872 | tf_op jit(solution)/shard_map/ppermute | solution.py:50
  80.5 19.9 %collective-permute-start.26 = (bf16[8,64,640]{2,1,0:T(8,128)(2,1)S(1)}, bf16[8,64,640]{2,1,0:T(8,128)(2,1)S(1)}, u32[]{:S(2)}, u32[]{:S(2)}) collective-permute-start(bf16[8,64,640]{2,1,0:T(8,128)(2,1)S(1)} %slice.139), channel_id=1, source_target_pairs={{0,8},{4,12},{8,0},{12,4},{16,24},{20,28},{24,16},{28,20},{1,9},{5... | collective-permute-start | bytes 1966088 | tf_op jit(solution)/shard_map/ppermute | solution.py:50
  97.7 3.0 %collective-permute-start.24 = (f32[48,128]{1,0:T(8,128)S(1)}, f32[48,128]{1,0:T(8,128)S(1)}, u32[]{:S(2)}, u32[]{:S(2)}) collective-permute-start(f32[48,128]{1,0:T(8,128)S(1)} %get-tuple-element.150), channel_id=1, source_target_pairs={{0,1},{1,0},{2,3},{3,2},{4,5},{5,4},{6,7},{7,6},{8,9},{9,8},{10,11... | collective-permute-start | bytes 73736 | tf_op jit(solution)/shard_map/ppermute | solution.py:50
  98.9 8.3 %collective-permute-start.29 = (bf16[4,64,512]{2,1,0:T(8,128)(2,1)S(1)}, bf16[4,64,512]{2,1,0:T(8,128)(2,1)S(1)}, u32[]{:S(2)}, u32[]{:S(2)}) collective-permute-start(bf16[4,64,512]{2,1,0:T(8,128)(2,1)S(1)} %slice.141), channel_id=1, source_target_pairs={{0,2},{1,3},{2,0},{3,1},{4,6},{5,7},{6,4},{7,5},{8,10},{9,11},{10,... | collective-permute-start | bytes 786440 | tf_op jit(solution)/shard_map/ppermute | solution.py:50
  100.6 9.4 %collective-permute-start.28 = (bf16[4,64,640]{2,1,0:T(8,128)(2,1)S(1)}, bf16[4,64,640]{2,1,0:T(8,128)(2,1)S(1)}, u32[]{:S(2)}, u32[]{:S(2)}) collective-permute-start(bf16[4,64,640]{2,1,0:T(8,128)(2,1)S(1)} %slice.143), channel_id=1, source_target_pairs={{0,4},{4,0},{8,12},{12,8},{16,20},{20,16},{24,28},{28,24},{1,5},{5... | collective-permute-start | bytes 983048 | tf_op jit(solution)/shard_map/ppermute | solution.py:50
  104.5 6.3 %collective-permute-start.32 = (bf16[512,512]{1,0:T(8,128)(2,1)S(1)}, bf16[512,512]{1,0:T(8,128)(2,1)S(1)}, u32[]{:S(2)}, u32[]{:S(2)}) collective-permute-start(bf16[512,512]{1,0:T(8,128)(2,1)S(1)} %get-tuple-element.162), channel_id=1, source_target_pairs={{0,1},{1,0},{2,3},{3,2},{4,5},{5,4},{6,7},{7,6},{8,9},{9,8},{10,11... | collective-permute-start | bytes 1572872 | tf_op jit(solution)/shard_map/ppermute | solution.py:50
  104.6 5.6 %collective-permute-start.27 = (f32[48,128]{1,0:T(8,128)S(1)}, f32[48,128]{1,0:T(8,128)S(1)}, u32[]{:S(2)}, u32[]{:S(2)}) collective-permute-start(f32[48,128]{1,0:T(8,128)S(1)} %add.88), channel_id=1, source_target_pairs={{0,2},{1,3},{2,0},{3,1},{4,6},{5,7},{6,4},{7,5},{8,10},{9,11},{10,... | collective-permute-start | bytes 73736 | tf_op jit(solution)/shard_map/ppermute | solution.py:50
  105.7 7.7 %collective-permute-start.31 = (bf16[4,64,384]{2,1,0:T(8,128)(2,1)S(1)}, bf16[4,64,384]{2,1,0:T(8,128)(2,1)S(1)}, u32[]{:S(2)}, u32[]{:S(2)}) collective-permute-start(bf16[4,64,384]{2,1,0:T(8,128)(2,1)S(1)} %slice.144), channel_id=1, source_target_pairs={{0,8},{4,12},{8,0},{12,4},{16,24},{20,28},{24,16},{28,20},{1,9},{5... | collective-permute-start | bytes 589832 | tf_op jit(solution)/shard_map/ppermute | solution.py:50
  107.3 8.2 %collective-permute-start.35 = (bf16[2,64,512]{2,1,0:T(8,128)(2,1)S(1)}, bf16[2,64,512]{2,1,0:T(8,128)(2,1)S(1)}, u32[]{:S(2)}, u32[]{:S(2)}) collective-permute-start(bf16[2,64,512]{2,1,0:T(8,128)(2,1)S(1)} %slice.147), channel_id=1, source_target_pairs={{0,8},{4,12},{8,0},{12,4},{16,24},{20,28},{24,16},{28,20},{1,9},{5... | collective-permute-start | bytes 393224 | tf_op jit(solution)/shard_map/ppermute | solution.py:50
  110.0 13.4 %collective-permute-start.36 = (bf16[512,512]{1,0:T(8,128)(2,1)S(1)}, bf16[512,512]{1,0:T(8,128)(2,1)S(1)}, u32[]{:S(2)}, u32[]{:S(2)}) collective-permute-start(bf16[512,512]{1,0:T(8,128)(2,1)S(1)} %get-tuple-element.170), channel_id=1, source_target_pairs={{0,1},{1,0},{2,3},{3,2},{4,5},{5,4},{6,7},{7,6},{8,9},{9,8},{10,11... | collective-permute-start | bytes 1572872 | tf_op jit(solution)/shard_map/ppermute | solution.py:50
  110.2 7.1 %collective-permute-start.34 = (bf16[2,64,640]{2,1,0:T(8,128)(2,1)S(1)}, bf16[2,64,640]{2,1,0:T(8,128)(2,1)S(1)}, u32[]{:S(2)}, u32[]{:S(2)}) collective-permute-start(bf16[2,64,640]{2,1,0:T(8,128)(2,1)S(1)} %slice.148), channel_id=1, source_target_pairs={{0,2},{1,3},{2,0},{3,1},{4,6},{5,7},{6,4},{7,5},{8,10},{9,11},{10,... | collective-permute-start | bytes 491528 | tf_op jit(solution)/shard_map/ppermute | solution.py:50
  110.8 12.4 %collective-permute-start.30 = (f32[48,128]{1,0:T(8,128)S(1)}, f32[48,128]{1,0:T(8,128)S(1)}, u32[]{:S(2)}, u32[]{:S(2)}) collective-permute-start(f32[48,128]{1,0:T(8,128)S(1)} %add.91), channel_id=1, source_target_pairs={{0,4},{4,0},{8,12},{12,8},{16,20},{20,16},{24,28},{28,24},{1,5},{5... | collective-permute-start | bytes 73736 | tf_op jit(solution)/shard_map/ppermute | solution.py:50
  113.5 15.4 %collective-permute-start.37 = (bf16[512,512]{1,0:T(8,128)(2,1)S(1)}, bf16[512,512]{1,0:T(8,128)(2,1)S(1)}, u32[]{:S(2)}, u32[]{:S(2)}) collective-permute-start(bf16[512,512]{1,0:T(8,128)(2,1)S(1)} %add_convert_fusion.3), channel_id=1, source_target_pairs={{0,2},{1,3},{2,0},{3,1},{4,6},{5,7},{6,4},{7,5},{8,10},{9,11},{10,... | collective-permute-start | bytes 1572872 | tf_op jit(solution)/shard_map/ppermute | solution.py:50
  115.5 4.9 %collective-permute-start.33 = (bf16[2,64,384]{2,1,0:T(8,128)(2,1)S(1)}, bf16[2,64,384]{2,1,0:T(8,128)(2,1)S(1)}, u32[]{:S(2)}, u32[]{:S(2)}) collective-permute-start(bf16[2,64,384]{2,1,0:T(8,128)(2,1)S(1)} %slice.151), channel_id=1, source_target_pairs={{0,4},{4,0},{8,12},{12,8},{16,20},{20,16},{24,28},{28,24},{1,5},{5... | collective-permute-start | bytes 294920 | tf_op jit(solution)/shard_map/ppermute | solution.py:50
  117.2 7.7 %collective-permute-start.39 = (bf16[1,64,512]{2,1,0:T(8,128)(2,1)S(1)}, bf16[1,64,512]{2,1,0:T(8,128)(2,1)S(1)}, u32[]{:S(2)}, u32[]{:S(2)}) collective-permute-start(bf16[1,64,512]{2,1,0:T(8,128)(2,1)S(1)} %get-tuple-element.207), channel_id=1, source_target_pairs={{0,16},{4,20},{8,24},{12,28},{16,0},{20,4},{24,8},{28,12},{1,17},{... | collective-permute-start | bytes 196616 | tf_op jit(solution)/shard_map/ppermute | solution.py:50
  120.4 7.8 %collective-permute-start.40 = (bf16[1,64,640]{2,1,0:T(8,128)(2,1)S(1)}, bf16[1,64,640]{2,1,0:T(8,128)(2,1)S(1)}, u32[]{:S(2)}, u32[]{:S(2)}) collective-permute-start(bf16[1,64,640]{2,1,0:T(8,128)(2,1)S(1)} %get-tuple-element.205), channel_id=1, source_target_pairs={{0,16},{4,20},{8,24},{12,28},{16,0},{20,4},{24,8},{28,12},{1,17},{... | collective-permute-start | bytes 245768 | tf_op jit(solution)/shard_map/ppermute | solution.py:50
  123.2 5.5 %collective-permute-start.38 = (bf16[1,64,384]{2,1,0:T(8,128)(2,1)S(1)}, bf16[1,64,384]{2,1,0:T(8,128)(2,1)S(1)}, u32[]{:S(2)}, u32[]{:S(2)}) collective-permute-start(bf16[1,64,384]{2,1,0:T(8,128)(2,1)S(1)} %get-tuple-element.209), channel_id=1, source_target_pairs={{0,16},{4,20},{8,24},{12,28},{16,0},{20,4},{24,8},{28,12},{1,17},{... | collective-permute-start | bytes 147464 | tf_op jit(solution)/shard_map/ppermute | solution.py:50
  123.5 6.7 %collective-permute-start.46 = (f32[48,128]{1,0:T(8,128)S(1)}, f32[48,128]{1,0:T(8,128)S(1)}, u32[]{:S(2)}, u32[]{:S(2)}) collective-permute-start(f32[48,128]{1,0:T(8,128)S(1)} %add.97), channel_id=1, source_target_pairs={{0,8},{4,12},{8,0},{12,4},{16,24},{20,28},{24,16},{28,20},{1,9},{5... | collective-permute-start | bytes 73736 | tf_op jit(solution)/shard_map/ppermute | solution.py:50
  128.7 1.5 collective-permute-start.41
  130.2 15.7 %collective-permute-start.47 = (f32[48,128]{1,0:T(8,128)S(1)}, f32[48,128]{1,0:T(8,128)S(1)}, u32[]{:S(2)}, u32[]{:S(2)}) collective-permute-start(f32[48,128]{1,0:T(8,128)S(1)} %add.105), channel_id=1, source_target_pairs={{0,16},{4,20},{8,24},{12,28},{16,0},{20,4},{24,8},{28,12},{1,17},{... | collective-permute-start | bytes 73736 | tf_op jit(solution)/shard_map/ppermute | solution.py:50
  132.6 4.5 %collective-permute-start.42 = (f32[8,128]{1,0:T(8,128)S(1)}, f32[8,128]{1,0:T(8,128)S(1)}, u32[]{:S(2)}, u32[]{:S(2)}) collective-permute-start(f32[8,128]{1,0:T(8,128)S(1)} %add.101), channel_id=1, source_target_pairs={{0,16},{4,20},{8,24},{12,28},{16,0},{20,4},{24,8},{28,12},{1,17},{... | collective-permute-start | bytes 12296 | tf_op jit(solution)/shard_map/ppermute | solution.py:50
  137.1 3.9 %collective-permute-start.43 = (f32[8,128]{1,0:T(8,128)S(1)}, f32[8,128]{1,0:T(8,128)S(1)}, u32[]{:S(2)}, u32[]{:S(2)}) collective-permute-start(f32[8,128]{1,0:T(8,128)S(1)} %add.102), channel_id=1, source_target_pairs={{0,8},{4,12},{8,0},{12,4},{16,24},{20,28},{24,16},{28,20},{1,9},{5... | collective-permute-start | bytes 12296 | tf_op jit(solution)/shard_map/ppermute | solution.py:50
  141.0 3.6 %collective-permute-start.44 = (f32[8,128]{1,0:T(8,128)S(1)}, f32[8,128]{1,0:T(8,128)S(1)}, u32[]{:S(2)}, u32[]{:S(2)}) collective-permute-start(f32[8,128]{1,0:T(8,128)S(1)} %add.103), channel_id=1, source_target_pairs={{0,4},{4,0},{8,12},{12,8},{16,20},{20,16},{24,28},{28,24},{1,5},{5... | collective-permute-start | bytes 12296 | tf_op jit(solution)/shard_map/ppermute | solution.py:50
  144.6 3.6 %collective-permute-start.45 = (f32[8,128]{1,0:T(8,128)S(1)}, f32[8,128]{1,0:T(8,128)S(1)}, u32[]{:S(2)}, u32[]{:S(2)}) collective-permute-start(f32[8,128]{1,0:T(8,128)S(1)} %add.104.sq_ref), channel_id=1, source_target_pairs={{0,2},{1,3},{2,0},{3,1},{4,6},{5,7},{6,4},{7,5},{8,10},{9,11},{10,... | collective-permute-start | bytes 12296 | tf_op jit(solution)/shard_map/ppermute | solution.py:50
  (23 other events, 342.1 us)

commit v4 on v3

--- a/solution.py
+++ b/solution.py
@@ -12,8 +12,6 @@
 HD = 64
 TQ = 256
 TK = 256
-SEQ_MOST = 1024
-KEY_BLOCKS = SEQ_MOST // TK + 1
 CH = 64
 
 EPS_NORM = 1e-05
@@ -87,24 +85,23 @@
         return total[:half].astype(BF), total[half:].astype(BF)
 
 
-class Total:
-    def __init__(self, value, steps):
-        self.value, self.steps = value, list(steps)
-        self.got = swap(value, self.steps[-1])
-
-    def advance(self, *ready):
-        if not self.steps:
-            return ()
-        self.steps.pop()
-        self.value = self.value + after(self.got, *ready)
-        if self.steps:
-            self.got = swap(self.value, self.steps[-1])
-        return (self.value,)
-
-    def result(self):
-        while self.steps:
-            self.advance(self.value)
-        return self.value
+def swap_both(v, one, two):
+    n_h = lax.axis_size("head")
+    flip = sum(bit * (n_h if axis == "dp" else 1) for axis, bit in (one, two))
+    return lax.ppermute(v, ("dp", "head"), [(i, i ^ flip) for i in range(n_h * lax.axis_size("dp"))])
+
+
+def sum_groups(value, groups, ready):
+    for i, group in enumerate(groups):
+        got = [value] + [swap(value, step) for step in group]
+        if len(group) == 2:
+            got.append(swap_both(value, *group))
+        if i == len(groups) - 1:
+            return got
+        if i == 1:
+            got[1] = after(got[1], *ready)
+        pairs = [a + b for a, b in zip(got[::2], got[1::2])]
+        value = functools.reduce(lambda a, b: a + b, pairs)
 
 
 class RowSums:
@@ -197,54 +194,70 @@
 
 def attend_kernel(lh, offs, idx_ref, seg_ref, q_ref, k_ref, vt_ref, inner_ref, *refs):
     pieces = refs[: len(offs)]
-    lse_ref, s_s, acc_s, start_s = refs[len(offs) :]
+    lse_ref, qb_s, lo_s, all_s, start_s, q2_s, acc_s, top_s, slot_a, slot_b = refs[len(offs) :]
     h = idx_ref[1]
     width = lh * HD
     rw = pieces[0].shape[0] - 16
-    start_s[...] = document_starts(seg_ref[...])
+    per_piece = rw // TQ
+    n_t = len(offs) * per_piece
     factor = SCORE_SCALE * LOG2E
     cols = lh * TQ
-
-    def query_block(piece_ref, place_at, base, i, carry):
-        inside = pl.multiple_of(i * TQ, TQ)
-        r0 = pl.multiple_of(base + inside, TQ)
-        qb = r0 // TQ
-        q2 = lane_mask_stack(q_ref[pl.ds(r0, TQ), :], lh)
-        start = start_s[:, pl.ds(r0, TQ)]
+    column = lax.broadcasted_iota(jnp.int32, (1, cols), 1) % TQ
+    all_s[...] = document_starts(seg_ref[...])
+    n_pairs = 0
+    for t in range(n_t):
+        qb = (h ^ offs[t // per_piece]) * per_piece + t % per_piece
+        at = pl.ds(pl.multiple_of(qb * TQ, TQ), TQ)
+        start = all_s[:, at]
         lo = (jnp.min(start) * (1.0 / TK)).astype(jnp.int32)
-        start = jnp.concatenate([start.astype(jnp.int32)] * lh, axis=1)
-        column = lax.broadcasted_iota(jnp.int32, (1, cols), 1) % TQ
-
-        def scores(kb, top):
-            c0 = pl.multiple_of(kb * TK, TK)
-            s = dot(k_ref[pl.ds(c0, TK), :], q2, 1, 1)
-            key = lax.broadcasted_iota(jnp.int32, (TK, cols), 0)
-            ok = (key >= start - c0) & (key <= column + (r0 - c0))
-            s = jnp.where(ok, s, NEG_LARGE)
-            s_s[kb - lo] = s
-            return jnp.maximum(top, jnp.max(s.reshape(TK // 8, 8, cols), axis=0))
-
-        top = lax.fori_loop(lo, qb + 1, scores, jnp.full((8, cols), NEG_LARGE, F32))
-        top = jnp.max(top, axis=0, keepdims=True)
-        acc_s[...] = jnp.zeros_like(acc_s)
-
-        def mix(kb, carry):
-            c0 = pl.multiple_of(kb * TK, TK)
-            p = jnp.exp2((s_s[kb - lo] - top) * factor).astype(BF)
-            acc_s[...] += dot(vt_ref[:, pl.ds(c0, TK)], p, 1, 0)
-            return carry
-
-        lax.fori_loop(lo, qb + 1, mix, 0)
-        total = acc_s[width : width + 1, :]
-        out_t = head_rows_merge(acc_s[:width, :] / total, lh)
-        piece_ref[pl.ds(inside, TQ), :] = out_t.T.astype(BF)
-        lse_ref[place_at + i] = jnp.broadcast_to(top * factor + jnp.log2(total), (8, cols))
-        return carry
-
-    for n, off in enumerate(offs):
-        body = functools.partial(query_block, pieces[n], n * (rw // TQ), (h ^ off) * rw)
-        lax.fori_loop(0, rw // TQ, body, 0)
-        pieces[n][rw:, :] = inner_ref[...]
+        qb_s[t] = qb * (TQ // TK) + (TQ // TK - 1)
+        lo_s[t] = lo
+        n_pairs = n_pairs + qb_s[t] + 1 - lo
+        start_s[t] = jnp.concatenate([start.astype(jnp.int32)] * lh, axis=1)
+        q2_s[t] = lane_mask_stack(q_ref[at, :], lh)
+    acc_s[...] = jnp.zeros_like(acc_s)
+    top_s[...] = jnp.full(top_s.shape, NEG_LARGE, F32)
+
+    def scores(t, kb, slot):
+        keys = pl.ds(pl.multiple_of(kb * TK, TK), TK)
+        slot[...] = dot(k_ref[keys, :], q2_s[t], 1, 1)
+
+    def mix(t, kb, slot, least):
+        c0 = pl.multiple_of(kb * TK, TK)
+        key = lax.broadcasted_iota(jnp.int32, (TK, cols), 0)
+        first = (qb_s[t] + 1) * TK - TQ
+        ok = (key >= start_s[t] - c0 + least) & (key <= column + (first - c0))
+        s = jnp.where(ok, slot[...], NEG_LARGE)
+        old = top_s[t]
+        top = jnp.maximum(old, jnp.max(s, axis=0, keepdims=True))
+        p = jnp.exp2((s - top) * factor).astype(BF)
+        acc_s[t] = acc_s[t] * jnp.exp2((old - top) * factor) + dot(vt_ref[:, pl.ds(c0, TK)], p, 1, 0)
+        top_s[t] = top
+
+    def following(t, kb):
+        done = kb >= qb_s[t]
+        nt = jnp.minimum(t + 1, n_t - 1)
+        return jnp.where(done, nt, t), jnp.where(done, lo_s[nt], kb + 1)
+
+    def two_pairs(i, carry):
+        one = following(*carry)
+        scores(*one, slot_b)
+        mix(*carry, slot_a, 0)
+        two = following(*one)
+        scores(*two, slot_a)
+        mix(*one, slot_b, jnp.where(2 * i + 1 < n_pairs, 0, 4 * q_ref.shape[0]))
+        return two
+
+    scores(0, lo_s[0], slot_a)
+    lax.fori_loop(0, (n_pairs + 1) // 2, two_pairs, (jnp.int32(0), lo_s[0]))
+    for t in range(n_t):
+        total = acc_s[t, width : width + 1, :]
+        out_t = head_rows_merge(acc_s[t, :width, :] / total, lh)
+        inside = (t % per_piece) * TQ
+        pieces[t // per_piece][inside : inside + TQ, :] = out_t.T.astype(BF)
+        lse_ref[t] = jnp.broadcast_to(top_s[t] * factor + jnp.log2(total), (8, cols))
+    for piece in pieces:
+        piece[rw:, :] = inner_ref[...]
 
 
 def document_starts(segment):
@@ -397,12 +410,12 @@
     for qb in range(start.shape[1] // TQ):
         lo = (jnp.min(start[:, qb * TQ : (qb + 1) * TQ]) * (1.0 / TK)).astype(jnp.int32)
         lo_ref[qb] = lo
-        total = total + (qb + 1 - lo)
+        total = total + ((qb + 1) * (TQ // TK) - lo)
     return total
 
 
 def next_pair(qb, kb, lo_ref, last):
-    done = kb >= qb
+    done = kb >= (qb + 1) * (TQ // TK) - 1
     following = jnp.minimum(qb + 1, last)
     return jnp.where(done, following, qb), jnp.where(done, lo_ref[following], kb + 1)
 
@@ -521,7 +534,7 @@
     return keep_ref[0].astype(F32) + got_ref[0].astype(F32)
 
 
-def squares_kernel(*refs):
+def squares_kernel(small_ref, *refs):
     out_ref = refs[-1]
     acc = jnp.zeros((8, 128), F32)
     for i in range(0, len(refs) - 1, 2):
@@ -531,18 +544,42 @@
             v = jnp.concatenate([v, jnp.zeros((8, 128 - v.shape[1] % 128), F32)], axis=1)
         for j in range(v.shape[1] // 128):
             acc = acc + v[:, j * 128 : (j + 1) * 128]
-    out_ref[...] = acc
-
-
-def adam_kernel(units, clip_ref, sq_ref, sq_got, small_ref, *refs):
-    share_bias, norm_grads = refs[6:8]
-    params, momenta, variances = refs[8:14], refs[14:20], refs[20:26]
-    norm_ref, clipped_ref = refs[26:28]
-    outs = list(refs[28:])
-    small = small_ref[...]
-    squares = jnp.sum(sq_ref[...] + sq_got[...]) + jnp.sum(small * small)
+    out_ref[:8, :] = acc
+    out_ref[8:, :] = small_ref[...]
+
+
+def adam_kernel(units, n_dp, lh, n_sums, idx_ref, clip_ref, *refs):
+    sums, refs = [r[...] for r in refs[:n_sums]], refs[n_sums:]
+    sums = [a + b for a, b in zip(sums[::2], sums[1::2])]
+    sums = functools.reduce(lambda a, b: a + b, sums)
+    params, momenta, variances = refs[6:12], refs[12:18], refs[18:24]
+    norm_ref, clipped_ref = refs[24:26]
+    outs, small_s = list(refs[26:-1]), refs[-1]
+    g, h = idx_ref[0], idx_ref[1]
+    small = sums[8:, :]
+    small_s[...] = small
+    squares = jnp.sum(sums[:8, :]) + jnp.sum(small * small)
+    norm_grads = jnp.concatenate(
+        [
+            jnp.concatenate([small[4 * i + j : 4 * i + j + 1, :] for j in range(D // 128)], axis=1)
+            for i in range(6)
+        ],
+        axis=0,
+    )
+    width = params[4].shape[1]
+    bias_rows = []
+    for l in range(lh):
+        head = h * lh + l
+        full = jnp.concatenate(
+            [small_s[pl.ds(at, 1), :] for at in (40 + head, 24 + 2 * head, 25 + 2 * head)], axis=1
+        )
+        share = jnp.zeros((1, width), F32)
+        for b in range(n_dp):
+            share = share + jnp.where(g == b, full[:, b * width : (b + 1) * width], 0.0)
+        bias_rows.append(share)
+    share_bias = jnp.concatenate(bias_rows, axis=0)
     norm = jnp.sqrt(jnp.full((8, 128), squares))
-    norm_ref[...] = norm
+    norm_ref[0] = jnp.max(norm)
     limit = clip_ref[0]
     factor = (limit / jnp.maximum(norm, limit))[:1, :1]
     shares = total_of_pair(refs[4], refs[5])
@@ -551,8 +588,8 @@
         shares[:, units:],
         total_of_pair(refs[2], refs[3]),
         shares[:, :units],
-        share_bias[...],
-        norm_grads[...],
+        share_bias,
+        norm_grads,
     )
     for w, m, va, grad, rate in zip(params, momenta, variances, grads, RATES):
         clipped = factor * grad
@@ -565,7 +602,7 @@
         outs.pop(0)[...] = master_new
         if len(outs) > 2:
             outs.pop(0)[...] = master_new.astype(BF)
-    clipped_ref[...] = factor * norm_grads[...]
+    clipped_ref[...] = factor * norm_grads
 
 
 def call(body, outs, scratch, n_smem, args, limit, us):
@@ -573,7 +610,7 @@
         body,
         out_shape=outs,
         in_specs=[SMEM] * n_smem + [VMEM] * (len(args) - n_smem),
-        out_specs=jax.tree.map(lambda _: VMEM, outs),
+        out_specs=jax.tree.map(lambda o: SMEM if o.shape == (1,) else VMEM, outs),
         scratch_shapes=scratch,
         compiler_params=pltpu.CompilerParams(vmem_limit_bytes=limit << 20),
         cost_estimate=pl.CostEstimate(flops=us * FLOPS_PER_US, bytes_accessed=1 << 20, transcendentals=0),
@@ -683,9 +720,15 @@
             functools.partial(attend_kernel, lh, offs),
             [sds((rw + 16, width), BF)] * len(offs) + [sds((n_q // 2, 8, cols), F32)],
             [
-                pltpu.VMEM((KEY_BLOCKS, TK, cols), F32),
-                pltpu.VMEM((width + 16, cols), F32),
+                pltpu.SMEM((n_q // 2,), jnp.int32),
+                pltpu.SMEM((n_q // 2,), jnp.int32),
                 pltpu.VMEM((1, n_rows), F32),
+                pltpu.VMEM((n_q // 2, 1, cols), jnp.int32),
+                pltpu.VMEM((n_q // 2, cols, width), BF),
+                pltpu.VMEM((n_q // 2, width + 16, cols), F32),
+                pltpu.VMEM((n_q // 2, 1, cols), F32),
+                pltpu.VMEM((TK, cols), F32),
+                pltpu.VMEM((TK, cols), F32),
             ],
             1,
             [idx, segment_ids, q, k, vt, inner],
@@ -774,8 +817,6 @@
         15,
     )
     sent = ge.advance(gqkv) + gc.advance(gqkv)
-    total = Total(small, dp_steps + h_steps)
-    sent = total.advance(*sent)
     ga = call(
         functools.partial(attend_grad_kernel, lh, n_dp, n_h, g_steps),
         sds((n_dp, ds_rows, a_cols), BF),
@@ -801,29 +842,16 @@
         sent = ge.advance(*sent)
         sent = gc.advance(*sent)
         if i == 0:
-            sent = total.advance(*sent)
             for _ in range(len(h_bits) - 1):
                 sent = back.advance(*sent)
         if i < n_d - 1:
             sent = ga.advance(*sent)
-    sent = total.advance(*sent)
     post_grad = back.finish(grad_mid1, *sent)
-    sent = (post_grad,)
     pairs = [ga.keep, ga.got, ge.keep, ge.got, gc.keep, gc.got]
-    squares = call(squares_kernel, sds((8, 128), F32), [], 0, pairs, 16, 1)
-    squares = Total(squares, h_steps[:-1] + dp_steps[::-1] + h_steps[-1:])
-    for _ in e_steps[:-1]:
-        total.advance(*squares.advance(*sent))
-    small = total.result()
-    norm_grads = small[:24].reshape(6, D)
-    bias_full = jnp.concatenate(
-        [
-            lax.dynamic_slice_in_dim(small, 40 + h * lh, lh, 0),
-            lax.dynamic_slice_in_dim(small, 24 + h * 2 * lh, 2 * lh, 0).reshape(lh, 256),
-        ],
-        axis=1,
-    )
-    share_bias = lax.dynamic_slice_in_dim(bias_full, g * shares, shares, 1)
+    squares = call(squares_kernel, sds((56, 128), F32), [], 0, [small] + pairs, 16, 1)
+    order = h_steps[-1:] + [step for step in h_steps[:-1] + dp_steps[::-1]]
+    groups = [order[:1]] + [order[i : i + 2] for i in range(1, len(order), 2)]
+    sums = sum_groups(squares, groups, (post_grad,))
     flip = lambda arrays: [a.T if i in (1, 3) else a for i, a in enumerate(arrays)]
     params = flip([attend_weight, output_weight, expand_weight, contract_weight, head_bias, norm_params])
     momenta = flip(
@@ -832,20 +860,20 @@
     variances = flip(
         [attend_variance, output_variance, expand_variance, contract_variance, bias_variance, norm_variance]
     )
-    shapes = [sds((8, 128), F32), sds((6, D), F32)]
+    shapes = [sds((1,), F32), sds((6, D), F32)]
     for i, w in enumerate(params):
         shapes += [sds(w.shape, F32)] * 3 + ([sds(w.shape, BF)] if i < 5 else [])
     norm, norm_clipped, *results = call(
-        functools.partial(adam_kernel, units),
+        functools.partial(adam_kernel, units, n_dp, lh, len(sums)),
         shapes,
-        [],
-        1,
-        [clip_limit, squares.value, squares.got, small] + pairs + [share_bias, norm_grads] + params + momenta + variances,
+        [pltpu.VMEM((48, 128), F32)],
+        2,
+        [idx, clip_limit] + sums + pairs + params + momenta + variances,
         24,
         2,
     )
     results = [a.T if i // 4 in (1, 3) else a for i, a in enumerate(results)]
-    return (post_out, dual_out, post_grad, norm[0, :1], *results, norm_clipped)
+    return (post_out, dual_out, post_grad, norm, *results, norm_clipped)
 
 
 def solution(mesh):

time: 150 us -> 147 us (0.980)
  Pallas kernels: 50.5 us -> 48 us
  starting transfers between devices: 47.5 us -> 45.1 us
  waiting for transfers between devices: 44.5 us -> 46 us
    ppermute x42 -> x37, waiting for transfers between devices: 37.5 us -> 29 us  [swap(): return lax.ppermute(v, axis, [(i, i ^ bit) for i in range(count)])]
    ppermute x0 -> x2, waiting for transfers between devices: none -> 6.72 us  [swap_both(): lax.ppermute(v, ('dp', 'head'), [(i, i ^ flip) for i in range(n_h * lax.a...]
    ppermute x3, waiting for transfers between devices: 4.75 us -> 8.08 us  [per_device(): lax.ppermute(pieces[off], 'head', [(i, i ^ off) for i in range(n_h)])]
    ppermute x42 -> x37, starting transfers between devices: 44.2 us -> 41.1 us  [swap(): return lax.ppermute(v, axis, [(i, i ^ bit) for i in range(count)])]
    pallas_call x9, Pallas kernels: 50.5 us -> 48 us  [call(): pl.pallas_call(body, out_shape=outs, in_specs=[SMEM] * n_smem + [VMEM] *...]
  transfers between devices with their start and end apart: 48 -> 45, of which waited for: 23 -> 23; matrix products, arithmetic and copies ran while one was open for 2% -> 2% of each run, Pallas kernels for 22% -> 21%
where the time goes in v4:
time: 147 us; the launch traced here: 146 us
  Pallas kernels  48 us (33%)
  waiting for transfers between devices  46 us (31%)
  starting transfers between devices  45.1 us (31%)
  other arithmetic  4.62 us (3%)
  between operations  2.18 us (1%)
    pallas_call x9, Pallas kernels, call(): pl.pallas_call(body, out_shape=outs, in_specs=[SMEM] * n_smem + [VMEM] *...  48 us
    ppermute x37, starting transfers between devices, swap(): return lax.ppermute(v, axis, [(i, i ^ bit) for i in range(count)])  41.1 us
    ppermute x37, waiting for transfers between devices, swap(): return lax.ppermute(v, axis, [(i, i ^ bit) for i in range(count)])  29 us
    ppermute x3, waiting for transfers between devices, per_device(): lax.ppermute(pieces[off], 'head', [(i, i ^ off) for i in range(n_h)])  8.08 us
    ppermute x2, waiting for transfers between devices, swap_both(): lax.ppermute(v, ('dp', 'head'), [(i, i ^ flip) for i in range(n_h * lax.a...  6.72 us
  transfers between devices with their start and end apart: 45, of which 23 were waited for; matrix products, arithmetic and copies ran while one was open for 2% of the time, Pallas kernels for 21%

profile of v4, /device:TPU:0, one launch (start us, length us, event | category | flops | bytes accessed | tf_op | source)
XLA Modules:
  0.0 146.4 jit_solution(15681948433767249619)
XLA Ops:
  0.7 1.4 convert_element_type.123.refs_0_
  2.1 3.0 %collective-permute-start.6 = (bf16[512,512]{1,0:T(8,128)(2,1)S(1)}, bf16[512,512]{1,0:T(8,128)(2,1)S(1)}, u32[]{:S(2)}, u32[]{:S(2)}) collective-permute-start(bf16[512,512]{1,0:T(8,128)(2,1)S(1)} %convert_element_type.123.refs_0_), channel_id=1, source_target_pairs={{0,2},{1,3},{2,0},{3,1},{4,6},{5,7},{6,4},{7,5},{8,10},{9,11},{10,... | collective-permute-start | bytes 1572872 | tf_op jit(solution)/shard_map/ppermute | solution.py:48
  5.3 2.7 %collective-permute-start = (bf16[1,80,384]{2,1,0:T(8,128)(2,1)S(1)}, bf16[1,80,384]{2,1,0:T(8,128)(2,1)S(1)}, u32[]{:S(2)}, u32[]{:S(2)}) collective-permute-start(bf16[1,80,384]{2,1,0:T(8,128)(2,1)S(1)} %fusion.4), channel_id=1, source_target_pairs={{0,16},{4,20},{8,24},{12,28},{16,0},{20,4},{24,8},{28,12},{1,17},{... | collective-permute-start | bytes 184328 | tf_op jit(solution)/shard_map/ppermute | solution.py:48
  8.5 3.6 %collective-permute-done = bf16[1,80,384]{2,1,0:T(8,128)(2,1)S(1)} collective-permute-done((bf16[1,80,384]{2,1,0:T(8,128)(2,1)S(1)}, bf16[1,80,384]{2,1,0:T(8,128)(2,1)S(1)}, u32[]{:S(2)}, u32[]{:S(2)}) %collective-permute-start) | collective-permute-done | bytes 61472 | tf_op jit(solution)/shard_map/ppermute | solution.py:48
  12.1 3.8 %collective-permute-start.1 = (bf16[2,80,384]{2,1,0:T(8,128)(2,1)S(1)}, bf16[2,80,384]{2,1,0:T(8,128)(2,1)S(1)}, u32[]{:S(2)}, u32[]{:S(2)}) collective-permute-start(bf16[2,80,384]{2,1,0:T(8,128)(2,1)S(1)} %pad_maximum_fusion.6), channel_id=1, source_target_pairs={{0,8},{4,12},{8,0},{12,4},{16,24},{20,28},{24,16},{28,20},{1,9},{5... | collective-permute-start | bytes 368648 | tf_op jit(solution)/shard_map/ppermute | solution.py:48
  15.9 2.5 %collective-permute-done.2 = bf16[1,64,1152]{2,1,0:T(8,128)(2,1)S(1)} collective-permute-done((bf16[1,64,1152]{2,1,0:T(8,128)(2,1)S(1)}, bf16[1,64,1152]{2,1,0:T(8,128)(2,1)S(1)}, u32[]{:S(2)}, u32[]{:S(2)}) %collective-permute-start.2) | collective-permute-done | bytes 147488 | tf_op jit(solution)/shard_map/ppermute | solution.py:48
  19.1 1.9 %collective-permute-done.1 = bf16[2,80,384]{2,1,0:T(8,128)(2,1)S(1)} collective-permute-done((bf16[2,80,384]{2,1,0:T(8,128)(2,1)S(1)}, bf16[2,80,384]{2,1,0:T(8,128)(2,1)S(1)}, u32[]{:S(2)}, u32[]{:S(2)}) %collective-permute-start.1) | collective-permute-done | bytes 122912 | tf_op jit(solution)/shard_map/ppermute | solution.py:48
  21.0 1.6 %collective-permute-start.4 = (bf16[4,80,384]{2,1,0:T(8,128)(2,1)S(1)}, bf16[4,80,384]{2,1,0:T(8,128)(2,1)S(1)}, u32[]{:S(2)}, u32[]{:S(2)}) collective-permute-start(bf16[4,80,384]{2,1,0:T(8,128)(2,1)S(1)} %pad_maximum_fusion.5.w_own), channel_id=1, source_target_pairs={{0,4},{4,0},{8,12},{12,8},{16,20},{20,16},{24,28},{28,24},{1,5},{5... | collective-permute-start | bytes 737288 | tf_op jit(solution)/shard_map/ppermute | solution.py:48
  22.6 4.7 %collective-permute-done.3 = bf16[2,64,1152]{2,1,0:T(8,128)(2,1)S(1)} collective-permute-done((bf16[2,64,1152]{2,1,0:T(8,128)(2,1)S(1)}, bf16[2,64,1152]{2,1,0:T(8,128)(2,1)S(1)}, u32[]{:S(2)}, u32[]{:S(2)}) %collective-permute-start.3) | collective-permute-done | bytes 294944 | tf_op jit(solution)/shard_map/ppermute | solution.py:48
  27.9 1.6 %collective-permute-start.8 = (bf16[4,64,512]{2,1,0:T(8,128)(2,1)S(1)}, bf16[4,64,512]{2,1,0:T(8,128)(2,1)S(1)}, u32[]{:S(2)}, u32[]{:S(2)}) collective-permute-start(bf16[4,64,512]{2,1,0:T(8,128)(2,1)S(1)} %pad_maximum_fusion.4), channel_id=1, source_target_pairs={{0,4},{4,0},{8,12},{12,8},{16,20},{20,16},{24,28},{28,24},{1,5},{5... | collective-permute-start | bytes 786440 | tf_op jit(solution)/shard_map/ppermute | solution.py:48
  29.5 2.0 %shard_map.447 = (bf16[2048,128]{1,0:T(8,128)(2,1)S(1)}, bf16[2048,128]{1,0:T(8,128)(2,1)S(1)}, bf16[2048,128]{1,0:T(8,128)(2,1)S(1)}, bf16[144,2048]{1,0:T(8,12...) custom-call(s32[2]{0:T(128)S(1)} %pad_add_fusion.idx_ref, ...), custom_call_target="tpu_custom_call" | custom-call | flops 4000000000 | bytes 1048576 | tf_op jit(solution)/shard_map/pallas_call | solution.py:609
  31.6 4.4 %collective-permute-done.9 = bf16[4,64,640]{2,1,0:T(8,128)(2,1)S(1)} collective-permute-done((bf16[4,64,640]{2,1,0:T(8,128)(2,1)S(1)}, bf16[4,64,640]{2,1,0:T(8,128)(2,1)S(1)}, u32[]{:S(2)}, u32[]{:S(2)}) %collective-permute-start.9) | collective-permute-done | bytes 327712 | tf_op jit(solution)/shard_map/ppermute | solution.py:48
  36.7 1.5 %collective-permute-start.17 = (bf16[8,64,640]{2,1,0:T(8,128)(2,1)S(1)}, bf16[8,64,640]{2,1,0:T(8,128)(2,1)S(1)}, u32[]{:S(2)}, u32[]{:S(2)}) collective-permute-start(bf16[8,64,640]{2,1,0:T(8,128)(2,1)S(1)} %pad_maximum_fusion.refs_8_), channel_id=1, source_target_pairs={{0,4},{4,0},{8,12},{12,8},{16,20},{20,16},{24,28},{28,24},{1,5},{5... | collective-permute-start | bytes 1966088 | tf_op jit(solution)/shard_map/ppermute | solution.py:48
  38.7 6.4 %shard_map.448 = (bf16[528,128]{1,0:T(8,128)(2,1)S(1)}, bf16[528,128]{1,0:T(8,128)(2,1)S(1)}, f32[4,8,512]{2,1,0:T(8,128)S(1)}) custom-call(s32[2]{0:T(128)S(1)} %pad_add_fusion.idx_ref, s32[1,2048]{1,0:T(1,128)S(1)} %copy-done.19, bf16[2048,128]{1,0:T(8,128)(2,1)S(1)} %get-tuple-element.119.q_ref, bf16[2048,128]{1,0:T(8,128)(2,1)S(1)} %get-tuple-element.115.k_ref, ...), custom_call_target="tpu_custom_call" | custom-call | flops 1000000000 | bytes 1048576 | tf_op jit(solution)/shard_map/pallas_call | solution.py:609
  45.3 0.9 collective-permute-start.14
  46.1 4.3 %shard_map.449 = (bf16[528,128]{1,0:T(8,128)(2,1)S(1)}, bf16[528,128]{1,0:T(8,128)(2,1)S(1)}, f32[4,8,512]{2,1,0:T(8,128)S(1)}) custom-call(s32[2]{0:T(128)S(1)} %pad_add_fusion.idx_ref, s32[1,2048]{1,0:T(1,128)S(1)} %copy-done.19, bf16[2048,128]{1,0:T(8,128)(2,1)S(1)} %get-tuple-element.119.q_ref, bf16[2048,128]{1,0:T(8,128)(2,1)S(1)} %get-tuple-element.115.k_ref, ...), custom_call_target="tpu_custom_call" | custom-call | flops 1000000000 | bytes 1048576 | tf_op jit(solution)/shard_map/pallas_call | solution.py:609
  50.5 5.4 %collective-permute-done.13.refs_2_ = bf16[528,128]{1,0:T(8,128)(2,1)S(1)} collective-permute-done((bf16[528,128]{1,0:T(8,128)(2,1)S(1)}, bf16[528,128]{1,0:T(8,128)(2,1)S(1)}, u32[]{:S(2)}, u32[]{:S(2)}) %collective-permute-start.13) | collective-permute-done | bytes 135200 | tf_op jit(solution)/shard_map/ppermute | solution.py:749
  56.4 1.0 collective-permute-start.18
  58.0 2.2 %collective-permute-done.12.refs_1_ = bf16[528,128]{1,0:T(8,128)(2,1)S(1)} collective-permute-done((bf16[528,128]{1,0:T(8,128)(2,1)S(1)}, bf16[528,128]{1,0:T(8,128)(2,1)S(1)}, u32[]{:S(2)}, u32[]{:S(2)}) %collective-permute-start.12) | collective-permute-done | bytes 135200 | tf_op jit(solution)/shard_map/ppermute | solution.py:749
  60.2 15.3 %shard_map.450 = (f32[512,512]{1,0:T(8,128)}, f32[512,512]{1,0:T(8,128)}, f32[512,512]{1,0:T(8,128)S(1)}, bf16[512,128]{1,0:T(8,128)(2,1)S(1)}, bf16[512,128]{1,...) custom-call(s32[2]{0:T(128)S(1)} %pad_add_fusion.idx_ref, ...), custom_call_target="tpu_custom_call" | custom-call | flops 20000000000 | bytes 1048576 | tf_op jit(solution)/shard_map/pallas_call | solution.py:609
  76.9 1.0 collective-permute-start.23
  79.2 0.9 collective-permute-done.20
  80.5 1.2 collective-permute-start.25
  81.7 1.1 collective-permute-done.22.refs_2_
  82.8 1.2 collective-permute-done.23.refs_3_
  83.9 14.0 %shard_map.451 = (bf16[2048,384]{1,0:T(8,128)(2,1)S(1)}, f32[48,128]{1,0:T(8,128)S(1)}) custom-call(s32[2]{0:T(128)S(1)} %pad_add_fusion.idx_ref, s32[1,2048]{1,0:T(1,128)S(1)} %copy-done.19, bf16[2048,128]{1,0:T(8,128)(2,1)S(1)} %get-tuple-element.119.q_ref, bf16[2048,128]{1,0:T(8,128)(2,1)S(1)} %get-tuple-element.115.k_ref, ...), custom_call_target="tpu_custom_call" | custom-call | flops 15000000512 | bytes 1048576 | tf_op jit(solution)/shard_map/pallas_call | solution.py:609
  99.5 1.9 %shard_map.452 = bf16[8,64,384]{2,1,0:T(8,128)(2,1)S(1)} custom-call(s32[2]{0:T(128)S(1)} %pad_add_fusion.idx_ref, bf16[2048,384]{1,0:T(8,128)(2,1)S(1)} %get-tuple-element.145.gqkv_ref, bf16[512,512]{1,0:T(8,128)(2,1)S(1)} %convert_element_type.123.refs_0_, bf16[512,512]{1,0:T(8,128)(2,1)S(1)} %collective-permute-done.5.refs_1_, ...), custom_call_target="tpu_custom_call" | custom-call | flops 2000000000 | bytes 1048576 | tf_op jit(solution)/shard_map/pallas_call | solution.py:609
  101.4 1.8 %shard_map.453 = (bf16[512,512]{1,0:T(8,128)(2,1)S(1)}, bf16[512,512]{1,0:T(8,128)(2,1)S(1)}, bf16[512,512]{1,0:T(8,128)(2,1)S(1)}, bf16[512,512]{1,0:T(8,128)(2,1)S(1)}) custom-call(s32[2]{0:T(128)S(1)} %pad_add_fusion.idx_ref, bf16[2048,384]{1,0:T(8,128)(2,1)S(1)} %get-tuple-element.145.gqkv_ref, bf16[512,384]{1,0:T(8,128)(2,1)S(1)} %get-tuple-element.146.wg_ref), custom_call_target="tpu_custom_call" | custom-call | flops 2000000000 | bytes 1048576 | tf_op jit(solution)/shard_map/pallas_call | solution.py:609
  103.7 1.1 collective-permute-start.26
  104.8 2.5 %collective-permute-done.29 = bf16[4,64,512]{2,1,0:T(8,128)(2,1)S(1)} collective-permute-done((bf16[4,64,512]{2,1,0:T(8,128)(2,1)S(1)}, bf16[4,64,512]{2,1,0:T(8,128)(2,1)S(1)}, u32[]{:S(2)}, u32[]{:S(2)}) %collective-permute-start.29) | collective-permute-done | bytes 262176 | tf_op jit(solution)/shard_map/ppermute | solution.py:48
  107.4 1.1 collective-permute-start.32
  108.6 0.7 collective-permute-done.28
  109.4 1.6 %collective-permute-start.31 = (bf16[2,64,640]{2,1,0:T(8,128)(2,1)S(1)}, bf16[2,64,640]{2,1,0:T(8,128)(2,1)S(1)}, u32[]{:S(2)}, u32[]{:S(2)}) collective-permute-start(bf16[2,64,640]{2,1,0:T(8,128)(2,1)S(1)} %slice.141), channel_id=1, source_target_pairs={{0,2},{1,3},{2,0},{3,1},{4,6},{5,7},{6,4},{7,5},{8,10},{9,11},{10,... | collective-permute-start | bytes 491528 | tf_op jit(solution)/shard_map/ppermute | solution.py:48
  111.7 1.4 collective-permute-start.30
  113.5 3.2 %collective-permute-start.36 = (bf16[1,64,512]{2,1,0:T(8,128)(2,1)S(1)}, bf16[1,64,512]{2,1,0:T(8,128)(2,1)S(1)}, u32[]{:S(2)}, u32[]{:S(2)}) collective-permute-start(bf16[1,64,512]{2,1,0:T(8,128)(2,1)S(1)} %get-tuple-element.191), channel_id=1, source_target_pairs={{0,16},{4,20},{8,24},{12,28},{16,0},{20,4},{24,8},{28,12},{1,17},{... | collective-permute-start | bytes 196616 | tf_op jit(solution)/shard_map/ppermute | solution.py:48
  116.7 2.9 %collective-permute-start.37 = (bf16[1,64,640]{2,1,0:T(8,128)(2,1)S(1)}, bf16[1,64,640]{2,1,0:T(8,128)(2,1)S(1)}, u32[]{:S(2)}, u32[]{:S(2)}) collective-permute-start(bf16[1,64,640]{2,1,0:T(8,128)(2,1)S(1)} %get-tuple-element.189), channel_id=1, source_target_pairs={{0,16},{4,20},{8,24},{12,28},{16,0},{20,4},{24,8},{28,12},{1,17},{... | collective-permute-start | bytes 245768 | tf_op jit(solution)/shard_map/ppermute | solution.py:48
  119.8 1.3 collective-permute-done.36.refs_3_.refs_7_
  121.1 3.3 %collective-permute-done.37.refs_5_.refs_9_ = bf16[1,64,640]{2,1,0:T(8,128)(2,1)S(1)} collective-permute-done((bf16[1,64,640]{2,1,0:T(8,128)(2,1)S(1)}, bf16[1,64,640]{2,1,0:T(8,128)(2,1)S(1)}, u32[]{:S(2)}, u32[]{:S(2)}) %collective-permute-start.37) | collective-permute-done | bytes 81952 | tf_op jit(solution)/shard_map/ppermute | solution.py:48
  124.4 0.7 collective-permute-done.35.refs_1_.refs_5_
  125.3 1.2 collective-permute-done.38
  126.4 1.2 collective-permute-start.39
  127.7 2.0 %collective-permute-start.40 = (f32[56,128]{1,0:T(8,128)S(1)}, f32[56,128]{1,0:T(8,128)S(1)}, u32[]{:S(2)}, u32[]{:S(2)}) collective-permute-start(f32[56,128]{1,0:T(8,128)S(1)} %add.70), channel_id=1, source_target_pairs={{0,4},{4,0},{8,12},{12,8},{16,20},{20,16},{24,28},{28,24},{1,5},{5... | collective-permute-start | bytes 86024 | tf_op jit(solution)/shard_map/ppermute | solution.py:48
  130.1 1.3 convert_add_fusion
  131.5 2.9 %collective-permute-done.41 = f32[56,128]{1,0:T(8,128)S(1)} collective-permute-done((f32[56,128]{1,0:T(8,128)S(1)}, f32[56,128]{1,0:T(8,128)S(1)}, u32[]{:S(2)}, u32[]{:S(2)}) %collective-permute-start.41) | collective-permute-done | bytes 28704 | tf_op jit(solution)/shard_map/ppermute | solution.py:91
  135.0 3.4 %collective-permute-start.43 = (f32[56,128]{1,0:T(8,128)S(1)}, f32[56,128]{1,0:T(8,128)S(1)}, u32[]{:S(2)}, u32[]{:S(2)}) collective-permute-start(f32[56,128]{1,0:T(8,128)S(1)} %add_add_fusion.refs_0_), channel_id=1, source_target_pairs={{0,16},{4,20},{8,24},{12,28},{16,0},{20,4},{24,8},{28,12},{1,17},{... | collective-permute-start | bytes 86024 | tf_op jit(solution)/shard_map/ppermute | solution.py:48
  139.6 0.7 collective-permute-done.43.refs_2_
  140.2 3.8 %collective-permute-done.44.refs_3_ = f32[56,128]{1,0:T(8,128)S(1)} collective-permute-done((f32[56,128]{1,0:T(8,128)S(1)}, f32[56,128]{1,0:T(8,128)S(1)}, u32[]{:S(2)}, u32[]{:S(2)}) %collective-permute-start.44) | collective-permute-done | bytes 28704 | tf_op jit(solution)/shard_map/ppermute | solution.py:91
  144.2 2.0 %shard_map.455 = (f32[1]{0:T(128)}, f32[6,512]{1,0:T(8,128)}, f32[64,384]{1,0:T(8,128)}, f32[64,384]{1,0:T(8,128)}, f32[64,384]{1,0:T(8,128)}, /*index=5*/bf16[6...) custom-call(s32[2]{0:T(128)S(1)} %pad_add_fusion.idx_ref, ...), custom_call_target="tpu_custom_call" | custom-call | flops 2000000000 | bytes 1048576 | tf_op jit(solution)/shard_map/pallas_call | solution.py:609
  (143 shorter events, 12.9 us)
Async XLA Ops:
  2.1 17.0 %collective-permute-start.6 = (bf16[512,512]{1,0:T(8,128)(2,1)S(1)}, bf16[512,512]{1,0:T(8,128)(2,1)S(1)}, u32[]{:S(2)}, u32[]{:S(2)}) collective-permute-start(bf16[512,512]{1,0:T(8,128)(2,1)S(1)} %convert_element_type.123.refs_0_), channel_id=1, source_target_pairs={{0,2},{1,3},{2,0},{3,1},{4,6},{5,7},{6,4},{7,5},{8,10},{9,11},{10,... | collective-permute-start | bytes 1572872 | tf_op jit(solution)/shard_map/ppermute | solution.py:48
  5.1 24.4 %collective-permute-start.5 = (bf16[512,512]{1,0:T(8,128)(2,1)S(1)}, bf16[512,512]{1,0:T(8,128)(2,1)S(1)}, u32[]{:S(2)}, u32[]{:S(2)}) collective-permute-start(bf16[512,512]{1,0:T(8,128)(2,1)S(1)} %convert_element_type.123.refs_0_), channel_id=1, source_target_pairs={{0,1},{1,0},{2,3},{3,2},{4,5},{5,4},{6,7},{7,6},{8,9},{9,8},{10,11... | collective-permute-start | bytes 1572872 | tf_op jit(solution)/shard_map/ppermute | solution.py:48
  5.3 6.8 %collective-permute-start = (bf16[1,80,384]{2,1,0:T(8,128)(2,1)S(1)}, bf16[1,80,384]{2,1,0:T(8,128)(2,1)S(1)}, u32[]{:S(2)}, u32[]{:S(2)}) collective-permute-start(bf16[1,80,384]{2,1,0:T(8,128)(2,1)S(1)} %fusion.4), channel_id=1, source_target_pairs={{0,16},{4,20},{8,24},{12,28},{16,0},{20,4},{24,8},{28,12},{1,17},{... | collective-permute-start | bytes 184328 | tf_op jit(solution)/shard_map/ppermute | solution.py:48
  8.0 10.4 %collective-permute-start.2 = (bf16[1,64,1152]{2,1,0:T(8,128)(2,1)S(1)}, bf16[1,64,1152]{2,1,0:T(8,128)(2,1)S(1)}, u32[]{:S(2)}, u32[]{:S(2)}) collective-permute-start(bf16[1,64,1152]{2,1,0:T(8,128)(2,1)S(1)} %maximum_bitcast_fusion), channel_id=1, source_target_pairs={{0,16},{4,20},{8,24},{12,28},{16,0},{20,4},{24,8},{28,12},{1,17},{... | collective-permute-start | bytes 442376 | tf_op jit(solution)/shard_map/ppermute | solution.py:48
  12.1 8.9 %collective-permute-start.1 = (bf16[2,80,384]{2,1,0:T(8,128)(2,1)S(1)}, bf16[2,80,384]{2,1,0:T(8,128)(2,1)S(1)}, u32[]{:S(2)}, u32[]{:S(2)}) collective-permute-start(bf16[2,80,384]{2,1,0:T(8,128)(2,1)S(1)} %pad_maximum_fusion.6), channel_id=1, source_target_pairs={{0,8},{4,12},{8,0},{12,4},{16,24},{20,28},{24,16},{28,20},{1,9},{5... | collective-permute-start | bytes 368648 | tf_op jit(solution)/shard_map/ppermute | solution.py:48
  18.4 8.8 %collective-permute-start.3 = (bf16[2,64,1152]{2,1,0:T(8,128)(2,1)S(1)}, bf16[2,64,1152]{2,1,0:T(8,128)(2,1)S(1)}, u32[]{:S(2)}, u32[]{:S(2)}) collective-permute-start(bf16[2,64,1152]{2,1,0:T(8,128)(2,1)S(1)} %pad_maximum_fusion.2), channel_id=1, source_target_pairs={{0,8},{4,12},{8,0},{12,4},{16,24},{20,28},{24,16},{28,20},{1,9},{5... | collective-permute-start | bytes 884744 | tf_op jit(solution)/shard_map/ppermute | solution.py:48
  19.1 10.4 %collective-permute-start.7 = (bf16[512,512]{1,0:T(8,128)(2,1)S(1)}, bf16[512,512]{1,0:T(8,128)(2,1)S(1)}, u32[]{:S(2)}, u32[]{:S(2)}) collective-permute-start(bf16[512,512]{1,0:T(8,128)(2,1)S(1)} %collective-permute-done.6.refs_2_), channel_id=1, source_target_pairs={{0,1},{1,0},{2,3},{3,2},{4,5},{5,4},{6,7},{7,6},{8,9},{9,8},{10,11... | collective-permute-start | bytes 1572872 | tf_op jit(solution)/shard_map/ppermute | solution.py:48
  21.0 8.5 %collective-permute-start.4 = (bf16[4,80,384]{2,1,0:T(8,128)(2,1)S(1)}, bf16[4,80,384]{2,1,0:T(8,128)(2,1)S(1)}, u32[]{:S(2)}, u32[]{:S(2)}) collective-permute-start(bf16[4,80,384]{2,1,0:T(8,128)(2,1)S(1)} %pad_maximum_fusion.5.w_own), channel_id=1, source_target_pairs={{0,4},{4,0},{8,12},{12,8},{16,20},{20,16},{24,28},{28,24},{1,5},{5... | collective-permute-start | bytes 737288 | tf_op jit(solution)/shard_map/ppermute | solution.py:48
  27.3 8.6 %collective-permute-start.9 = (bf16[4,64,640]{2,1,0:T(8,128)(2,1)S(1)}, bf16[4,64,640]{2,1,0:T(8,128)(2,1)S(1)}, u32[]{:S(2)}, u32[]{:S(2)}) collective-permute-start(bf16[4,64,640]{2,1,0:T(8,128)(2,1)S(1)} %pad_maximum_fusion.3), channel_id=1, source_target_pairs={{0,2},{1,3},{2,0},{3,1},{4,6},{5,7},{6,4},{7,5},{8,10},{9,11},{10,... | collective-permute-start | bytes 983048 | tf_op jit(solution)/shard_map/ppermute | solution.py:48
  27.9 8.1 %collective-permute-start.8 = (bf16[4,64,512]{2,1,0:T(8,128)(2,1)S(1)}, bf16[4,64,512]{2,1,0:T(8,128)(2,1)S(1)}, u32[]{:S(2)}, u32[]{:S(2)}) collective-permute-start(bf16[4,64,512]{2,1,0:T(8,128)(2,1)S(1)} %pad_maximum_fusion.4), channel_id=1, source_target_pairs={{0,4},{4,0},{8,12},{12,8},{16,20},{20,16},{24,28},{28,24},{1,5},{5... | collective-permute-start | bytes 786440 | tf_op jit(solution)/shard_map/ppermute | solution.py:48
  36.0 10.1 %collective-permute-start.11 = (bf16[8,64,640]{2,1,0:T(8,128)(2,1)S(1)}, bf16[8,64,640]{2,1,0:T(8,128)(2,1)S(1)}, u32[]{:S(2)}, u32[]{:S(2)}) collective-permute-start(bf16[8,64,640]{2,1,0:T(8,128)(2,1)S(1)} %pad_maximum_fusion.refs_8_), channel_id=1, source_target_pairs={{0,1},{1,0},{2,3},{3,2},{4,5},{5,4},{6,7},{7,6},{8,9},{9,8},{10,11... | collective-permute-start | bytes 1966088 | tf_op jit(solution)/shard_map/ppermute | solution.py:48
  36.2 9.1 %collective-permute-start.10 = (bf16[8,64,512]{2,1,0:T(8,128)(2,1)S(1)}, bf16[8,64,512]{2,1,0:T(8,128)(2,1)S(1)}, u32[]{:S(2)}, u32[]{:S(2)}) collective-permute-start(bf16[8,64,512]{2,1,0:T(8,128)(2,1)S(1)} %pad_maximum_fusion.1.refs_4_), channel_id=1, source_target_pairs={{0,1},{1,0},{2,3},{3,2},{4,5},{5,4},{6,7},{7,6},{8,9},{9,8},{10,11... | collective-permute-start | bytes 1572872 | tf_op jit(solution)/shard_map/ppermute | solution.py:48
  36.7 19.7 %collective-permute-start.17 = (bf16[8,64,640]{2,1,0:T(8,128)(2,1)S(1)}, bf16[8,64,640]{2,1,0:T(8,128)(2,1)S(1)}, u32[]{:S(2)}, u32[]{:S(2)}) collective-permute-start(bf16[8,64,640]{2,1,0:T(8,128)(2,1)S(1)} %pad_maximum_fusion.refs_8_), channel_id=1, source_target_pairs={{0,4},{4,0},{8,12},{12,8},{16,20},{20,16},{24,28},{28,24},{1,5},{5... | collective-permute-start | bytes 1966088 | tf_op jit(solution)/shard_map/ppermute | solution.py:48
  38.2 19.2 %collective-permute-start.15 = (bf16[8,64,512]{2,1,0:T(8,128)(2,1)S(1)}, bf16[8,64,512]{2,1,0:T(8,128)(2,1)S(1)}, u32[]{:S(2)}, u32[]{:S(2)}) collective-permute-start(bf16[8,64,512]{2,1,0:T(8,128)(2,1)S(1)} %pad_maximum_fusion.1.refs_4_), channel_id=1, source_target_pairs={{0,2},{1,3},{2,0},{3,1},{4,6},{5,7},{6,4},{7,5},{8,10},{9,11},{10,... | collective-permute-start | bytes 1572872 | tf_op jit(solution)/shard_map/ppermute | solution.py:48
  38.7 21.4 %copy-start.7 = (f32[512,512]{1,0:T(8,128)S(1)}, f32[512,512]{1,0:T(8,128)}, u32[]{:S(2)}) copy-start(f32[512,512]{1,0:T(8,128)} %refs_15_.2) | copy-start | bytes 3145732
  45.1 10.8 %collective-permute-start.13 = (bf16[528,128]{1,0:T(8,128)(2,1)S(1)}, bf16[528,128]{1,0:T(8,128)(2,1)S(1)}, u32[]{:S(2)}, u32[]{:S(2)}) collective-permute-start(bf16[528,128]{1,0:T(8,128)(2,1)S(1)} %get-tuple-element.118.refs_6_), channel_id=1, source_target_pairs={{0,2},{1,3},{2,0},{3,1},{4,6},{5,7},{6,4},{7,5},{8,10},{9,11},{10,... | collective-permute-start | bytes 405512 | tf_op jit(solution)/shard_map/ppermute | solution.py:749
  45.2 14.9 %copy-start = (f32[512,512]{1,0:T(8,128)S(1)}, f32[512,512]{1,0:T(8,128)}, u32[]{:S(2)}) copy-start(f32[512,512]{1,0:T(8,128)} %refs_12_.2) | copy-start | bytes 3145732
  45.2 14.9 %copy-start.5 = (f32[512,512]{1,0:T(8,128)S(1)}, f32[512,512]{1,0:T(8,128)}, u32[]{:S(2)}) copy-start(f32[512,512]{1,0:T(8,128)} %refs_13_.1) | copy-start | bytes 3145732
  45.3 11.2 %collective-permute-start.14 = (bf16[528,128]{1,0:T(8,128)(2,1)S(1)}, bf16[528,128]{1,0:T(8,128)(2,1)S(1)}, u32[]{:S(2)}, u32[]{:S(2)}) collective-permute-start(bf16[528,128]{1,0:T(8,128)(2,1)S(1)} %get-tuple-element.122.refs_7_), channel_id=1, source_target_pairs={{0,3},{1,2},{2,1},{3,0},{4,7},{5,6},{6,5},{7,4},{8,11},{9,10},{10,... | collective-permute-start | bytes 405512 | tf_op jit(solution)/shard_map/ppermute | solution.py:749
  56.4 3.7 %collective-permute-start.18 = (bf16[8,64,640]{2,1,0:T(8,128)(2,1)S(1)}, bf16[8,64,640]{2,1,0:T(8,128)(2,1)S(1)}, u32[]{:S(2)}, u32[]{:S(2)}) collective-permute-start(bf16[8,64,640]{2,1,0:T(8,128)(2,1)S(1)} %collective-permute-done.17.refs_9_), channel_id=1, source_target_pairs={{0,1},{1,0},{2,3},{3,2},{4,5},{5,4},{6,7},{7,6},{8,9},{9,8},{10,11... | collective-permute-start | bytes 1966088 | tf_op jit(solution)/shard_map/ppermute | solution.py:48
  57.4 2.7 %collective-permute-start.16 = (bf16[8,64,512]{2,1,0:T(8,128)(2,1)S(1)}, bf16[8,64,512]{2,1,0:T(8,128)(2,1)S(1)}, u32[]{:S(2)}, u32[]{:S(2)}) collective-permute-start(bf16[8,64,512]{2,1,0:T(8,128)(2,1)S(1)} %collective-permute-done.15.refs_5_), channel_id=1, source_target_pairs={{0,1},{1,0},{2,3},{3,2},{4,5},{5,4},{6,7},{7,6},{8,9},{9,8},{10,11... | collective-permute-start | bytes 1572872 | tf_op jit(solution)/shard_map/ppermute | solution.py:48
  57.5 2.6 %collective-permute-start.12 = (bf16[528,128]{1,0:T(8,128)(2,1)S(1)}, bf16[528,128]{1,0:T(8,128)(2,1)S(1)}, u32[]{:S(2)}, u32[]{:S(2)}) collective-permute-start(bf16[528,128]{1,0:T(8,128)(2,1)S(1)} %get-tuple-element.121.refs_5_), channel_id=1, source_target_pairs={{0,1},{1,0},{2,3},{3,2},{4,5},{5,4},{6,7},{7,6},{8,9},{9,8},{10,11... | collective-permute-start | bytes 405512 | tf_op jit(solution)/shard_map/ppermute | solution.py:749
  75.5 2.7 %collective-permute-start.19 = (bf16[16,64,512]{2,1,0:T(8,128)(2,1)S(1)}, bf16[16,64,512]{2,1,0:T(8,128)(2,1)S(1)}, u32[]{:S(2)}, u32[]{:S(2)}) collective-permute-start(bf16[16,64,512]{2,1,0:T(8,128)(2,1)S(1)} %get-tuple-element.134), channel_id=1, source_target_pairs={{0,1},{1,0},{2,3},{3,2},{4,5},{5,4},{6,7},{7,6},{8,9},{9,8},{10,11... | collective-permute-start | bytes 3145736 | tf_op jit(solution)/shard_map/ppermute | solution.py:48
  75.9 4.2 %collective-permute-start.20 = (bf16[16,64,640]{2,1,0:T(8,128)(2,1)S(1)}, bf16[16,64,640]{2,1,0:T(8,128)(2,1)S(1)}, u32[]{:S(2)}, u32[]{:S(2)}) collective-permute-start(bf16[16,64,640]{2,1,0:T(8,128)(2,1)S(1)} %get-tuple-element.136), channel_id=1, source_target_pairs={{0,1},{1,0},{2,3},{3,2},{4,5},{5,4},{6,7},{7,6},{8,9},{9,8},{10,11... | collective-permute-start | bytes 3932168 | tf_op jit(solution)/shard_map/ppermute | solution.py:48
  76.0 5.7 %collective-permute-start.21 = (bf16[512,128]{1,0:T(8,128)(2,1)S(1)}, bf16[512,128]{1,0:T(8,128)(2,1)S(1)}, u32[]{:S(2)}, u32[]{:S(2)}) collective-permute-start(bf16[512,128]{1,0:T(8,128)(2,1)S(1)} %get-tuple-element.138), channel_id=1, source_target_pairs={{0,1},{1,0},{2,3},{3,2},{4,5},{5,4},{6,7},{7,6},{8,9},{9,8},{10,11... | collective-permute-start | bytes 393224 | tf_op jit(solution)/shard_map/ppermute | solution.py:794
  76.4 6.4 %collective-permute-start.22 = (bf16[512,128]{1,0:T(8,128)(2,1)S(1)}, bf16[512,128]{1,0:T(8,128)(2,1)S(1)}, u32[]{:S(2)}, u32[]{:S(2)}) collective-permute-start(bf16[512,128]{1,0:T(8,128)(2,1)S(1)} %get-tuple-element.139), channel_id=1, source_target_pairs={{0,2},{1,3},{2,0},{3,1},{4,6},{5,7},{6,4},{7,5},{8,10},{9,11},{10,... | collective-permute-start | bytes 393224 | tf_op jit(solution)/shard_map/ppermute | solution.py:794
  76.9 7.0 %collective-permute-start.23 = (bf16[512,128]{1,0:T(8,128)(2,1)S(1)}, bf16[512,128]{1,0:T(8,128)(2,1)S(1)}, u32[]{:S(2)}, u32[]{:S(2)}) collective-permute-start(bf16[512,128]{1,0:T(8,128)(2,1)S(1)} %get-tuple-element.140), channel_id=1, source_target_pairs={{0,3},{1,2},{2,1},{3,0},{4,7},{5,6},{6,5},{7,4},{8,11},{9,10},{10,... | collective-permute-start | bytes 393224 | tf_op jit(solution)/shard_map/ppermute | solution.py:794
  78.6 19.4 %collective-permute-start.24 = (bf16[8,64,512]{2,1,0:T(8,128)(2,1)S(1)}, bf16[8,64,512]{2,1,0:T(8,128)(2,1)S(1)}, u32[]{:S(2)}, u32[]{:S(2)}) collective-permute-start(bf16[8,64,512]{2,1,0:T(8,128)(2,1)S(1)} %slice.130), channel_id=1, source_target_pairs={{0,4},{4,0},{8,12},{12,8},{16,20},{20,16},{24,28},{28,24},{1,5},{5... | collective-permute-start | bytes 1572872 | tf_op jit(solution)/shard_map/ppermute | solution.py:48
  80.5 18.2 %collective-permute-start.25 = (bf16[8,64,640]{2,1,0:T(8,128)(2,1)S(1)}, bf16[8,64,640]{2,1,0:T(8,128)(2,1)S(1)}, u32[]{:S(2)}, u32[]{:S(2)}) collective-permute-start(bf16[8,64,640]{2,1,0:T(8,128)(2,1)S(1)} %slice.131), channel_id=1, source_target_pairs={{0,8},{4,12},{8,0},{12,4},{16,24},{20,28},{24,16},{28,20},{1,9},{5... | collective-permute-start | bytes 1966088 | tf_op jit(solution)/shard_map/ppermute | solution.py:48
  98.1 9.2 %collective-permute-start.29 = (bf16[4,64,512]{2,1,0:T(8,128)(2,1)S(1)}, bf16[4,64,512]{2,1,0:T(8,128)(2,1)S(1)}, u32[]{:S(2)}, u32[]{:S(2)}) collective-permute-start(bf16[4,64,512]{2,1,0:T(8,128)(2,1)S(1)} %slice.133), channel_id=1, source_target_pairs={{0,2},{1,3},{2,0},{3,1},{4,6},{5,7},{6,4},{7,5},{8,10},{9,11},{10,... | collective-permute-start | bytes 786440 | tf_op jit(solution)/shard_map/ppermute | solution.py:48
  98.9 10.3 %collective-permute-start.28 = (bf16[4,64,640]{2,1,0:T(8,128)(2,1)S(1)}, bf16[4,64,640]{2,1,0:T(8,128)(2,1)S(1)}, u32[]{:S(2)}, u32[]{:S(2)}) collective-permute-start(bf16[4,64,640]{2,1,0:T(8,128)(2,1)S(1)} %slice.135), channel_id=1, source_target_pairs={{0,4},{4,0},{8,12},{12,8},{16,20},{20,16},{24,28},{28,24},{1,5},{5... | collective-permute-start | bytes 983048 | tf_op jit(solution)/shard_map/ppermute | solution.py:48
  103.2 7.7 %collective-permute-start.27 = (bf16[512,512]{1,0:T(8,128)(2,1)S(1)}, bf16[512,512]{1,0:T(8,128)(2,1)S(1)}, u32[]{:S(2)}, u32[]{:S(2)}) collective-permute-start(bf16[512,512]{1,0:T(8,128)(2,1)S(1)} %get-tuple-element.149), channel_id=1, source_target_pairs={{0,1},{1,0},{2,3},{3,2},{4,5},{5,4},{6,7},{7,6},{8,9},{9,8},{10,11... | collective-permute-start | bytes 1572872 | tf_op jit(solution)/shard_map/ppermute | solution.py:48
  103.7 8.0 %collective-permute-start.26 = (bf16[4,64,384]{2,1,0:T(8,128)(2,1)S(1)}, bf16[4,64,384]{2,1,0:T(8,128)(2,1)S(1)}, u32[]{:S(2)}, u32[]{:S(2)}) collective-permute-start(bf16[4,64,384]{2,1,0:T(8,128)(2,1)S(1)} %slice.136), channel_id=1, source_target_pairs={{0,8},{4,12},{8,0},{12,4},{16,24},{20,28},{24,16},{28,20},{1,9},{5... | collective-permute-start | bytes 589832 | tf_op jit(solution)/shard_map/ppermute | solution.py:48
  107.4 6.0 %collective-permute-start.32 = (bf16[2,64,512]{2,1,0:T(8,128)(2,1)S(1)}, bf16[2,64,512]{2,1,0:T(8,128)(2,1)S(1)}, u32[]{:S(2)}, u32[]{:S(2)}) collective-permute-start(bf16[2,64,512]{2,1,0:T(8,128)(2,1)S(1)} %slice.140), channel_id=1, source_target_pairs={{0,8},{4,12},{8,0},{12,4},{16,24},{20,28},{24,16},{28,20},{1,9},{5... | collective-permute-start | bytes 393224 | tf_op jit(solution)/shard_map/ppermute | solution.py:48
  108.6 16.7 %collective-permute-start.33 = (bf16[512,512]{1,0:T(8,128)(2,1)S(1)}, bf16[512,512]{1,0:T(8,128)(2,1)S(1)}, u32[]{:S(2)}, u32[]{:S(2)}) collective-permute-start(bf16[512,512]{1,0:T(8,128)(2,1)S(1)} %get-tuple-element.158), channel_id=1, source_target_pairs={{0,1},{1,0},{2,3},{3,2},{4,5},{5,4},{6,7},{7,6},{8,9},{9,8},{10,11... | collective-permute-start | bytes 1572872 | tf_op jit(solution)/shard_map/ppermute | solution.py:48
  109.4 7.3 %collective-permute-start.31 = (bf16[2,64,640]{2,1,0:T(8,128)(2,1)S(1)}, bf16[2,64,640]{2,1,0:T(8,128)(2,1)S(1)}, u32[]{:S(2)}, u32[]{:S(2)}) collective-permute-start(bf16[2,64,640]{2,1,0:T(8,128)(2,1)S(1)} %slice.141), channel_id=1, source_target_pairs={{0,2},{1,3},{2,0},{3,1},{4,6},{5,7},{6,4},{7,5},{8,10},{9,11},{10,... | collective-permute-start | bytes 491528 | tf_op jit(solution)/shard_map/ppermute | solution.py:48
  111.1 18.8 %collective-permute-start.34 = (bf16[512,512]{1,0:T(8,128)(2,1)S(1)}, bf16[512,512]{1,0:T(8,128)(2,1)S(1)}, u32[]{:S(2)}, u32[]{:S(2)}) collective-permute-start(bf16[512,512]{1,0:T(8,128)(2,1)S(1)} %add_convert_fusion.3), channel_id=1, source_target_pairs={{0,2},{1,3},{2,0},{3,1},{4,6},{5,7},{6,4},{7,5},{8,10},{9,11},{10,... | collective-permute-start | bytes 1572872 | tf_op jit(solution)/shard_map/ppermute | solution.py:48
  111.7 7.9 %collective-permute-start.30 = (bf16[2,64,384]{2,1,0:T(8,128)(2,1)S(1)}, bf16[2,64,384]{2,1,0:T(8,128)(2,1)S(1)}, u32[]{:S(2)}, u32[]{:S(2)}) collective-permute-start(bf16[2,64,384]{2,1,0:T(8,128)(2,1)S(1)} %slice.143), channel_id=1, source_target_pairs={{0,4},{4,0},{8,12},{12,8},{16,20},{20,16},{24,28},{28,24},{1,5},{5... | collective-permute-start | bytes 294920 | tf_op jit(solution)/shard_map/ppermute | solution.py:48
  113.5 7.7 %collective-permute-start.36 = (bf16[1,64,512]{2,1,0:T(8,128)(2,1)S(1)}, bf16[1,64,512]{2,1,0:T(8,128)(2,1)S(1)}, u32[]{:S(2)}, u32[]{:S(2)}) collective-permute-start(bf16[1,64,512]{2,1,0:T(8,128)(2,1)S(1)} %get-tuple-element.191), channel_id=1, source_target_pairs={{0,16},{4,20},{8,24},{12,28},{16,0},{20,4},{24,8},{28,12},{1,17},{... | collective-permute-start | bytes 196616 | tf_op jit(solution)/shard_map/ppermute | solution.py:48
  116.7 7.7 %collective-permute-start.37 = (bf16[1,64,640]{2,1,0:T(8,128)(2,1)S(1)}, bf16[1,64,640]{2,1,0:T(8,128)(2,1)S(1)}, u32[]{:S(2)}, u32[]{:S(2)}) collective-permute-start(bf16[1,64,640]{2,1,0:T(8,128)(2,1)S(1)} %get-tuple-element.189), channel_id=1, source_target_pairs={{0,16},{4,20},{8,24},{12,28},{16,0},{20,4},{24,8},{28,12},{1,17},{... | collective-permute-start | bytes 245768 | tf_op jit(solution)/shard_map/ppermute | solution.py:48
  119.7 5.4 %collective-permute-start.35 = (bf16[1,64,384]{2,1,0:T(8,128)(2,1)S(1)}, bf16[1,64,384]{2,1,0:T(8,128)(2,1)S(1)}, u32[]{:S(2)}, u32[]{:S(2)}) collective-permute-start(bf16[1,64,384]{2,1,0:T(8,128)(2,1)S(1)} %get-tuple-element.193), channel_id=1, source_target_pairs={{0,16},{4,20},{8,24},{12,28},{16,0},{20,4},{24,8},{28,12},{1,17},{... | collective-permute-start | bytes 147464 | tf_op jit(solution)/shard_map/ppermute | solution.py:48
  125.2 1.3 collective-permute-start.38
  126.4 4.9 %collective-permute-start.39 = (f32[56,128]{1,0:T(8,128)S(1)}, f32[56,128]{1,0:T(8,128)S(1)}, u32[]{:S(2)}, u32[]{:S(2)}) collective-permute-start(f32[56,128]{1,0:T(8,128)S(1)} %add.70), channel_id=1, source_target_pairs={{0,2},{1,3},{2,0},{3,1},{4,6},{5,7},{6,4},{7,5},{8,10},{9,11},{10,... | collective-permute-start | bytes 86024 | tf_op jit(solution)/shard_map/ppermute | solution.py:48
  127.7 3.9 %collective-permute-start.40 = (f32[56,128]{1,0:T(8,128)S(1)}, f32[56,128]{1,0:T(8,128)S(1)}, u32[]{:S(2)}, u32[]{:S(2)}) collective-permute-start(f32[56,128]{1,0:T(8,128)S(1)} %add.70), channel_id=1, source_target_pairs={{0,4},{4,0},{8,12},{12,8},{16,20},{20,16},{24,28},{28,24},{1,5},{5... | collective-permute-start | bytes 86024 | tf_op jit(solution)/shard_map/ppermute | solution.py:48
  129.7 4.8 %collective-permute-start.41 = (f32[56,128]{1,0:T(8,128)S(1)}, f32[56,128]{1,0:T(8,128)S(1)}, u32[]{:S(2)}, u32[]{:S(2)}) collective-permute-start(f32[56,128]{1,0:T(8,128)S(1)} %add.70), channel_id=1, source_target_pairs={{0,6},{1,7},{2,4},{3,5},{4,2},{5,3},{6,0},{7,1},{8,14},{9,15},{10,... | collective-permute-start | bytes 86024 | tf_op jit(solution)/shard_map/ppermute | solution.py:91
  134.4 5.1 %collective-permute-start.42 = (f32[56,128]{1,0:T(8,128)S(1)}, f32[56,128]{1,0:T(8,128)S(1)}, u32[]{:S(2)}, u32[]{:S(2)}) collective-permute-start(f32[56,128]{1,0:T(8,128)S(1)} %add_add_fusion.refs_0_), channel_id=1, source_target_pairs={{0,8},{4,12},{8,0},{12,4},{16,24},{20,28},{24,16},{28,20},{1,9},{5... | collective-permute-start | bytes 86024 | tf_op jit(solution)/shard_map/ppermute | solution.py:48
  135.0 5.2 %collective-permute-start.43 = (f32[56,128]{1,0:T(8,128)S(1)}, f32[56,128]{1,0:T(8,128)S(1)}, u32[]{:S(2)}, u32[]{:S(2)}) collective-permute-start(f32[56,128]{1,0:T(8,128)S(1)} %add_add_fusion.refs_0_), channel_id=1, source_target_pairs={{0,16},{4,20},{8,24},{12,28},{16,0},{20,4},{24,8},{28,12},{1,17},{... | collective-permute-start | bytes 86024 | tf_op jit(solution)/shard_map/ppermute | solution.py:48
  138.4 5.7 %collective-permute-start.44 = (f32[56,128]{1,0:T(8,128)S(1)}, f32[56,128]{1,0:T(8,128)S(1)}, u32[]{:S(2)}, u32[]{:S(2)}) collective-permute-start(f32[56,128]{1,0:T(8,128)S(1)} %add_add_fusion.refs_0_), channel_id=1, source_target_pairs={{0,24},{1,25},{2,26},{3,27},{4,28},{5,29},{6,30},{7,31},{8,16},{9,... | collective-permute-start | bytes 86024 | tf_op jit(solution)/shard_map/ppermute | solution.py:91
  (20 other events, 237.3 us)

commit v5 on v4

--- a/solution.py
+++ b/solution.py
@@ -12,7 +12,7 @@
 HD = 64
 TQ = 256
 TK = 256
-CH = 64
+CHUNK = 512
 
 EPS_NORM = 1e-05
 NEG_LARGE = -1e30
@@ -294,6 +294,7 @@
     ]
     g, h = idx_ref[0], idx_ref[1]
     rw = post_in.shape[0]
+    chunk = min(CHUNK, rw)
     ds_rows = D // n_dp
     units = hid_s.shape[1] // n_h
     row = lambda i: norm_ref[i : i + 1, :]
@@ -316,7 +317,7 @@
     acc_s[...] = dot(mix_s[...], o_s[...], 1, 1)
 
     def chunk_one(i, carry):
-        at = pl.ds(pl.multiple_of(i * CH, CH), CH)
+        at = pl.ds(pl.multiple_of(i * chunk, chunk), chunk)
         attn_out = acc_s[at, :] + row(2)
         v = post_in[at, :] + attn_out
         centered = v - jnp.mean(v, axis=-1, keepdims=True)
@@ -324,13 +325,13 @@
         xhat = centered * rstd
         pn = xhat * row(0) + row(1)
         xh_s[at, :] = xhat
-        rs_s[at, :] = jnp.broadcast_to(rstd, (CH, 128))
+        rs_s[at, :] = jnp.broadcast_to(rstd, (chunk, 128))
         pn_s[at, :] = pn
         xb_s[at, :] = pn.astype(BF)
         dual_out[at, :] = dual_in[at, :] + attn_out
         return carry
 
-    lax.fori_loop(0, rw // CH, chunk_one, 0)
+    lax.fori_loop(0, rw // chunk, chunk_one, 0)
     xt_s[...] = xb_s[...].T
     for oh in range(n_h):
         part = slice(oh * units, (oh + 1) * units)
@@ -340,7 +341,7 @@
 
     def chunk_two(i, carry):
         gain_sum, shift_sum, ffn_sum = carry
-        at = pl.ds(pl.multiple_of(i * CH, CH), CH)
+        at = pl.ds(pl.multiple_of(i * chunk, chunk), chunk)
         ffn_out = acc_s[at, :] + row(5)
         v = pn_s[at, :] + ffn_out
         centered = v - jnp.mean(v, axis=-1, keepdims=True)
@@ -356,7 +357,7 @@
         return gain_sum + fold(cot * xhat), shift_sum + fold(cot), ffn_sum + fold(gffn)
 
     zero = jnp.zeros((8, D), F32)
-    gain2, shift2, ffn_sum = lax.fori_loop(0, rw // CH, chunk_two, (zero, zero, zero))
+    gain2, shift2, ffn_sum = lax.fori_loop(0, rw // chunk, chunk_two, (zero, zero, zero))
     gt_s[...] = gb_s[...].T
     for oh in range(n_h):
         part = slice(oh * units, (oh + 1) * units)
@@ -375,7 +376,7 @@
 
     def chunk_three(i, carry):
         gain_sum, shift_sum, attn_sum = carry
-        at = pl.ds(pl.multiple_of(i * CH, CH), CH)
+        at = pl.ds(pl.multiple_of(i * chunk, chunk), chunk)
         grad = gmid2_s[at, :] + acc_s[at, :]
         xhat = xh_s[at, :]
         gmid1 = norm_back(grad, xhat, rs_s[at, :1], row(0))
@@ -384,7 +385,7 @@
         gb_s[at, :] = gattn.astype(BF)
         return gain_sum + fold(grad * xhat), shift_sum + fold(grad), attn_sum + fold(gattn)
 
-    gain1, shift1, attn_sum = lax.fori_loop(0, rw // CH, chunk_three, (zero, zero, zero))
+    gain1, shift1, attn_sum = lax.fori_loop(0, rw // chunk, chunk_three, (zero, zero, zero))
     grad_mixed = dot(gb_s[...], o_s[...], 1, 0).astype(BF)
     for off in range(n_h):
         gm[off][...] = grad_mixed[:, off * width : (off + 1) * width]

time: 147 us -> 143 us (0.973)
  Pallas kernels: 48 us -> 40.4 us
  starting transfers between devices: 45.1 us -> 47.8 us
    pallas_call x9, Pallas kernels: 48 us -> 40.4 us  [call(): pl.pallas_call(body, out_shape=outs, in_specs=[SMEM] * n_smem + [VMEM] *...]
    ppermute x37, starting transfers between devices: 41.1 us -> 43.1 us  [swap(): return lax.ppermute(v, axis, [(i, i ^ bit) for i in range(count)])]
    ppermute x3, waiting for transfers between devices: 8.08 us -> 9.57 us  [per_device(): lax.ppermute(pieces[off], 'head', [(i, i ^ off) for i in range(n_h)])]
  transfers between devices with their start and end apart: 45 -> 45, of which waited for: 23 -> 23; matrix products, arithmetic and copies ran while one was open for 2% -> 3% of each run, Pallas kernels for 21% -> 19%
where the time goes in v5:
time: 143 us; the launch traced here: 142 us
  starting transfers between devices  47.8 us (33%)
  waiting for transfers between devices  46.9 us (33%)
  Pallas kernels  40.4 us (28%)
  other arithmetic  4.62 us (3%)
  between operations  2.15 us (2%)
    ppermute x37, starting transfers between devices, swap(): return lax.ppermute(v, axis, [(i, i ^ bit) for i in range(count)])  43.1 us
    pallas_call x9, Pallas kernels, call(): pl.pallas_call(body, out_shape=outs, in_specs=[SMEM] * n_smem + [VMEM] *...  40.4 us
    ppermute x37, waiting for transfers between devices, swap(): return lax.ppermute(v, axis, [(i, i ^ bit) for i in range(count)])  28.9 us
    ppermute x3, waiting for transfers between devices, per_device(): lax.ppermute(pieces[off], 'head', [(i, i ^ off) for i in range(n_h)])  9.57 us
    ppermute x2, waiting for transfers between devices, swap_both(): lax.ppermute(v, ('dp', 'head'), [(i, i ^ flip) for i in range(n_h * lax.a...  6.29 us
  transfers between devices with their start and end apart: 45, of which 23 were waited for; matrix products, arithmetic and copies ran while one was open for 3% of the time, Pallas kernels for 19%

profile of v5, /device:TPU:0, one launch (start us, length us, event | category | flops | bytes accessed | tf_op | source)
XLA Modules:
  0.0 142.4 jit_solution(12327603857959146348)
XLA Ops:
  0.7 1.4 convert_element_type.123.refs_0_
  2.1 3.0 %collective-permute-start.6 = (bf16[512,512]{1,0:T(8,128)(2,1)S(1)}, bf16[512,512]{1,0:T(8,128)(2,1)S(1)}, u32[]{:S(2)}, u32[]{:S(2)}) collective-permute-start(bf16[512,512]{1,0:T(8,128)(2,1)S(1)} %convert_element_type.123.refs_0_), channel_id=1, source_target_pairs={{0,2},{1,3},{2,0},{3,1},{4,6},{5,7},{6,4},{7,5},{8,10},{9,11},{10,... | collective-permute-start | bytes 1572872 | tf_op jit(solution)/shard_map/ppermute | solution.py:48
  5.3 2.7 %collective-permute-start = (bf16[1,80,384]{2,1,0:T(8,128)(2,1)S(1)}, bf16[1,80,384]{2,1,0:T(8,128)(2,1)S(1)}, u32[]{:S(2)}, u32[]{:S(2)}) collective-permute-start(bf16[1,80,384]{2,1,0:T(8,128)(2,1)S(1)} %fusion.4), channel_id=1, source_target_pairs={{0,16},{4,20},{8,24},{12,28},{16,0},{20,4},{24,8},{28,12},{1,17},{... | collective-permute-start | bytes 184328 | tf_op jit(solution)/shard_map/ppermute | solution.py:48
  8.5 3.6 %collective-permute-done = bf16[1,80,384]{2,1,0:T(8,128)(2,1)S(1)} collective-permute-done((bf16[1,80,384]{2,1,0:T(8,128)(2,1)S(1)}, bf16[1,80,384]{2,1,0:T(8,128)(2,1)S(1)}, u32[]{:S(2)}, u32[]{:S(2)}) %collective-permute-start) | collective-permute-done | bytes 61472 | tf_op jit(solution)/shard_map/ppermute | solution.py:48
  12.1 3.8 %collective-permute-start.1 = (bf16[2,80,384]{2,1,0:T(8,128)(2,1)S(1)}, bf16[2,80,384]{2,1,0:T(8,128)(2,1)S(1)}, u32[]{:S(2)}, u32[]{:S(2)}) collective-permute-start(bf16[2,80,384]{2,1,0:T(8,128)(2,1)S(1)} %pad_maximum_fusion.6), channel_id=1, source_target_pairs={{0,8},{4,12},{8,0},{12,4},{16,24},{20,28},{24,16},{28,20},{1,9},{5... | collective-permute-start | bytes 368648 | tf_op jit(solution)/shard_map/ppermute | solution.py:48
  15.9 2.5 %collective-permute-done.2 = bf16[1,64,1152]{2,1,0:T(8,128)(2,1)S(1)} collective-permute-done((bf16[1,64,1152]{2,1,0:T(8,128)(2,1)S(1)}, bf16[1,64,1152]{2,1,0:T(8,128)(2,1)S(1)}, u32[]{:S(2)}, u32[]{:S(2)}) %collective-permute-start.2) | collective-permute-done | bytes 147488 | tf_op jit(solution)/shard_map/ppermute | solution.py:48
  19.1 1.9 %collective-permute-done.1 = bf16[2,80,384]{2,1,0:T(8,128)(2,1)S(1)} collective-permute-done((bf16[2,80,384]{2,1,0:T(8,128)(2,1)S(1)}, bf16[2,80,384]{2,1,0:T(8,128)(2,1)S(1)}, u32[]{:S(2)}, u32[]{:S(2)}) %collective-permute-start.1) | collective-permute-done | bytes 122912 | tf_op jit(solution)/shard_map/ppermute | solution.py:48
  21.0 1.6 %collective-permute-start.4 = (bf16[4,80,384]{2,1,0:T(8,128)(2,1)S(1)}, bf16[4,80,384]{2,1,0:T(8,128)(2,1)S(1)}, u32[]{:S(2)}, u32[]{:S(2)}) collective-permute-start(bf16[4,80,384]{2,1,0:T(8,128)(2,1)S(1)} %pad_maximum_fusion.5.w_own), channel_id=1, source_target_pairs={{0,4},{4,0},{8,12},{12,8},{16,20},{20,16},{24,28},{28,24},{1,5},{5... | collective-permute-start | bytes 737288 | tf_op jit(solution)/shard_map/ppermute | solution.py:48
  22.6 4.7 %collective-permute-done.3 = bf16[2,64,1152]{2,1,0:T(8,128)(2,1)S(1)} collective-permute-done((bf16[2,64,1152]{2,1,0:T(8,128)(2,1)S(1)}, bf16[2,64,1152]{2,1,0:T(8,128)(2,1)S(1)}, u32[]{:S(2)}, u32[]{:S(2)}) %collective-permute-start.3) | collective-permute-done | bytes 294944 | tf_op jit(solution)/shard_map/ppermute | solution.py:48
  27.9 1.6 %collective-permute-start.8 = (bf16[4,64,512]{2,1,0:T(8,128)(2,1)S(1)}, bf16[4,64,512]{2,1,0:T(8,128)(2,1)S(1)}, u32[]{:S(2)}, u32[]{:S(2)}) collective-permute-start(bf16[4,64,512]{2,1,0:T(8,128)(2,1)S(1)} %pad_maximum_fusion.4), channel_id=1, source_target_pairs={{0,4},{4,0},{8,12},{12,8},{16,20},{20,16},{24,28},{28,24},{1,5},{5... | collective-permute-start | bytes 786440 | tf_op jit(solution)/shard_map/ppermute | solution.py:48
  29.5 2.0 %shard_map.447 = (bf16[2048,128]{1,0:T(8,128)(2,1)S(1)}, bf16[2048,128]{1,0:T(8,128)(2,1)S(1)}, bf16[2048,128]{1,0:T(8,128)(2,1)S(1)}, bf16[144,2048]{1,0:T(8,12...) custom-call(s32[2]{0:T(128)S(1)} %pad_add_fusion.idx_ref, ...), custom_call_target="tpu_custom_call" | custom-call | flops 4000000000 | bytes 1048576 | tf_op jit(solution)/shard_map/pallas_call | solution.py:610
  31.6 4.4 %collective-permute-done.9 = bf16[4,64,640]{2,1,0:T(8,128)(2,1)S(1)} collective-permute-done((bf16[4,64,640]{2,1,0:T(8,128)(2,1)S(1)}, bf16[4,64,640]{2,1,0:T(8,128)(2,1)S(1)}, u32[]{:S(2)}, u32[]{:S(2)}) %collective-permute-start.9) | collective-permute-done | bytes 327712 | tf_op jit(solution)/shard_map/ppermute | solution.py:48
  36.7 1.5 %collective-permute-start.17 = (bf16[8,64,640]{2,1,0:T(8,128)(2,1)S(1)}, bf16[8,64,640]{2,1,0:T(8,128)(2,1)S(1)}, u32[]{:S(2)}, u32[]{:S(2)}) collective-permute-start(bf16[8,64,640]{2,1,0:T(8,128)(2,1)S(1)} %pad_maximum_fusion.refs_8_), channel_id=1, source_target_pairs={{0,4},{4,0},{8,12},{12,8},{16,20},{20,16},{24,28},{28,24},{1,5},{5... | collective-permute-start | bytes 1966088 | tf_op jit(solution)/shard_map/ppermute | solution.py:48
  38.7 4.9 %shard_map.448 = (bf16[528,128]{1,0:T(8,128)(2,1)S(1)}, bf16[528,128]{1,0:T(8,128)(2,1)S(1)}, f32[4,8,512]{2,1,0:T(8,128)S(1)}) custom-call(s32[2]{0:T(128)S(1)} %pad_add_fusion.idx_ref, s32[1,2048]{1,0:T(1,128)S(1)} %copy-done.19, bf16[2048,128]{1,0:T(8,128)(2,1)S(1)} %get-tuple-element.119.q_ref, bf16[2048,128]{1,0:T(8,128)(2,1)S(1)} %get-tuple-element.115.k_ref, ...), custom_call_target="tpu_custom_call" | custom-call | flops 1000000000 | bytes 1048576 | tf_op jit(solution)/shard_map/pallas_call | solution.py:610
  43.6 0.8 collective-permute-start.13
  44.7 4.3 %shard_map.449 = (bf16[528,128]{1,0:T(8,128)(2,1)S(1)}, bf16[528,128]{1,0:T(8,128)(2,1)S(1)}, f32[4,8,512]{2,1,0:T(8,128)S(1)}) custom-call(s32[2]{0:T(128)S(1)} %pad_add_fusion.idx_ref, s32[1,2048]{1,0:T(1,128)S(1)} %copy-done.19, bf16[2048,128]{1,0:T(8,128)(2,1)S(1)} %get-tuple-element.119.q_ref, bf16[2048,128]{1,0:T(8,128)(2,1)S(1)} %get-tuple-element.115.k_ref, ...), custom_call_target="tpu_custom_call" | custom-call | flops 1000000000 | bytes 1048576 | tf_op jit(solution)/shard_map/pallas_call | solution.py:610
  49.0 6.9 %collective-permute-done.13.refs_2_ = bf16[528,128]{1,0:T(8,128)(2,1)S(1)} collective-permute-done((bf16[528,128]{1,0:T(8,128)(2,1)S(1)}, bf16[528,128]{1,0:T(8,128)(2,1)S(1)}, u32[]{:S(2)}, u32[]{:S(2)}) %collective-permute-start.13) | collective-permute-done | bytes 135200 | tf_op jit(solution)/shard_map/ppermute | solution.py:750
  56.4 1.0 collective-permute-start.18
  58.0 2.2 %collective-permute-done.12.refs_1_ = bf16[528,128]{1,0:T(8,128)(2,1)S(1)} collective-permute-done((bf16[528,128]{1,0:T(8,128)(2,1)S(1)}, bf16[528,128]{1,0:T(8,128)(2,1)S(1)}, u32[]{:S(2)}, u32[]{:S(2)}) %collective-permute-start.12) | collective-permute-done | bytes 135200 | tf_op jit(solution)/shard_map/ppermute | solution.py:750
  60.2 11.4 %shard_map.450 = (f32[512,512]{1,0:T(8,128)}, f32[512,512]{1,0:T(8,128)}, f32[512,512]{1,0:T(8,128)S(1)}, bf16[512,128]{1,0:T(8,128)(2,1)S(1)}, bf16[512,128]{1,...) custom-call(s32[2]{0:T(128)S(1)} %pad_add_fusion.idx_ref, ...), custom_call_target="tpu_custom_call" | custom-call | flops 20000000000 | bytes 1048576 | tf_op jit(solution)/shard_map/pallas_call | solution.py:610
  72.9 1.0 collective-permute-start.23
  75.2 0.8 collective-permute-done.20
  76.5 1.2 collective-permute-start.25
  77.7 1.0 collective-permute-done.22.refs_2_
  78.8 1.2 collective-permute-done.23.refs_3_
  79.9 12.0 %shard_map.451 = (bf16[2048,384]{1,0:T(8,128)(2,1)S(1)}, f32[48,128]{1,0:T(8,128)S(1)}) custom-call(s32[2]{0:T(128)S(1)} %pad_add_fusion.idx_ref, s32[1,2048]{1,0:T(1,128)S(1)} %copy-done.19, bf16[2048,128]{1,0:T(8,128)(2,1)S(1)} %get-tuple-element.119.q_ref, bf16[2048,128]{1,0:T(8,128)(2,1)S(1)} %get-tuple-element.115.k_ref, ...), custom_call_target="tpu_custom_call" | custom-call | flops 15000000512 | bytes 1048576 | tf_op jit(solution)/shard_map/pallas_call | solution.py:610
  92.7 0.9 collective-permute-done.25
  93.8 1.7 %collective-permute-start.28 = (bf16[4,64,640]{2,1,0:T(8,128)(2,1)S(1)}, bf16[4,64,640]{2,1,0:T(8,128)(2,1)S(1)}, u32[]{:S(2)}, u32[]{:S(2)}) collective-permute-start(bf16[4,64,640]{2,1,0:T(8,128)(2,1)S(1)} %slice.135), channel_id=1, source_target_pairs={{0,4},{4,0},{8,12},{12,8},{16,20},{20,16},{24,28},{28,24},{1,5},{5... | collective-permute-start | bytes 983048 | tf_op jit(solution)/shard_map/ppermute | solution.py:48
  95.5 1.9 %shard_map.452 = bf16[8,64,384]{2,1,0:T(8,128)(2,1)S(1)} custom-call(s32[2]{0:T(128)S(1)} %pad_add_fusion.idx_ref, bf16[2048,384]{1,0:T(8,128)(2,1)S(1)} %get-tuple-element.145.gqkv_ref, bf16[512,512]{1,0:T(8,128)(2,1)S(1)} %convert_element_type.123.refs_0_, bf16[512,512]{1,0:T(8,128)(2,1)S(1)} %collective-permute-done.5.refs_1_, ...), custom_call_target="tpu_custom_call" | custom-call | flops 2000000000 | bytes 1048576 | tf_op jit(solution)/shard_map/pallas_call | solution.py:610
  97.4 1.8 %shard_map.453 = (bf16[512,512]{1,0:T(8,128)(2,1)S(1)}, bf16[512,512]{1,0:T(8,128)(2,1)S(1)}, bf16[512,512]{1,0:T(8,128)(2,1)S(1)}, bf16[512,512]{1,0:T(8,128)(2,1)S(1)}) custom-call(s32[2]{0:T(128)S(1)} %pad_add_fusion.idx_ref, bf16[2048,384]{1,0:T(8,128)(2,1)S(1)} %get-tuple-element.145.gqkv_ref, bf16[512,384]{1,0:T(8,128)(2,1)S(1)} %get-tuple-element.146.wg_ref), custom_call_target="tpu_custom_call" | custom-call | flops 2000000000 | bytes 1048576 | tf_op jit(solution)/shard_map/pallas_call | solution.py:610
  99.7 1.1 collective-permute-start.26
  101.4 3.2 %collective-permute-start.32 = (bf16[2,64,512]{2,1,0:T(8,128)(2,1)S(1)}, bf16[2,64,512]{2,1,0:T(8,128)(2,1)S(1)}, u32[]{:S(2)}, u32[]{:S(2)}) collective-permute-start(bf16[2,64,512]{2,1,0:T(8,128)(2,1)S(1)} %slice.140), channel_id=1, source_target_pairs={{0,8},{4,12},{8,0},{12,4},{16,24},{20,28},{24,16},{28,20},{1,9},{5... | collective-permute-start | bytes 393224 | tf_op jit(solution)/shard_map/ppermute | solution.py:48
  104.7 1.0 collective-permute-start.31
  105.9 1.1 collective-permute-start.34
  107.5 0.8 collective-permute-start.30
  108.3 1.1 collective-permute-done.32
  109.5 3.2 %collective-permute-start.36 = (bf16[1,64,512]{2,1,0:T(8,128)(2,1)S(1)}, bf16[1,64,512]{2,1,0:T(8,128)(2,1)S(1)}, u32[]{:S(2)}, u32[]{:S(2)}) collective-permute-start(bf16[1,64,512]{2,1,0:T(8,128)(2,1)S(1)} %get-tuple-element.191), channel_id=1, source_target_pairs={{0,16},{4,20},{8,24},{12,28},{16,0},{20,4},{24,8},{28,12},{1,17},{... | collective-permute-start | bytes 196616 | tf_op jit(solution)/shard_map/ppermute | solution.py:48
  112.7 2.6 %collective-permute-start.37 = (bf16[1,64,640]{2,1,0:T(8,128)(2,1)S(1)}, bf16[1,64,640]{2,1,0:T(8,128)(2,1)S(1)}, u32[]{:S(2)}, u32[]{:S(2)}) collective-permute-start(bf16[1,64,640]{2,1,0:T(8,128)(2,1)S(1)} %get-tuple-element.189), channel_id=1, source_target_pairs={{0,16},{4,20},{8,24},{12,28},{16,0},{20,4},{24,8},{28,12},{1,17},{... | collective-permute-start | bytes 245768 | tf_op jit(solution)/shard_map/ppermute | solution.py:48
  116.6 4.1 %collective-permute-done.37.refs_5_.refs_9_ = bf16[1,64,640]{2,1,0:T(8,128)(2,1)S(1)} collective-permute-done((bf16[1,64,640]{2,1,0:T(8,128)(2,1)S(1)}, bf16[1,64,640]{2,1,0:T(8,128)(2,1)S(1)}, u32[]{:S(2)}, u32[]{:S(2)}) %collective-permute-start.37) | collective-permute-done | bytes 81952 | tf_op jit(solution)/shard_map/ppermute | solution.py:48
  120.7 1.1 collective-permute-done.35.refs_1_.refs_5_
  121.9 1.2 collective-permute-done.38
  123.7 2.0 %collective-permute-start.40 = (f32[56,128]{1,0:T(8,128)S(1)}, f32[56,128]{1,0:T(8,128)S(1)}, u32[]{:S(2)}, u32[]{:S(2)}) collective-permute-start(f32[56,128]{1,0:T(8,128)S(1)} %add.70), channel_id=1, source_target_pairs={{0,4},{4,0},{8,12},{12,8},{16,20},{20,16},{24,28},{28,24},{1,5},{5... | collective-permute-start | bytes 86024 | tf_op jit(solution)/shard_map/ppermute | solution.py:48
  125.7 0.9 collective-permute-start.41
  126.7 1.3 convert_add_fusion
  128.0 2.5 %collective-permute-done.41 = f32[56,128]{1,0:T(8,128)S(1)} collective-permute-done((f32[56,128]{1,0:T(8,128)S(1)}, f32[56,128]{1,0:T(8,128)S(1)}, u32[]{:S(2)}, u32[]{:S(2)}) %collective-permute-start.41) | collective-permute-done | bytes 28704 | tf_op jit(solution)/shard_map/ppermute | solution.py:91
  131.1 3.4 %collective-permute-start.43 = (f32[56,128]{1,0:T(8,128)S(1)}, f32[56,128]{1,0:T(8,128)S(1)}, u32[]{:S(2)}, u32[]{:S(2)}) collective-permute-start(f32[56,128]{1,0:T(8,128)S(1)} %add_add_fusion.refs_0_), channel_id=1, source_target_pairs={{0,16},{4,20},{8,24},{12,28},{16,0},{20,4},{24,8},{28,12},{1,17},{... | collective-permute-start | bytes 86024 | tf_op jit(solution)/shard_map/ppermute | solution.py:48
  136.3 3.8 %collective-permute-done.44.refs_3_ = f32[56,128]{1,0:T(8,128)S(1)} collective-permute-done((f32[56,128]{1,0:T(8,128)S(1)}, f32[56,128]{1,0:T(8,128)S(1)}, u32[]{:S(2)}, u32[]{:S(2)}) %collective-permute-start.44) | collective-permute-done | bytes 28704 | tf_op jit(solution)/shard_map/ppermute | solution.py:91
  140.2 2.0 %shard_map.455 = (f32[1]{0:T(128)}, f32[6,512]{1,0:T(8,128)}, f32[64,384]{1,0:T(8,128)}, f32[64,384]{1,0:T(8,128)}, f32[64,384]{1,0:T(8,128)}, /*index=5*/bf16[6...) custom-call(s32[2]{0:T(128)S(1)} %pad_add_fusion.idx_ref, ...), custom_call_target="tpu_custom_call" | custom-call | flops 2000000000 | bytes 1048576 | tf_op jit(solution)/shard_map/pallas_call | solution.py:610
  (143 shorter events, 14.4 us)
Async XLA Ops:
  2.1 17.0 %collective-permute-start.6 = (bf16[512,512]{1,0:T(8,128)(2,1)S(1)}, bf16[512,512]{1,0:T(8,128)(2,1)S(1)}, u32[]{:S(2)}, u32[]{:S(2)}) collective-permute-start(bf16[512,512]{1,0:T(8,128)(2,1)S(1)} %convert_element_type.123.refs_0_), channel_id=1, source_target_pairs={{0,2},{1,3},{2,0},{3,1},{4,6},{5,7},{6,4},{7,5},{8,10},{9,11},{10,... | collective-permute-start | bytes 1572872 | tf_op jit(solution)/shard_map/ppermute | solution.py:48
  5.1 24.4 %collective-permute-start.5 = (bf16[512,512]{1,0:T(8,128)(2,1)S(1)}, bf16[512,512]{1,0:T(8,128)(2,1)S(1)}, u32[]{:S(2)}, u32[]{:S(2)}) collective-permute-start(bf16[512,512]{1,0:T(8,128)(2,1)S(1)} %convert_element_type.123.refs_0_), channel_id=1, source_target_pairs={{0,1},{1,0},{2,3},{3,2},{4,5},{5,4},{6,7},{7,6},{8,9},{9,8},{10,11... | collective-permute-start | bytes 1572872 | tf_op jit(solution)/shard_map/ppermute | solution.py:48
  5.3 6.8 %collective-permute-start = (bf16[1,80,384]{2,1,0:T(8,128)(2,1)S(1)}, bf16[1,80,384]{2,1,0:T(8,128)(2,1)S(1)}, u32[]{:S(2)}, u32[]{:S(2)}) collective-permute-start(bf16[1,80,384]{2,1,0:T(8,128)(2,1)S(1)} %fusion.4), channel_id=1, source_target_pairs={{0,16},{4,20},{8,24},{12,28},{16,0},{20,4},{24,8},{28,12},{1,17},{... | collective-permute-start | bytes 184328 | tf_op jit(solution)/shard_map/ppermute | solution.py:48
  8.0 10.4 %collective-permute-start.2 = (bf16[1,64,1152]{2,1,0:T(8,128)(2,1)S(1)}, bf16[1,64,1152]{2,1,0:T(8,128)(2,1)S(1)}, u32[]{:S(2)}, u32[]{:S(2)}) collective-permute-start(bf16[1,64,1152]{2,1,0:T(8,128)(2,1)S(1)} %maximum_bitcast_fusion), channel_id=1, source_target_pairs={{0,16},{4,20},{8,24},{12,28},{16,0},{20,4},{24,8},{28,12},{1,17},{... | collective-permute-start | bytes 442376 | tf_op jit(solution)/shard_map/ppermute | solution.py:48
  12.1 8.9 %collective-permute-start.1 = (bf16[2,80,384]{2,1,0:T(8,128)(2,1)S(1)}, bf16[2,80,384]{2,1,0:T(8,128)(2,1)S(1)}, u32[]{:S(2)}, u32[]{:S(2)}) collective-permute-start(bf16[2,80,384]{2,1,0:T(8,128)(2,1)S(1)} %pad_maximum_fusion.6), channel_id=1, source_target_pairs={{0,8},{4,12},{8,0},{12,4},{16,24},{20,28},{24,16},{28,20},{1,9},{5... | collective-permute-start | bytes 368648 | tf_op jit(solution)/shard_map/ppermute | solution.py:48
  18.4 8.8 %collective-permute-start.3 = (bf16[2,64,1152]{2,1,0:T(8,128)(2,1)S(1)}, bf16[2,64,1152]{2,1,0:T(8,128)(2,1)S(1)}, u32[]{:S(2)}, u32[]{:S(2)}) collective-permute-start(bf16[2,64,1152]{2,1,0:T(8,128)(2,1)S(1)} %pad_maximum_fusion.2), channel_id=1, source_target_pairs={{0,8},{4,12},{8,0},{12,4},{16,24},{20,28},{24,16},{28,20},{1,9},{5... | collective-permute-start | bytes 884744 | tf_op jit(solution)/shard_map/ppermute | solution.py:48
  19.1 10.4 %collective-permute-start.7 = (bf16[512,512]{1,0:T(8,128)(2,1)S(1)}, bf16[512,512]{1,0:T(8,128)(2,1)S(1)}, u32[]{:S(2)}, u32[]{:S(2)}) collective-permute-start(bf16[512,512]{1,0:T(8,128)(2,1)S(1)} %collective-permute-done.6.refs_2_), channel_id=1, source_target_pairs={{0,1},{1,0},{2,3},{3,2},{4,5},{5,4},{6,7},{7,6},{8,9},{9,8},{10,11... | collective-permute-start | bytes 1572872 | tf_op jit(solution)/shard_map/ppermute | solution.py:48
  21.0 8.5 %collective-permute-start.4 = (bf16[4,80,384]{2,1,0:T(8,128)(2,1)S(1)}, bf16[4,80,384]{2,1,0:T(8,128)(2,1)S(1)}, u32[]{:S(2)}, u32[]{:S(2)}) collective-permute-start(bf16[4,80,384]{2,1,0:T(8,128)(2,1)S(1)} %pad_maximum_fusion.5.w_own), channel_id=1, source_target_pairs={{0,4},{4,0},{8,12},{12,8},{16,20},{20,16},{24,28},{28,24},{1,5},{5... | collective-permute-start | bytes 737288 | tf_op jit(solution)/shard_map/ppermute | solution.py:48
  27.3 8.6 %collective-permute-start.9 = (bf16[4,64,640]{2,1,0:T(8,128)(2,1)S(1)}, bf16[4,64,640]{2,1,0:T(8,128)(2,1)S(1)}, u32[]{:S(2)}, u32[]{:S(2)}) collective-permute-start(bf16[4,64,640]{2,1,0:T(8,128)(2,1)S(1)} %pad_maximum_fusion.3), channel_id=1, source_target_pairs={{0,2},{1,3},{2,0},{3,1},{4,6},{5,7},{6,4},{7,5},{8,10},{9,11},{10,... | collective-permute-start | bytes 983048 | tf_op jit(solution)/shard_map/ppermute | solution.py:48
  27.9 8.1 %collective-permute-start.8 = (bf16[4,64,512]{2,1,0:T(8,128)(2,1)S(1)}, bf16[4,64,512]{2,1,0:T(8,128)(2,1)S(1)}, u32[]{:S(2)}, u32[]{:S(2)}) collective-permute-start(bf16[4,64,512]{2,1,0:T(8,128)(2,1)S(1)} %pad_maximum_fusion.4), channel_id=1, source_target_pairs={{0,4},{4,0},{8,12},{12,8},{16,20},{20,16},{24,28},{28,24},{1,5},{5... | collective-permute-start | bytes 786440 | tf_op jit(solution)/shard_map/ppermute | solution.py:48
  36.0 8.6 %collective-permute-start.11 = (bf16[8,64,640]{2,1,0:T(8,128)(2,1)S(1)}, bf16[8,64,640]{2,1,0:T(8,128)(2,1)S(1)}, u32[]{:S(2)}, u32[]{:S(2)}) collective-permute-start(bf16[8,64,640]{2,1,0:T(8,128)(2,1)S(1)} %pad_maximum_fusion.refs_8_), channel_id=1, source_target_pairs={{0,1},{1,0},{2,3},{3,2},{4,5},{5,4},{6,7},{7,6},{8,9},{9,8},{10,11... | collective-permute-start | bytes 1966088 | tf_op jit(solution)/shard_map/ppermute | solution.py:48
  36.2 8.3 %collective-permute-start.10 = (bf16[8,64,512]{2,1,0:T(8,128)(2,1)S(1)}, bf16[8,64,512]{2,1,0:T(8,128)(2,1)S(1)}, u32[]{:S(2)}, u32[]{:S(2)}) collective-permute-start(bf16[8,64,512]{2,1,0:T(8,128)(2,1)S(1)} %pad_maximum_fusion.1.refs_4_), channel_id=1, source_target_pairs={{0,1},{1,0},{2,3},{3,2},{4,5},{5,4},{6,7},{7,6},{8,9},{9,8},{10,11... | collective-permute-start | bytes 1572872 | tf_op jit(solution)/shard_map/ppermute | solution.py:48
  36.7 19.7 %collective-permute-start.17 = (bf16[8,64,640]{2,1,0:T(8,128)(2,1)S(1)}, bf16[8,64,640]{2,1,0:T(8,128)(2,1)S(1)}, u32[]{:S(2)}, u32[]{:S(2)}) collective-permute-start(bf16[8,64,640]{2,1,0:T(8,128)(2,1)S(1)} %pad_maximum_fusion.refs_8_), channel_id=1, source_target_pairs={{0,4},{4,0},{8,12},{12,8},{16,20},{20,16},{24,28},{28,24},{1,5},{5... | collective-permute-start | bytes 1966088 | tf_op jit(solution)/shard_map/ppermute | solution.py:48
  38.2 19.2 %collective-permute-start.15 = (bf16[8,64,512]{2,1,0:T(8,128)(2,1)S(1)}, bf16[8,64,512]{2,1,0:T(8,128)(2,1)S(1)}, u32[]{:S(2)}, u32[]{:S(2)}) collective-permute-start(bf16[8,64,512]{2,1,0:T(8,128)(2,1)S(1)} %pad_maximum_fusion.1.refs_4_), channel_id=1, source_target_pairs={{0,2},{1,3},{2,0},{3,1},{4,6},{5,7},{6,4},{7,5},{8,10},{9,11},{10,... | collective-permute-start | bytes 1572872 | tf_op jit(solution)/shard_map/ppermute | solution.py:48
  38.7 21.4 %copy-start.7 = (f32[512,512]{1,0:T(8,128)S(1)}, f32[512,512]{1,0:T(8,128)}, u32[]{:S(2)}) copy-start(f32[512,512]{1,0:T(8,128)} %refs_15_.2) | copy-start | bytes 3145732
  43.6 12.3 %collective-permute-start.13 = (bf16[528,128]{1,0:T(8,128)(2,1)S(1)}, bf16[528,128]{1,0:T(8,128)(2,1)S(1)}, u32[]{:S(2)}, u32[]{:S(2)}) collective-permute-start(bf16[528,128]{1,0:T(8,128)(2,1)S(1)} %get-tuple-element.118.refs_6_), channel_id=1, source_target_pairs={{0,2},{1,3},{2,0},{3,1},{4,6},{5,7},{6,4},{7,5},{8,10},{9,11},{10,... | collective-permute-start | bytes 405512 | tf_op jit(solution)/shard_map/ppermute | solution.py:750
  44.5 15.7 %copy-start.6 = (f32[512,512]{1,0:T(8,128)S(1)}, f32[512,512]{1,0:T(8,128)}, u32[]{:S(2)}) copy-start(f32[512,512]{1,0:T(8,128)} %refs_14_.2) | copy-start | bytes 3145732
  44.5 15.7 %copy-start.16 = (f32[6,512]{1,0:T(8,128)S(1)}, f32[6,512]{1,0:T(8,128)}, u32[]{:S(2)}) copy-start(f32[6,512]{1,0:T(8,128)} %refs_15_.3) | copy-start | bytes 36868
  44.5 11.9 %collective-permute-start.14 = (bf16[528,128]{1,0:T(8,128)(2,1)S(1)}, bf16[528,128]{1,0:T(8,128)(2,1)S(1)}, u32[]{:S(2)}, u32[]{:S(2)}) collective-permute-start(bf16[528,128]{1,0:T(8,128)(2,1)S(1)} %get-tuple-element.122.refs_7_), channel_id=1, source_target_pairs={{0,3},{1,2},{2,1},{3,0},{4,7},{5,6},{6,5},{7,4},{8,11},{9,10},{10,... | collective-permute-start | bytes 405512 | tf_op jit(solution)/shard_map/ppermute | solution.py:750
  56.4 3.7 %collective-permute-start.18 = (bf16[8,64,640]{2,1,0:T(8,128)(2,1)S(1)}, bf16[8,64,640]{2,1,0:T(8,128)(2,1)S(1)}, u32[]{:S(2)}, u32[]{:S(2)}) collective-permute-start(bf16[8,64,640]{2,1,0:T(8,128)(2,1)S(1)} %collective-permute-done.17.refs_9_), channel_id=1, source_target_pairs={{0,1},{1,0},{2,3},{3,2},{4,5},{5,4},{6,7},{7,6},{8,9},{9,8},{10,11... | collective-permute-start | bytes 1966088 | tf_op jit(solution)/shard_map/ppermute | solution.py:48
  57.4 2.7 %collective-permute-start.16 = (bf16[8,64,512]{2,1,0:T(8,128)(2,1)S(1)}, bf16[8,64,512]{2,1,0:T(8,128)(2,1)S(1)}, u32[]{:S(2)}, u32[]{:S(2)}) collective-permute-start(bf16[8,64,512]{2,1,0:T(8,128)(2,1)S(1)} %collective-permute-done.15.refs_5_), channel_id=1, source_target_pairs={{0,1},{1,0},{2,3},{3,2},{4,5},{5,4},{6,7},{7,6},{8,9},{9,8},{10,11... | collective-permute-start | bytes 1572872 | tf_op jit(solution)/shard_map/ppermute | solution.py:48
  57.5 2.6 %collective-permute-start.12 = (bf16[528,128]{1,0:T(8,128)(2,1)S(1)}, bf16[528,128]{1,0:T(8,128)(2,1)S(1)}, u32[]{:S(2)}, u32[]{:S(2)}) collective-permute-start(bf16[528,128]{1,0:T(8,128)(2,1)S(1)} %get-tuple-element.121.refs_5_), channel_id=1, source_target_pairs={{0,1},{1,0},{2,3},{3,2},{4,5},{5,4},{6,7},{7,6},{8,9},{9,8},{10,11... | collective-permute-start | bytes 405512 | tf_op jit(solution)/shard_map/ppermute | solution.py:750
  71.5 2.7 %collective-permute-start.19 = (bf16[16,64,512]{2,1,0:T(8,128)(2,1)S(1)}, bf16[16,64,512]{2,1,0:T(8,128)(2,1)S(1)}, u32[]{:S(2)}, u32[]{:S(2)}) collective-permute-start(bf16[16,64,512]{2,1,0:T(8,128)(2,1)S(1)} %get-tuple-element.134), channel_id=1, source_target_pairs={{0,1},{1,0},{2,3},{3,2},{4,5},{5,4},{6,7},{7,6},{8,9},{9,8},{10,11... | collective-permute-start | bytes 3145736 | tf_op jit(solution)/shard_map/ppermute | solution.py:48
  71.9 4.2 %collective-permute-start.20 = (bf16[16,64,640]{2,1,0:T(8,128)(2,1)S(1)}, bf16[16,64,640]{2,1,0:T(8,128)(2,1)S(1)}, u32[]{:S(2)}, u32[]{:S(2)}) collective-permute-start(bf16[16,64,640]{2,1,0:T(8,128)(2,1)S(1)} %get-tuple-element.136), channel_id=1, source_target_pairs={{0,1},{1,0},{2,3},{3,2},{4,5},{5,4},{6,7},{7,6},{8,9},{9,8},{10,11... | collective-permute-start | bytes 3932168 | tf_op jit(solution)/shard_map/ppermute | solution.py:48
  72.0 5.7 %collective-permute-start.21 = (bf16[512,128]{1,0:T(8,128)(2,1)S(1)}, bf16[512,128]{1,0:T(8,128)(2,1)S(1)}, u32[]{:S(2)}, u32[]{:S(2)}) collective-permute-start(bf16[512,128]{1,0:T(8,128)(2,1)S(1)} %get-tuple-element.138), channel_id=1, source_target_pairs={{0,1},{1,0},{2,3},{3,2},{4,5},{5,4},{6,7},{7,6},{8,9},{9,8},{10,11... | collective-permute-start | bytes 393224 | tf_op jit(solution)/shard_map/ppermute | solution.py:795
  72.4 6.4 %collective-permute-start.22 = (bf16[512,128]{1,0:T(8,128)(2,1)S(1)}, bf16[512,128]{1,0:T(8,128)(2,1)S(1)}, u32[]{:S(2)}, u32[]{:S(2)}) collective-permute-start(bf16[512,128]{1,0:T(8,128)(2,1)S(1)} %get-tuple-element.139), channel_id=1, source_target_pairs={{0,2},{1,3},{2,0},{3,1},{4,6},{5,7},{6,4},{7,5},{8,10},{9,11},{10,... | collective-permute-start | bytes 393224 | tf_op jit(solution)/shard_map/ppermute | solution.py:795
  72.9 7.0 %collective-permute-start.23 = (bf16[512,128]{1,0:T(8,128)(2,1)S(1)}, bf16[512,128]{1,0:T(8,128)(2,1)S(1)}, u32[]{:S(2)}, u32[]{:S(2)}) collective-permute-start(bf16[512,128]{1,0:T(8,128)(2,1)S(1)} %get-tuple-element.140), channel_id=1, source_target_pairs={{0,3},{1,2},{2,1},{3,0},{4,7},{5,6},{6,5},{7,4},{8,11},{9,10},{10,... | collective-permute-start | bytes 393224 | tf_op jit(solution)/shard_map/ppermute | solution.py:795
  74.6 17.3 %collective-permute-start.24 = (bf16[8,64,512]{2,1,0:T(8,128)(2,1)S(1)}, bf16[8,64,512]{2,1,0:T(8,128)(2,1)S(1)}, u32[]{:S(2)}, u32[]{:S(2)}) collective-permute-start(bf16[8,64,512]{2,1,0:T(8,128)(2,1)S(1)} %slice.130), channel_id=1, source_target_pairs={{0,4},{4,0},{8,12},{12,8},{16,20},{20,16},{24,28},{28,24},{1,5},{5... | collective-permute-start | bytes 1572872 | tf_op jit(solution)/shard_map/ppermute | solution.py:48
  76.5 17.1 %collective-permute-start.25 = (bf16[8,64,640]{2,1,0:T(8,128)(2,1)S(1)}, bf16[8,64,640]{2,1,0:T(8,128)(2,1)S(1)}, u32[]{:S(2)}, u32[]{:S(2)}) collective-permute-start(bf16[8,64,640]{2,1,0:T(8,128)(2,1)S(1)} %slice.131), channel_id=1, source_target_pairs={{0,8},{4,12},{8,0},{12,4},{16,24},{20,28},{24,16},{28,20},{1,9},{5... | collective-permute-start | bytes 1966088 | tf_op jit(solution)/shard_map/ppermute | solution.py:48
  92.1 9.2 %collective-permute-start.29 = (bf16[4,64,512]{2,1,0:T(8,128)(2,1)S(1)}, bf16[4,64,512]{2,1,0:T(8,128)(2,1)S(1)}, u32[]{:S(2)}, u32[]{:S(2)}) collective-permute-start(bf16[4,64,512]{2,1,0:T(8,128)(2,1)S(1)} %slice.133), channel_id=1, source_target_pairs={{0,2},{1,3},{2,0},{3,1},{4,6},{5,7},{6,4},{7,5},{8,10},{9,11},{10,... | collective-permute-start | bytes 786440 | tf_op jit(solution)/shard_map/ppermute | solution.py:48
  93.8 10.8 %collective-permute-start.28 = (bf16[4,64,640]{2,1,0:T(8,128)(2,1)S(1)}, bf16[4,64,640]{2,1,0:T(8,128)(2,1)S(1)}, u32[]{:S(2)}, u32[]{:S(2)}) collective-permute-start(bf16[4,64,640]{2,1,0:T(8,128)(2,1)S(1)} %slice.135), channel_id=1, source_target_pairs={{0,4},{4,0},{8,12},{12,8},{16,20},{20,16},{24,28},{28,24},{1,5},{5... | collective-permute-start | bytes 983048 | tf_op jit(solution)/shard_map/ppermute | solution.py:48
  99.2 6.5 %collective-permute-start.27 = (bf16[512,512]{1,0:T(8,128)(2,1)S(1)}, bf16[512,512]{1,0:T(8,128)(2,1)S(1)}, u32[]{:S(2)}, u32[]{:S(2)}) collective-permute-start(bf16[512,512]{1,0:T(8,128)(2,1)S(1)} %get-tuple-element.149), channel_id=1, source_target_pairs={{0,1},{1,0},{2,3},{3,2},{4,5},{5,4},{6,7},{7,6},{8,9},{9,8},{10,11... | collective-permute-start | bytes 1572872 | tf_op jit(solution)/shard_map/ppermute | solution.py:48
  99.7 7.7 %collective-permute-start.26 = (bf16[4,64,384]{2,1,0:T(8,128)(2,1)S(1)}, bf16[4,64,384]{2,1,0:T(8,128)(2,1)S(1)}, u32[]{:S(2)}, u32[]{:S(2)}) collective-permute-start(bf16[4,64,384]{2,1,0:T(8,128)(2,1)S(1)} %slice.136), channel_id=1, source_target_pairs={{0,8},{4,12},{8,0},{12,4},{16,24},{20,28},{24,16},{28,20},{1,9},{5... | collective-permute-start | bytes 589832 | tf_op jit(solution)/shard_map/ppermute | solution.py:48
  101.4 8.0 %collective-permute-start.32 = (bf16[2,64,512]{2,1,0:T(8,128)(2,1)S(1)}, bf16[2,64,512]{2,1,0:T(8,128)(2,1)S(1)}, u32[]{:S(2)}, u32[]{:S(2)}) collective-permute-start(bf16[2,64,512]{2,1,0:T(8,128)(2,1)S(1)} %slice.140), channel_id=1, source_target_pairs={{0,8},{4,12},{8,0},{12,4},{16,24},{20,28},{24,16},{28,20},{1,9},{5... | collective-permute-start | bytes 393224 | tf_op jit(solution)/shard_map/ppermute | solution.py:48
  104.6 17.3 %collective-permute-start.33 = (bf16[512,512]{1,0:T(8,128)(2,1)S(1)}, bf16[512,512]{1,0:T(8,128)(2,1)S(1)}, u32[]{:S(2)}, u32[]{:S(2)}) collective-permute-start(bf16[512,512]{1,0:T(8,128)(2,1)S(1)} %get-tuple-element.158), channel_id=1, source_target_pairs={{0,1},{1,0},{2,3},{3,2},{4,5},{5,4},{6,7},{7,6},{8,9},{9,8},{10,11... | collective-permute-start | bytes 1572872 | tf_op jit(solution)/shard_map/ppermute | solution.py:48
  104.7 7.9 %collective-permute-start.31 = (bf16[2,64,640]{2,1,0:T(8,128)(2,1)S(1)}, bf16[2,64,640]{2,1,0:T(8,128)(2,1)S(1)}, u32[]{:S(2)}, u32[]{:S(2)}) collective-permute-start(bf16[2,64,640]{2,1,0:T(8,128)(2,1)S(1)} %slice.141), channel_id=1, source_target_pairs={{0,2},{1,3},{2,0},{3,1},{4,6},{5,7},{6,4},{7,5},{8,10},{9,11},{10,... | collective-permute-start | bytes 491528 | tf_op jit(solution)/shard_map/ppermute | solution.py:48
  105.9 20.7 %collective-permute-start.34 = (bf16[512,512]{1,0:T(8,128)(2,1)S(1)}, bf16[512,512]{1,0:T(8,128)(2,1)S(1)}, u32[]{:S(2)}, u32[]{:S(2)}) collective-permute-start(bf16[512,512]{1,0:T(8,128)(2,1)S(1)} %add_convert_fusion.3), channel_id=1, source_target_pairs={{0,2},{1,3},{2,0},{3,1},{4,6},{5,7},{6,4},{7,5},{8,10},{9,11},{10,... | collective-permute-start | bytes 1572872 | tf_op jit(solution)/shard_map/ppermute | solution.py:48
  107.5 7.8 %collective-permute-start.30 = (bf16[2,64,384]{2,1,0:T(8,128)(2,1)S(1)}, bf16[2,64,384]{2,1,0:T(8,128)(2,1)S(1)}, u32[]{:S(2)}, u32[]{:S(2)}) collective-permute-start(bf16[2,64,384]{2,1,0:T(8,128)(2,1)S(1)} %slice.143), channel_id=1, source_target_pairs={{0,4},{4,0},{8,12},{12,8},{16,20},{20,16},{24,28},{28,24},{1,5},{5... | collective-permute-start | bytes 294920 | tf_op jit(solution)/shard_map/ppermute | solution.py:48
  109.5 7.1 %collective-permute-start.36 = (bf16[1,64,512]{2,1,0:T(8,128)(2,1)S(1)}, bf16[1,64,512]{2,1,0:T(8,128)(2,1)S(1)}, u32[]{:S(2)}, u32[]{:S(2)}) collective-permute-start(bf16[1,64,512]{2,1,0:T(8,128)(2,1)S(1)} %get-tuple-element.191), channel_id=1, source_target_pairs={{0,16},{4,20},{8,24},{12,28},{16,0},{20,4},{24,8},{28,12},{1,17},{... | collective-permute-start | bytes 196616 | tf_op jit(solution)/shard_map/ppermute | solution.py:48
  112.7 8.0 %collective-permute-start.37 = (bf16[1,64,640]{2,1,0:T(8,128)(2,1)S(1)}, bf16[1,64,640]{2,1,0:T(8,128)(2,1)S(1)}, u32[]{:S(2)}, u32[]{:S(2)}) collective-permute-start(bf16[1,64,640]{2,1,0:T(8,128)(2,1)S(1)} %get-tuple-element.189), channel_id=1, source_target_pairs={{0,16},{4,20},{8,24},{12,28},{16,0},{20,4},{24,8},{28,12},{1,17},{... | collective-permute-start | bytes 245768 | tf_op jit(solution)/shard_map/ppermute | solution.py:48
  115.3 6.4 %collective-permute-start.35 = (bf16[1,64,384]{2,1,0:T(8,128)(2,1)S(1)}, bf16[1,64,384]{2,1,0:T(8,128)(2,1)S(1)}, u32[]{:S(2)}, u32[]{:S(2)}) collective-permute-start(bf16[1,64,384]{2,1,0:T(8,128)(2,1)S(1)} %get-tuple-element.193), channel_id=1, source_target_pairs={{0,16},{4,20},{8,24},{12,28},{16,0},{20,4},{24,8},{28,12},{1,17},{... | collective-permute-start | bytes 147464 | tf_op jit(solution)/shard_map/ppermute | solution.py:48
  121.8 1.3 collective-permute-start.38
  123.1 4.9 %collective-permute-start.39 = (f32[56,128]{1,0:T(8,128)S(1)}, f32[56,128]{1,0:T(8,128)S(1)}, u32[]{:S(2)}, u32[]{:S(2)}) collective-permute-start(f32[56,128]{1,0:T(8,128)S(1)} %add.70), channel_id=1, source_target_pairs={{0,2},{1,3},{2,0},{3,1},{4,6},{5,7},{6,4},{7,5},{8,10},{9,11},{10,... | collective-permute-start | bytes 86024 | tf_op jit(solution)/shard_map/ppermute | solution.py:48
  123.7 4.3 %collective-permute-start.40 = (f32[56,128]{1,0:T(8,128)S(1)}, f32[56,128]{1,0:T(8,128)S(1)}, u32[]{:S(2)}, u32[]{:S(2)}) collective-permute-start(f32[56,128]{1,0:T(8,128)S(1)} %add.70), channel_id=1, source_target_pairs={{0,4},{4,0},{8,12},{12,8},{16,20},{20,16},{24,28},{28,24},{1,5},{5... | collective-permute-start | bytes 86024 | tf_op jit(solution)/shard_map/ppermute | solution.py:48
  125.7 4.8 %collective-permute-start.41 = (f32[56,128]{1,0:T(8,128)S(1)}, f32[56,128]{1,0:T(8,128)S(1)}, u32[]{:S(2)}, u32[]{:S(2)}) collective-permute-start(f32[56,128]{1,0:T(8,128)S(1)} %add.70), channel_id=1, source_target_pairs={{0,6},{1,7},{2,4},{3,5},{4,2},{5,3},{6,0},{7,1},{8,14},{9,15},{10,... | collective-permute-start | bytes 86024 | tf_op jit(solution)/shard_map/ppermute | solution.py:91
  130.5 5.1 %collective-permute-start.42 = (f32[56,128]{1,0:T(8,128)S(1)}, f32[56,128]{1,0:T(8,128)S(1)}, u32[]{:S(2)}, u32[]{:S(2)}) collective-permute-start(f32[56,128]{1,0:T(8,128)S(1)} %add_add_fusion.refs_0_), channel_id=1, source_target_pairs={{0,8},{4,12},{8,0},{12,4},{16,24},{20,28},{24,16},{28,20},{1,9},{5... | collective-permute-start | bytes 86024 | tf_op jit(solution)/shard_map/ppermute | solution.py:48
  131.1 5.2 %collective-permute-start.43 = (f32[56,128]{1,0:T(8,128)S(1)}, f32[56,128]{1,0:T(8,128)S(1)}, u32[]{:S(2)}, u32[]{:S(2)}) collective-permute-start(f32[56,128]{1,0:T(8,128)S(1)} %add_add_fusion.refs_0_), channel_id=1, source_target_pairs={{0,16},{4,20},{8,24},{12,28},{16,0},{20,4},{24,8},{28,12},{1,17},{... | collective-permute-start | bytes 86024 | tf_op jit(solution)/shard_map/ppermute | solution.py:48
  134.4 5.7 %collective-permute-start.44 = (f32[56,128]{1,0:T(8,128)S(1)}, f32[56,128]{1,0:T(8,128)S(1)}, u32[]{:S(2)}, u32[]{:S(2)}) collective-permute-start(f32[56,128]{1,0:T(8,128)S(1)} %add_add_fusion.refs_0_), channel_id=1, source_target_pairs={{0,24},{1,25},{2,26},{3,27},{4,28},{5,29},{6,30},{7,31},{8,16},{9,... | collective-permute-start | bytes 86024 | tf_op jit(solution)/shard_map/ppermute | solution.py:91
  (20 other events, 231.1 us)

commit v6 on v5

--- a/solution.py
+++ b/solution.py
@@ -138,6 +138,16 @@
     zero = jnp.zeros_like(v)
     return jnp.concatenate(
         [jnp.where((lane >= l * HD) & (lane < (l + 1) * HD), v, zero) for l in range(lh)], axis=0
+    )
+
+
+def row_mask_stack(vt, lh):
+    if lh == 1:
+        return vt
+    row = lax.broadcasted_iota(jnp.int32, vt.shape, 0)
+    zero = jnp.zeros_like(vt)
+    return jnp.concatenate(
+        [jnp.where((row >= l * HD) & (row < (l + 1) * HD), vt, zero) for l in range(lh)], axis=1
     )
 
 
@@ -439,13 +449,13 @@
     starts = starts.astype(jnp.int32)
     for qb in range(n_q):
         start_s[qb] = jnp.concatenate([starts[:, qb * TQ : (qb + 1) * TQ]] * lh, axis=1)
-        q2_s[qb] = lane_mask_stack(q_ref[qb * TQ : (qb + 1) * TQ, :], lh)
+        q2_s[qb] = row_mask_stack(q_ref[qb * TQ : (qb + 1) * TQ, :].T, lh)
     for off in range(n_h):
         lse_part, n = (lse_near, off) if off < n_h // 2 else (lse_far, off - n_h // 2)
         for i in range(rw // TQ):
             qb = (h ^ off) * (rw // TQ) + i
             do = gm[off][i * TQ : (i + 1) * TQ, :]
-            do2_s[qb] = lane_mask_stack(do, lh)
+            do2_s[qb] = row_mask_stack(do.T, lh)
             prod = (do.astype(F32) * pieces[off][i * TQ : (i + 1) * TQ, :].astype(F32)).T
             delta_s[qb] = jnp.concatenate(
                 [jnp.sum(prod[l * HD : (l + 1) * HD, :], axis=0, keepdims=True) for l in range(lh)], axis=1
@@ -459,8 +469,8 @@
 
     def products(qb, kb, slot):
         keys = pl.ds(pl.multiple_of(kb * TK, TK), TK)
-        slot[0][...] = dot(k_ref[keys, :], q2_s[qb], 1, 1)
-        slot[1][...] = dot(v_ref[keys, :], do2_s[qb], 1, 1)
+        slot[0][...] = dot(k_ref[keys, :], q2_s[qb], 1, 0)
+        slot[1][...] = dot(v_ref[keys, :], do2_s[qb], 1, 0)
 
     def gradients(qb, kb, slot, least):
         c0 = pl.multiple_of(kb * TK, TK)
@@ -469,8 +479,8 @@
         ok = (key >= start_s[qb] - c0 + least) & (key <= column + (qb * TQ - c0))
         p = jnp.exp2(jnp.where(ok, slot[0][...], NEG_LARGE) * factor - lse_s[qb])
         grad = (p * (slot[1][...] - delta_s[qb])).astype(BF)
-        dv_s[keys, :] += dot(p.astype(BF), do2_s[qb], 1, 0)
-        dk_s[keys, :] += dot(grad, q2_s[qb], 1, 0)
+        dv_s[:, keys] += dot(do2_s[qb], p.astype(BF), 1, 1)
+        dk_s[:, keys] += dot(q2_s[qb], grad, 1, 1)
         dq_s[qb] += dot(kt_s[:, keys], grad, 1, 0)
 
     products(0, 0, slots[0])
@@ -491,8 +501,8 @@
         dq = (head_rows_merge(dq_s[qb], lh) * SCORE_SCALE).T.astype(BF)
         gqkv_ref[qb * TQ : (qb + 1) * TQ, :width] = dq
         q_sum = q_sum + jnp.sum(dq.astype(F32), axis=0, keepdims=True)
-    gqkv_ref[:, width : 2 * width] = (dk_s[...] * SCORE_SCALE).astype(BF)
-    dv = dv_s[...].astype(BF)
+    gqkv_ref[:, width : 2 * width] = (dk_s[...] * SCORE_SCALE).astype(BF).T
+    dv = dv_s[...].astype(BF).T
     gqkv_ref[:, 2 * width :] = dv
     v_sum = jnp.sum(dv.astype(F32), axis=0, keepdims=True)
     small_ref[:40, :] = small_in[...]
@@ -738,11 +748,11 @@
         )
         return out[:-1], out[-1]
 
-    exchange(n_d, q)
-    far, lse_far = attend(range(n_h // 2, n_h), after(q, e_in, c_in))
+    far, lse_far = attend(range(n_h // 2, n_h), q)
+    exchange(n_d, far[0])
     early = n_d + 1 == n_s - 1
     crossed = [swap(e_in, e_steps[-1]), swap(c_in, c_steps[-1])] if early else []
-    near, lse_near = attend(range(n_h // 2), after(q, far[0], *crossed))
+    near, lse_near = attend(range(n_h // 2), after(q, far[0], e_in, c_in))
     for i in range(n_d + 1, n_s - 1):
         exchange(i, near[0])
     pieces = list(near) + list(far)
@@ -801,14 +811,14 @@
         [sds((n_rows, 3 * width), BF), sds((48, 128), F32)],
         [
             pltpu.SMEM((n_q,), jnp.int32),
-            pltpu.VMEM((n_q, cols, width), BF),
-            pltpu.VMEM((n_q, cols, width), BF),
+            pltpu.VMEM((n_q, width, cols), BF),
+            pltpu.VMEM((n_q, width, cols), BF),
             pltpu.VMEM((n_q, 1, cols), F32),
             pltpu.VMEM((n_q, 1, cols), F32),
             pltpu.VMEM((n_q, 1, cols), jnp.int32),
             pltpu.VMEM((width, n_rows), BF),
-            pltpu.VMEM((n_rows, width), F32),
-            pltpu.VMEM((n_rows, width), F32),
+            pltpu.VMEM((width, n_rows), F32),
+            pltpu.VMEM((width, n_rows), F32),
             pltpu.VMEM((n_q, width, cols), F32),
         ]
         + [pltpu.VMEM((TK, cols), F32)] * 4,

time: 143 us -> 142 us (level)
  starting transfers between devices: 47.8 us -> 42.4 us
  Pallas kernels: 40.4 us -> 43.3 us
  waiting for transfers between devices: 46.9 us -> 48.5 us
    ppermute x37, starting transfers between devices: 43.1 us -> 36.7 us  [swap(): return lax.ppermute(v, axis, [(i, i ^ bit) for i in range(count)])]
    ppermute x3, waiting for transfers between devices: 9.57 us -> 13.3 us  [per_device(): lax.ppermute(pieces[off], 'head', [(i, i ^ off) for i in range(n_h)])]
    pallas_call x9, Pallas kernels: 40.4 us -> 43.3 us  [call(): pl.pallas_call(body, out_shape=outs, in_specs=[SMEM] * n_smem + [VMEM] *...]
    ppermute x37, waiting for transfers between devices: 28.9 us -> 26.1 us  [swap(): return lax.ppermute(v, axis, [(i, i ^ bit) for i in range(count)])]
  transfers between devices with their start and end apart: 45 -> 45, of which waited for: 23 -> 20; matrix products, arithmetic and copies ran while one was open for 3% -> 3% of each run, Pallas kernels for 19% -> 21%
where the time goes in v6:
time: 142 us; the launch traced here: 141 us
  waiting for transfers between devices  48.5 us (34%)
  Pallas kernels  43.3 us (30%)
  starting transfers between devices  42.4 us (30%)
  other arithmetic  4.6 us (3%)
  between operations  2.18 us (2%)
    pallas_call x9, Pallas kernels, call(): pl.pallas_call(body, out_shape=outs, in_specs=[SMEM] * n_smem + [VMEM] *...  43.3 us
    ppermute x37, starting transfers between devices, swap(): return lax.ppermute(v, axis, [(i, i ^ bit) for i in range(count)])  36.7 us
    ppermute x37, waiting for transfers between devices, swap(): return lax.ppermute(v, axis, [(i, i ^ bit) for i in range(count)])  26.1 us
    ppermute x3, waiting for transfers between devices, per_device(): lax.ppermute(pieces[off], 'head', [(i, i ^ off) for i in range(n_h)])  13.3 us
    ppermute x2, waiting for transfers between devices, swap_both(): lax.ppermute(v, ('dp', 'head'), [(i, i ^ flip) for i in range(n_h * lax.a...  5.88 us
    ppermute x3, waiting for transfers between devices, per_device(): lax.ppermute(gm[off], 'head', [(i, i ^ off) for i in range(n_h)])  3.32 us
  transfers between devices with their start and end apart: 45, of which 20 were waited for; matrix products, arithmetic and copies ran while one was open for 3% of the time, Pallas kernels for 21%

profile of v6, /device:TPU:0, one launch (start us, length us, event | category | flops | bytes accessed | tf_op | source)
XLA Modules:
  0.0 141.5 jit_solution(13169568013221787686)
XLA Ops:
  0.7 1.4 convert_element_type.123.refs_0_
  2.1 3.0 %collective-permute-start.6 = (bf16[512,512]{1,0:T(8,128)(2,1)S(1)}, bf16[512,512]{1,0:T(8,128)(2,1)S(1)}, u32[]{:S(2)}, u32[]{:S(2)}) collective-permute-start(bf16[512,512]{1,0:T(8,128)(2,1)S(1)} %convert_element_type.123.refs_0_), channel_id=1, source_target_pairs={{0,2},{1,3},{2,0},{3,1},{4,6},{5,7},{6,4},{7,5},{8,10},{9,11},{10,... | collective-permute-start | bytes 1572872 | tf_op jit(solution)/shard_map/ppermute | solution.py:48
  5.3 2.7 %collective-permute-start = (bf16[1,80,384]{2,1,0:T(8,128)(2,1)S(1)}, bf16[1,80,384]{2,1,0:T(8,128)(2,1)S(1)}, u32[]{:S(2)}, u32[]{:S(2)}) collective-permute-start(bf16[1,80,384]{2,1,0:T(8,128)(2,1)S(1)} %fusion.4), channel_id=1, source_target_pairs={{0,16},{4,20},{8,24},{12,28},{16,0},{20,4},{24,8},{28,12},{1,17},{... | collective-permute-start | bytes 184328 | tf_op jit(solution)/shard_map/ppermute | solution.py:48
  8.5 3.6 %collective-permute-done = bf16[1,80,384]{2,1,0:T(8,128)(2,1)S(1)} collective-permute-done((bf16[1,80,384]{2,1,0:T(8,128)(2,1)S(1)}, bf16[1,80,384]{2,1,0:T(8,128)(2,1)S(1)}, u32[]{:S(2)}, u32[]{:S(2)}) %collective-permute-start) | collective-permute-done | bytes 61472 | tf_op jit(solution)/shard_map/ppermute | solution.py:48
  12.1 3.8 %collective-permute-start.1 = (bf16[2,80,384]{2,1,0:T(8,128)(2,1)S(1)}, bf16[2,80,384]{2,1,0:T(8,128)(2,1)S(1)}, u32[]{:S(2)}, u32[]{:S(2)}) collective-permute-start(bf16[2,80,384]{2,1,0:T(8,128)(2,1)S(1)} %pad_maximum_fusion.6), channel_id=1, source_target_pairs={{0,8},{4,12},{8,0},{12,4},{16,24},{20,28},{24,16},{28,20},{1,9},{5... | collective-permute-start | bytes 368648 | tf_op jit(solution)/shard_map/ppermute | solution.py:48
  15.9 2.5 %collective-permute-done.2 = bf16[1,64,1152]{2,1,0:T(8,128)(2,1)S(1)} collective-permute-done((bf16[1,64,1152]{2,1,0:T(8,128)(2,1)S(1)}, bf16[1,64,1152]{2,1,0:T(8,128)(2,1)S(1)}, u32[]{:S(2)}, u32[]{:S(2)}) %collective-permute-start.2) | collective-permute-done | bytes 147488 | tf_op jit(solution)/shard_map/ppermute | solution.py:48
  18.4 0.7 collective-permute-start.3
  19.1 1.9 %collective-permute-done.1 = bf16[2,80,384]{2,1,0:T(8,128)(2,1)S(1)} collective-permute-done((bf16[2,80,384]{2,1,0:T(8,128)(2,1)S(1)}, bf16[2,80,384]{2,1,0:T(8,128)(2,1)S(1)}, u32[]{:S(2)}, u32[]{:S(2)}) %collective-permute-start.1) | collective-permute-done | bytes 122912 | tf_op jit(solution)/shard_map/ppermute | solution.py:48
  21.0 1.6 %collective-permute-start.4 = (bf16[4,80,384]{2,1,0:T(8,128)(2,1)S(1)}, bf16[4,80,384]{2,1,0:T(8,128)(2,1)S(1)}, u32[]{:S(2)}, u32[]{:S(2)}) collective-permute-start(bf16[4,80,384]{2,1,0:T(8,128)(2,1)S(1)} %pad_maximum_fusion.5.w_own), channel_id=1, source_target_pairs={{0,4},{4,0},{8,12},{12,8},{16,20},{20,16},{24,28},{28,24},{1,5},{5... | collective-permute-start | bytes 737288 | tf_op jit(solution)/shard_map/ppermute | solution.py:48
  22.6 4.7 %collective-permute-done.3 = bf16[2,64,1152]{2,1,0:T(8,128)(2,1)S(1)} collective-permute-done((bf16[2,64,1152]{2,1,0:T(8,128)(2,1)S(1)}, bf16[2,64,1152]{2,1,0:T(8,128)(2,1)S(1)}, u32[]{:S(2)}, u32[]{:S(2)}) %collective-permute-start.3) | collective-permute-done | bytes 294944 | tf_op jit(solution)/shard_map/ppermute | solution.py:48
  27.9 1.6 %collective-permute-start.8 = (bf16[4,64,512]{2,1,0:T(8,128)(2,1)S(1)}, bf16[4,64,512]{2,1,0:T(8,128)(2,1)S(1)}, u32[]{:S(2)}, u32[]{:S(2)}) collective-permute-start(bf16[4,64,512]{2,1,0:T(8,128)(2,1)S(1)} %pad_maximum_fusion.4), channel_id=1, source_target_pairs={{0,4},{4,0},{8,12},{12,8},{16,20},{20,16},{24,28},{28,24},{1,5},{5... | collective-permute-start | bytes 786440 | tf_op jit(solution)/shard_map/ppermute | solution.py:48
  29.5 2.0 %shard_map.447 = (bf16[2048,128]{1,0:T(8,128)(2,1)S(1)}, bf16[2048,128]{1,0:T(8,128)(2,1)S(1)}, bf16[2048,128]{1,0:T(8,128)(2,1)S(1)}, bf16[144,2048]{1,0:T(8,12...) custom-call(s32[2]{0:T(128)S(1)} %pad_add_fusion.idx_ref, ...), custom_call_target="tpu_custom_call" | custom-call | flops 4000000000 | bytes 1048576 | tf_op jit(solution)/shard_map/pallas_call | solution.py:620
  31.6 6.4 %shard_map.448 = (bf16[528,128]{1,0:T(8,128)(2,1)S(1)}, bf16[528,128]{1,0:T(8,128)(2,1)S(1)}, f32[4,8,512]{2,1,0:T(8,128)S(1)}) custom-call(s32[2]{0:T(128)S(1)} %pad_add_fusion.idx_ref, s32[1,2048]{1,0:T(1,128)S(1)} %copy-done.19, bf16[2048,128]{1,0:T(8,128)(2,1)S(1)} %get-tuple-element.117.q_ref, bf16[2048,128]{1,0:T(8,128)(2,1)S(1)} %get-tuple-element.111.k_ref, ...), custom_call_target="tpu_custom_call" | custom-call | flops 1000000000 | bytes 1048576 | tf_op jit(solution)/shard_map/pallas_call | solution.py:620
  38.1 1.0 collective-permute-start.16
  39.2 2.0 %collective-permute-start.11 = (bf16[528,128]{1,0:T(8,128)(2,1)S(1)}, bf16[528,128]{1,0:T(8,128)(2,1)S(1)}, u32[]{:S(2)}, u32[]{:S(2)}) collective-permute-start(bf16[528,128]{1,0:T(8,128)(2,1)S(1)} %get-tuple-element.114.refs_6_), channel_id=1, source_target_pairs={{0,2},{1,3},{2,0},{3,1},{4,6},{5,7},{6,4},{7,5},{8,10},{9,11},{10,... | collective-permute-start | bytes 405512 | tf_op jit(solution)/shard_map/ppermute | solution.py:760
  41.5 4.3 %shard_map.449 = (bf16[528,128]{1,0:T(8,128)(2,1)S(1)}, bf16[528,128]{1,0:T(8,128)(2,1)S(1)}, f32[4,8,512]{2,1,0:T(8,128)S(1)}) custom-call(s32[2]{0:T(128)S(1)} %pad_add_fusion.idx_ref, s32[1,2048]{1,0:T(1,128)S(1)} %copy-done.19, bf16[2048,128]{1,0:T(8,128)(2,1)S(1)} %get-tuple-element.117.q_ref, bf16[2048,128]{1,0:T(8,128)(2,1)S(1)} %get-tuple-element.111.k_ref, ...), custom_call_target="tpu_custom_call" | custom-call | flops 1000000000 | bytes 1048576 | tf_op jit(solution)/shard_map/pallas_call | solution.py:620
  45.8 10.4 %collective-permute-done.11.refs_2_ = bf16[528,128]{1,0:T(8,128)(2,1)S(1)} collective-permute-done((bf16[528,128]{1,0:T(8,128)(2,1)S(1)}, bf16[528,128]{1,0:T(8,128)(2,1)S(1)}, u32[]{:S(2)}, u32[]{:S(2)}) %collective-permute-start.11) | collective-permute-done | bytes 135200 | tf_op jit(solution)/shard_map/ppermute | solution.py:760
  56.3 1.3 collective-permute-start.18
  58.0 2.9 %collective-permute-done.10.refs_1_ = bf16[528,128]{1,0:T(8,128)(2,1)S(1)} collective-permute-done((bf16[528,128]{1,0:T(8,128)(2,1)S(1)}, bf16[528,128]{1,0:T(8,128)(2,1)S(1)}, u32[]{:S(2)}, u32[]{:S(2)}) %collective-permute-start.10) | collective-permute-done | bytes 135200 | tf_op jit(solution)/shard_map/ppermute | solution.py:760
  61.0 11.3 %shard_map.450 = (f32[512,512]{1,0:T(8,128)}, f32[512,512]{1,0:T(8,128)}, f32[512,512]{1,0:T(8,128)S(1)}, bf16[512,128]{1,0:T(8,128)(2,1)S(1)}, bf16[512,128]{1,...) custom-call(s32[2]{0:T(128)S(1)} %pad_add_fusion.idx_ref, ...), custom_call_target="tpu_custom_call" | custom-call | flops 20000000000 | bytes 1048576 | tf_op jit(solution)/shard_map/pallas_call | solution.py:620
  73.5 1.2 collective-permute-start.23
  75.4 0.6 collective-permute-start.24
  76.0 0.8 collective-permute-done.20
  77.5 2.1 %collective-permute-done.22.refs_2_ = bf16[512,128]{1,0:T(8,128)(2,1)S(1)} collective-permute-done((bf16[512,128]{1,0:T(8,128)(2,1)S(1)}, bf16[512,128]{1,0:T(8,128)(2,1)S(1)}, u32[]{:S(2)}, u32[]{:S(2)}) %collective-permute-start.22) | collective-permute-done | bytes 131104 | tf_op jit(solution)/shard_map/ppermute | solution.py:805
  79.6 1.2 collective-permute-done.23.refs_3_
  80.8 13.3 %shard_map.451 = (bf16[2048,384]{1,0:T(8,128)(2,1)S(1)}, f32[48,128]{1,0:T(8,128)S(1)}) custom-call(s32[2]{0:T(128)S(1)} %pad_add_fusion.idx_ref, s32[1,2048]{1,0:T(1,128)S(1)} %copy-done.19, bf16[2048,128]{1,0:T(8,128)(2,1)S(1)} %get-tuple-element.117.q_ref, bf16[2048,128]{1,0:T(8,128)(2,1)S(1)} %get-tuple-element.111.k_ref, ...), custom_call_target="tpu_custom_call" | custom-call | flops 15000000512 | bytes 1048576 | tf_op jit(solution)/shard_map/pallas_call | solution.py:620
  95.5 1.9 %shard_map.452 = bf16[8,64,384]{2,1,0:T(8,128)(2,1)S(1)} custom-call(s32[2]{0:T(128)S(1)} %pad_add_fusion.idx_ref, bf16[2048,384]{1,0:T(8,128)(2,1)S(1)} %get-tuple-element.143.gqkv_ref, bf16[512,512]{1,0:T(8,128)(2,1)S(1)} %convert_element_type.123.refs_0_, bf16[512,512]{1,0:T(8,128)(2,1)S(1)} %collective-permute-done.5.refs_1_, ...), custom_call_target="tpu_custom_call" | custom-call | flops 2000000000 | bytes 1048576 | tf_op jit(solution)/shard_map/pallas_call | solution.py:620
  97.5 1.8 %shard_map.453 = (bf16[512,512]{1,0:T(8,128)(2,1)S(1)}, bf16[512,512]{1,0:T(8,128)(2,1)S(1)}, bf16[512,512]{1,0:T(8,128)(2,1)S(1)}, bf16[512,512]{1,0:T(8,128)(2,1)S(1)}) custom-call(s32[2]{0:T(128)S(1)} %pad_add_fusion.idx_ref, bf16[2048,384]{1,0:T(8,128)(2,1)S(1)} %get-tuple-element.143.gqkv_ref, bf16[512,384]{1,0:T(8,128)(2,1)S(1)} %get-tuple-element.144.wg_ref), custom_call_target="tpu_custom_call" | custom-call | flops 2000000000 | bytes 1048576 | tf_op jit(solution)/shard_map/pallas_call | solution.py:620
  99.7 0.9 collective-permute-start.26
  100.5 2.9 %collective-permute-done.29 = bf16[4,64,512]{2,1,0:T(8,128)(2,1)S(1)} collective-permute-done((bf16[4,64,512]{2,1,0:T(8,128)(2,1)S(1)}, bf16[4,64,512]{2,1,0:T(8,128)(2,1)S(1)}, u32[]{:S(2)}, u32[]{:S(2)}) %collective-permute-start.29) | collective-permute-done | bytes 262176 | tf_op jit(solution)/shard_map/ppermute | solution.py:48
  103.8 1.4 collective-permute-done.28
  105.3 1.8 %collective-permute-start.31 = (bf16[2,64,640]{2,1,0:T(8,128)(2,1)S(1)}, bf16[2,64,640]{2,1,0:T(8,128)(2,1)S(1)}, u32[]{:S(2)}, u32[]{:S(2)}) collective-permute-start(bf16[2,64,640]{2,1,0:T(8,128)(2,1)S(1)} %slice.141), channel_id=1, source_target_pairs={{0,2},{1,3},{2,0},{3,1},{4,6},{5,7},{6,4},{7,5},{8,10},{9,11},{10,... | collective-permute-start | bytes 491528 | tf_op jit(solution)/shard_map/ppermute | solution.py:48
  107.7 1.3 collective-permute-start.30
  109.5 2.9 %collective-permute-start.36 = (bf16[1,64,512]{2,1,0:T(8,128)(2,1)S(1)}, bf16[1,64,512]{2,1,0:T(8,128)(2,1)S(1)}, u32[]{:S(2)}, u32[]{:S(2)}) collective-permute-start(bf16[1,64,512]{2,1,0:T(8,128)(2,1)S(1)} %get-tuple-element.189), channel_id=1, source_target_pairs={{0,16},{4,20},{8,24},{12,28},{16,0},{20,4},{24,8},{28,12},{1,17},{... | collective-permute-start | bytes 196616 | tf_op jit(solution)/shard_map/ppermute | solution.py:48
  112.5 1.7 %collective-permute-start.37 = (bf16[1,64,640]{2,1,0:T(8,128)(2,1)S(1)}, bf16[1,64,640]{2,1,0:T(8,128)(2,1)S(1)}, u32[]{:S(2)}, u32[]{:S(2)}) collective-permute-start(bf16[1,64,640]{2,1,0:T(8,128)(2,1)S(1)} %get-tuple-element.187), channel_id=1, source_target_pairs={{0,16},{4,20},{8,24},{12,28},{16,0},{20,4},{24,8},{28,12},{1,17},{... | collective-permute-start | bytes 245768 | tf_op jit(solution)/shard_map/ppermute | solution.py:48
  114.3 1.4 collective-permute-start.35
  115.6 5.0 %collective-permute-done.37.refs_5_.refs_9_ = bf16[1,64,640]{2,1,0:T(8,128)(2,1)S(1)} collective-permute-done((bf16[1,64,640]{2,1,0:T(8,128)(2,1)S(1)}, bf16[1,64,640]{2,1,0:T(8,128)(2,1)S(1)}, u32[]{:S(2)}, u32[]{:S(2)}) %collective-permute-start.37) | collective-permute-done | bytes 81952 | tf_op jit(solution)/shard_map/ppermute | solution.py:48
  121.4 1.2 collective-permute-done.38
  122.6 1.6 %collective-permute-start.39 = (f32[56,128]{1,0:T(8,128)S(1)}, f32[56,128]{1,0:T(8,128)S(1)}, u32[]{:S(2)}, u32[]{:S(2)}) collective-permute-start(f32[56,128]{1,0:T(8,128)S(1)} %add.70), channel_id=1, source_target_pairs={{0,2},{1,3},{2,0},{3,1},{4,6},{5,7},{6,4},{7,5},{8,10},{9,11},{10,... | collective-permute-start | bytes 86024 | tf_op jit(solution)/shard_map/ppermute | solution.py:48
  124.2 1.2 collective-permute-start.40
  125.4 0.7 collective-permute-start.41
  126.2 1.3 convert_add_fusion
  127.4 0.6 collective-permute-done.40
  128.1 2.1 %collective-permute-done.41 = f32[56,128]{1,0:T(8,128)S(1)} collective-permute-done((f32[56,128]{1,0:T(8,128)S(1)}, f32[56,128]{1,0:T(8,128)S(1)}, u32[]{:S(2)}, u32[]{:S(2)}) %collective-permute-start.41) | collective-permute-done | bytes 28704 | tf_op jit(solution)/shard_map/ppermute | solution.py:91
  130.5 3.0 %collective-permute-start.43 = (f32[56,128]{1,0:T(8,128)S(1)}, f32[56,128]{1,0:T(8,128)S(1)}, u32[]{:S(2)}, u32[]{:S(2)}) collective-permute-start(f32[56,128]{1,0:T(8,128)S(1)} %add_add_fusion.refs_0_), channel_id=1, source_target_pairs={{0,16},{4,20},{8,24},{12,28},{16,0},{20,4},{24,8},{28,12},{1,17},{... | collective-permute-start | bytes 86024 | tf_op jit(solution)/shard_map/ppermute | solution.py:48
  133.5 1.1 collective-permute-start.44
  135.3 3.8 %collective-permute-done.44.refs_3_ = f32[56,128]{1,0:T(8,128)S(1)} collective-permute-done((f32[56,128]{1,0:T(8,128)S(1)}, f32[56,128]{1,0:T(8,128)S(1)}, u32[]{:S(2)}, u32[]{:S(2)}) %collective-permute-start.44) | collective-permute-done | bytes 28704 | tf_op jit(solution)/shard_map/ppermute | solution.py:91
  139.3 2.0 %shard_map.455 = (f32[1]{0:T(128)}, f32[6,512]{1,0:T(8,128)}, f32[64,384]{1,0:T(8,128)}, f32[64,384]{1,0:T(8,128)}, f32[64,384]{1,0:T(8,128)}, /*index=5*/bf16[6...) custom-call(s32[2]{0:T(128)S(1)} %pad_add_fusion.idx_ref, ...), custom_call_target="tpu_custom_call" | custom-call | flops 2000000000 | bytes 1048576 | tf_op jit(solution)/shard_map/pallas_call | solution.py:620
  (143 shorter events, 9.5 us)
Async XLA Ops:
  2.1 17.0 %collective-permute-start.6 = (bf16[512,512]{1,0:T(8,128)(2,1)S(1)}, bf16[512,512]{1,0:T(8,128)(2,1)S(1)}, u32[]{:S(2)}, u32[]{:S(2)}) collective-permute-start(bf16[512,512]{1,0:T(8,128)(2,1)S(1)} %convert_element_type.123.refs_0_), channel_id=1, source_target_pairs={{0,2},{1,3},{2,0},{3,1},{4,6},{5,7},{6,4},{7,5},{8,10},{9,11},{10,... | collective-permute-start | bytes 1572872 | tf_op jit(solution)/shard_map/ppermute | solution.py:48
  5.1 24.4 %collective-permute-start.5 = (bf16[512,512]{1,0:T(8,128)(2,1)S(1)}, bf16[512,512]{1,0:T(8,128)(2,1)S(1)}, u32[]{:S(2)}, u32[]{:S(2)}) collective-permute-start(bf16[512,512]{1,0:T(8,128)(2,1)S(1)} %convert_element_type.123.refs_0_), channel_id=1, source_target_pairs={{0,1},{1,0},{2,3},{3,2},{4,5},{5,4},{6,7},{7,6},{8,9},{9,8},{10,11... | collective-permute-start | bytes 1572872 | tf_op jit(solution)/shard_map/ppermute | solution.py:48
  5.3 6.8 %collective-permute-start = (bf16[1,80,384]{2,1,0:T(8,128)(2,1)S(1)}, bf16[1,80,384]{2,1,0:T(8,128)(2,1)S(1)}, u32[]{:S(2)}, u32[]{:S(2)}) collective-permute-start(bf16[1,80,384]{2,1,0:T(8,128)(2,1)S(1)} %fusion.4), channel_id=1, source_target_pairs={{0,16},{4,20},{8,24},{12,28},{16,0},{20,4},{24,8},{28,12},{1,17},{... | collective-permute-start | bytes 184328 | tf_op jit(solution)/shard_map/ppermute | solution.py:48
  8.0 10.4 %collective-permute-start.2 = (bf16[1,64,1152]{2,1,0:T(8,128)(2,1)S(1)}, bf16[1,64,1152]{2,1,0:T(8,128)(2,1)S(1)}, u32[]{:S(2)}, u32[]{:S(2)}) collective-permute-start(bf16[1,64,1152]{2,1,0:T(8,128)(2,1)S(1)} %maximum_bitcast_fusion), channel_id=1, source_target_pairs={{0,16},{4,20},{8,24},{12,28},{16,0},{20,4},{24,8},{28,12},{1,17},{... | collective-permute-start | bytes 442376 | tf_op jit(solution)/shard_map/ppermute | solution.py:48
  12.1 8.9 %collective-permute-start.1 = (bf16[2,80,384]{2,1,0:T(8,128)(2,1)S(1)}, bf16[2,80,384]{2,1,0:T(8,128)(2,1)S(1)}, u32[]{:S(2)}, u32[]{:S(2)}) collective-permute-start(bf16[2,80,384]{2,1,0:T(8,128)(2,1)S(1)} %pad_maximum_fusion.6), channel_id=1, source_target_pairs={{0,8},{4,12},{8,0},{12,4},{16,24},{20,28},{24,16},{28,20},{1,9},{5... | collective-permute-start | bytes 368648 | tf_op jit(solution)/shard_map/ppermute | solution.py:48
  18.4 8.8 %collective-permute-start.3 = (bf16[2,64,1152]{2,1,0:T(8,128)(2,1)S(1)}, bf16[2,64,1152]{2,1,0:T(8,128)(2,1)S(1)}, u32[]{:S(2)}, u32[]{:S(2)}) collective-permute-start(bf16[2,64,1152]{2,1,0:T(8,128)(2,1)S(1)} %pad_maximum_fusion.2), channel_id=1, source_target_pairs={{0,8},{4,12},{8,0},{12,4},{16,24},{20,28},{24,16},{28,20},{1,9},{5... | collective-permute-start | bytes 884744 | tf_op jit(solution)/shard_map/ppermute | solution.py:48
  19.1 10.4 %collective-permute-start.7 = (bf16[512,512]{1,0:T(8,128)(2,1)S(1)}, bf16[512,512]{1,0:T(8,128)(2,1)S(1)}, u32[]{:S(2)}, u32[]{:S(2)}) collective-permute-start(bf16[512,512]{1,0:T(8,128)(2,1)S(1)} %collective-permute-done.6.refs_2_), channel_id=1, source_target_pairs={{0,1},{1,0},{2,3},{3,2},{4,5},{5,4},{6,7},{7,6},{8,9},{9,8},{10,11... | collective-permute-start | bytes 1572872 | tf_op jit(solution)/shard_map/ppermute | solution.py:48
  21.0 8.5 %collective-permute-start.4 = (bf16[4,80,384]{2,1,0:T(8,128)(2,1)S(1)}, bf16[4,80,384]{2,1,0:T(8,128)(2,1)S(1)}, u32[]{:S(2)}, u32[]{:S(2)}) collective-permute-start(bf16[4,80,384]{2,1,0:T(8,128)(2,1)S(1)} %pad_maximum_fusion.5.w_own), channel_id=1, source_target_pairs={{0,4},{4,0},{8,12},{12,8},{16,20},{20,16},{24,28},{28,24},{1,5},{5... | collective-permute-start | bytes 737288 | tf_op jit(solution)/shard_map/ppermute | solution.py:48
  27.3 10.7 %collective-permute-start.9 = (bf16[4,64,640]{2,1,0:T(8,128)(2,1)S(1)}, bf16[4,64,640]{2,1,0:T(8,128)(2,1)S(1)}, u32[]{:S(2)}, u32[]{:S(2)}) collective-permute-start(bf16[4,64,640]{2,1,0:T(8,128)(2,1)S(1)} %pad_maximum_fusion.3), channel_id=1, source_target_pairs={{0,2},{1,3},{2,0},{3,1},{4,6},{5,7},{6,4},{7,5},{8,10},{9,11},{10,... | collective-permute-start | bytes 983048 | tf_op jit(solution)/shard_map/ppermute | solution.py:48
  27.9 11.2 %collective-permute-start.8 = (bf16[4,64,512]{2,1,0:T(8,128)(2,1)S(1)}, bf16[4,64,512]{2,1,0:T(8,128)(2,1)S(1)}, u32[]{:S(2)}, u32[]{:S(2)}) collective-permute-start(bf16[4,64,512]{2,1,0:T(8,128)(2,1)S(1)} %pad_maximum_fusion.4), channel_id=1, source_target_pairs={{0,4},{4,0},{8,12},{12,8},{16,20},{20,16},{24,28},{28,24},{1,5},{5... | collective-permute-start | bytes 786440 | tf_op jit(solution)/shard_map/ppermute | solution.py:48
  38.1 18.2 %collective-permute-start.16 = (bf16[8,64,640]{2,1,0:T(8,128)(2,1)S(1)}, bf16[8,64,640]{2,1,0:T(8,128)(2,1)S(1)}, u32[]{:S(2)}, u32[]{:S(2)}) collective-permute-start(bf16[8,64,640]{2,1,0:T(8,128)(2,1)S(1)} %pad_maximum_fusion.refs_8_), channel_id=1, source_target_pairs={{0,4},{4,0},{8,12},{12,8},{16,20},{20,16},{24,28},{28,24},{1,5},{5... | collective-permute-start | bytes 1966088 | tf_op jit(solution)/shard_map/ppermute | solution.py:48
  39.1 21.9 %copy-start.7 = (f32[512,512]{1,0:T(8,128)S(1)}, f32[512,512]{1,0:T(8,128)}, u32[]{:S(2)}) copy-start(f32[512,512]{1,0:T(8,128)} %refs_15_.2) | copy-start | bytes 3145732
  39.1 18.4 %collective-permute-start.13 = (bf16[8,64,512]{2,1,0:T(8,128)(2,1)S(1)}, bf16[8,64,512]{2,1,0:T(8,128)(2,1)S(1)}, u32[]{:S(2)}, u32[]{:S(2)}) collective-permute-start(bf16[8,64,512]{2,1,0:T(8,128)(2,1)S(1)} %pad_maximum_fusion.1.refs_4_), channel_id=1, source_target_pairs={{0,2},{1,3},{2,0},{3,1},{4,6},{5,7},{6,4},{7,5},{8,10},{9,11},{10,... | collective-permute-start | bytes 1572872 | tf_op jit(solution)/shard_map/ppermute | solution.py:48
  39.2 17.0 %collective-permute-start.11 = (bf16[528,128]{1,0:T(8,128)(2,1)S(1)}, bf16[528,128]{1,0:T(8,128)(2,1)S(1)}, u32[]{:S(2)}, u32[]{:S(2)}) collective-permute-start(bf16[528,128]{1,0:T(8,128)(2,1)S(1)} %get-tuple-element.114.refs_6_), channel_id=1, source_target_pairs={{0,2},{1,3},{2,0},{3,1},{4,6},{5,7},{6,4},{7,5},{8,10},{9,11},{10,... | collective-permute-start | bytes 405512 | tf_op jit(solution)/shard_map/ppermute | solution.py:760
  41.2 19.8 %copy-start.6 = (f32[512,512]{1,0:T(8,128)S(1)}, f32[512,512]{1,0:T(8,128)}, u32[]{:S(2)}) copy-start(f32[512,512]{1,0:T(8,128)} %refs_14_.2) | copy-start | bytes 3145732
  41.2 19.8 %copy-start.16 = (f32[6,512]{1,0:T(8,128)S(1)}, f32[6,512]{1,0:T(8,128)}, u32[]{:S(2)}) copy-start(f32[6,512]{1,0:T(8,128)} %refs_15_.3) | copy-start | bytes 36868
  41.2 15.0 %collective-permute-start.12 = (bf16[528,128]{1,0:T(8,128)(2,1)S(1)}, bf16[528,128]{1,0:T(8,128)(2,1)S(1)}, u32[]{:S(2)}, u32[]{:S(2)}) collective-permute-start(bf16[528,128]{1,0:T(8,128)(2,1)S(1)} %get-tuple-element.120.refs_7_), channel_id=1, source_target_pairs={{0,3},{1,2},{2,1},{3,0},{4,7},{5,6},{6,5},{7,4},{8,11},{9,10},{10,... | collective-permute-start | bytes 405512 | tf_op jit(solution)/shard_map/ppermute | solution.py:760
  41.3 19.6 %collective-permute-start.17 = (bf16[8,64,640]{2,1,0:T(8,128)(2,1)S(1)}, bf16[8,64,640]{2,1,0:T(8,128)(2,1)S(1)}, u32[]{:S(2)}, u32[]{:S(2)}) collective-permute-start(bf16[8,64,640]{2,1,0:T(8,128)(2,1)S(1)} %pad_maximum_fusion.refs_8_), channel_id=1, source_target_pairs={{0,1},{1,0},{2,3},{3,2},{4,5},{5,4},{6,7},{7,6},{8,9},{9,8},{10,11... | collective-permute-start | bytes 1966088 | tf_op jit(solution)/shard_map/ppermute | solution.py:48
  56.3 4.7 %collective-permute-start.18 = (bf16[8,64,640]{2,1,0:T(8,128)(2,1)S(1)}, bf16[8,64,640]{2,1,0:T(8,128)(2,1)S(1)}, u32[]{:S(2)}, u32[]{:S(2)}) collective-permute-start(bf16[8,64,640]{2,1,0:T(8,128)(2,1)S(1)} %collective-permute-done.16.refs_9_), channel_id=1, source_target_pairs={{0,1},{1,0},{2,3},{3,2},{4,5},{5,4},{6,7},{7,6},{8,9},{9,8},{10,11... | collective-permute-start | bytes 1966088 | tf_op jit(solution)/shard_map/ppermute | solution.py:48
  57.5 3.4 %collective-permute-start.14 = (bf16[8,64,512]{2,1,0:T(8,128)(2,1)S(1)}, bf16[8,64,512]{2,1,0:T(8,128)(2,1)S(1)}, u32[]{:S(2)}, u32[]{:S(2)}) collective-permute-start(bf16[8,64,512]{2,1,0:T(8,128)(2,1)S(1)} %pad_maximum_fusion.1.refs_4_), channel_id=1, source_target_pairs={{0,1},{1,0},{2,3},{3,2},{4,5},{5,4},{6,7},{7,6},{8,9},{9,8},{10,11... | collective-permute-start | bytes 1572872 | tf_op jit(solution)/shard_map/ppermute | solution.py:48
  57.5 3.4 %collective-permute-start.15 = (bf16[8,64,512]{2,1,0:T(8,128)(2,1)S(1)}, bf16[8,64,512]{2,1,0:T(8,128)(2,1)S(1)}, u32[]{:S(2)}, u32[]{:S(2)}) collective-permute-start(bf16[8,64,512]{2,1,0:T(8,128)(2,1)S(1)} %collective-permute-done.13.refs_5_), channel_id=1, source_target_pairs={{0,1},{1,0},{2,3},{3,2},{4,5},{5,4},{6,7},{7,6},{8,9},{9,8},{10,11... | collective-permute-start | bytes 1572872 | tf_op jit(solution)/shard_map/ppermute | solution.py:48
  58.0 2.9 %collective-permute-start.10 = (bf16[528,128]{1,0:T(8,128)(2,1)S(1)}, bf16[528,128]{1,0:T(8,128)(2,1)S(1)}, u32[]{:S(2)}, u32[]{:S(2)}) collective-permute-start(bf16[528,128]{1,0:T(8,128)(2,1)S(1)} %get-tuple-element.119.refs_5_), channel_id=1, source_target_pairs={{0,1},{1,0},{2,3},{3,2},{4,5},{5,4},{6,7},{7,6},{8,9},{9,8},{10,11... | collective-permute-start | bytes 405512 | tf_op jit(solution)/shard_map/ppermute | solution.py:760
  72.4 2.7 %collective-permute-start.19 = (bf16[16,64,512]{2,1,0:T(8,128)(2,1)S(1)}, bf16[16,64,512]{2,1,0:T(8,128)(2,1)S(1)}, u32[]{:S(2)}, u32[]{:S(2)}) collective-permute-start(bf16[16,64,512]{2,1,0:T(8,128)(2,1)S(1)} %get-tuple-element.132), channel_id=1, source_target_pairs={{0,1},{1,0},{2,3},{3,2},{4,5},{5,4},{6,7},{7,6},{8,9},{9,8},{10,11... | collective-permute-start | bytes 3145736 | tf_op jit(solution)/shard_map/ppermute | solution.py:48
  72.7 4.2 %collective-permute-start.20 = (bf16[16,64,640]{2,1,0:T(8,128)(2,1)S(1)}, bf16[16,64,640]{2,1,0:T(8,128)(2,1)S(1)}, u32[]{:S(2)}, u32[]{:S(2)}) collective-permute-start(bf16[16,64,640]{2,1,0:T(8,128)(2,1)S(1)} %get-tuple-element.134), channel_id=1, source_target_pairs={{0,1},{1,0},{2,3},{3,2},{4,5},{5,4},{6,7},{7,6},{8,9},{9,8},{10,11... | collective-permute-start | bytes 3932168 | tf_op jit(solution)/shard_map/ppermute | solution.py:48
  72.9 4.6 %collective-permute-start.21 = (bf16[512,128]{1,0:T(8,128)(2,1)S(1)}, bf16[512,128]{1,0:T(8,128)(2,1)S(1)}, u32[]{:S(2)}, u32[]{:S(2)}) collective-permute-start(bf16[512,128]{1,0:T(8,128)(2,1)S(1)} %get-tuple-element.136), channel_id=1, source_target_pairs={{0,1},{1,0},{2,3},{3,2},{4,5},{5,4},{6,7},{7,6},{8,9},{9,8},{10,11... | collective-permute-start | bytes 393224 | tf_op jit(solution)/shard_map/ppermute | solution.py:805
  73.2 6.3 %collective-permute-start.22 = (bf16[512,128]{1,0:T(8,128)(2,1)S(1)}, bf16[512,128]{1,0:T(8,128)(2,1)S(1)}, u32[]{:S(2)}, u32[]{:S(2)}) collective-permute-start(bf16[512,128]{1,0:T(8,128)(2,1)S(1)} %get-tuple-element.137), channel_id=1, source_target_pairs={{0,2},{1,3},{2,0},{3,1},{4,6},{5,7},{6,4},{7,5},{8,10},{9,11},{10,... | collective-permute-start | bytes 393224 | tf_op jit(solution)/shard_map/ppermute | solution.py:805
  73.5 7.2 %collective-permute-start.23 = (bf16[512,128]{1,0:T(8,128)(2,1)S(1)}, bf16[512,128]{1,0:T(8,128)(2,1)S(1)}, u32[]{:S(2)}, u32[]{:S(2)}) collective-permute-start(bf16[512,128]{1,0:T(8,128)(2,1)S(1)} %get-tuple-element.138), channel_id=1, source_target_pairs={{0,3},{1,2},{2,1},{3,0},{4,7},{5,6},{6,5},{7,4},{8,11},{9,10},{10,... | collective-permute-start | bytes 393224 | tf_op jit(solution)/shard_map/ppermute | solution.py:805
  75.4 18.7 %collective-permute-start.24 = (bf16[8,64,512]{2,1,0:T(8,128)(2,1)S(1)}, bf16[8,64,512]{2,1,0:T(8,128)(2,1)S(1)}, u32[]{:S(2)}, u32[]{:S(2)}) collective-permute-start(bf16[8,64,512]{2,1,0:T(8,128)(2,1)S(1)} %slice.130), channel_id=1, source_target_pairs={{0,4},{4,0},{8,12},{12,8},{16,20},{20,16},{24,28},{28,24},{1,5},{5... | collective-permute-start | bytes 1572872 | tf_op jit(solution)/shard_map/ppermute | solution.py:48
  77.4 17.3 %collective-permute-start.25 = (bf16[8,64,640]{2,1,0:T(8,128)(2,1)S(1)}, bf16[8,64,640]{2,1,0:T(8,128)(2,1)S(1)}, u32[]{:S(2)}, u32[]{:S(2)}) collective-permute-start(bf16[8,64,640]{2,1,0:T(8,128)(2,1)S(1)} %slice.131), channel_id=1, source_target_pairs={{0,8},{4,12},{8,0},{12,4},{16,24},{20,28},{24,16},{28,20},{1,9},{5... | collective-permute-start | bytes 1966088 | tf_op jit(solution)/shard_map/ppermute | solution.py:48
  94.3 9.2 %collective-permute-start.29 = (bf16[4,64,512]{2,1,0:T(8,128)(2,1)S(1)}, bf16[4,64,512]{2,1,0:T(8,128)(2,1)S(1)}, u32[]{:S(2)}, u32[]{:S(2)}) collective-permute-start(bf16[4,64,512]{2,1,0:T(8,128)(2,1)S(1)} %slice.133), channel_id=1, source_target_pairs={{0,2},{1,3},{2,0},{3,1},{4,6},{5,7},{6,4},{7,5},{8,10},{9,11},{10,... | collective-permute-start | bytes 786440 | tf_op jit(solution)/shard_map/ppermute | solution.py:48
  94.9 10.3 %collective-permute-start.28 = (bf16[4,64,640]{2,1,0:T(8,128)(2,1)S(1)}, bf16[4,64,640]{2,1,0:T(8,128)(2,1)S(1)}, u32[]{:S(2)}, u32[]{:S(2)}) collective-permute-start(bf16[4,64,640]{2,1,0:T(8,128)(2,1)S(1)} %slice.135), channel_id=1, source_target_pairs={{0,4},{4,0},{8,12},{12,8},{16,20},{20,16},{24,28},{28,24},{1,5},{5... | collective-permute-start | bytes 983048 | tf_op jit(solution)/shard_map/ppermute | solution.py:48
  99.3 7.8 %collective-permute-start.27 = (bf16[512,512]{1,0:T(8,128)(2,1)S(1)}, bf16[512,512]{1,0:T(8,128)(2,1)S(1)}, u32[]{:S(2)}, u32[]{:S(2)}) collective-permute-start(bf16[512,512]{1,0:T(8,128)(2,1)S(1)} %get-tuple-element.147), channel_id=1, source_target_pairs={{0,1},{1,0},{2,3},{3,2},{4,5},{5,4},{6,7},{7,6},{8,9},{9,8},{10,11... | collective-permute-start | bytes 1572872 | tf_op jit(solution)/shard_map/ppermute | solution.py:48
  99.7 7.9 %collective-permute-start.26 = (bf16[4,64,384]{2,1,0:T(8,128)(2,1)S(1)}, bf16[4,64,384]{2,1,0:T(8,128)(2,1)S(1)}, u32[]{:S(2)}, u32[]{:S(2)}) collective-permute-start(bf16[4,64,384]{2,1,0:T(8,128)(2,1)S(1)} %slice.136), channel_id=1, source_target_pairs={{0,8},{4,12},{8,0},{12,4},{16,24},{20,28},{24,16},{28,20},{1,9},{5... | collective-permute-start | bytes 589832 | tf_op jit(solution)/shard_map/ppermute | solution.py:48
  103.6 5.9 %collective-permute-start.32 = (bf16[2,64,512]{2,1,0:T(8,128)(2,1)S(1)}, bf16[2,64,512]{2,1,0:T(8,128)(2,1)S(1)}, u32[]{:S(2)}, u32[]{:S(2)}) collective-permute-start(bf16[2,64,512]{2,1,0:T(8,128)(2,1)S(1)} %slice.140), channel_id=1, source_target_pairs={{0,8},{4,12},{8,0},{12,4},{16,24},{20,28},{24,16},{28,20},{1,9},{5... | collective-permute-start | bytes 393224 | tf_op jit(solution)/shard_map/ppermute | solution.py:48
  103.7 17.7 %collective-permute-start.33 = (bf16[512,512]{1,0:T(8,128)(2,1)S(1)}, bf16[512,512]{1,0:T(8,128)(2,1)S(1)}, u32[]{:S(2)}, u32[]{:S(2)}) collective-permute-start(bf16[512,512]{1,0:T(8,128)(2,1)S(1)} %get-tuple-element.156), channel_id=1, source_target_pairs={{0,1},{1,0},{2,3},{3,2},{4,5},{5,4},{6,7},{7,6},{8,9},{9,8},{10,11... | collective-permute-start | bytes 1572872 | tf_op jit(solution)/shard_map/ppermute | solution.py:48
  105.3 7.2 %collective-permute-start.31 = (bf16[2,64,640]{2,1,0:T(8,128)(2,1)S(1)}, bf16[2,64,640]{2,1,0:T(8,128)(2,1)S(1)}, u32[]{:S(2)}, u32[]{:S(2)}) collective-permute-start(bf16[2,64,640]{2,1,0:T(8,128)(2,1)S(1)} %slice.141), channel_id=1, source_target_pairs={{0,2},{1,3},{2,0},{3,1},{4,6},{5,7},{6,4},{7,5},{8,10},{9,11},{10,... | collective-permute-start | bytes 491528 | tf_op jit(solution)/shard_map/ppermute | solution.py:48
  107.2 18.8 %collective-permute-start.34 = (bf16[512,512]{1,0:T(8,128)(2,1)S(1)}, bf16[512,512]{1,0:T(8,128)(2,1)S(1)}, u32[]{:S(2)}, u32[]{:S(2)}) collective-permute-start(bf16[512,512]{1,0:T(8,128)(2,1)S(1)} %add_convert_fusion.3), channel_id=1, source_target_pairs={{0,2},{1,3},{2,0},{3,1},{4,6},{5,7},{6,4},{7,5},{8,10},{9,11},{10,... | collective-permute-start | bytes 1572872 | tf_op jit(solution)/shard_map/ppermute | solution.py:48
  107.7 6.5 %collective-permute-start.30 = (bf16[2,64,384]{2,1,0:T(8,128)(2,1)S(1)}, bf16[2,64,384]{2,1,0:T(8,128)(2,1)S(1)}, u32[]{:S(2)}, u32[]{:S(2)}) collective-permute-start(bf16[2,64,384]{2,1,0:T(8,128)(2,1)S(1)} %slice.143), channel_id=1, source_target_pairs={{0,4},{4,0},{8,12},{12,8},{16,20},{20,16},{24,28},{28,24},{1,5},{5... | collective-permute-start | bytes 294920 | tf_op jit(solution)/shard_map/ppermute | solution.py:48
  109.5 6.1 %collective-permute-start.36 = (bf16[1,64,512]{2,1,0:T(8,128)(2,1)S(1)}, bf16[1,64,512]{2,1,0:T(8,128)(2,1)S(1)}, u32[]{:S(2)}, u32[]{:S(2)}) collective-permute-start(bf16[1,64,512]{2,1,0:T(8,128)(2,1)S(1)} %get-tuple-element.189), channel_id=1, source_target_pairs={{0,16},{4,20},{8,24},{12,28},{16,0},{20,4},{24,8},{28,12},{1,17},{... | collective-permute-start | bytes 196616 | tf_op jit(solution)/shard_map/ppermute | solution.py:48
  112.5 8.1 %collective-permute-start.37 = (bf16[1,64,640]{2,1,0:T(8,128)(2,1)S(1)}, bf16[1,64,640]{2,1,0:T(8,128)(2,1)S(1)}, u32[]{:S(2)}, u32[]{:S(2)}) collective-permute-start(bf16[1,64,640]{2,1,0:T(8,128)(2,1)S(1)} %get-tuple-element.187), channel_id=1, source_target_pairs={{0,16},{4,20},{8,24},{12,28},{16,0},{20,4},{24,8},{28,12},{1,17},{... | collective-permute-start | bytes 245768 | tf_op jit(solution)/shard_map/ppermute | solution.py:48
  114.3 6.9 %collective-permute-start.35 = (bf16[1,64,384]{2,1,0:T(8,128)(2,1)S(1)}, bf16[1,64,384]{2,1,0:T(8,128)(2,1)S(1)}, u32[]{:S(2)}, u32[]{:S(2)}) collective-permute-start(bf16[1,64,384]{2,1,0:T(8,128)(2,1)S(1)} %get-tuple-element.191), channel_id=1, source_target_pairs={{0,16},{4,20},{8,24},{12,28},{16,0},{20,4},{24,8},{28,12},{1,17},{... | collective-permute-start | bytes 147464 | tf_op jit(solution)/shard_map/ppermute | solution.py:48
  121.3 1.3 collective-permute-start.38
  122.6 4.9 %collective-permute-start.39 = (f32[56,128]{1,0:T(8,128)S(1)}, f32[56,128]{1,0:T(8,128)S(1)}, u32[]{:S(2)}, u32[]{:S(2)}) collective-permute-start(f32[56,128]{1,0:T(8,128)S(1)} %add.70), channel_id=1, source_target_pairs={{0,2},{1,3},{2,0},{3,1},{4,6},{5,7},{6,4},{7,5},{8,10},{9,11},{10,... | collective-permute-start | bytes 86024 | tf_op jit(solution)/shard_map/ppermute | solution.py:48
  124.2 3.9 %collective-permute-start.40 = (f32[56,128]{1,0:T(8,128)S(1)}, f32[56,128]{1,0:T(8,128)S(1)}, u32[]{:S(2)}, u32[]{:S(2)}) collective-permute-start(f32[56,128]{1,0:T(8,128)S(1)} %add.70), channel_id=1, source_target_pairs={{0,4},{4,0},{8,12},{12,8},{16,20},{20,16},{24,28},{28,24},{1,5},{5... | collective-permute-start | bytes 86024 | tf_op jit(solution)/shard_map/ppermute | solution.py:48
  125.4 4.8 %collective-permute-start.41 = (f32[56,128]{1,0:T(8,128)S(1)}, f32[56,128]{1,0:T(8,128)S(1)}, u32[]{:S(2)}, u32[]{:S(2)}) collective-permute-start(f32[56,128]{1,0:T(8,128)S(1)} %add.70), channel_id=1, source_target_pairs={{0,6},{1,7},{2,4},{3,5},{4,2},{5,3},{6,0},{7,1},{8,14},{9,15},{10,... | collective-permute-start | bytes 86024 | tf_op jit(solution)/shard_map/ppermute | solution.py:91
  130.1 5.1 %collective-permute-start.42 = (f32[56,128]{1,0:T(8,128)S(1)}, f32[56,128]{1,0:T(8,128)S(1)}, u32[]{:S(2)}, u32[]{:S(2)}) collective-permute-start(f32[56,128]{1,0:T(8,128)S(1)} %add_add_fusion.refs_0_), channel_id=1, source_target_pairs={{0,8},{4,12},{8,0},{12,4},{16,24},{20,28},{24,16},{28,20},{1,9},{5... | collective-permute-start | bytes 86024 | tf_op jit(solution)/shard_map/ppermute | solution.py:48
  130.5 4.8 %collective-permute-start.43 = (f32[56,128]{1,0:T(8,128)S(1)}, f32[56,128]{1,0:T(8,128)S(1)}, u32[]{:S(2)}, u32[]{:S(2)}) collective-permute-start(f32[56,128]{1,0:T(8,128)S(1)} %add_add_fusion.refs_0_), channel_id=1, source_target_pairs={{0,16},{4,20},{8,24},{12,28},{16,0},{20,4},{24,8},{28,12},{1,17},{... | collective-permute-start | bytes 86024 | tf_op jit(solution)/shard_map/ppermute | solution.py:48
  133.5 5.7 %collective-permute-start.44 = (f32[56,128]{1,0:T(8,128)S(1)}, f32[56,128]{1,0:T(8,128)S(1)}, u32[]{:S(2)}, u32[]{:S(2)}) collective-permute-start(f32[56,128]{1,0:T(8,128)S(1)} %add_add_fusion.refs_0_), channel_id=1, source_target_pairs={{0,24},{1,25},{2,26},{3,27},{4,28},{5,29},{6,30},{7,31},{8,16},{9,... | collective-permute-start | bytes 86024 | tf_op jit(solution)/shard_map/ppermute | solution.py:91
  (20 other events, 231.2 us)

commit v7 on v6

--- a/solution.py
+++ b/solution.py
@@ -762,7 +762,7 @@
     arrived = [near[0]] + mixed[n_h // 2 :]
     if not early:
         crossed = [swap(e_in, e_steps[-1]), swap(c_in, c_steps[-1])]
-    e_got, c_got = after(e_got, *arrived), after(c_got, *arrived)
+    e_got, c_got = after(e_got, *arrived), after(c_got, near[0])
     e_parts = [e_in, e_got, crossed[0], swap(e_got, e_steps[-1])]
     c_parts = [c_in, c_got, crossed[1], swap(c_got, c_steps[-1])]
 

time: 142 us -> 140 us (0.986)
  waiting for transfers between devices: 48.5 us -> 41.9 us
  starting transfers between devices: 42.4 us -> 47.2 us
    ppermute x3, waiting for transfers between devices: 13.3 us -> 3.87 us  [per_device(): lax.ppermute(pieces[off], 'head', [(i, i ^ off) for i in range(n_h)])]
    ppermute x37, waiting for transfers between devices: 26.1 us -> 31.8 us  [swap(): return lax.ppermute(v, axis, [(i, i ^ bit) for i in range(count)])]
    ppermute x37, starting transfers between devices: 36.7 us -> 41.1 us  [swap(): return lax.ppermute(v, axis, [(i, i ^ bit) for i in range(count)])]
    ppermute x2, waiting for transfers between devices: 5.88 us -> 4.37 us  [swap_both(): lax.ppermute(v, ('dp', 'head'), [(i, i ^ flip) for i in range(n_h * lax.a...]
    ppermute x3, waiting for transfers between devices: 3.32 us -> 1.87 us  [per_device(): lax.ppermute(gm[off], 'head', [(i, i ^ off) for i in range(n_h)])]
  transfers between devices with their start and end apart: 45 -> 45, of which waited for: 20 -> 23; matrix products, arithmetic and copies ran while one was open for 3% -> 3% of each run, Pallas kernels for 21% -> 21%
where the time goes in v7:
time: 140 us
  starting transfers between devices  47.2 us (34%)
  Pallas kernels  43.3 us (31%)
  waiting for transfers between devices  41.9 us (30%)
  other arithmetic  4.6 us (3%)
  between operations  2.17 us (2%)
    pallas_call x9, Pallas kernels, call(): pl.pallas_call(body, out_shape=outs, in_specs=[SMEM] * n_smem + [VMEM] *...  43.3 us
    ppermute x37, starting transfers between devices, swap(): return lax.ppermute(v, axis, [(i, i ^ bit) for i in range(count)])  41.1 us
    ppermute x37, waiting for transfers between devices, swap(): return lax.ppermute(v, axis, [(i, i ^ bit) for i in range(count)])  31.8 us
    ppermute x2, waiting for transfers between devices, swap_both(): lax.ppermute(v, ('dp', 'head'), [(i, i ^ flip) for i in range(n_h * lax.a...  4.37 us
    ppermute x3, waiting for transfers between devices, per_device(): lax.ppermute(pieces[off], 'head', [(i, i ^ off) for i in range(n_h)])  3.87 us
  transfers between devices with their start and end apart: 45, of which 23 were waited for; matrix products, arithmetic and copies ran while one was open for 3% of the time, Pallas kernels for 21%

profile of v7, /device:TPU:0, one launch (start us, length us, event | category | flops | bytes accessed | tf_op | source)
XLA Modules:
  0.0 139.6 jit_solution(9792002871309742567)
XLA Ops:
  0.7 1.4 convert_element_type.123.refs_0_
  2.1 3.0 %collective-permute-start.6 = (bf16[512,512]{1,0:T(8,128)(2,1)S(1)}, bf16[512,512]{1,0:T(8,128)(2,1)S(1)}, u32[]{:S(2)}, u32[]{:S(2)}) collective-permute-start(bf16[512,512]{1,0:T(8,128)(2,1)S(1)} %convert_element_type.123.refs_0_), channel_id=1, source_target_pairs={{0,2},{1,3},{2,0},{3,1},{4,6},{5,7},{6,4},{7,5},{8,10},{9,11},{10,... | collective-permute-start | bytes 1572872 | tf_op jit(solution)/shard_map/ppermute | solution.py:48
  5.3 2.7 %collective-permute-start = (bf16[1,80,384]{2,1,0:T(8,128)(2,1)S(1)}, bf16[1,80,384]{2,1,0:T(8,128)(2,1)S(1)}, u32[]{:S(2)}, u32[]{:S(2)}) collective-permute-start(bf16[1,80,384]{2,1,0:T(8,128)(2,1)S(1)} %fusion.4), channel_id=1, source_target_pairs={{0,16},{4,20},{8,24},{12,28},{16,0},{20,4},{24,8},{28,12},{1,17},{... | collective-permute-start | bytes 184328 | tf_op jit(solution)/shard_map/ppermute | solution.py:48
  8.5 3.6 %collective-permute-done = bf16[1,80,384]{2,1,0:T(8,128)(2,1)S(1)} collective-permute-done((bf16[1,80,384]{2,1,0:T(8,128)(2,1)S(1)}, bf16[1,80,384]{2,1,0:T(8,128)(2,1)S(1)}, u32[]{:S(2)}, u32[]{:S(2)}) %collective-permute-start) | collective-permute-done | bytes 61472 | tf_op jit(solution)/shard_map/ppermute | solution.py:48
  12.1 3.8 %collective-permute-start.1 = (bf16[2,80,384]{2,1,0:T(8,128)(2,1)S(1)}, bf16[2,80,384]{2,1,0:T(8,128)(2,1)S(1)}, u32[]{:S(2)}, u32[]{:S(2)}) collective-permute-start(bf16[2,80,384]{2,1,0:T(8,128)(2,1)S(1)} %pad_maximum_fusion.6), channel_id=1, source_target_pairs={{0,8},{4,12},{8,0},{12,4},{16,24},{20,28},{24,16},{28,20},{1,9},{5... | collective-permute-start | bytes 368648 | tf_op jit(solution)/shard_map/ppermute | solution.py:48
  15.9 2.5 %collective-permute-done.2 = bf16[1,64,1152]{2,1,0:T(8,128)(2,1)S(1)} collective-permute-done((bf16[1,64,1152]{2,1,0:T(8,128)(2,1)S(1)}, bf16[1,64,1152]{2,1,0:T(8,128)(2,1)S(1)}, u32[]{:S(2)}, u32[]{:S(2)}) %collective-permute-start.2) | collective-permute-done | bytes 147488 | tf_op jit(solution)/shard_map/ppermute | solution.py:48
  19.1 1.9 %collective-permute-done.1 = bf16[2,80,384]{2,1,0:T(8,128)(2,1)S(1)} collective-permute-done((bf16[2,80,384]{2,1,0:T(8,128)(2,1)S(1)}, bf16[2,80,384]{2,1,0:T(8,128)(2,1)S(1)}, u32[]{:S(2)}, u32[]{:S(2)}) %collective-permute-start.1) | collective-permute-done | bytes 122912 | tf_op jit(solution)/shard_map/ppermute | solution.py:48
  21.0 1.6 %collective-permute-start.4 = (bf16[4,80,384]{2,1,0:T(8,128)(2,1)S(1)}, bf16[4,80,384]{2,1,0:T(8,128)(2,1)S(1)}, u32[]{:S(2)}, u32[]{:S(2)}) collective-permute-start(bf16[4,80,384]{2,1,0:T(8,128)(2,1)S(1)} %pad_maximum_fusion.5.w_own), channel_id=1, source_target_pairs={{0,4},{4,0},{8,12},{12,8},{16,20},{20,16},{24,28},{28,24},{1,5},{5... | collective-permute-start | bytes 737288 | tf_op jit(solution)/shard_map/ppermute | solution.py:48
  22.6 4.7 %collective-permute-done.3 = bf16[2,64,1152]{2,1,0:T(8,128)(2,1)S(1)} collective-permute-done((bf16[2,64,1152]{2,1,0:T(8,128)(2,1)S(1)}, bf16[2,64,1152]{2,1,0:T(8,128)(2,1)S(1)}, u32[]{:S(2)}, u32[]{:S(2)}) %collective-permute-start.3) | collective-permute-done | bytes 294944 | tf_op jit(solution)/shard_map/ppermute | solution.py:48
  27.9 1.6 %collective-permute-start.8 = (bf16[4,64,512]{2,1,0:T(8,128)(2,1)S(1)}, bf16[4,64,512]{2,1,0:T(8,128)(2,1)S(1)}, u32[]{:S(2)}, u32[]{:S(2)}) collective-permute-start(bf16[4,64,512]{2,1,0:T(8,128)(2,1)S(1)} %pad_maximum_fusion.4), channel_id=1, source_target_pairs={{0,4},{4,0},{8,12},{12,8},{16,20},{20,16},{24,28},{28,24},{1,5},{5... | collective-permute-start | bytes 786440 | tf_op jit(solution)/shard_map/ppermute | solution.py:48
  29.5 2.0 %shard_map.447 = (bf16[2048,128]{1,0:T(8,128)(2,1)S(1)}, bf16[2048,128]{1,0:T(8,128)(2,1)S(1)}, bf16[2048,128]{1,0:T(8,128)(2,1)S(1)}, bf16[144,2048]{1,0:T(8,12...) custom-call(s32[2]{0:T(128)S(1)} %pad_add_fusion.idx_ref, ...), custom_call_target="tpu_custom_call" | custom-call | flops 4000000000 | bytes 1048576 | tf_op jit(solution)/shard_map/pallas_call | solution.py:620
  31.6 5.7 %shard_map.448 = (bf16[528,128]{1,0:T(8,128)(2,1)S(1)}, bf16[528,128]{1,0:T(8,128)(2,1)S(1)}, f32[4,8,512]{2,1,0:T(8,128)S(1)}) custom-call(s32[2]{0:T(128)S(1)} %pad_add_fusion.idx_ref, s32[1,2048]{1,0:T(1,128)S(1)} %copy-done.19, bf16[2048,128]{1,0:T(8,128)(2,1)S(1)} %get-tuple-element.117.q_ref, bf16[2048,128]{1,0:T(8,128)(2,1)S(1)} %get-tuple-element.111.k_ref, ...), custom_call_target="tpu_custom_call" | custom-call | flops 1000000000 | bytes 1048576 | tf_op jit(solution)/shard_map/pallas_call | solution.py:620
  38.3 1.4 %collective-permute-start.11 = (bf16[528,128]{1,0:T(8,128)(2,1)S(1)}, bf16[528,128]{1,0:T(8,128)(2,1)S(1)}, u32[]{:S(2)}, u32[]{:S(2)}) collective-permute-start(bf16[528,128]{1,0:T(8,128)(2,1)S(1)} %get-tuple-element.114.refs_6_), channel_id=1, source_target_pairs={{0,2},{1,3},{2,0},{3,1},{4,6},{5,7},{6,4},{7,5},{8,10},{9,11},{10,... | collective-permute-start | bytes 405512 | tf_op jit(solution)/shard_map/ppermute | solution.py:760
  39.8 0.8 collective-permute-start.12
  40.6 5.1 %shard_map.449 = (bf16[528,128]{1,0:T(8,128)(2,1)S(1)}, bf16[528,128]{1,0:T(8,128)(2,1)S(1)}, f32[4,8,512]{2,1,0:T(8,128)S(1)}) custom-call(s32[2]{0:T(128)S(1)} %pad_add_fusion.idx_ref, s32[1,2048]{1,0:T(1,128)S(1)} %copy-done.19, bf16[2048,128]{1,0:T(8,128)(2,1)S(1)} %get-tuple-element.117.q_ref, bf16[2048,128]{1,0:T(8,128)(2,1)S(1)} %get-tuple-element.111.k_ref, ...), custom_call_target="tpu_custom_call" | custom-call | flops 1000000000 | bytes 1048576 | tf_op jit(solution)/shard_map/pallas_call | solution.py:620
  45.7 7.0 %collective-permute-done.16.refs_9_ = bf16[8,64,640]{2,1,0:T(8,128)(2,1)S(1)} collective-permute-done((bf16[8,64,640]{2,1,0:T(8,128)(2,1)S(1)}, bf16[8,64,640]{2,1,0:T(8,128)(2,1)S(1)}, u32[]{:S(2)}, u32[]{:S(2)}) %collective-permute-start.16) | collective-permute-done | bytes 655392 | tf_op jit(solution)/shard_map/ppermute | solution.py:48
  52.6 2.1 %collective-permute-done.11.refs_2_ = bf16[528,128]{1,0:T(8,128)(2,1)S(1)} collective-permute-done((bf16[528,128]{1,0:T(8,128)(2,1)S(1)}, bf16[528,128]{1,0:T(8,128)(2,1)S(1)}, u32[]{:S(2)}, u32[]{:S(2)}) %collective-permute-start.11) | collective-permute-done | bytes 135200 | tf_op jit(solution)/shard_map/ppermute | solution.py:760
  54.8 1.3 collective-permute-start.15
  56.0 1.7 %collective-permute-done.10.refs_1_ = bf16[528,128]{1,0:T(8,128)(2,1)S(1)} collective-permute-done((bf16[528,128]{1,0:T(8,128)(2,1)S(1)}, bf16[528,128]{1,0:T(8,128)(2,1)S(1)}, u32[]{:S(2)}, u32[]{:S(2)}) %collective-permute-start.10) | collective-permute-done | bytes 135200 | tf_op jit(solution)/shard_map/ppermute | solution.py:760
  57.8 11.4 %shard_map.450 = (f32[512,512]{1,0:T(8,128)}, f32[512,512]{1,0:T(8,128)}, f32[512,512]{1,0:T(8,128)S(1)}, bf16[512,128]{1,0:T(8,128)(2,1)S(1)}, bf16[512,128]{1,...) custom-call(s32[2]{0:T(128)S(1)} %pad_add_fusion.idx_ref, ...), custom_call_target="tpu_custom_call" | custom-call | flops 20000000000 | bytes 1048576 | tf_op jit(solution)/shard_map/pallas_call | solution.py:620
  70.4 1.2 collective-permute-start.23
  72.3 1.3 collective-permute-start.24
  74.2 1.5 %collective-permute-start.25 = (bf16[8,64,640]{2,1,0:T(8,128)(2,1)S(1)}, bf16[8,64,640]{2,1,0:T(8,128)(2,1)S(1)}, u32[]{:S(2)}, u32[]{:S(2)}) collective-permute-start(bf16[8,64,640]{2,1,0:T(8,128)(2,1)S(1)} %slice.131), channel_id=1, source_target_pairs={{0,8},{4,12},{8,0},{12,4},{16,24},{20,28},{24,16},{28,20},{1,9},{5... | collective-permute-start | bytes 1966088 | tf_op jit(solution)/shard_map/ppermute | solution.py:48
  76.4 1.2 collective-permute-done.23.refs_3_
  77.6 13.3 %shard_map.451 = (bf16[2048,384]{1,0:T(8,128)(2,1)S(1)}, f32[48,128]{1,0:T(8,128)S(1)}) custom-call(s32[2]{0:T(128)S(1)} %pad_add_fusion.idx_ref, s32[1,2048]{1,0:T(1,128)S(1)} %copy-done.19, bf16[2048,128]{1,0:T(8,128)(2,1)S(1)} %get-tuple-element.117.q_ref, bf16[2048,128]{1,0:T(8,128)(2,1)S(1)} %get-tuple-element.111.k_ref, ...), custom_call_target="tpu_custom_call" | custom-call | flops 15000000512 | bytes 1048576 | tf_op jit(solution)/shard_map/pallas_call | solution.py:620
  91.8 1.1 collective-permute-start.28
  92.8 1.9 %shard_map.452 = bf16[8,64,384]{2,1,0:T(8,128)(2,1)S(1)} custom-call(s32[2]{0:T(128)S(1)} %pad_add_fusion.idx_ref, bf16[2048,384]{1,0:T(8,128)(2,1)S(1)} %get-tuple-element.143.gqkv_ref, bf16[512,512]{1,0:T(8,128)(2,1)S(1)} %convert_element_type.123.refs_0_, bf16[512,512]{1,0:T(8,128)(2,1)S(1)} %collective-permute-done.5.refs_1_, ...), custom_call_target="tpu_custom_call" | custom-call | flops 2000000000 | bytes 1048576 | tf_op jit(solution)/shard_map/pallas_call | solution.py:620
  94.7 1.8 %shard_map.453 = (bf16[512,512]{1,0:T(8,128)(2,1)S(1)}, bf16[512,512]{1,0:T(8,128)(2,1)S(1)}, bf16[512,512]{1,0:T(8,128)(2,1)S(1)}, bf16[512,512]{1,0:T(8,128)(2,1)S(1)}) custom-call(s32[2]{0:T(128)S(1)} %pad_add_fusion.idx_ref, bf16[2048,384]{1,0:T(8,128)(2,1)S(1)} %get-tuple-element.143.gqkv_ref, bf16[512,384]{1,0:T(8,128)(2,1)S(1)} %get-tuple-element.144.wg_ref), custom_call_target="tpu_custom_call" | custom-call | flops 2000000000 | bytes 1048576 | tf_op jit(solution)/shard_map/pallas_call | solution.py:620
  96.7 2.2 %collective-permute-start.26 = (bf16[4,64,384]{2,1,0:T(8,128)(2,1)S(1)}, bf16[4,64,384]{2,1,0:T(8,128)(2,1)S(1)}, u32[]{:S(2)}, u32[]{:S(2)}) collective-permute-start(bf16[4,64,384]{2,1,0:T(8,128)(2,1)S(1)} %slice.136), channel_id=1, source_target_pairs={{0,8},{4,12},{8,0},{12,4},{16,24},{20,28},{24,16},{28,20},{1,9},{5... | collective-permute-start | bytes 589832 | tf_op jit(solution)/shard_map/ppermute | solution.py:48
  98.9 1.5 %collective-permute-done.29 = bf16[4,64,512]{2,1,0:T(8,128)(2,1)S(1)} collective-permute-done((bf16[4,64,512]{2,1,0:T(8,128)(2,1)S(1)}, bf16[4,64,512]{2,1,0:T(8,128)(2,1)S(1)}, u32[]{:S(2)}, u32[]{:S(2)}) %collective-permute-start.29) | collective-permute-done | bytes 262176 | tf_op jit(solution)/shard_map/ppermute | solution.py:48
  100.4 1.5 %collective-permute-start.32 = (bf16[2,64,512]{2,1,0:T(8,128)(2,1)S(1)}, bf16[2,64,512]{2,1,0:T(8,128)(2,1)S(1)}, u32[]{:S(2)}, u32[]{:S(2)}) collective-permute-start(bf16[2,64,512]{2,1,0:T(8,128)(2,1)S(1)} %slice.140), channel_id=1, source_target_pairs={{0,8},{4,12},{8,0},{12,4},{16,24},{20,28},{24,16},{28,20},{1,9},{5... | collective-permute-start | bytes 393224 | tf_op jit(solution)/shard_map/ppermute | solution.py:48
  102.2 1.8 %collective-permute-start.31 = (bf16[2,64,640]{2,1,0:T(8,128)(2,1)S(1)}, bf16[2,64,640]{2,1,0:T(8,128)(2,1)S(1)}, u32[]{:S(2)}, u32[]{:S(2)}) collective-permute-start(bf16[2,64,640]{2,1,0:T(8,128)(2,1)S(1)} %slice.141), channel_id=1, source_target_pairs={{0,2},{1,3},{2,0},{3,1},{4,6},{5,7},{6,4},{7,5},{8,10},{9,11},{10,... | collective-permute-start | bytes 491528 | tf_op jit(solution)/shard_map/ppermute | solution.py:48
  104.6 1.3 collective-permute-start.30
  105.9 1.0 collective-permute-done.32
  107.0 3.4 %collective-permute-start.36 = (bf16[1,64,512]{2,1,0:T(8,128)(2,1)S(1)}, bf16[1,64,512]{2,1,0:T(8,128)(2,1)S(1)}, u32[]{:S(2)}, u32[]{:S(2)}) collective-permute-start(bf16[1,64,512]{2,1,0:T(8,128)(2,1)S(1)} %get-tuple-element.189), channel_id=1, source_target_pairs={{0,16},{4,20},{8,24},{12,28},{16,0},{20,4},{24,8},{28,12},{1,17},{... | collective-permute-start | bytes 196616 | tf_op jit(solution)/shard_map/ppermute | solution.py:48
  110.5 1.9 %collective-permute-start.37 = (bf16[1,64,640]{2,1,0:T(8,128)(2,1)S(1)}, bf16[1,64,640]{2,1,0:T(8,128)(2,1)S(1)}, u32[]{:S(2)}, u32[]{:S(2)}) collective-permute-start(bf16[1,64,640]{2,1,0:T(8,128)(2,1)S(1)} %get-tuple-element.187), channel_id=1, source_target_pairs={{0,16},{4,20},{8,24},{12,28},{16,0},{20,4},{24,8},{28,12},{1,17},{... | collective-permute-start | bytes 245768 | tf_op jit(solution)/shard_map/ppermute | solution.py:48
  112.4 1.2 collective-permute-start.35
  114.0 4.9 %collective-permute-done.37.refs_5_.refs_9_ = bf16[1,64,640]{2,1,0:T(8,128)(2,1)S(1)} collective-permute-done((bf16[1,64,640]{2,1,0:T(8,128)(2,1)S(1)}, bf16[1,64,640]{2,1,0:T(8,128)(2,1)S(1)}, u32[]{:S(2)}, u32[]{:S(2)}) %collective-permute-start.37) | collective-permute-done | bytes 81952 | tf_op jit(solution)/shard_map/ppermute | solution.py:48
  119.7 1.2 collective-permute-done.38
  120.9 1.6 %collective-permute-start.39 = (f32[56,128]{1,0:T(8,128)S(1)}, f32[56,128]{1,0:T(8,128)S(1)}, u32[]{:S(2)}, u32[]{:S(2)}) collective-permute-start(f32[56,128]{1,0:T(8,128)S(1)} %add.70), channel_id=1, source_target_pairs={{0,2},{1,3},{2,0},{3,1},{4,6},{5,7},{6,4},{7,5},{8,10},{9,11},{10,... | collective-permute-start | bytes 86024 | tf_op jit(solution)/shard_map/ppermute | solution.py:48
  122.5 1.9 %collective-permute-start.41 = (f32[56,128]{1,0:T(8,128)S(1)}, f32[56,128]{1,0:T(8,128)S(1)}, u32[]{:S(2)}, u32[]{:S(2)}) collective-permute-start(f32[56,128]{1,0:T(8,128)S(1)} %add.70), channel_id=1, source_target_pairs={{0,6},{1,7},{2,4},{3,5},{4,2},{5,3},{6,0},{7,1},{8,14},{9,15},{10,... | collective-permute-start | bytes 86024 | tf_op jit(solution)/shard_map/ppermute | solution.py:91
  124.5 1.3 convert_add_fusion
  126.3 0.9 collective-permute-done.41
  127.3 1.5 %collective-permute-start.42 = (f32[56,128]{1,0:T(8,128)S(1)}, f32[56,128]{1,0:T(8,128)S(1)}, u32[]{:S(2)}, u32[]{:S(2)}) collective-permute-start(f32[56,128]{1,0:T(8,128)S(1)} %add_add_fusion.refs_0_), channel_id=1, source_target_pairs={{0,8},{4,12},{8,0},{12,4},{16,24},{20,28},{24,16},{28,20},{1,9},{5... | collective-permute-start | bytes 86024 | tf_op jit(solution)/shard_map/ppermute | solution.py:48
  128.7 2.9 %collective-permute-start.43 = (f32[56,128]{1,0:T(8,128)S(1)}, f32[56,128]{1,0:T(8,128)S(1)}, u32[]{:S(2)}, u32[]{:S(2)}) collective-permute-start(f32[56,128]{1,0:T(8,128)S(1)} %add_add_fusion.refs_0_), channel_id=1, source_target_pairs={{0,16},{4,20},{8,24},{12,28},{16,0},{20,4},{24,8},{28,12},{1,17},{... | collective-permute-start | bytes 86024 | tf_op jit(solution)/shard_map/ppermute | solution.py:48
  132.4 1.4 %collective-permute-done.43.refs_2_ = f32[56,128]{1,0:T(8,128)S(1)} collective-permute-done((f32[56,128]{1,0:T(8,128)S(1)}, f32[56,128]{1,0:T(8,128)S(1)}, u32[]{:S(2)}, u32[]{:S(2)}) %collective-permute-start.43) | collective-permute-done | bytes 28704 | tf_op jit(solution)/shard_map/ppermute | solution.py:48
  133.8 3.5 %collective-permute-done.44.refs_3_ = f32[56,128]{1,0:T(8,128)S(1)} collective-permute-done((f32[56,128]{1,0:T(8,128)S(1)}, f32[56,128]{1,0:T(8,128)S(1)}, u32[]{:S(2)}, u32[]{:S(2)}) %collective-permute-start.44) | collective-permute-done | bytes 28704 | tf_op jit(solution)/shard_map/ppermute | solution.py:91
  137.4 2.0 %shard_map.455 = (f32[1]{0:T(128)}, f32[6,512]{1,0:T(8,128)}, f32[64,384]{1,0:T(8,128)}, f32[64,384]{1,0:T(8,128)}, f32[64,384]{1,0:T(8,128)}, /*index=5*/bf16[6...) custom-call(s32[2]{0:T(128)S(1)} %pad_add_fusion.idx_ref, ...), custom_call_target="tpu_custom_call" | custom-call | flops 2000000000 | bytes 1048576 | tf_op jit(solution)/shard_map/pallas_call | solution.py:620
  (143 shorter events, 10.2 us)
Async XLA Ops:
  2.1 17.0 %collective-permute-start.6 = (bf16[512,512]{1,0:T(8,128)(2,1)S(1)}, bf16[512,512]{1,0:T(8,128)(2,1)S(1)}, u32[]{:S(2)}, u32[]{:S(2)}) collective-permute-start(bf16[512,512]{1,0:T(8,128)(2,1)S(1)} %convert_element_type.123.refs_0_), channel_id=1, source_target_pairs={{0,2},{1,3},{2,0},{3,1},{4,6},{5,7},{6,4},{7,5},{8,10},{9,11},{10,... | collective-permute-start | bytes 1572872 | tf_op jit(solution)/shard_map/ppermute | solution.py:48
  5.1 24.4 %collective-permute-start.5 = (bf16[512,512]{1,0:T(8,128)(2,1)S(1)}, bf16[512,512]{1,0:T(8,128)(2,1)S(1)}, u32[]{:S(2)}, u32[]{:S(2)}) collective-permute-start(bf16[512,512]{1,0:T(8,128)(2,1)S(1)} %convert_element_type.123.refs_0_), channel_id=1, source_target_pairs={{0,1},{1,0},{2,3},{3,2},{4,5},{5,4},{6,7},{7,6},{8,9},{9,8},{10,11... | collective-permute-start | bytes 1572872 | tf_op jit(solution)/shard_map/ppermute | solution.py:48
  5.3 6.8 %collective-permute-start = (bf16[1,80,384]{2,1,0:T(8,128)(2,1)S(1)}, bf16[1,80,384]{2,1,0:T(8,128)(2,1)S(1)}, u32[]{:S(2)}, u32[]{:S(2)}) collective-permute-start(bf16[1,80,384]{2,1,0:T(8,128)(2,1)S(1)} %fusion.4), channel_id=1, source_target_pairs={{0,16},{4,20},{8,24},{12,28},{16,0},{20,4},{24,8},{28,12},{1,17},{... | collective-permute-start | bytes 184328 | tf_op jit(solution)/shard_map/ppermute | solution.py:48
  8.0 10.4 %collective-permute-start.2 = (bf16[1,64,1152]{2,1,0:T(8,128)(2,1)S(1)}, bf16[1,64,1152]{2,1,0:T(8,128)(2,1)S(1)}, u32[]{:S(2)}, u32[]{:S(2)}) collective-permute-start(bf16[1,64,1152]{2,1,0:T(8,128)(2,1)S(1)} %maximum_bitcast_fusion), channel_id=1, source_target_pairs={{0,16},{4,20},{8,24},{12,28},{16,0},{20,4},{24,8},{28,12},{1,17},{... | collective-permute-start | bytes 442376 | tf_op jit(solution)/shard_map/ppermute | solution.py:48
  12.1 8.9 %collective-permute-start.1 = (bf16[2,80,384]{2,1,0:T(8,128)(2,1)S(1)}, bf16[2,80,384]{2,1,0:T(8,128)(2,1)S(1)}, u32[]{:S(2)}, u32[]{:S(2)}) collective-permute-start(bf16[2,80,384]{2,1,0:T(8,128)(2,1)S(1)} %pad_maximum_fusion.6), channel_id=1, source_target_pairs={{0,8},{4,12},{8,0},{12,4},{16,24},{20,28},{24,16},{28,20},{1,9},{5... | collective-permute-start | bytes 368648 | tf_op jit(solution)/shard_map/ppermute | solution.py:48
  18.4 8.8 %collective-permute-start.3 = (bf16[2,64,1152]{2,1,0:T(8,128)(2,1)S(1)}, bf16[2,64,1152]{2,1,0:T(8,128)(2,1)S(1)}, u32[]{:S(2)}, u32[]{:S(2)}) collective-permute-start(bf16[2,64,1152]{2,1,0:T(8,128)(2,1)S(1)} %pad_maximum_fusion.2), channel_id=1, source_target_pairs={{0,8},{4,12},{8,0},{12,4},{16,24},{20,28},{24,16},{28,20},{1,9},{5... | collective-permute-start | bytes 884744 | tf_op jit(solution)/shard_map/ppermute | solution.py:48
  19.1 10.4 %collective-permute-start.7 = (bf16[512,512]{1,0:T(8,128)(2,1)S(1)}, bf16[512,512]{1,0:T(8,128)(2,1)S(1)}, u32[]{:S(2)}, u32[]{:S(2)}) collective-permute-start(bf16[512,512]{1,0:T(8,128)(2,1)S(1)} %collective-permute-done.6.refs_2_), channel_id=1, source_target_pairs={{0,1},{1,0},{2,3},{3,2},{4,5},{5,4},{6,7},{7,6},{8,9},{9,8},{10,11... | collective-permute-start | bytes 1572872 | tf_op jit(solution)/shard_map/ppermute | solution.py:48
  21.0 8.5 %collective-permute-start.4 = (bf16[4,80,384]{2,1,0:T(8,128)(2,1)S(1)}, bf16[4,80,384]{2,1,0:T(8,128)(2,1)S(1)}, u32[]{:S(2)}, u32[]{:S(2)}) collective-permute-start(bf16[4,80,384]{2,1,0:T(8,128)(2,1)S(1)} %pad_maximum_fusion.5.w_own), channel_id=1, source_target_pairs={{0,4},{4,0},{8,12},{12,8},{16,20},{20,16},{24,28},{28,24},{1,5},{5... | collective-permute-start | bytes 737288 | tf_op jit(solution)/shard_map/ppermute | solution.py:48
  27.3 9.9 %collective-permute-start.9 = (bf16[4,64,640]{2,1,0:T(8,128)(2,1)S(1)}, bf16[4,64,640]{2,1,0:T(8,128)(2,1)S(1)}, u32[]{:S(2)}, u32[]{:S(2)}) collective-permute-start(bf16[4,64,640]{2,1,0:T(8,128)(2,1)S(1)} %pad_maximum_fusion.3), channel_id=1, source_target_pairs={{0,2},{1,3},{2,0},{3,1},{4,6},{5,7},{6,4},{7,5},{8,10},{9,11},{10,... | collective-permute-start | bytes 983048 | tf_op jit(solution)/shard_map/ppermute | solution.py:48
  27.9 9.7 %collective-permute-start.8 = (bf16[4,64,512]{2,1,0:T(8,128)(2,1)S(1)}, bf16[4,64,512]{2,1,0:T(8,128)(2,1)S(1)}, u32[]{:S(2)}, u32[]{:S(2)}) collective-permute-start(bf16[4,64,512]{2,1,0:T(8,128)(2,1)S(1)} %pad_maximum_fusion.4), channel_id=1, source_target_pairs={{0,4},{4,0},{8,12},{12,8},{16,20},{20,16},{24,28},{28,24},{1,5},{5... | collective-permute-start | bytes 786440 | tf_op jit(solution)/shard_map/ppermute | solution.py:48
  37.3 15.3 %collective-permute-start.16 = (bf16[8,64,640]{2,1,0:T(8,128)(2,1)S(1)}, bf16[8,64,640]{2,1,0:T(8,128)(2,1)S(1)}, u32[]{:S(2)}, u32[]{:S(2)}) collective-permute-start(bf16[8,64,640]{2,1,0:T(8,128)(2,1)S(1)} %pad_maximum_fusion.refs_8_), channel_id=1, source_target_pairs={{0,4},{4,0},{8,12},{12,8},{16,20},{20,16},{24,28},{28,24},{1,5},{5... | collective-permute-start | bytes 1966088 | tf_op jit(solution)/shard_map/ppermute | solution.py:48
  37.6 20.2 %copy-start.7 = (f32[512,512]{1,0:T(8,128)S(1)}, f32[512,512]{1,0:T(8,128)}, u32[]{:S(2)}) copy-start(f32[512,512]{1,0:T(8,128)} %refs_15_.2) | copy-start | bytes 3145732
  37.7 17.1 %collective-permute-start.13 = (bf16[8,64,512]{2,1,0:T(8,128)(2,1)S(1)}, bf16[8,64,512]{2,1,0:T(8,128)(2,1)S(1)}, u32[]{:S(2)}, u32[]{:S(2)}) collective-permute-start(bf16[8,64,512]{2,1,0:T(8,128)(2,1)S(1)} %pad_maximum_fusion.1.refs_4_), channel_id=1, source_target_pairs={{0,2},{1,3},{2,0},{3,1},{4,6},{5,7},{6,4},{7,5},{8,10},{9,11},{10,... | collective-permute-start | bytes 1572872 | tf_op jit(solution)/shard_map/ppermute | solution.py:48
  38.3 16.4 %collective-permute-start.11 = (bf16[528,128]{1,0:T(8,128)(2,1)S(1)}, bf16[528,128]{1,0:T(8,128)(2,1)S(1)}, u32[]{:S(2)}, u32[]{:S(2)}) collective-permute-start(bf16[528,128]{1,0:T(8,128)(2,1)S(1)} %get-tuple-element.114.refs_6_), channel_id=1, source_target_pairs={{0,2},{1,3},{2,0},{3,1},{4,6},{5,7},{6,4},{7,5},{8,10},{9,11},{10,... | collective-permute-start | bytes 405512 | tf_op jit(solution)/shard_map/ppermute | solution.py:760
  39.7 18.0 %collective-permute-start.17 = (bf16[8,64,640]{2,1,0:T(8,128)(2,1)S(1)}, bf16[8,64,640]{2,1,0:T(8,128)(2,1)S(1)}, u32[]{:S(2)}, u32[]{:S(2)}) collective-permute-start(bf16[8,64,640]{2,1,0:T(8,128)(2,1)S(1)} %pad_maximum_fusion.refs_8_), channel_id=1, source_target_pairs={{0,1},{1,0},{2,3},{3,2},{4,5},{5,4},{6,7},{7,6},{8,9},{9,8},{10,11... | collective-permute-start | bytes 1966088 | tf_op jit(solution)/shard_map/ppermute | solution.py:48
  39.8 18.1 %copy-start.6 = (f32[512,512]{1,0:T(8,128)S(1)}, f32[512,512]{1,0:T(8,128)}, u32[]{:S(2)}) copy-start(f32[512,512]{1,0:T(8,128)} %refs_14_.2) | copy-start | bytes 3145732
  39.8 18.1 %copy-start.16 = (f32[6,512]{1,0:T(8,128)S(1)}, f32[6,512]{1,0:T(8,128)}, u32[]{:S(2)}) copy-start(f32[6,512]{1,0:T(8,128)} %refs_15_.3) | copy-start | bytes 36868
  39.8 15.0 %collective-permute-start.12 = (bf16[528,128]{1,0:T(8,128)(2,1)S(1)}, bf16[528,128]{1,0:T(8,128)(2,1)S(1)}, u32[]{:S(2)}, u32[]{:S(2)}) collective-permute-start(bf16[528,128]{1,0:T(8,128)(2,1)S(1)} %get-tuple-element.120.refs_7_), channel_id=1, source_target_pairs={{0,3},{1,2},{2,1},{3,0},{4,7},{5,6},{6,5},{7,4},{8,11},{9,10},{10,... | collective-permute-start | bytes 405512 | tf_op jit(solution)/shard_map/ppermute | solution.py:760
  52.6 5.2 %collective-permute-start.18 = (bf16[8,64,640]{2,1,0:T(8,128)(2,1)S(1)}, bf16[8,64,640]{2,1,0:T(8,128)(2,1)S(1)}, u32[]{:S(2)}, u32[]{:S(2)}) collective-permute-start(bf16[8,64,640]{2,1,0:T(8,128)(2,1)S(1)} %collective-permute-done.16.refs_9_), channel_id=1, source_target_pairs={{0,1},{1,0},{2,3},{3,2},{4,5},{5,4},{6,7},{7,6},{8,9},{9,8},{10,11... | collective-permute-start | bytes 1966088 | tf_op jit(solution)/shard_map/ppermute | solution.py:48
  54.8 3.0 %collective-permute-start.14 = (bf16[8,64,512]{2,1,0:T(8,128)(2,1)S(1)}, bf16[8,64,512]{2,1,0:T(8,128)(2,1)S(1)}, u32[]{:S(2)}, u32[]{:S(2)}) collective-permute-start(bf16[8,64,512]{2,1,0:T(8,128)(2,1)S(1)} %pad_maximum_fusion.1.refs_4_), channel_id=1, source_target_pairs={{0,1},{1,0},{2,3},{3,2},{4,5},{5,4},{6,7},{7,6},{8,9},{9,8},{10,11... | collective-permute-start | bytes 1572872 | tf_op jit(solution)/shard_map/ppermute | solution.py:48
  54.8 3.0 %collective-permute-start.15 = (bf16[8,64,512]{2,1,0:T(8,128)(2,1)S(1)}, bf16[8,64,512]{2,1,0:T(8,128)(2,1)S(1)}, u32[]{:S(2)}, u32[]{:S(2)}) collective-permute-start(bf16[8,64,512]{2,1,0:T(8,128)(2,1)S(1)} %collective-permute-done.13.refs_5_), channel_id=1, source_target_pairs={{0,1},{1,0},{2,3},{3,2},{4,5},{5,4},{6,7},{7,6},{8,9},{9,8},{10,11... | collective-permute-start | bytes 1572872 | tf_op jit(solution)/shard_map/ppermute | solution.py:48
  56.0 1.7 %collective-permute-start.10 = (bf16[528,128]{1,0:T(8,128)(2,1)S(1)}, bf16[528,128]{1,0:T(8,128)(2,1)S(1)}, u32[]{:S(2)}, u32[]{:S(2)}) collective-permute-start(bf16[528,128]{1,0:T(8,128)(2,1)S(1)} %get-tuple-element.119.refs_5_), channel_id=1, source_target_pairs={{0,1},{1,0},{2,3},{3,2},{4,5},{5,4},{6,7},{7,6},{8,9},{9,8},{10,11... | collective-permute-start | bytes 405512 | tf_op jit(solution)/shard_map/ppermute | solution.py:760
  69.2 2.7 %collective-permute-start.19 = (bf16[16,64,512]{2,1,0:T(8,128)(2,1)S(1)}, bf16[16,64,512]{2,1,0:T(8,128)(2,1)S(1)}, u32[]{:S(2)}, u32[]{:S(2)}) collective-permute-start(bf16[16,64,512]{2,1,0:T(8,128)(2,1)S(1)} %get-tuple-element.132), channel_id=1, source_target_pairs={{0,1},{1,0},{2,3},{3,2},{4,5},{5,4},{6,7},{7,6},{8,9},{9,8},{10,11... | collective-permute-start | bytes 3145736 | tf_op jit(solution)/shard_map/ppermute | solution.py:48
  69.6 4.2 %collective-permute-start.20 = (bf16[16,64,640]{2,1,0:T(8,128)(2,1)S(1)}, bf16[16,64,640]{2,1,0:T(8,128)(2,1)S(1)}, u32[]{:S(2)}, u32[]{:S(2)}) collective-permute-start(bf16[16,64,640]{2,1,0:T(8,128)(2,1)S(1)} %get-tuple-element.134), channel_id=1, source_target_pairs={{0,1},{1,0},{2,3},{3,2},{4,5},{5,4},{6,7},{7,6},{8,9},{9,8},{10,11... | collective-permute-start | bytes 3932168 | tf_op jit(solution)/shard_map/ppermute | solution.py:48
  69.7 6.1 %collective-permute-start.21 = (bf16[512,128]{1,0:T(8,128)(2,1)S(1)}, bf16[512,128]{1,0:T(8,128)(2,1)S(1)}, u32[]{:S(2)}, u32[]{:S(2)}) collective-permute-start(bf16[512,128]{1,0:T(8,128)(2,1)S(1)} %get-tuple-element.136), channel_id=1, source_target_pairs={{0,1},{1,0},{2,3},{3,2},{4,5},{5,4},{6,7},{7,6},{8,9},{9,8},{10,11... | collective-permute-start | bytes 393224 | tf_op jit(solution)/shard_map/ppermute | solution.py:805
  70.1 6.3 %collective-permute-start.22 = (bf16[512,128]{1,0:T(8,128)(2,1)S(1)}, bf16[512,128]{1,0:T(8,128)(2,1)S(1)}, u32[]{:S(2)}, u32[]{:S(2)}) collective-permute-start(bf16[512,128]{1,0:T(8,128)(2,1)S(1)} %get-tuple-element.137), channel_id=1, source_target_pairs={{0,2},{1,3},{2,0},{3,1},{4,6},{5,7},{6,4},{7,5},{8,10},{9,11},{10,... | collective-permute-start | bytes 393224 | tf_op jit(solution)/shard_map/ppermute | solution.py:805
  70.4 7.3 %collective-permute-start.23 = (bf16[512,128]{1,0:T(8,128)(2,1)S(1)}, bf16[512,128]{1,0:T(8,128)(2,1)S(1)}, u32[]{:S(2)}, u32[]{:S(2)}) collective-permute-start(bf16[512,128]{1,0:T(8,128)(2,1)S(1)} %get-tuple-element.138), channel_id=1, source_target_pairs={{0,3},{1,2},{2,1},{3,0},{4,7},{5,6},{6,5},{7,4},{8,11},{9,10},{10,... | collective-permute-start | bytes 393224 | tf_op jit(solution)/shard_map/ppermute | solution.py:805
  72.3 18.7 %collective-permute-start.24 = (bf16[8,64,512]{2,1,0:T(8,128)(2,1)S(1)}, bf16[8,64,512]{2,1,0:T(8,128)(2,1)S(1)}, u32[]{:S(2)}, u32[]{:S(2)}) collective-permute-start(bf16[8,64,512]{2,1,0:T(8,128)(2,1)S(1)} %slice.130), channel_id=1, source_target_pairs={{0,4},{4,0},{8,12},{12,8},{16,20},{20,16},{24,28},{28,24},{1,5},{5... | collective-permute-start | bytes 1572872 | tf_op jit(solution)/shard_map/ppermute | solution.py:48
  74.2 17.3 %collective-permute-start.25 = (bf16[8,64,640]{2,1,0:T(8,128)(2,1)S(1)}, bf16[8,64,640]{2,1,0:T(8,128)(2,1)S(1)}, u32[]{:S(2)}, u32[]{:S(2)}) collective-permute-start(bf16[8,64,640]{2,1,0:T(8,128)(2,1)S(1)} %slice.131), channel_id=1, source_target_pairs={{0,8},{4,12},{8,0},{12,4},{16,24},{20,28},{24,16},{28,20},{1,9},{5... | collective-permute-start | bytes 1966088 | tf_op jit(solution)/shard_map/ppermute | solution.py:48
  91.2 9.2 %collective-permute-start.29 = (bf16[4,64,512]{2,1,0:T(8,128)(2,1)S(1)}, bf16[4,64,512]{2,1,0:T(8,128)(2,1)S(1)}, u32[]{:S(2)}, u32[]{:S(2)}) collective-permute-start(bf16[4,64,512]{2,1,0:T(8,128)(2,1)S(1)} %slice.133), channel_id=1, source_target_pairs={{0,2},{1,3},{2,0},{3,1},{4,6},{5,7},{6,4},{7,5},{8,10},{9,11},{10,... | collective-permute-start | bytes 786440 | tf_op jit(solution)/shard_map/ppermute | solution.py:48
  91.8 10.3 %collective-permute-start.28 = (bf16[4,64,640]{2,1,0:T(8,128)(2,1)S(1)}, bf16[4,64,640]{2,1,0:T(8,128)(2,1)S(1)}, u32[]{:S(2)}, u32[]{:S(2)}) collective-permute-start(bf16[4,64,640]{2,1,0:T(8,128)(2,1)S(1)} %slice.135), channel_id=1, source_target_pairs={{0,4},{4,0},{8,12},{12,8},{16,20},{20,16},{24,28},{28,24},{1,5},{5... | collective-permute-start | bytes 983048 | tf_op jit(solution)/shard_map/ppermute | solution.py:48
  96.6 7.4 %collective-permute-start.27 = (bf16[512,512]{1,0:T(8,128)(2,1)S(1)}, bf16[512,512]{1,0:T(8,128)(2,1)S(1)}, u32[]{:S(2)}, u32[]{:S(2)}) collective-permute-start(bf16[512,512]{1,0:T(8,128)(2,1)S(1)} %get-tuple-element.147), channel_id=1, source_target_pairs={{0,1},{1,0},{2,3},{3,2},{4,5},{5,4},{6,7},{7,6},{8,9},{9,8},{10,11... | collective-permute-start | bytes 1572872 | tf_op jit(solution)/shard_map/ppermute | solution.py:48
  96.7 7.9 %collective-permute-start.26 = (bf16[4,64,384]{2,1,0:T(8,128)(2,1)S(1)}, bf16[4,64,384]{2,1,0:T(8,128)(2,1)S(1)}, u32[]{:S(2)}, u32[]{:S(2)}) collective-permute-start(bf16[4,64,384]{2,1,0:T(8,128)(2,1)S(1)} %slice.136), channel_id=1, source_target_pairs={{0,8},{4,12},{8,0},{12,4},{16,24},{20,28},{24,16},{28,20},{1,9},{5... | collective-permute-start | bytes 589832 | tf_op jit(solution)/shard_map/ppermute | solution.py:48
  100.4 6.5 %collective-permute-start.32 = (bf16[2,64,512]{2,1,0:T(8,128)(2,1)S(1)}, bf16[2,64,512]{2,1,0:T(8,128)(2,1)S(1)}, u32[]{:S(2)}, u32[]{:S(2)}) collective-permute-start(bf16[2,64,512]{2,1,0:T(8,128)(2,1)S(1)} %slice.140), channel_id=1, source_target_pairs={{0,8},{4,12},{8,0},{12,4},{16,24},{20,28},{24,16},{28,20},{1,9},{5... | collective-permute-start | bytes 393224 | tf_op jit(solution)/shard_map/ppermute | solution.py:48
  102.0 17.7 %collective-permute-start.33 = (bf16[512,512]{1,0:T(8,128)(2,1)S(1)}, bf16[512,512]{1,0:T(8,128)(2,1)S(1)}, u32[]{:S(2)}, u32[]{:S(2)}) collective-permute-start(bf16[512,512]{1,0:T(8,128)(2,1)S(1)} %get-tuple-element.156), channel_id=1, source_target_pairs={{0,1},{1,0},{2,3},{3,2},{4,5},{5,4},{6,7},{7,6},{8,9},{9,8},{10,11... | collective-permute-start | bytes 1572872 | tf_op jit(solution)/shard_map/ppermute | solution.py:48
  102.2 8.2 %collective-permute-start.31 = (bf16[2,64,640]{2,1,0:T(8,128)(2,1)S(1)}, bf16[2,64,640]{2,1,0:T(8,128)(2,1)S(1)}, u32[]{:S(2)}, u32[]{:S(2)}) collective-permute-start(bf16[2,64,640]{2,1,0:T(8,128)(2,1)S(1)} %slice.141), channel_id=1, source_target_pairs={{0,2},{1,3},{2,0},{3,1},{4,6},{5,7},{6,4},{7,5},{8,10},{9,11},{10,... | collective-permute-start | bytes 491528 | tf_op jit(solution)/shard_map/ppermute | solution.py:48
  104.1 20.3 %collective-permute-start.34 = (bf16[512,512]{1,0:T(8,128)(2,1)S(1)}, bf16[512,512]{1,0:T(8,128)(2,1)S(1)}, u32[]{:S(2)}, u32[]{:S(2)}) collective-permute-start(bf16[512,512]{1,0:T(8,128)(2,1)S(1)} %add_convert_fusion.3), channel_id=1, source_target_pairs={{0,2},{1,3},{2,0},{3,1},{4,6},{5,7},{6,4},{7,5},{8,10},{9,11},{10,... | collective-permute-start | bytes 1572872 | tf_op jit(solution)/shard_map/ppermute | solution.py:48
  104.6 7.7 %collective-permute-start.30 = (bf16[2,64,384]{2,1,0:T(8,128)(2,1)S(1)}, bf16[2,64,384]{2,1,0:T(8,128)(2,1)S(1)}, u32[]{:S(2)}, u32[]{:S(2)}) collective-permute-start(bf16[2,64,384]{2,1,0:T(8,128)(2,1)S(1)} %slice.143), channel_id=1, source_target_pairs={{0,4},{4,0},{8,12},{12,8},{16,20},{20,16},{24,28},{28,24},{1,5},{5... | collective-permute-start | bytes 294920 | tf_op jit(solution)/shard_map/ppermute | solution.py:48
  107.0 7.0 %collective-permute-start.36 = (bf16[1,64,512]{2,1,0:T(8,128)(2,1)S(1)}, bf16[1,64,512]{2,1,0:T(8,128)(2,1)S(1)}, u32[]{:S(2)}, u32[]{:S(2)}) collective-permute-start(bf16[1,64,512]{2,1,0:T(8,128)(2,1)S(1)} %get-tuple-element.189), channel_id=1, source_target_pairs={{0,16},{4,20},{8,24},{12,28},{16,0},{20,4},{24,8},{28,12},{1,17},{... | collective-permute-start | bytes 196616 | tf_op jit(solution)/shard_map/ppermute | solution.py:48
  110.5 8.4 %collective-permute-start.37 = (bf16[1,64,640]{2,1,0:T(8,128)(2,1)S(1)}, bf16[1,64,640]{2,1,0:T(8,128)(2,1)S(1)}, u32[]{:S(2)}, u32[]{:S(2)}) collective-permute-start(bf16[1,64,640]{2,1,0:T(8,128)(2,1)S(1)} %get-tuple-element.187), channel_id=1, source_target_pairs={{0,16},{4,20},{8,24},{12,28},{16,0},{20,4},{24,8},{28,12},{1,17},{... | collective-permute-start | bytes 245768 | tf_op jit(solution)/shard_map/ppermute | solution.py:48
  112.4 7.1 %collective-permute-start.35 = (bf16[1,64,384]{2,1,0:T(8,128)(2,1)S(1)}, bf16[1,64,384]{2,1,0:T(8,128)(2,1)S(1)}, u32[]{:S(2)}, u32[]{:S(2)}) collective-permute-start(bf16[1,64,384]{2,1,0:T(8,128)(2,1)S(1)} %get-tuple-element.191), channel_id=1, source_target_pairs={{0,16},{4,20},{8,24},{12,28},{16,0},{20,4},{24,8},{28,12},{1,17},{... | collective-permute-start | bytes 147464 | tf_op jit(solution)/shard_map/ppermute | solution.py:48
  119.6 1.3 collective-permute-start.38
  120.9 4.9 %collective-permute-start.39 = (f32[56,128]{1,0:T(8,128)S(1)}, f32[56,128]{1,0:T(8,128)S(1)}, u32[]{:S(2)}, u32[]{:S(2)}) collective-permute-start(f32[56,128]{1,0:T(8,128)S(1)} %add.70), channel_id=1, source_target_pairs={{0,2},{1,3},{2,0},{3,1},{4,6},{5,7},{6,4},{7,5},{8,10},{9,11},{10,... | collective-permute-start | bytes 86024 | tf_op jit(solution)/shard_map/ppermute | solution.py:48
  122.5 3.9 %collective-permute-start.40 = (f32[56,128]{1,0:T(8,128)S(1)}, f32[56,128]{1,0:T(8,128)S(1)}, u32[]{:S(2)}, u32[]{:S(2)}) collective-permute-start(f32[56,128]{1,0:T(8,128)S(1)} %add.70), channel_id=1, source_target_pairs={{0,4},{4,0},{8,12},{12,8},{16,20},{20,16},{24,28},{28,24},{1,5},{5... | collective-permute-start | bytes 86024 | tf_op jit(solution)/shard_map/ppermute | solution.py:48
  122.5 4.8 %collective-permute-start.41 = (f32[56,128]{1,0:T(8,128)S(1)}, f32[56,128]{1,0:T(8,128)S(1)}, u32[]{:S(2)}, u32[]{:S(2)}) collective-permute-start(f32[56,128]{1,0:T(8,128)S(1)} %add.70), channel_id=1, source_target_pairs={{0,6},{1,7},{2,4},{3,5},{4,2},{5,3},{6,0},{7,1},{8,14},{9,15},{10,... | collective-permute-start | bytes 86024 | tf_op jit(solution)/shard_map/ppermute | solution.py:91
  127.3 5.1 %collective-permute-start.42 = (f32[56,128]{1,0:T(8,128)S(1)}, f32[56,128]{1,0:T(8,128)S(1)}, u32[]{:S(2)}, u32[]{:S(2)}) collective-permute-start(f32[56,128]{1,0:T(8,128)S(1)} %add_add_fusion.refs_0_), channel_id=1, source_target_pairs={{0,8},{4,12},{8,0},{12,4},{16,24},{20,28},{24,16},{28,20},{1,9},{5... | collective-permute-start | bytes 86024 | tf_op jit(solution)/shard_map/ppermute | solution.py:48
  128.7 5.1 %collective-permute-start.43 = (f32[56,128]{1,0:T(8,128)S(1)}, f32[56,128]{1,0:T(8,128)S(1)}, u32[]{:S(2)}, u32[]{:S(2)}) collective-permute-start(f32[56,128]{1,0:T(8,128)S(1)} %add_add_fusion.refs_0_), channel_id=1, source_target_pairs={{0,16},{4,20},{8,24},{12,28},{16,0},{20,4},{24,8},{28,12},{1,17},{... | collective-permute-start | bytes 86024 | tf_op jit(solution)/shard_map/ppermute | solution.py:48
  131.6 5.7 %collective-permute-start.44 = (f32[56,128]{1,0:T(8,128)S(1)}, f32[56,128]{1,0:T(8,128)S(1)}, u32[]{:S(2)}, u32[]{:S(2)}) collective-permute-start(f32[56,128]{1,0:T(8,128)S(1)} %add_add_fusion.refs_0_), channel_id=1, source_target_pairs={{0,24},{1,25},{2,26},{3,27},{4,28},{5,29},{6,30},{7,31},{8,16},{9,... | collective-permute-start | bytes 86024 | tf_op jit(solution)/shard_map/ppermute | solution.py:91
  (20 other events, 225.3 us)
